TPU v7x, 128 devices: a whole 4x4x4 slice. The times are simulated.
128 devices in a mesh: dp: 4 (over x_lo, core), seq: 32 (over y, x_hi, z).
Axes of the slice: x: 4 (x_hi: 2, x_lo: 2; x = x_hi * 2 + x_lo), y: 4, z: 4, core: 2. Of those that a mesh axis runs over, the one named last changes fastest.
Arguments:
- hist_x: bfloat16 [4, 4096, 1024], P('dp', 'seq'), may hold values from -6 to 6
- hist_cot: bfloat16 [4, 4096, 1024], P('dp', 'seq'), may hold values from -6 to 6
- cand_x: bfloat16 [32768, 1024], P(('dp', 'seq')), may hold values from -6 to 6
- cand_loop: int32 [32768, 1], P(('dp', 'seq')), may hold values from 0 to 3; in each aligned block of 256 rows (0 to 255, 256 to 511, ...) at most 128 rows name the same one
- hist_len: int32 [4], P('dp'), may hold values from 512 to 4096, as said below
- w_proj: bfloat16 [1024, 2048], replicated, may hold values from -0.1875 to 0.1875
- w_out: bfloat16 [512, 1024], replicated, may hold values from -0.25 to 0.25
Outputs:
- hist_out: bfloat16 [4, 4096, 1024], P('dp', 'seq')
- hist_grad: bfloat16 [4, 4096, 1024], P('dp', 'seq')
- cand_out: bfloat16 [32768, 1024], P(('dp', 'seq'))
Inputs may be any that keep to these rules, and one draw needn't show every extreme that they name: `cand_loop`: among the 256 rows of one device (aligned blocks) no user is named more than 128 times, and some block names one user exactly 128 times. `hist_len`: one user's history fills all 4096 events.
All inputs are finite; a program needn't handle non-finite values.
Results may differ from a plain program's by a relative error of at most 0.022.
Values may be sent and summed in bfloat16 or wider, within the bound.
No kernel may reach another device: no remote copies, remote signals or barrier semaphores. Data moves between devices by JAX's collectives and lax.ppermute only.
A program may use at most 64 MiB of HBM per device.

v0:
```python
import jax
import jax.numpy as jnp
from jax import lax
from jax.sharding import PartitionSpec as P

HS = 128
CAP = 128


layer_eps = 1e-05


def passed_along(value, axis, steps):
    count = lax.axis_size(axis)
    pairs = [(source, (source + steps) % count) for source in range(count)]
    return lax.ppermute(value, axis, pairs)


def normalize(values):
    center = values - jnp.mean(values, axis=-1, keepdims=True)
    spread = lax.rsqrt(jnp.mean(center * center, axis=-1, keepdims=True) + layer_eps)
    return (center * spread, spread)


def norm_back(grad_in, normed, spread):
    return spread * (
        grad_in
        - jnp.mean(grad_in, axis=-1, keepdims=True)
        - normed * jnp.mean(grad_in * normed, axis=-1, keepdims=True)
    )


def silu_slope(pre_act):
    sigmoid_gate = jax.nn.sigmoid(pre_act)
    return sigmoid_gate * (1.0 + pre_act * (1.0 - sigmoid_gate))


def attend(queries, key_block, value_block, weight):
    score_scale = queries.shape[2] ** (-0.5)
    scores = (
        jnp.einsum("rhe,khe->hrk", queries, key_block, preferred_element_type=jnp.float32)
        * score_scale
    )
    probabilities = (scores * jax.nn.sigmoid(scores) * weight[None]).astype(jnp.bfloat16)
    return jnp.einsum(
        "hrk,khe->rhe", probabilities, value_block, preferred_element_type=jnp.float32
    )


def attend_grads(queries, grad_att, key_block, value_block, weight):
    score_scale = queries.shape[2] ** (-0.5)
    scores = (
        jnp.einsum("rhe,khe->hrk", queries, key_block, preferred_element_type=jnp.float32)
        * score_scale
    )
    sigmoid_gate = jax.nn.sigmoid(scores)
    probabilities = (scores * sigmoid_gate * weight[None]).astype(jnp.bfloat16)
    grad_probs = jnp.einsum(
        "rhe,khe->hrk", grad_att, value_block, preferred_element_type=jnp.float32
    )
    grad_scores = (
        grad_probs * sigmoid_gate * (1.0 + scores * (1.0 - sigmoid_gate)) * weight[None]
    ).astype(jnp.bfloat16)
    grad_q = (
        jnp.einsum("hrk,khe->rhe", grad_scores, key_block, preferred_element_type=jnp.float32)
        * score_scale
    )
    grad_k = (
        jnp.einsum("hrk,rhe->khe", grad_scores, queries, preferred_element_type=jnp.float32)
        * score_scale
    )
    grad_v = jnp.einsum("hrk,rhe->khe", probabilities, grad_att, preferred_element_type=jnp.float32)
    return (grad_q, grad_k, grad_v)


def per_device(hist_x, hist_cot, cand_x, cand_loop, hist_len, w_proj, w_out):
    rows_dev = hist_x.shape[1]
    att_width = w_out.shape[0]
    head_count = att_width // HS
    loop_size = lax.axis_size("seq")
    position = lax.axis_index("seq")
    group_count = lax.axis_size("dp")
    slot_count = group_count * CAP
    length = hist_len[0]
    inv_len = 1.0 / length.astype(jnp.float32)
    x_rows = hist_x[0].astype(jnp.float32)
    x_normed, x_spread = normalize(x_rows)
    pre_act = jnp.dot(x_normed.astype(jnp.bfloat16), w_proj, preferred_element_type=jnp.float32)
    hidden = (pre_act * jax.nn.sigmoid(pre_act)).astype(jnp.bfloat16)
    gate_rows = hidden[:, :att_width]
    value_rows = hidden[:, att_width : 2 * att_width].reshape(rows_dev, head_count, HS)
    query_rows = hidden[:, 2 * att_width : 3 * att_width].reshape(rows_dev, head_count, HS)
    key_rows = hidden[:, 3 * att_width :].reshape(rows_dev, head_count, HS)
    cand_rows = cand_x.astype(jnp.float32)
    cand_normed, _ = normalize(cand_rows)
    cand_in = cand_normed.astype(jnp.bfloat16)
    cand_u_pre = jnp.dot(cand_in, w_proj[:, :att_width], preferred_element_type=jnp.float32)
    cand_q_pre = jnp.dot(
        cand_in, w_proj[:, 2 * att_width : 3 * att_width], preferred_element_type=jnp.float32
    )
    cand_gate = (cand_u_pre * jax.nn.sigmoid(cand_u_pre)).astype(jnp.bfloat16)
    cand_query = (cand_q_pre * jax.nn.sigmoid(cand_q_pre)).astype(jnp.bfloat16)
    loop_ids = cand_loop[:, 0]
    loop_hits = (loop_ids[:, None] == jnp.arange(group_count, dtype=jnp.int32)[None, :]).astype(
        jnp.int32
    )
    loop_rank = jnp.sum((jnp.cumsum(loop_hits, axis=0) - 1) * loop_hits, axis=1)
    slot_index = loop_ids * CAP + loop_rank
    dispatch = jnp.arange(slot_count, dtype=jnp.int32)[:, None] == slot_index[None, :]
    sent_rows = jnp.dot(
        dispatch.astype(jnp.bfloat16), cand_query, preferred_element_type=jnp.float32
    ).astype(jnp.bfloat16)
    arrived = lax.all_to_all(
        sent_rows.reshape(group_count, CAP, att_width),
        "dp",
        split_axis=0,
        concat_axis=0,
        tiled=True,
    )
    arrived = arrived.reshape(slot_count, head_count, HS)
    local_pos = jnp.arange(rows_dev, dtype=jnp.int32)

    def pair_weight(query_owner, key_owner):
        query_pos = query_owner * rows_dev + local_pos
        key_pos = key_owner * rows_dev + local_pos
        return jnp.where(
            (key_pos[None, :] <= query_pos[:, None]) & (key_pos[None, :] < length), inv_len, 0.0
        )

    def cand_weight(key_owner):
        key_pos = key_owner * rows_dev + local_pos
        return jnp.broadcast_to(
            jnp.where(key_pos < length, inv_len, 0.0)[None, :], (slot_count, rows_dev)
        )

    def contribute(owner_index, key_block, value_block):
        hist_part = attend(query_rows, key_block, value_block, pair_weight(position, owner_index))
        cand_part = attend(arrived, key_block, value_block, cand_weight(owner_index))
        return (hist_part, cand_part)

    hist_start, cand_start = contribute(position, key_rows, value_rows)

    def turn_one(turn_index, state_tuple):
        key_block, value_block, hist_total, cand_total = state_tuple
        key_block, value_block = passed_along((key_block, value_block), "seq", 1)
        hist_more, cand_more = contribute(
            (position - turn_index) % loop_size, key_block, value_block
        )
        return (key_block, value_block, hist_total + hist_more, cand_total + cand_more)

    final_state = lax.fori_loop(
        1, loop_size, turn_one, (key_rows, value_rows, hist_start, cand_start)
    )
    hist_att = final_state[2]
    cand_att = final_state[3]
    att_normed, att_spread = normalize(hist_att.reshape(rows_dev, att_width))
    gate_f = gate_rows.astype(jnp.float32)
    mixed_rows = (att_normed * gate_f).astype(jnp.bfloat16)
    hist_out = (x_rows + jnp.dot(mixed_rows, w_out, preferred_element_type=jnp.float32)).astype(
        jnp.bfloat16
    )
    returned = lax.all_to_all(
        cand_att.reshape(group_count, CAP, att_width).astype(jnp.bfloat16),
        "dp",
        split_axis=0,
        concat_axis=0,
        tiled=True,
    ).astype(jnp.float32)
    cand_flat = jnp.dot(
        dispatch.astype(jnp.float32).T,
        returned.reshape(slot_count, att_width),
        precision=lax.Precision.HIGHEST,
    )
    cand_att_normed, _ = normalize(cand_flat)
    cand_mixed = (cand_att_normed * cand_gate.astype(jnp.float32)).astype(jnp.bfloat16)
    cand_out = (cand_rows + jnp.dot(cand_mixed, w_out, preferred_element_type=jnp.float32)).astype(
        jnp.bfloat16
    )
    cot_rows = hist_cot[0]
    grad_mixed = jnp.dot(cot_rows, w_out.T, preferred_element_type=jnp.float32)
    grad_gate = grad_mixed * att_normed
    grad_att = (
        norm_back(grad_mixed * gate_f, att_normed, att_spread)
        .astype(jnp.bfloat16)
        .reshape(rows_dev, head_count, HS)
    )
    zero_rows = jnp.zeros((rows_dev, head_count, HS), jnp.float32)

    def carry_turn(turn_index, state_tuple):
        key_block, value_block, key_total, value_total, query_total = state_tuple
        more_q, more_k, more_v = attend_grads(
            query_rows,
            grad_att,
            key_block,
            value_block,
            pair_weight(position, (position - turn_index) % loop_size),
        )
        key_block, value_block, key_total, value_total = (
            passed_along(key_block.astype(jnp.float32), "seq", 1).astype(key_block.dtype),
            passed_along(value_block.astype(jnp.float32), "seq", 1).astype(value_block.dtype),
            passed_along(key_total + more_k, "seq", 1),
            passed_along(value_total + more_v, "seq", 1),
        )
        return (key_block, value_block, key_total, value_total, query_total + more_q)

    carry_state = lax.fori_loop(
        0, loop_size, carry_turn, (key_rows, value_rows, zero_rows, zero_rows, zero_rows)
    )
    key_grad = carry_state[2]
    value_grad = carry_state[3]
    query_grad = carry_state[4]
    grad_hidden = jnp.concatenate(
        [
            grad_gate,
            value_grad.reshape(rows_dev, att_width),
            query_grad.reshape(rows_dev, att_width),
            key_grad.reshape(rows_dev, att_width),
        ],
        axis=1,
    )
    grad_pre = (grad_hidden * silu_slope(pre_act)).astype(jnp.bfloat16)
    grad_in = jnp.dot(grad_pre, w_proj.T, preferred_element_type=jnp.float32)
    hist_grad = (cot_rows.astype(jnp.float32) + norm_back(grad_in, x_normed, x_spread)).astype(
        jnp.bfloat16
    )
    return (hist_out[None], hist_grad[None], cand_out)


def solution(mesh):
    in_specs = (
        P("dp", "seq", None),
        P("dp", "seq", None),
        P(("dp", "seq"), None),
        P(("dp", "seq"), None),
        P("dp"),
        P(),
        P(),
    )
    out_specs = (P("dp", "seq", None), P("dp", "seq", None), P(("dp", "seq"), None))
    return jax.shard_map(
        per_device, mesh=mesh, in_specs=in_specs, out_specs=out_specs, check_vma=False
    )
```

profile of v0, /device:TPU:0, one launch (start us, length us, event | category | flops | bytes accessed | tf_op | source)
XLA Modules:
  0.0 1293.7 jit_solution(149557095986473041)
XLA Ops:
  26.6 515.3 %while.48 = (s32[]{:T(128)}, bf16[128,4,128]{2,0,1:T(8,128)(2,1)}, bf16[128,4,128]{2,0,1:T(8,128)(2,1)}, f32[128,4,128]{2,0,1:T(8,128)S(1)}, f32[512,4,128]{2,0,...) while((s32[]{:T(128)}, bf16[128,4,128]{2,0,1:T(8,128)(2,1)}, ...), condition=%wide.region_8.9_spmd.clone.clone, body=%wide.region_7.8_spmd.clone.clone.sunk | while | flops 170443408 | bytes 5508738 | solution.py:151
  47.7 10.9 collective-permute-done
  65.1 10.0 collective-permute-done
  81.7 9.4 collective-permute-done
  97.6 9.4 collective-permute-done
  113.6 9.4 collective-permute-done
  129.6 9.4 collective-permute-done
  225.7 9.4 collective-permute-done
  243.1 10.6 collective-permute-done
  261.7 10.8 collective-permute-done
  279.6 10.5 collective-permute-done
  296.7 9.6 collective-permute-done
  457.3 9.8 collective-permute-done
  475.1 10.8 collective-permute-done
  493.7 10.8 collective-permute-done
  552.1 728.6 %while.49 = (s32[]{:T(128)}, bf16[128,4,128]{2,0,1:T(8,128)(2,1)S(1)}, bf16[128,4,128]{2,0,1:T(8,128)(2,1)S(1)}, f32[128,4,128]{2,0,1:T(8,128)S(1)}, f32[128,4,1...) while((s32[]{:T(128)}, ...), condition=%wide.region_14.15_spmd.clone.clone, body=%wide.region_13.14_spmd.clone.clone.sunk | while | flops 85443072 | bytes 7539424 | solution.py:206
  555.8 21.1 %collective-permute-done.2 = bf16[128,4,128]{2,0,1:T(8,128)(2,1)S(1)} collective-permute-done((bf16[128,4,128]{2,0,1:T(8,128)(2,1)S(1)}, bf16[128,4,128]{2,0,1:T(8,128)(2,1)S(1)}, u32[]{:S(2)}, u32[]{:S(2)}) %collective-permute-start.2) | collective-permute-done | bytes 131104 | tf_op jit(solution)/shard_map/while/body/eval_jaxpr/ppermute | solution.py:16
  582.8 21.0 %collective-permute-done.2 = bf16[128,4,128]{2,0,1:T(8,128)(2,1)S(1)} collective-permute-done((bf16[128,4,128]{2,0,1:T(8,128)(2,1)S(1)}, bf16[128,4,128]{2,0,1:T(8,128)(2,1)S(1)}, u32[]{:S(2)}, u32[]{:S(2)}) %collective-permute-start.2) | collective-permute-done | bytes 131104 | tf_op jit(solution)/shard_map/while/body/eval_jaxpr/ppermute | solution.py:16
  609.0 20.1 %collective-permute-done.2 = bf16[128,4,128]{2,0,1:T(8,128)(2,1)S(1)} collective-permute-done((bf16[128,4,128]{2,0,1:T(8,128)(2,1)S(1)}, bf16[128,4,128]{2,0,1:T(8,128)(2,1)S(1)}, u32[]{:S(2)}, u32[]{:S(2)}) %collective-permute-start.2) | collective-permute-done | bytes 131104 | tf_op jit(solution)/shard_map/while/body/eval_jaxpr/ppermute | solution.py:16
  634.3 19.2 %collective-permute-done.2 = bf16[128,4,128]{2,0,1:T(8,128)(2,1)S(1)} collective-permute-done((bf16[128,4,128]{2,0,1:T(8,128)(2,1)S(1)}, bf16[128,4,128]{2,0,1:T(8,128)(2,1)S(1)}, u32[]{:S(2)}, u32[]{:S(2)}) %collective-permute-start.2) | collective-permute-done | bytes 131104 | tf_op jit(solution)/shard_map/while/body/eval_jaxpr/ppermute | solution.py:16
  658.6 18.4 %collective-permute-done.2 = bf16[128,4,128]{2,0,1:T(8,128)(2,1)S(1)} collective-permute-done((bf16[128,4,128]{2,0,1:T(8,128)(2,1)S(1)}, bf16[128,4,128]{2,0,1:T(8,128)(2,1)S(1)}, u32[]{:S(2)}, u32[]{:S(2)}) %collective-permute-start.2) | collective-permute-done | bytes 131104 | tf_op jit(solution)/shard_map/while/body/eval_jaxpr/ppermute | solution.py:16
  682.2 17.6 %collective-permute-done.2 = bf16[128,4,128]{2,0,1:T(8,128)(2,1)S(1)} collective-permute-done((bf16[128,4,128]{2,0,1:T(8,128)(2,1)S(1)}, bf16[128,4,128]{2,0,1:T(8,128)(2,1)S(1)}, u32[]{:S(2)}, u32[]{:S(2)}) %collective-permute-start.2) | collective-permute-done | bytes 131104 | tf_op jit(solution)/shard_map/while/body/eval_jaxpr/ppermute | solution.py:16
  704.9 16.8 %collective-permute-done.2 = bf16[128,4,128]{2,0,1:T(8,128)(2,1)S(1)} collective-permute-done((bf16[128,4,128]{2,0,1:T(8,128)(2,1)S(1)}, bf16[128,4,128]{2,0,1:T(8,128)(2,1)S(1)}, u32[]{:S(2)}, u32[]{:S(2)}) %collective-permute-start.2) | collective-permute-done | bytes 131104 | tf_op jit(solution)/shard_map/while/body/eval_jaxpr/ppermute | solution.py:16
  726.8 15.8 %collective-permute-done.2 = bf16[128,4,128]{2,0,1:T(8,128)(2,1)S(1)} collective-permute-done((bf16[128,4,128]{2,0,1:T(8,128)(2,1)S(1)}, bf16[128,4,128]{2,0,1:T(8,128)(2,1)S(1)}, u32[]{:S(2)}, u32[]{:S(2)}) %collective-permute-start.2) | collective-permute-done | bytes 131104 | tf_op jit(solution)/shard_map/while/body/eval_jaxpr/ppermute | solution.py:16
  747.8 14.9 %collective-permute-done.2 = bf16[128,4,128]{2,0,1:T(8,128)(2,1)S(1)} collective-permute-done((bf16[128,4,128]{2,0,1:T(8,128)(2,1)S(1)}, bf16[128,4,128]{2,0,1:T(8,128)(2,1)S(1)}, u32[]{:S(2)}, u32[]{:S(2)}) %collective-permute-start.2) | collective-permute-done | bytes 131104 | tf_op jit(solution)/shard_map/while/body/eval_jaxpr/ppermute | solution.py:16
  767.8 14.1 %collective-permute-done.2 = bf16[128,4,128]{2,0,1:T(8,128)(2,1)S(1)} collective-permute-done((bf16[128,4,128]{2,0,1:T(8,128)(2,1)S(1)}, bf16[128,4,128]{2,0,1:T(8,128)(2,1)S(1)}, u32[]{:S(2)}, u32[]{:S(2)}) %collective-permute-start.2) | collective-permute-done | bytes 131104 | tf_op jit(solution)/shard_map/while/body/eval_jaxpr/ppermute | solution.py:16
  787.1 14.1 %collective-permute-done.2 = bf16[128,4,128]{2,0,1:T(8,128)(2,1)S(1)} collective-permute-done((bf16[128,4,128]{2,0,1:T(8,128)(2,1)S(1)}, bf16[128,4,128]{2,0,1:T(8,128)(2,1)S(1)}, u32[]{:S(2)}, u32[]{:S(2)}) %collective-permute-start.2) | collective-permute-done | bytes 131104 | tf_op jit(solution)/shard_map/while/body/eval_jaxpr/ppermute | solution.py:16
  806.4 14.1 %collective-permute-done.2 = bf16[128,4,128]{2,0,1:T(8,128)(2,1)S(1)} collective-permute-done((bf16[128,4,128]{2,0,1:T(8,128)(2,1)S(1)}, bf16[128,4,128]{2,0,1:T(8,128)(2,1)S(1)}, u32[]{:S(2)}, u32[]{:S(2)}) %collective-permute-start.2) | collective-permute-done | bytes 131104 | tf_op jit(solution)/shard_map/while/body/eval_jaxpr/ppermute | solution.py:16
  826.8 14.9 %collective-permute-done.2 = bf16[128,4,128]{2,0,1:T(8,128)(2,1)S(1)} collective-permute-done((bf16[128,4,128]{2,0,1:T(8,128)(2,1)S(1)}, bf16[128,4,128]{2,0,1:T(8,128)(2,1)S(1)}, u32[]{:S(2)}, u32[]{:S(2)}) %collective-permute-start.2) | collective-permute-done | bytes 131104 | tf_op jit(solution)/shard_map/while/body/eval_jaxpr/ppermute | solution.py:16
  848.2 16.0 %collective-permute-done.2 = bf16[128,4,128]{2,0,1:T(8,128)(2,1)S(1)} collective-permute-done((bf16[128,4,128]{2,0,1:T(8,128)(2,1)S(1)}, bf16[128,4,128]{2,0,1:T(8,128)(2,1)S(1)}, u32[]{:S(2)}, u32[]{:S(2)}) %collective-permute-start.2) | collective-permute-done | bytes 131104 | tf_op jit(solution)/shard_map/while/body/eval_jaxpr/ppermute | solution.py:16
  870.7 17.0 %collective-permute-done.2 = bf16[128,4,128]{2,0,1:T(8,128)(2,1)S(1)} collective-permute-done((bf16[128,4,128]{2,0,1:T(8,128)(2,1)S(1)}, bf16[128,4,128]{2,0,1:T(8,128)(2,1)S(1)}, u32[]{:S(2)}, u32[]{:S(2)}) %collective-permute-start.2) | collective-permute-done | bytes 131104 | tf_op jit(solution)/shard_map/while/body/eval_jaxpr/ppermute | solution.py:16
  894.3 18.1 %collective-permute-done.2 = bf16[128,4,128]{2,0,1:T(8,128)(2,1)S(1)} collective-permute-done((bf16[128,4,128]{2,0,1:T(8,128)(2,1)S(1)}, bf16[128,4,128]{2,0,1:T(8,128)(2,1)S(1)}, u32[]{:S(2)}, u32[]{:S(2)}) %collective-permute-start.2) | collective-permute-done | bytes 131104 | tf_op jit(solution)/shard_map/while/body/eval_jaxpr/ppermute | solution.py:16
  919.0 19.2 %collective-permute-done.2 = bf16[128,4,128]{2,0,1:T(8,128)(2,1)S(1)} collective-permute-done((bf16[128,4,128]{2,0,1:T(8,128)(2,1)S(1)}, bf16[128,4,128]{2,0,1:T(8,128)(2,1)S(1)}, u32[]{:S(2)}, u32[]{:S(2)}) %collective-permute-start.2) | collective-permute-done | bytes 131104 | tf_op jit(solution)/shard_map/while/body/eval_jaxpr/ppermute | solution.py:16
  944.8 20.4 %collective-permute-done.2 = bf16[128,4,128]{2,0,1:T(8,128)(2,1)S(1)} collective-permute-done((bf16[128,4,128]{2,0,1:T(8,128)(2,1)S(1)}, bf16[128,4,128]{2,0,1:T(8,128)(2,1)S(1)}, u32[]{:S(2)}, u32[]{:S(2)}) %collective-permute-start.2) | collective-permute-done | bytes 131104 | tf_op jit(solution)/shard_map/while/body/eval_jaxpr/ppermute | solution.py:16
  971.7 21.1 %collective-permute-done.2 = bf16[128,4,128]{2,0,1:T(8,128)(2,1)S(1)} collective-permute-done((bf16[128,4,128]{2,0,1:T(8,128)(2,1)S(1)}, bf16[128,4,128]{2,0,1:T(8,128)(2,1)S(1)}, u32[]{:S(2)}, u32[]{:S(2)}) %collective-permute-start.2) | collective-permute-done | bytes 131104 | tf_op jit(solution)/shard_map/while/body/eval_jaxpr/ppermute | solution.py:16
  999.0 21.2 %collective-permute-done.2 = bf16[128,4,128]{2,0,1:T(8,128)(2,1)S(1)} collective-permute-done((bf16[128,4,128]{2,0,1:T(8,128)(2,1)S(1)}, bf16[128,4,128]{2,0,1:T(8,128)(2,1)S(1)}, u32[]{:S(2)}, u32[]{:S(2)}) %collective-permute-start.2) | collective-permute-done | bytes 131104 | tf_op jit(solution)/shard_map/while/body/eval_jaxpr/ppermute | solution.py:16
  1025.6 20.5 %collective-permute-done.2 = bf16[128,4,128]{2,0,1:T(8,128)(2,1)S(1)} collective-permute-done((bf16[128,4,128]{2,0,1:T(8,128)(2,1)S(1)}, bf16[128,4,128]{2,0,1:T(8,128)(2,1)S(1)}, u32[]{:S(2)}, u32[]{:S(2)}) %collective-permute-start.2) | collective-permute-done | bytes 131104 | tf_op jit(solution)/shard_map/while/body/eval_jaxpr/ppermute | solution.py:16
  1051.2 19.6 %collective-permute-done.2 = bf16[128,4,128]{2,0,1:T(8,128)(2,1)S(1)} collective-permute-done((bf16[128,4,128]{2,0,1:T(8,128)(2,1)S(1)}, bf16[128,4,128]{2,0,1:T(8,128)(2,1)S(1)}, u32[]{:S(2)}, u32[]{:S(2)}) %collective-permute-start.2) | collective-permute-done | bytes 131104 | tf_op jit(solution)/shard_map/while/body/eval_jaxpr/ppermute | solution.py:16
  1076.0 18.8 %collective-permute-done.2 = bf16[128,4,128]{2,0,1:T(8,128)(2,1)S(1)} collective-permute-done((bf16[128,4,128]{2,0,1:T(8,128)(2,1)S(1)}, bf16[128,4,128]{2,0,1:T(8,128)(2,1)S(1)}, u32[]{:S(2)}, u32[]{:S(2)}) %collective-permute-start.2) | collective-permute-done | bytes 131104 | tf_op jit(solution)/shard_map/while/body/eval_jaxpr/ppermute | solution.py:16
  1099.9 18.0 %collective-permute-done.2 = bf16[128,4,128]{2,0,1:T(8,128)(2,1)S(1)} collective-permute-done((bf16[128,4,128]{2,0,1:T(8,128)(2,1)S(1)}, bf16[128,4,128]{2,0,1:T(8,128)(2,1)S(1)}, u32[]{:S(2)}, u32[]{:S(2)}) %collective-permute-start.2) | collective-permute-done | bytes 131104 | tf_op jit(solution)/shard_map/while/body/eval_jaxpr/ppermute | solution.py:16
  1123.0 17.1 %collective-permute-done.2 = bf16[128,4,128]{2,0,1:T(8,128)(2,1)S(1)} collective-permute-done((bf16[128,4,128]{2,0,1:T(8,128)(2,1)S(1)}, bf16[128,4,128]{2,0,1:T(8,128)(2,1)S(1)}, u32[]{:S(2)}, u32[]{:S(2)}) %collective-permute-start.2) | collective-permute-done | bytes 131104 | tf_op jit(solution)/shard_map/while/body/eval_jaxpr/ppermute | solution.py:16
  1145.3 16.3 %collective-permute-done.2 = bf16[128,4,128]{2,0,1:T(8,128)(2,1)S(1)} collective-permute-done((bf16[128,4,128]{2,0,1:T(8,128)(2,1)S(1)}, bf16[128,4,128]{2,0,1:T(8,128)(2,1)S(1)}, u32[]{:S(2)}, u32[]{:S(2)}) %collective-permute-start.2) | collective-permute-done | bytes 131104 | tf_op jit(solution)/shard_map/while/body/eval_jaxpr/ppermute | solution.py:16
  1166.8 15.4 %collective-permute-done.2 = bf16[128,4,128]{2,0,1:T(8,128)(2,1)S(1)} collective-permute-done((bf16[128,4,128]{2,0,1:T(8,128)(2,1)S(1)}, bf16[128,4,128]{2,0,1:T(8,128)(2,1)S(1)}, u32[]{:S(2)}, u32[]{:S(2)}) %collective-permute-start.2) | collective-permute-done | bytes 131104 | tf_op jit(solution)/shard_map/while/body/eval_jaxpr/ppermute | solution.py:16
  1187.3 14.5 %collective-permute-done.2 = bf16[128,4,128]{2,0,1:T(8,128)(2,1)S(1)} collective-permute-done((bf16[128,4,128]{2,0,1:T(8,128)(2,1)S(1)}, bf16[128,4,128]{2,0,1:T(8,128)(2,1)S(1)}, u32[]{:S(2)}, u32[]{:S(2)}) %collective-permute-start.2) | collective-permute-done | bytes 131104 | tf_op jit(solution)/shard_map/while/body/eval_jaxpr/ppermute | solution.py:16
  1207.0 14.1 %collective-permute-done.2 = bf16[128,4,128]{2,0,1:T(8,128)(2,1)S(1)} collective-permute-done((bf16[128,4,128]{2,0,1:T(8,128)(2,1)S(1)}, bf16[128,4,128]{2,0,1:T(8,128)(2,1)S(1)}, u32[]{:S(2)}, u32[]{:S(2)}) %collective-permute-start.2) | collective-permute-done | bytes 131104 | tf_op jit(solution)/shard_map/while/body/eval_jaxpr/ppermute | solution.py:16
  1226.3 14.1 %collective-permute-done.2 = bf16[128,4,128]{2,0,1:T(8,128)(2,1)S(1)} collective-permute-done((bf16[128,4,128]{2,0,1:T(8,128)(2,1)S(1)}, bf16[128,4,128]{2,0,1:T(8,128)(2,1)S(1)}, u32[]{:S(2)}, u32[]{:S(2)}) %collective-permute-start.2) | collective-permute-done | bytes 131104 | tf_op jit(solution)/shard_map/while/body/eval_jaxpr/ppermute | solution.py:16
  1245.9 14.1 %collective-permute-done.2 = bf16[128,4,128]{2,0,1:T(8,128)(2,1)S(1)} collective-permute-done((bf16[128,4,128]{2,0,1:T(8,128)(2,1)S(1)}, bf16[128,4,128]{2,0,1:T(8,128)(2,1)S(1)}, u32[]{:S(2)}, u32[]{:S(2)}) %collective-permute-start.2) | collective-permute-done | bytes 131104 | tf_op jit(solution)/shard_map/while/body/eval_jaxpr/ppermute | solution.py:16
  1265.2 14.1 %collective-permute-done.2 = bf16[128,4,128]{2,0,1:T(8,128)(2,1)S(1)} collective-permute-done((bf16[128,4,128]{2,0,1:T(8,128)(2,1)S(1)}, bf16[128,4,128]{2,0,1:T(8,128)(2,1)S(1)}, u32[]{:S(2)}, u32[]{:S(2)}) %collective-permute-start.2) | collective-permute-done | bytes 131104 | tf_op jit(solution)/shard_map/while/body/eval_jaxpr/ppermute | solution.py:16
  (993 shorter events, 593.9 us)
Async XLA Ops:
  543.4 745.7 %all-to-all-start.1 = ((bf16[4,128,512]{2,1,0:T(8,128)(2,1)}), bf16[4,128,512]{2,1,0:T(8,128)(2,1)}, u32[]{:S(2)}, u32[]{:S(2)}) async-start(bf16[4,128,512]{2,1,0:T(8,128)(2,1)} %convert_element_type.180), calls=%async_computation.1 | async-start | bytes 1048576 | tf_op jit(solution)/shard_map/all_to_all | solution.py:162
  553.6 25.5 %collective-permute-start.4 = (f32[128,4,128]{2,0,1:T(8,128)S(1)}, f32[128,4,128]{2,0,1:T(8,128)S(1)}, u32[]{:S(2)}, u32[]{:S(2)}) collective-permute-start(f32[128,4,128]{2,0,1:T(8,128)S(1)} %fusion.178), channel_id=1, source_target_pairs={{0,1},{1,2},{2,3},{3,4},{4,5},{5,6},{6,7},{7,8},{8,9},{9,10},{10,1... | collective-permute-start | bytes 786440 | tf_op jit(solution)/shard_map/while/body/eval_jaxpr/ppermute | solution.py:16
  555.6 23.5 %collective-permute-start.5 = (f32[128,4,128]{2,0,1:T(8,128)}, f32[128,4,128]{2,0,1:T(8,128)}, u32[]{:S(2)}, u32[]{:S(2)}) collective-permute-start(f32[128,4,128]{2,0,1:T(8,128)} %fusion.179), channel_id=1, source_target_pairs={{0,1},{1,2},{2,3},{3,4},{4,5},{5,6},{6,7},{7,8},{8,9},{9,10},{10,1... | collective-permute-start | bytes 786440 | tf_op jit(solution)/shard_map/while/body/eval_jaxpr/ppermute | solution.py:16
  555.6 21.3 %collective-permute-start.2 = (bf16[128,4,128]{2,0,1:T(8,128)(2,1)S(1)}, bf16[128,4,128]{2,0,1:T(8,128)(2,1)S(1)}, u32[]{:S(2)}, u32[]{:S(2)}) collective-permute-start(bf16[128,4,128]{2,0,1:T(8,128)(2,1)S(1)} %copy.121), channel_id=1, source_target_pairs={{0,1},{1,2},{2,3},{3,4},{4,5},{5,6},{6,7},{7,8},{8,9},{9,10},{10,1... | collective-permute-start | bytes 393224 | tf_op jit(solution)/shard_map/while/body/eval_jaxpr/ppermute | solution.py:16
  555.6 23.5 %collective-permute-start.3 = (bf16[128,4,128]{2,0,1:T(8,128)(2,1)S(1)}, bf16[128,4,128]{2,0,1:T(8,128)(2,1)S(1)}, u32[]{:S(2)}, u32[]{:S(2)}) collective-permute-start(bf16[128,4,128]{2,0,1:T(8,128)(2,1)S(1)} %copy.122), channel_id=1, source_target_pairs={{0,1},{1,2},{2,3},{3,4},{4,5},{5,6},{6,7},{7,8},{8,9},{9,10},{10,1... | collective-permute-start | bytes 393224 | tf_op jit(solution)/shard_map/while/body/eval_jaxpr/ppermute | solution.py:16
  580.6 24.7 %collective-permute-start.4 = (f32[128,4,128]{2,0,1:T(8,128)S(1)}, f32[128,4,128]{2,0,1:T(8,128)S(1)}, u32[]{:S(2)}, u32[]{:S(2)}) collective-permute-start(f32[128,4,128]{2,0,1:T(8,128)S(1)} %fusion.178), channel_id=1, source_target_pairs={{0,1},{1,2},{2,3},{3,4},{4,5},{5,6},{6,7},{7,8},{8,9},{9,10},{10,1... | collective-permute-start | bytes 786440 | tf_op jit(solution)/shard_map/while/body/eval_jaxpr/ppermute | solution.py:16
  582.6 22.7 %collective-permute-start.5 = (f32[128,4,128]{2,0,1:T(8,128)}, f32[128,4,128]{2,0,1:T(8,128)}, u32[]{:S(2)}, u32[]{:S(2)}) collective-permute-start(f32[128,4,128]{2,0,1:T(8,128)} %fusion.179), channel_id=1, source_target_pairs={{0,1},{1,2},{2,3},{3,4},{4,5},{5,6},{6,7},{7,8},{8,9},{9,10},{10,1... | collective-permute-start | bytes 786440 | tf_op jit(solution)/shard_map/while/body/eval_jaxpr/ppermute | solution.py:16
  582.6 21.3 %collective-permute-start.2 = (bf16[128,4,128]{2,0,1:T(8,128)(2,1)S(1)}, bf16[128,4,128]{2,0,1:T(8,128)(2,1)S(1)}, u32[]{:S(2)}, u32[]{:S(2)}) collective-permute-start(bf16[128,4,128]{2,0,1:T(8,128)(2,1)S(1)} %copy.121), channel_id=1, source_target_pairs={{0,1},{1,2},{2,3},{3,4},{4,5},{5,6},{6,7},{7,8},{8,9},{9,10},{10,1... | collective-permute-start | bytes 393224 | tf_op jit(solution)/shard_map/while/body/eval_jaxpr/ppermute | solution.py:16
  582.6 22.7 %collective-permute-start.3 = (bf16[128,4,128]{2,0,1:T(8,128)(2,1)S(1)}, bf16[128,4,128]{2,0,1:T(8,128)(2,1)S(1)}, u32[]{:S(2)}, u32[]{:S(2)}) collective-permute-start(bf16[128,4,128]{2,0,1:T(8,128)(2,1)S(1)} %copy.122), channel_id=1, source_target_pairs={{0,1},{1,2},{2,3},{3,4},{4,5},{5,6},{6,7},{7,8},{8,9},{9,10},{10,1... | collective-permute-start | bytes 393224 | tf_op jit(solution)/shard_map/while/body/eval_jaxpr/ppermute | solution.py:16
  606.8 23.8 %collective-permute-start.4 = (f32[128,4,128]{2,0,1:T(8,128)S(1)}, f32[128,4,128]{2,0,1:T(8,128)S(1)}, u32[]{:S(2)}, u32[]{:S(2)}) collective-permute-start(f32[128,4,128]{2,0,1:T(8,128)S(1)} %fusion.178), channel_id=1, source_target_pairs={{0,1},{1,2},{2,3},{3,4},{4,5},{5,6},{6,7},{7,8},{8,9},{9,10},{10,1... | collective-permute-start | bytes 786440 | tf_op jit(solution)/shard_map/while/body/eval_jaxpr/ppermute | solution.py:16
  608.8 21.8 %collective-permute-start.5 = (f32[128,4,128]{2,0,1:T(8,128)}, f32[128,4,128]{2,0,1:T(8,128)}, u32[]{:S(2)}, u32[]{:S(2)}) collective-permute-start(f32[128,4,128]{2,0,1:T(8,128)} %fusion.179), channel_id=1, source_target_pairs={{0,1},{1,2},{2,3},{3,4},{4,5},{5,6},{6,7},{7,8},{8,9},{9,10},{10,1... | collective-permute-start | bytes 786440 | tf_op jit(solution)/shard_map/while/body/eval_jaxpr/ppermute | solution.py:16
  608.8 21.8 %collective-permute-start.3 = (bf16[128,4,128]{2,0,1:T(8,128)(2,1)S(1)}, bf16[128,4,128]{2,0,1:T(8,128)(2,1)S(1)}, u32[]{:S(2)}, u32[]{:S(2)}) collective-permute-start(bf16[128,4,128]{2,0,1:T(8,128)(2,1)S(1)} %copy.122), channel_id=1, source_target_pairs={{0,1},{1,2},{2,3},{3,4},{4,5},{5,6},{6,7},{7,8},{8,9},{9,10},{10,1... | collective-permute-start | bytes 393224 | tf_op jit(solution)/shard_map/while/body/eval_jaxpr/ppermute | solution.py:16
  632.0 22.9 %collective-permute-start.4 = (f32[128,4,128]{2,0,1:T(8,128)S(1)}, f32[128,4,128]{2,0,1:T(8,128)S(1)}, u32[]{:S(2)}, u32[]{:S(2)}) collective-permute-start(f32[128,4,128]{2,0,1:T(8,128)S(1)} %fusion.178), channel_id=1, source_target_pairs={{0,1},{1,2},{2,3},{3,4},{4,5},{5,6},{6,7},{7,8},{8,9},{9,10},{10,1... | collective-permute-start | bytes 786440 | tf_op jit(solution)/shard_map/while/body/eval_jaxpr/ppermute | solution.py:16
  634.1 20.8 %collective-permute-start.5 = (f32[128,4,128]{2,0,1:T(8,128)}, f32[128,4,128]{2,0,1:T(8,128)}, u32[]{:S(2)}, u32[]{:S(2)}) collective-permute-start(f32[128,4,128]{2,0,1:T(8,128)} %fusion.179), channel_id=1, source_target_pairs={{0,1},{1,2},{2,3},{3,4},{4,5},{5,6},{6,7},{7,8},{8,9},{9,10},{10,1... | collective-permute-start | bytes 786440 | tf_op jit(solution)/shard_map/while/body/eval_jaxpr/ppermute | solution.py:16
  634.1 20.8 %collective-permute-start.3 = (bf16[128,4,128]{2,0,1:T(8,128)(2,1)S(1)}, bf16[128,4,128]{2,0,1:T(8,128)(2,1)S(1)}, u32[]{:S(2)}, u32[]{:S(2)}) collective-permute-start(bf16[128,4,128]{2,0,1:T(8,128)(2,1)S(1)} %copy.122), channel_id=1, source_target_pairs={{0,1},{1,2},{2,3},{3,4},{4,5},{5,6},{6,7},{7,8},{8,9},{9,10},{10,1... | collective-permute-start | bytes 393224 | tf_op jit(solution)/shard_map/while/body/eval_jaxpr/ppermute | solution.py:16
  656.4 22.0 %collective-permute-start.4 = (f32[128,4,128]{2,0,1:T(8,128)S(1)}, f32[128,4,128]{2,0,1:T(8,128)S(1)}, u32[]{:S(2)}, u32[]{:S(2)}) collective-permute-start(f32[128,4,128]{2,0,1:T(8,128)S(1)} %fusion.178), channel_id=1, source_target_pairs={{0,1},{1,2},{2,3},{3,4},{4,5},{5,6},{6,7},{7,8},{8,9},{9,10},{10,1... | collective-permute-start | bytes 786440 | tf_op jit(solution)/shard_map/while/body/eval_jaxpr/ppermute | solution.py:16
  679.9 21.2 %collective-permute-start.4 = (f32[128,4,128]{2,0,1:T(8,128)S(1)}, f32[128,4,128]{2,0,1:T(8,128)S(1)}, u32[]{:S(2)}, u32[]{:S(2)}) collective-permute-start(f32[128,4,128]{2,0,1:T(8,128)S(1)} %fusion.178), channel_id=1, source_target_pairs={{0,1},{1,2},{2,3},{3,4},{4,5},{5,6},{6,7},{7,8},{8,9},{9,10},{10,1... | collective-permute-start | bytes 786440 | tf_op jit(solution)/shard_map/while/body/eval_jaxpr/ppermute | solution.py:16
  845.9 21.0 %collective-permute-start.4 = (f32[128,4,128]{2,0,1:T(8,128)S(1)}, f32[128,4,128]{2,0,1:T(8,128)S(1)}, u32[]{:S(2)}, u32[]{:S(2)}) collective-permute-start(f32[128,4,128]{2,0,1:T(8,128)S(1)} %fusion.178), channel_id=1, source_target_pairs={{0,1},{1,2},{2,3},{3,4},{4,5},{5,6},{6,7},{7,8},{8,9},{9,10},{10,1... | collective-permute-start | bytes 786440 | tf_op jit(solution)/shard_map/while/body/eval_jaxpr/ppermute | solution.py:16
  868.5 22.1 %collective-permute-start.4 = (f32[128,4,128]{2,0,1:T(8,128)S(1)}, f32[128,4,128]{2,0,1:T(8,128)S(1)}, u32[]{:S(2)}, u32[]{:S(2)}) collective-permute-start(f32[128,4,128]{2,0,1:T(8,128)S(1)} %fusion.178), channel_id=1, source_target_pairs={{0,1},{1,2},{2,3},{3,4},{4,5},{5,6},{6,7},{7,8},{8,9},{9,10},{10,1... | collective-permute-start | bytes 786440 | tf_op jit(solution)/shard_map/while/body/eval_jaxpr/ppermute | solution.py:16
  892.1 23.2 %collective-permute-start.4 = (f32[128,4,128]{2,0,1:T(8,128)S(1)}, f32[128,4,128]{2,0,1:T(8,128)S(1)}, u32[]{:S(2)}, u32[]{:S(2)}) collective-permute-start(f32[128,4,128]{2,0,1:T(8,128)S(1)} %fusion.178), channel_id=1, source_target_pairs={{0,1},{1,2},{2,3},{3,4},{4,5},{5,6},{6,7},{7,8},{8,9},{9,10},{10,1... | collective-permute-start | bytes 786440 | tf_op jit(solution)/shard_map/while/body/eval_jaxpr/ppermute | solution.py:16
  894.1 21.2 %collective-permute-start.5 = (f32[128,4,128]{2,0,1:T(8,128)}, f32[128,4,128]{2,0,1:T(8,128)}, u32[]{:S(2)}, u32[]{:S(2)}) collective-permute-start(f32[128,4,128]{2,0,1:T(8,128)} %fusion.179), channel_id=1, source_target_pairs={{0,1},{1,2},{2,3},{3,4},{4,5},{5,6},{6,7},{7,8},{8,9},{9,10},{10,1... | collective-permute-start | bytes 786440 | tf_op jit(solution)/shard_map/while/body/eval_jaxpr/ppermute | solution.py:16
  894.1 21.2 %collective-permute-start.3 = (bf16[128,4,128]{2,0,1:T(8,128)(2,1)S(1)}, bf16[128,4,128]{2,0,1:T(8,128)(2,1)S(1)}, u32[]{:S(2)}, u32[]{:S(2)}) collective-permute-start(bf16[128,4,128]{2,0,1:T(8,128)(2,1)S(1)} %copy.122), channel_id=1, source_target_pairs={{0,1},{1,2},{2,3},{3,4},{4,5},{5,6},{6,7},{7,8},{8,9},{9,10},{10,1... | collective-permute-start | bytes 393224 | tf_op jit(solution)/shard_map/while/body/eval_jaxpr/ppermute | solution.py:16
  916.7 24.3 %collective-permute-start.4 = (f32[128,4,128]{2,0,1:T(8,128)S(1)}, f32[128,4,128]{2,0,1:T(8,128)S(1)}, u32[]{:S(2)}, u32[]{:S(2)}) collective-permute-start(f32[128,4,128]{2,0,1:T(8,128)S(1)} %fusion.178), channel_id=1, source_target_pairs={{0,1},{1,2},{2,3},{3,4},{4,5},{5,6},{6,7},{7,8},{8,9},{9,10},{10,1... | collective-permute-start | bytes 786440 | tf_op jit(solution)/shard_map/while/body/eval_jaxpr/ppermute | solution.py:16
  918.8 22.3 %collective-permute-start.5 = (f32[128,4,128]{2,0,1:T(8,128)}, f32[128,4,128]{2,0,1:T(8,128)}, u32[]{:S(2)}, u32[]{:S(2)}) collective-permute-start(f32[128,4,128]{2,0,1:T(8,128)} %fusion.179), channel_id=1, source_target_pairs={{0,1},{1,2},{2,3},{3,4},{4,5},{5,6},{6,7},{7,8},{8,9},{9,10},{10,1... | collective-permute-start | bytes 786440 | tf_op jit(solution)/shard_map/while/body/eval_jaxpr/ppermute | solution.py:16
  918.8 22.2 %collective-permute-start.3 = (bf16[128,4,128]{2,0,1:T(8,128)(2,1)S(1)}, bf16[128,4,128]{2,0,1:T(8,128)(2,1)S(1)}, u32[]{:S(2)}, u32[]{:S(2)}) collective-permute-start(bf16[128,4,128]{2,0,1:T(8,128)(2,1)S(1)} %copy.122), channel_id=1, source_target_pairs={{0,1},{1,2},{2,3},{3,4},{4,5},{5,6},{6,7},{7,8},{8,9},{9,10},{10,1... | collective-permute-start | bytes 393224 | tf_op jit(solution)/shard_map/while/body/eval_jaxpr/ppermute | solution.py:16
  942.5 25.4 %collective-permute-start.4 = (f32[128,4,128]{2,0,1:T(8,128)S(1)}, f32[128,4,128]{2,0,1:T(8,128)S(1)}, u32[]{:S(2)}, u32[]{:S(2)}) collective-permute-start(f32[128,4,128]{2,0,1:T(8,128)S(1)} %fusion.178), channel_id=1, source_target_pairs={{0,1},{1,2},{2,3},{3,4},{4,5},{5,6},{6,7},{7,8},{8,9},{9,10},{10,1... | collective-permute-start | bytes 786440 | tf_op jit(solution)/shard_map/while/body/eval_jaxpr/ppermute | solution.py:16
  944.5 23.4 %collective-permute-start.5 = (f32[128,4,128]{2,0,1:T(8,128)}, f32[128,4,128]{2,0,1:T(8,128)}, u32[]{:S(2)}, u32[]{:S(2)}) collective-permute-start(f32[128,4,128]{2,0,1:T(8,128)} %fusion.179), channel_id=1, source_target_pairs={{0,1},{1,2},{2,3},{3,4},{4,5},{5,6},{6,7},{7,8},{8,9},{9,10},{10,1... | collective-permute-start | bytes 786440 | tf_op jit(solution)/shard_map/while/body/eval_jaxpr/ppermute | solution.py:16
  944.5 20.6 %collective-permute-start.2 = (bf16[128,4,128]{2,0,1:T(8,128)(2,1)S(1)}, bf16[128,4,128]{2,0,1:T(8,128)(2,1)S(1)}, u32[]{:S(2)}, u32[]{:S(2)}) collective-permute-start(bf16[128,4,128]{2,0,1:T(8,128)(2,1)S(1)} %copy.121), channel_id=1, source_target_pairs={{0,1},{1,2},{2,3},{3,4},{4,5},{5,6},{6,7},{7,8},{8,9},{9,10},{10,1... | collective-permute-start | bytes 393224 | tf_op jit(solution)/shard_map/while/body/eval_jaxpr/ppermute | solution.py:16
  944.5 23.4 %collective-permute-start.3 = (bf16[128,4,128]{2,0,1:T(8,128)(2,1)S(1)}, bf16[128,4,128]{2,0,1:T(8,128)(2,1)S(1)}, u32[]{:S(2)}, u32[]{:S(2)}) collective-permute-start(bf16[128,4,128]{2,0,1:T(8,128)(2,1)S(1)} %copy.122), channel_id=1, source_target_pairs={{0,1},{1,2},{2,3},{3,4},{4,5},{5,6},{6,7},{7,8},{8,9},{9,10},{10,1... | collective-permute-start | bytes 393224 | tf_op jit(solution)/shard_map/while/body/eval_jaxpr/ppermute | solution.py:16
  969.4 25.8 %collective-permute-start.4 = (f32[128,4,128]{2,0,1:T(8,128)S(1)}, f32[128,4,128]{2,0,1:T(8,128)S(1)}, u32[]{:S(2)}, u32[]{:S(2)}) collective-permute-start(f32[128,4,128]{2,0,1:T(8,128)S(1)} %fusion.178), channel_id=1, source_target_pairs={{0,1},{1,2},{2,3},{3,4},{4,5},{5,6},{6,7},{7,8},{8,9},{9,10},{10,1... | collective-permute-start | bytes 786440 | tf_op jit(solution)/shard_map/while/body/eval_jaxpr/ppermute | solution.py:16
  971.5 23.8 %collective-permute-start.5 = (f32[128,4,128]{2,0,1:T(8,128)}, f32[128,4,128]{2,0,1:T(8,128)}, u32[]{:S(2)}, u32[]{:S(2)}) collective-permute-start(f32[128,4,128]{2,0,1:T(8,128)} %fusion.179), channel_id=1, source_target_pairs={{0,1},{1,2},{2,3},{3,4},{4,5},{5,6},{6,7},{7,8},{8,9},{9,10},{10,1... | collective-permute-start | bytes 786440 | tf_op jit(solution)/shard_map/while/body/eval_jaxpr/ppermute | solution.py:16
  971.5 21.3 %collective-permute-start.2 = (bf16[128,4,128]{2,0,1:T(8,128)(2,1)S(1)}, bf16[128,4,128]{2,0,1:T(8,128)(2,1)S(1)}, u32[]{:S(2)}, u32[]{:S(2)}) collective-permute-start(bf16[128,4,128]{2,0,1:T(8,128)(2,1)S(1)} %copy.121), channel_id=1, source_target_pairs={{0,1},{1,2},{2,3},{3,4},{4,5},{5,6},{6,7},{7,8},{8,9},{9,10},{10,1... | collective-permute-start | bytes 393224 | tf_op jit(solution)/shard_map/while/body/eval_jaxpr/ppermute | solution.py:16
  971.5 23.8 %collective-permute-start.3 = (bf16[128,4,128]{2,0,1:T(8,128)(2,1)S(1)}, bf16[128,4,128]{2,0,1:T(8,128)(2,1)S(1)}, u32[]{:S(2)}, u32[]{:S(2)}) collective-permute-start(bf16[128,4,128]{2,0,1:T(8,128)(2,1)S(1)} %copy.122), channel_id=1, source_target_pairs={{0,1},{1,2},{2,3},{3,4},{4,5},{5,6},{6,7},{7,8},{8,9},{9,10},{10,1... | collective-permute-start | bytes 393224 | tf_op jit(solution)/shard_map/while/body/eval_jaxpr/ppermute | solution.py:16
  996.8 25.1 %collective-permute-start.4 = (f32[128,4,128]{2,0,1:T(8,128)S(1)}, f32[128,4,128]{2,0,1:T(8,128)S(1)}, u32[]{:S(2)}, u32[]{:S(2)}) collective-permute-start(f32[128,4,128]{2,0,1:T(8,128)S(1)} %fusion.178), channel_id=1, source_target_pairs={{0,1},{1,2},{2,3},{3,4},{4,5},{5,6},{6,7},{7,8},{8,9},{9,10},{10,1... | collective-permute-start | bytes 786440 | tf_op jit(solution)/shard_map/while/body/eval_jaxpr/ppermute | solution.py:16
  998.8 23.0 %collective-permute-start.5 = (f32[128,4,128]{2,0,1:T(8,128)}, f32[128,4,128]{2,0,1:T(8,128)}, u32[]{:S(2)}, u32[]{:S(2)}) collective-permute-start(f32[128,4,128]{2,0,1:T(8,128)} %fusion.179), channel_id=1, source_target_pairs={{0,1},{1,2},{2,3},{3,4},{4,5},{5,6},{6,7},{7,8},{8,9},{9,10},{10,1... | collective-permute-start | bytes 786440 | tf_op jit(solution)/shard_map/while/body/eval_jaxpr/ppermute | solution.py:16
  998.8 21.4 %collective-permute-start.2 = (bf16[128,4,128]{2,0,1:T(8,128)(2,1)S(1)}, bf16[128,4,128]{2,0,1:T(8,128)(2,1)S(1)}, u32[]{:S(2)}, u32[]{:S(2)}) collective-permute-start(bf16[128,4,128]{2,0,1:T(8,128)(2,1)S(1)} %copy.121), channel_id=1, source_target_pairs={{0,1},{1,2},{2,3},{3,4},{4,5},{5,6},{6,7},{7,8},{8,9},{9,10},{10,1... | collective-permute-start | bytes 393224 | tf_op jit(solution)/shard_map/while/body/eval_jaxpr/ppermute | solution.py:16
  998.8 23.0 %collective-permute-start.3 = (bf16[128,4,128]{2,0,1:T(8,128)(2,1)S(1)}, bf16[128,4,128]{2,0,1:T(8,128)(2,1)S(1)}, u32[]{:S(2)}, u32[]{:S(2)}) collective-permute-start(bf16[128,4,128]{2,0,1:T(8,128)(2,1)S(1)} %copy.122), channel_id=1, source_target_pairs={{0,1},{1,2},{2,3},{3,4},{4,5},{5,6},{6,7},{7,8},{8,9},{9,10},{10,1... | collective-permute-start | bytes 393224 | tf_op jit(solution)/shard_map/while/body/eval_jaxpr/ppermute | solution.py:16
  1023.3 24.2 %collective-permute-start.4 = (f32[128,4,128]{2,0,1:T(8,128)S(1)}, f32[128,4,128]{2,0,1:T(8,128)S(1)}, u32[]{:S(2)}, u32[]{:S(2)}) collective-permute-start(f32[128,4,128]{2,0,1:T(8,128)S(1)} %fusion.178), channel_id=1, source_target_pairs={{0,1},{1,2},{2,3},{3,4},{4,5},{5,6},{6,7},{7,8},{8,9},{9,10},{10,1... | collective-permute-start | bytes 786440 | tf_op jit(solution)/shard_map/while/body/eval_jaxpr/ppermute | solution.py:16
  1025.3 22.2 %collective-permute-start.5 = (f32[128,4,128]{2,0,1:T(8,128)}, f32[128,4,128]{2,0,1:T(8,128)}, u32[]{:S(2)}, u32[]{:S(2)}) collective-permute-start(f32[128,4,128]{2,0,1:T(8,128)} %fusion.179), channel_id=1, source_target_pairs={{0,1},{1,2},{2,3},{3,4},{4,5},{5,6},{6,7},{7,8},{8,9},{9,10},{10,1... | collective-permute-start | bytes 786440 | tf_op jit(solution)/shard_map/while/body/eval_jaxpr/ppermute | solution.py:16
  1025.3 20.8 %collective-permute-start.2 = (bf16[128,4,128]{2,0,1:T(8,128)(2,1)S(1)}, bf16[128,4,128]{2,0,1:T(8,128)(2,1)S(1)}, u32[]{:S(2)}, u32[]{:S(2)}) collective-permute-start(bf16[128,4,128]{2,0,1:T(8,128)(2,1)S(1)} %copy.121), channel_id=1, source_target_pairs={{0,1},{1,2},{2,3},{3,4},{4,5},{5,6},{6,7},{7,8},{8,9},{9,10},{10,1... | collective-permute-start | bytes 393224 | tf_op jit(solution)/shard_map/while/body/eval_jaxpr/ppermute | solution.py:16
  1025.3 22.2 %collective-permute-start.3 = (bf16[128,4,128]{2,0,1:T(8,128)(2,1)S(1)}, bf16[128,4,128]{2,0,1:T(8,128)(2,1)S(1)}, u32[]{:S(2)}, u32[]{:S(2)}) collective-permute-start(bf16[128,4,128]{2,0,1:T(8,128)(2,1)S(1)} %copy.122), channel_id=1, source_target_pairs={{0,1},{1,2},{2,3},{3,4},{4,5},{5,6},{6,7},{7,8},{8,9},{9,10},{10,1... | collective-permute-start | bytes 393224 | tf_op jit(solution)/shard_map/while/body/eval_jaxpr/ppermute | solution.py:16
  1049.0 23.3 %collective-permute-start.4 = (f32[128,4,128]{2,0,1:T(8,128)S(1)}, f32[128,4,128]{2,0,1:T(8,128)S(1)}, u32[]{:S(2)}, u32[]{:S(2)}) collective-permute-start(f32[128,4,128]{2,0,1:T(8,128)S(1)} %fusion.178), channel_id=1, source_target_pairs={{0,1},{1,2},{2,3},{3,4},{4,5},{5,6},{6,7},{7,8},{8,9},{9,10},{10,1... | collective-permute-start | bytes 786440 | tf_op jit(solution)/shard_map/while/body/eval_jaxpr/ppermute | solution.py:16
  1051.0 21.2 %collective-permute-start.5 = (f32[128,4,128]{2,0,1:T(8,128)}, f32[128,4,128]{2,0,1:T(8,128)}, u32[]{:S(2)}, u32[]{:S(2)}) collective-permute-start(f32[128,4,128]{2,0,1:T(8,128)} %fusion.179), channel_id=1, source_target_pairs={{0,1},{1,2},{2,3},{3,4},{4,5},{5,6},{6,7},{7,8},{8,9},{9,10},{10,1... | collective-permute-start | bytes 786440 | tf_op jit(solution)/shard_map/while/body/eval_jaxpr/ppermute | solution.py:16
  1051.0 21.2 %collective-permute-start.3 = (bf16[128,4,128]{2,0,1:T(8,128)(2,1)S(1)}, bf16[128,4,128]{2,0,1:T(8,128)(2,1)S(1)}, u32[]{:S(2)}, u32[]{:S(2)}) collective-permute-start(bf16[128,4,128]{2,0,1:T(8,128)(2,1)S(1)} %copy.122), channel_id=1, source_target_pairs={{0,1},{1,2},{2,3},{3,4},{4,5},{5,6},{6,7},{7,8},{8,9},{9,10},{10,1... | collective-permute-start | bytes 393224 | tf_op jit(solution)/shard_map/while/body/eval_jaxpr/ppermute | solution.py:16
  1073.7 22.4 %collective-permute-start.4 = (f32[128,4,128]{2,0,1:T(8,128)S(1)}, f32[128,4,128]{2,0,1:T(8,128)S(1)}, u32[]{:S(2)}, u32[]{:S(2)}) collective-permute-start(f32[128,4,128]{2,0,1:T(8,128)S(1)} %fusion.178), channel_id=1, source_target_pairs={{0,1},{1,2},{2,3},{3,4},{4,5},{5,6},{6,7},{7,8},{8,9},{9,10},{10,1... | collective-permute-start | bytes 786440 | tf_op jit(solution)/shard_map/while/body/eval_jaxpr/ppermute | solution.py:16
  1075.7 20.4 %collective-permute-start.5 = (f32[128,4,128]{2,0,1:T(8,128)}, f32[128,4,128]{2,0,1:T(8,128)}, u32[]{:S(2)}, u32[]{:S(2)}) collective-permute-start(f32[128,4,128]{2,0,1:T(8,128)} %fusion.179), channel_id=1, source_target_pairs={{0,1},{1,2},{2,3},{3,4},{4,5},{5,6},{6,7},{7,8},{8,9},{9,10},{10,1... | collective-permute-start | bytes 786440 | tf_op jit(solution)/shard_map/while/body/eval_jaxpr/ppermute | solution.py:16
  1097.7 21.6 %collective-permute-start.4 = (f32[128,4,128]{2,0,1:T(8,128)S(1)}, f32[128,4,128]{2,0,1:T(8,128)S(1)}, u32[]{:S(2)}, u32[]{:S(2)}) collective-permute-start(f32[128,4,128]{2,0,1:T(8,128)S(1)} %fusion.178), channel_id=1, source_target_pairs={{0,1},{1,2},{2,3},{3,4},{4,5},{5,6},{6,7},{7,8},{8,9},{9,10},{10,1... | collective-permute-start | bytes 786440 | tf_op jit(solution)/shard_map/while/body/eval_jaxpr/ppermute | solution.py:16
  1120.8 20.8 %collective-permute-start.4 = (f32[128,4,128]{2,0,1:T(8,128)S(1)}, f32[128,4,128]{2,0,1:T(8,128)S(1)}, u32[]{:S(2)}, u32[]{:S(2)}) collective-permute-start(f32[128,4,128]{2,0,1:T(8,128)S(1)} %fusion.178), channel_id=1, source_target_pairs={{0,1},{1,2},{2,3},{3,4},{4,5},{5,6},{6,7},{7,8},{8,9},{9,10},{10,1... | collective-permute-start | bytes 786440 | tf_op jit(solution)/shard_map/while/body/eval_jaxpr/ppermute | solution.py:16
  (156 other events, 2786.2 us)
where the time goes:
time: 1300 us; the launch traced here: 1290 us
  waiting for transfers between devices  940 us (72%)
  matrix products  201 us (15%)
  other arithmetic  76.4 us (6%)
  local copies, waits for them, and re-layouts  49.7 us (4%)
  starting transfers between devices  18.9 us (1%)
    ppermute x190, waiting for transfers between devices, passed_along(): return lax.ppermute(value, axis, pairs)  940 us
    dot_general x64, matrix products, attend(): jnp.einsum('hrk,khe->rhe', probabilities, value_block, preferred_element_...  92.5 us
    dot_general x32, matrix products, attend_grads(): jnp.einsum('hrk,rhe->khe', probabilities, grad_att, preferred_element_typ...  61.8 us
    while x126, local copies, waits for them, and re-layouts  41.3 us
  transfers between devices with their start and end apart: 192, of which 127 were waited for; matrix products, arithmetic and copies ran while one was open for 15% of the time, Pallas kernels for 0%

commit v1 on v0

v1 whole, which is shorter than its diff:
```python
import functools

import jax
import jax.numpy as jnp
from jax import lax
from jax.experimental import pallas as pl
from jax.experimental.pallas import tpu as pltpu
from jax.sharding import Mesh, PartitionSpec as P

HS = 128
CAP = 128
HEADS = 4
EPS = 1e-05
SCALE = HS ** (-0.5)
BF = jnp.bfloat16
F32 = jnp.float32

NN = (((1,), (0,)), ((), ()))
NT = (((1,), (1,)), ((), ()))
SMEM = pl.BlockSpec(memory_space=pltpu.SMEM)


def dot(a, b, dims=NN):
    return lax.dot_general(a, b, dims, preferred_element_type=F32)


def whole(shape):
    return pl.BlockSpec(shape, lambda *i: (0,) * len(shape))


def call(body, name, grid, in_specs, outs, out_specs, scratch, flops):
    return pl.pallas_call(
        body,
        out_shape=outs,
        grid=grid,
        in_specs=in_specs,
        out_specs=out_specs,
        scratch_shapes=scratch,
        compiler_params=pltpu.CompilerParams(vmem_limit_bytes=48 * 1024 * 1024),
        cost_estimate=pl.CostEstimate(flops=flops, transcendentals=0, bytes_accessed=1 << 20),
        name=name,
    )


def shaped(shape, dtype=BF):
    return jax.ShapeDtypeStruct(shape, dtype)


def normalize(values):
    center = values - jnp.mean(values, axis=-1, keepdims=True)
    spread = lax.rsqrt(jnp.mean(center * center, axis=-1, keepdims=True) + EPS)
    return center * spread, spread


def silu_parts(pre):
    half = 0.5 * pre
    sig = 0.5 + 0.5 * jnp.tanh(half)
    act = pre * sig
    return act, sig + act * (1.0 - sig)


def project_kv(info, x_ref, w_ref, k0, k1, k2, k3, slope_ref, xn_ref, act_ref):
    outs = (k0, k1, k2, k3)
    step = pl.program_id(0)

    @pl.when(step == 0)
    def _():
        normed, _ = normalize(x_ref[...].astype(F32))
        xn_ref[...] = normed.astype(BF)

    act, slope = silu_parts(dot(xn_ref[...], w_ref[...]))
    slope_ref[0] = slope.astype(BF)
    length = info[0]
    rows = info[1] + lax.broadcasted_iota(jnp.int32, (128, 1), 0)
    len_f = jnp.full((128, 1), length, jnp.int32).astype(F32)
    factor = jnp.where(rows < length, jnp.where(step == 0, 1.0, 1.0 / len_f), 0.0)
    act_ref[...] = (act * factor).astype(BF)
    for k in range(4):
        head = (info[2] + k) & 3
        part = act_ref[:, pl.ds(pl.multiple_of(head * HS, HS), HS)]

        @pl.when(step == 0)
        def _():
            outs[k][:, :HS] = part

        @pl.when(step == 1)
        def _():
            outs[k][:, HS:] = part


def project_qg(info, xn_ref, cot_ref, wo_ref, w_ref, k0, k1, k2, k3, slope_ref, act_ref):
    outs = (k0, k1, k2, k3)
    step = pl.program_id(0)
    act, slope = silu_parts(dot(xn_ref[...], w_ref[...]))
    slope_ref[0] = slope.astype(BF)
    act_ref[...] = jnp.where(step == 0, act * (0.5 * SCALE), act).astype(BF)

    def put(lane):
        for k in range(4):
            head = (info[2] + k) & 3
            outs[k][:, lane : lane + HS] = act_ref[:, pl.ds(pl.multiple_of(head * HS, HS), HS)]

    @pl.when(step == 0)
    def _():
        put(0)

    @pl.when(step == 1)
    def _():
        put(HS)
        act_ref[...] = dot(cot_ref[...], wo_ref[...], NT).astype(BF)
        put(2 * HS)


def slot_ids(ids_ref):
    col = ids_ref[...]
    first = lax.broadcasted_iota(jnp.int32, (256, 256), 0)
    second = lax.broadcasted_iota(jnp.int32, (256, 256), 1)
    row = jnp.sum(jnp.where(first == second, col, 0), axis=0, keepdims=True)
    return col, row, first, second


def project_cand(ids_ref, x_ref, w_ref, sent_ref, gate_ref, xn_ref):
    step = pl.program_id(0)

    @pl.when(step == 0)
    def _():
        normed, _ = normalize(x_ref[...].astype(F32))
        xn_ref[...] = normed.astype(BF)

    act, _ = silu_parts(dot(xn_ref[...], w_ref[...]))

    @pl.when(step == 0)
    def _():
        col, row, first, second = slot_ids(ids_ref)
        rank = jnp.sum(jnp.where((col == row) & (first < second), 1, 0), axis=0, keepdims=True)
        slot = row * CAP + rank
        hits = (lax.broadcasted_iota(jnp.int32, (4 * CAP, 256), 0) == slot).astype(F32).astype(BF)
        placed = dot(hits, (act * (0.5 * SCALE)).astype(BF)).astype(BF)
        for u in range(4):
            for h in range(HEADS):
                sent_ref[u * HEADS + h] = placed[u * CAP : (u + 1) * CAP, h * HS : (h + 1) * HS]

    @pl.when(step == 1)
    def _():
        gate_ref[...] = act.astype(BF)


def arrange(info, a0, a1, a2, a3, out_ref):
    for k, a in enumerate((a0, a1, a2, a3)):
        out_ref[(info[2] - k) & 3] = a[...]


def cand_attend(q_ref, *refs):
    kvs, out_ref = refs[:8], refs[8]
    q = q_ref[...].reshape(2 * CAP, HS)
    total = None
    for kv in kvs:
        block = kv[...].reshape(512, 2 * HS)
        half = dot(q, block[:, :HS], NT).astype(BF)
        probs = half + half * jnp.tanh(half)
        more = dot(probs, block[:, HS:])
        total = more if total is None else total + more
    out_ref[...] = total.astype(BF).reshape(2, CAP, HS)


def group_of(info, j):
    core = info[3] if j < 4 else 1 - info[3]
    return core * 4 + ((info[4] - (j & 3)) & 3)


def hist_forward(info, p0, p1, p2, p3, *refs):
    kvs, (att_ref, stat_ref, q_ref, g_ref) = refs[:8], refs[8:]
    for k, part in enumerate((p0, p1, p2, p3)):
        y = (info[2] - k) & 3
        rows = pl.ds(pl.multiple_of(y * 128, 128), 128)
        q_ref[rows, :] = part[:, :HS]
        g_ref[rows, :] = part[:, HS : 2 * HS].astype(F32) * part[:, 2 * HS :].astype(F32)
    mine = group_of(info, 0)
    first = lax.broadcasted_iota(jnp.int32, (128, 128), 0)
    second = lax.broadcasted_iota(jnp.int32, (128, 128), 1)
    masks = []
    for j in range(8):
        lead = jnp.where(group_of(info, j) < mine, 128, jnp.where(group_of(info, j) == mine, 0, -128))
        masks.append((second <= first + lead).astype(F32).astype(BF))
    for y in range(4):
        q = q_ref[y * 128 : (y + 1) * 128, :]
        total = None
        for j, kv in enumerate(kvs):
            block = kv[...].reshape(512, 2 * HS)[: 128 * (y + 1)]
            half = dot(q, block[:, :HS], NT).astype(BF)
            probs = half + half * jnp.tanh(half)
            last = probs[:, 128 * y :] * masks[j]
            probs = last if y == 0 else jnp.concatenate([probs[:, : 128 * y], last], axis=1)
            more = dot(probs, block[:, HS:])
            total = more if total is None else total + more
        att_ref[y * 128 : (y + 1) * 128, :] = total
    att = att_ref[...]
    g = g_ref[...]
    mean = jnp.mean(att, axis=1, keepdims=True)
    center = att - mean
    lane = lax.broadcasted_iota(jnp.int32, (512, 128), 1)
    stats = jnp.where(lane == 0, mean, 0.0)
    stats = jnp.where(lane == 1, jnp.sum(center * center, axis=1, keepdims=True), stats)
    stats = jnp.where(lane == 2, jnp.sum(g, axis=1, keepdims=True), stats)
    stats = jnp.where(lane == 3, jnp.sum(g * center, axis=1, keepdims=True), stats)
    stat_ref[...] = jnp.transpose(stats)[:8]


def normed_grads(info, p0, p1, p2, p3, att_ref, s0, s1, s2, s3, ga_ref, b0, b1, b2, b3, gate_ref, gm_ref):
    for k, part in enumerate((p0, p1, p2, p3)):
        y = (info[2] - k) & 3
        rows = pl.ds(pl.multiple_of(y * 128, 128), 128)
        gate_ref[rows, :] = part[:, HS : 2 * HS].astype(F32)
        gm_ref[rows, :] = part[:, 2 * HS :].astype(F32)
    stats = [s[...] for s in (s0, s1, s2, s3)]
    mean = sum(s[0:1] for s in stats) * 0.25
    squares = sum(s[1:2] + HS * (s[0:1] - mean) * (s[0:1] - mean) for s in stats)
    spread = lax.rsqrt(squares * (1.0 / (HEADS * HS)) + EPS)
    g_mean = sum(s[2:3] for s in stats) * (1.0 / (HEADS * HS))
    ga_sum = sum(s[3:4] + s[2:3] * (s[0:1] - mean) for s in stats)
    ga_mean = ga_sum * spread * (1.0 / (HEADS * HS))
    line = lax.broadcasted_iota(jnp.int32, (128, 512), 0)
    packed = jnp.where(line == 0, mean, 0.0)
    packed = jnp.where(line == 1, spread, packed)
    packed = jnp.where(line == 2, g_mean, packed)
    packed = jnp.where(line == 3, ga_mean, packed)
    cols = jnp.transpose(packed)
    spread_c = cols[:, 1:2]
    normed = (att_ref[...] - cols[:, 0:1]) * spread_c
    gate = gate_ref[...]
    gm = gm_ref[...]
    ga_ref[...] = (spread_c * (gate * gm - cols[:, 2:3] - normed * cols[:, 3:4])).astype(BF)
    gate_ref[...] = normed * gate
    gm_ref[...] = normed * gm
    for k, out in enumerate((b0, b1, b2, b3)):
        y = (info[2] + k) & 3
        rows = pl.ds(pl.multiple_of(y * 128, 128), 128)
        out[:, :HS] = gate_ref[rows, :].astype(BF)
        out[:, HS:] = gm_ref[rows, :].astype(BF)


def slope_times(half, grads):
    t = jnp.tanh(half)
    probs = half + half * t
    slope = (1.0 + t + probs * (1.0 - t)).astype(BF)
    return probs, grads * slope


def hist_dq(info, q_in, ga_ref, *refs):
    kvs, dq_ref = refs[:8], refs[8]
    mine = group_of(info, 0)
    first = lax.broadcasted_iota(jnp.int32, (128, 128), 0)
    second = lax.broadcasted_iota(jnp.int32, (128, 128), 1)
    masks = []
    for j in range(8):
        lead = jnp.where(group_of(info, j) < mine, 128, jnp.where(group_of(info, j) == mine, 0, -128))
        masks.append((second <= first + lead).astype(F32).astype(BF))
    for y in range(4):
        q = q_in[y * 128 : (y + 1) * 128, :]
        ga = ga_ref[y * 128 : (y + 1) * 128, :]
        total = None
        for j, kv in enumerate(kvs):
            block = kv[...].reshape(512, 2 * HS)[: 128 * (y + 1)]
            half = dot(q, block[:, :HS], NT).astype(BF)
            _, ds = slope_times(half, dot(ga, block[:, HS:], NT).astype(BF))
            last = ds[:, 128 * y :] * masks[j]
            ds = last if y == 0 else jnp.concatenate([ds[:, : 128 * y], last], axis=1)
            more = dot(ds, block[:, :HS])
            total = more if total is None else total + more
        dq_ref[y * 128 : (y + 1) * 128, :] = (total * (0.5 * SCALE)).astype(BF)


def hist_dkv(info, dq_ref, kv_ref, *refs):
    qs, gas, outs, all_ref = refs[:8], refs[8:16], refs[16:20], refs[20]
    mine = group_of(info, 0)
    first = lax.broadcasted_iota(jnp.int32, (128, 128), 0)
    second = lax.broadcasted_iota(jnp.int32, (128, 128), 1)
    masks = []
    for j in range(8):
        lead = jnp.where(group_of(info, j) > mine, 128, jnp.where(group_of(info, j) == mine, 0, -128))
        masks.append((first <= second + lead).astype(F32).astype(BF))
    for y in range(4):
        key = kv_ref[y, :, :HS]
        value = kv_ref[y, :, HS:]
        dk = dv = None
        for j in range(8):
            q = qs[j][128 * y :, :]
            ga = gas[j][128 * y :, :]
            half = dot(key, q, NT).astype(BF)
            probs, ds = slope_times(half, dot(value, ga, NT).astype(BF))
            p_first = probs[:, :128] * masks[j]
            d_first = ds[:, :128] * masks[j]
            if y < 3:
                probs = jnp.concatenate([p_first, probs[:, 128:]], axis=1)
                ds = jnp.concatenate([d_first, ds[:, 128:]], axis=1)
            else:
                probs, ds = p_first, d_first
            more_k = dot(ds, q)
            more_v = dot(probs, ga)
            dk = more_k if dk is None else dk + more_k
            dv = more_v if dv is None else dv + more_v
        all_ref[y, :, :HS] = dq_ref[y * 128 : (y + 1) * 128, :]
        all_ref[y, :, HS : 2 * HS] = dk.astype(BF)
        all_ref[y, :, 2 * HS :] = dv.astype(BF)
    for k in range(4):
        outs[k][...] = all_ref[(info[2] + k) & 3]


def hist_close(info, x_ref, wo_ref, b0, b1, b2, b3, out_ref, mixed_ref):
    for k, b in enumerate((b0, b1, b2, b3)):
        head = (info[2] - k) & 3
        mixed_ref[:, pl.ds(pl.multiple_of(head * HS, HS), HS)] = b[:, :HS]
    out_ref[0] = (x_ref[...].astype(F32) + dot(mixed_ref[...], wo_ref[...])).astype(BF)


def grad_close(info, x_ref, cot_ref, skv_ref, sqg_ref, w_ref, *refs):
    ones, twos, out_ref, hid_ref, e_ref = refs[:4], refs[4:8], refs[8], refs[9], refs[10]
    step = pl.program_id(0)

    @pl.when(step == 0)
    def _():
        len_f = jnp.full((128, 1), info[0], jnp.int32).astype(F32)
        for k in range(4):
            head = (info[2] - k) & 3
            cols = pl.ds(pl.multiple_of(head * HS, HS), HS)
            hid_ref[0, :, cols] = ones[k][:, HS:]
            hid_ref[1, :, cols] = (twos[k][:, 2 * HS :].astype(F32) / len_f).astype(BF)
            hid_ref[2, :, cols] = twos[k][:, :HS]
            hid_ref[3, :, cols] = twos[k][:, HS : 2 * HS]
        hid_ref[0] = (hid_ref[0].astype(F32) * sqg_ref[1].astype(F32)).astype(BF)
        hid_ref[1] = (hid_ref[1].astype(F32) * skv_ref[1].astype(F32)).astype(BF)
        hid_ref[2] = (hid_ref[2].astype(F32) * sqg_ref[0].astype(F32)).astype(BF)
        hid_ref[3] = (hid_ref[3].astype(F32) * skv_ref[0].astype(F32)).astype(BF)
        e_ref[...] = jnp.zeros_like(e_ref)

    e_ref[...] += dot(hid_ref[step], w_ref[...], NT)

    @pl.when(step == 3)
    def _():
        normed, spread = normalize(x_ref[...].astype(F32))
        e = e_ref[...]
        back = spread * (
            e
            - jnp.mean(e, axis=-1, keepdims=True)
            - normed * jnp.mean(e * normed, axis=-1, keepdims=True)
        )
        out_ref[0] = (cot_ref[...].astype(F32) + back).astype(BF)


def cand_close(ids_ref, x_ref, gate_ref, wo_ref, ret_ref, out_ref):
    col, row, first, second = slot_ids(ids_ref)
    rank = jnp.sum(jnp.where((col == row) & (second < first), 1, 0), axis=1, keepdims=True)
    slot = col * CAP + rank
    hits = (lax.broadcasted_iota(jnp.int32, (256, 4 * CAP), 1) == slot).astype(F32).astype(BF)
    heads = []
    for h in range(HEADS):
        rows = jnp.concatenate([ret_ref[u * HEADS + h] for u in range(4)], axis=0)
        heads.append(dot(hits, rows))
    normed, _ = normalize(jnp.concatenate(heads, axis=1))
    mixed = (normed * gate_ref[...].astype(F32)).astype(BF)
    out_ref[...] = (x_ref[...].astype(F32) + dot(mixed, wo_ref[...])).astype(BF)


def turned(value, axis, size, steps):
    return lax.ppermute(value, axis, [(i, (i + steps) % size) for i in range(size)])


def crossed(value, steps):
    pairs = []
    for c in range(2):
        for y in range(4):
            for xh in range(2):
                pairs.append(((c * 4 + y) * 2 + xh, (xh * 4 + (y + steps) % 4) * 2 + c))
    return lax.ppermute(value, ("c", "y", "xh"), pairs)


def gathered(value):
    mine = [value] + [turned(value, "z", 4, k) for k in (1, 2, 3)]
    return mine + [turned(v, "c", 2, 1) for v in mine]


def per_device(hist_x, hist_cot, cand_x, cand_loop, hist_len, w_proj, w_out):
    y, xh, z = lax.axis_index("y"), lax.axis_index("xh"), lax.axis_index("z")
    info = jnp.stack(
        [hist_len[0], (y * 8 + xh * 4 + z) * 128, y, lax.axis_index("c"), z]
    ).astype(jnp.int32)
    x_rows = hist_x.reshape(128, 1024)
    cot = hist_cot.reshape(128, 1024)
    row_part = whole((128, 1024))

    def pieces(width):
        return [shaped((128, width))] * 4

    def piece_specs(width):
        return [whole((128, width))] * 4

    def wcol(pick):
        return pl.BlockSpec((1024, 512), lambda i: (0, pick(i)))

    slope = pl.BlockSpec((1, 128, 512), lambda i: (i, 0, 0))
    *kv_out, slope_kv, xn = call(
        project_kv, "project_kv", (2,),
        [SMEM, row_part, wcol(lambda i: 3 - 2 * i)],
        pieces(256) + [shaped((2, 128, 512)), shaped((128, 1024))],
        piece_specs(256) + [slope, row_part],
        [pltpu.VMEM((128, 512), BF)], 270_000_000,
    )(info, x_rows, w_proj)
    kv_in = [crossed(v, k) for k, v in enumerate(kv_out)]

    *qg_out, slope_qg = call(
        project_qg, "project_qg", (2,),
        [SMEM, row_part, row_part, whole((512, 1024)), wcol(lambda i: 2 - 2 * i)],
        pieces(384) + [shaped((2, 128, 512))],
        piece_specs(384) + [slope],
        [pltpu.VMEM((128, 512), BF)], 400_000_000,
    )(info, xn, cot, w_out, w_proj)
    qg_in = [crossed(v, k) for k, v in enumerate(qg_out)]

    sent, cand_gate = call(
        project_cand, "project_cand", (2,),
        [whole((256, 1)), whole((256, 1024)), wcol(lambda i: 2 - 2 * i)],
        [shaped((16, 128, 128)), shaped((256, 512))],
        [whole((16, 128, 128)), whole((256, 512))],
        [pltpu.VMEM((256, 1024), BF)], 700_000_000,
    )(cand_loop, cand_x, w_proj)
    arrived = lax.all_to_all(sent, ("xl", "xh", "y"), 0, 0, tiled=True)

    def arranged(parts, width):
        return call(
            arrange, "arrange", (1,), [SMEM] + piece_specs(width),
            shaped((4, 128, width)), whole((4, 128, width)), [], 1_000_000,
        )(info, *parts)

    kv_mine = arranged(kv_in, 256)
    kvs = gathered(kv_mine)
    q_mine = arranged([v[:, :HS] for v in qg_in], HS).reshape(512, HS)
    qs = gathered(q_mine)
    kv_specs = [whole((4, 128, 256))] * 8
    flat = whole((512, 128))

    att, stats = call(
        hist_forward, "hist_forward", (1,), [SMEM] + piece_specs(384) + kv_specs,
        [shaped((512, 128), F32), shaped((8, 512), F32)], [flat, whole((8, 512))],
        [pltpu.VMEM((512, 128), BF), pltpu.VMEM((512, 128), F32)], 1_400_000_000,
    )(info, *qg_in, *kvs)

    halves = []
    for part in range(2):
        halves.append(
            call(
                cand_attend, "cand_attend", (4,),
                [pl.BlockSpec((2, 128, 128), functools.partial(lambda p, i: (i + 4 * p, 0, 0), part))] + kv_specs,
                shaped((8, 128, 128)), pl.BlockSpec((2, 128, 128), lambda i: (i, 0, 0)),
                [], 4_300_000_000,
            )(arrived, *kvs)
        )
    returned = lax.all_to_all(
        jnp.concatenate(halves, axis=0), ("xl", "xh", "y"), 0, 0, tiled=True
    )

    all_stats = [stats] + [turned(stats, "y", 4, k) for k in (1, 2, 3)]
    ga, *back_one = call(
        normed_grads, "normed_grads", (1,),
        [SMEM] + piece_specs(384) + [flat] + [whole((8, 512))] * 4,
        [shaped((512, 128))] + pieces(256), [flat] + piece_specs(256),
        [pltpu.VMEM((512, 128), F32)] * 2, 1_000_000,
    )(info, *qg_in, att, *all_stats)
    gas = gathered(ga)
    one_in = [crossed(v, k) for k, v in enumerate(back_one)]

    dq = call(
        hist_dq, "hist_dq", (1,), [SMEM, flat, flat] + kv_specs,
        shaped((512, 128)), flat, [], 2_000_000_000,
    )(info, q_mine, ga, *kvs)
    back_two = call(
        hist_dkv, "hist_dkv", (1,), [SMEM, flat, whole((4, 128, 256))] + [flat] * 16,
        pieces(384), piece_specs(384), [pltpu.VMEM((4, 128, 384), BF)], 2_800_000_000,
    )(info, dq, kv_mine, *qs, *gas)
    two_in = [crossed(v, k) for k, v in enumerate(back_two)]

    cand_out = call(
        cand_close, "cand_close", (1,),
        [whole((256, 1)), whole((256, 1024)), whole((256, 512)), whole((512, 1024)), whole((16, 128, 128))],
        shaped((256, 1024)), whole((256, 1024)), [], 400_000_000,
    )(cand_loop, cand_x, cand_gate, w_out, returned)

    out_spec = whole((1, 128, 1024))
    hist_out = call(
        hist_close, "hist_close", (1,),
        [SMEM, row_part, whole((512, 1024))] + piece_specs(256),
        shaped((1, 128, 1024)), out_spec, [pltpu.VMEM((128, 512), BF)], 140_000_000,
    )(info, x_rows, w_out, *one_in)

    hist_grad = call(
        grad_close, "grad_close", (4,),
        [SMEM, row_part, row_part, whole((2, 128, 512)), whole((2, 128, 512)), wcol(lambda i: i)]
        + piece_specs(256) + piece_specs(384),
        shaped((1, 128, 1024)), out_spec,
        [pltpu.VMEM((4, 128, 512), BF), pltpu.VMEM((128, 1024), F32)], 550_000_000,
    )(info, x_rows, cot, slope_kv, slope_qg, w_proj, *one_in, *two_in)
    return hist_out, hist_grad, cand_out


def solution(mesh):
    split = Mesh(mesh.devices.reshape(2, 2, 4, 2, 4), ("xl", "c", "y", "xh", "z"))
    users, rows = ("xl", "c"), ("y", "xh", "z")
    hist = P(users, rows, None)
    cand = P(users + rows, None)
    return jax.shard_map(
        per_device,
        mesh=split,
        in_specs=(hist, hist, cand, cand, P(users), P(), P()),
        out_specs=(hist, hist, cand),
        check_vma=False,
    )
```

time: 1300 us -> 186 us (0.14)
  the two profiles are of different devices: /device:TPU:0 before, /device:TPU:1 now
where the time goes in v1:
time: 186 us; the launch traced here: 185 us
  starting transfers between devices  78.2 us (42%)
  Pallas kernels  56.8 us (31%)
  waiting for transfers between devices  28 us (15%)
  local copies, waits for them, and re-layouts  19.1 us (10%)
    ppermute x16, starting transfers between devices, crossed(): return lax.ppermute(value, ('c', 'y', 'xh'), pairs)  47.7 us
    ppermute x16, waiting for transfers between devices, crossed(): return lax.ppermute(value, ('c', 'y', 'xh'), pairs)  27.9 us
    ppermute x24, starting transfers between devices, turned(): lax.ppermute(value, axis, [(i, (i + steps) % size) for i in range(size)])  20.9 us
    unnamed x83, local copies, waits for them, and re-layouts  18.2 us
    pallas_call x2, Pallas kernels, per_device(): call(cand_attend, 'cand_attend', (4,), [pl.BlockSpec((2, 128, 128), funct...  17.4 us
    pallas_call x1, Pallas kernels, per_device(): call(hist_dkv, 'hist_dkv', (1,), [SMEM, flat, whole((4, 128, 256))] + [fl...  7.95 us
    pallas_call x1, Pallas kernels, per_device(): call(hist_dq, 'hist_dq', (1,), [SMEM, flat, flat] + kv_specs, shaped((512...  6.43 us
    pallas_call x1, Pallas kernels, per_device(): call(hist_forward, 'hist_forward', (1,), [SMEM] + piece_specs(384) + kv_s...  5.39 us
  transfers between devices with their start and end apart: 42, of which 6 were waited for; matrix products, arithmetic and copies ran while one was open for 1% of the time, Pallas kernels for 28%

profile of v1, /device:TPU:1, one launch (start us, length us, event | category | flops | bytes accessed | tf_op | source)
XLA Modules:
  0.0 184.6 jit_solution(14217951862502276046)
XLA Ops:
  1.4 2.2 %copy-done = bf16[1024,2048]{1,0:T(8,128)(2,1)S(1)} copy-done((bf16[1024,2048]{1,0:T(8,128)(2,1)S(1)}, bf16[1024,2048]{1,0:T(8,128)(2,1)}, u32[]{:S(2)}) %copy-start) | copy-done | bytes 4194328
  3.6 0.9 copy-done.4
  4.5 1.8 project_kv.1
  6.4 6.2 %collective-permute-start.4 = (bf16[128,256]{1,0:T(8,128)(2,1)S(1)}, bf16[128,256]{1,0:T(8,128)(2,1)S(1)}, u32[]{:S(2)}, u32[]{:S(2)}) collective-permute-start(bf16[128,256]{1,0:T(8,128)(2,1)S(1)} %get-tuple-element.32), channel_id=1, source_target_pairs={{0,0},{4,32},{8,8},{12,40},{16,16},{20,48},{24,24},{28,56},{32,4},... | collective-permute-start | bytes 196616 | tf_op jit(solution)/shard_map/ppermute | solution.py:374
  12.5 1.1 collective-permute-start.5
  13.6 5.6 %collective-permute-start.6 = (bf16[128,256]{1,0:T(8,128)(2,1)S(1)}, bf16[128,256]{1,0:T(8,128)(2,1)S(1)}, u32[]{:S(2)}, u32[]{:S(2)}) collective-permute-start(bf16[128,256]{1,0:T(8,128)(2,1)S(1)} %get-tuple-element.34), channel_id=1, source_target_pairs={{0,16},{4,48},{8,24},{12,56},{16,0},{20,32},{24,8},{28,40},{32,20}... | collective-permute-start | bytes 196616 | tf_op jit(solution)/shard_map/ppermute | solution.py:374
  20.0 1.8 collective-permute-done.6.a2
  21.9 3.4 %collective-permute-done.7.a3 = bf16[128,256]{1,0:T(8,128)(2,1)S(1)} collective-permute-done((bf16[128,256]{1,0:T(8,128)(2,1)S(1)}, bf16[128,256]{1,0:T(8,128)(2,1)S(1)}, u32[]{:S(2)}, u32[]{:S(2)}) %collective-permute-start.7) | collective-permute-done | bytes 65568 | tf_op jit(solution)/shard_map/ppermute | solution.py:374
  25.9 1.7 collective-permute-start.8
  27.6 3.3 %collective-permute-start.9 = (bf16[4,128,256]{2,1,0:T(8,128)(2,1)S(1)}, bf16[4,128,256]{2,1,0:T(8,128)(2,1)}, u32[]{:S(2)}, u32[]{:S(2)}) collective-permute-start(bf16[4,128,256]{2,1,0:T(8,128)(2,1)S(1)} %arrange.2.refs_0_.kv_ref), channel_id=1, source_target_pairs={{0,2},{1,3},{2,0},{3,1},{4,6},{5,7},{6,4},{7,5},{8,10},{9,11},{10,... | collective-permute-start | bytes 786440 | tf_op jit(solution)/shard_map/ppermute | solution.py:365
  31.6 3.2 %project_qg.1 = (bf16[128,384]{1,0:T(8,128)(2,1)}, bf16[128,384]{1,0:T(8,128)(2,1)S(1)}, bf16[128,384]{1,0:T(8,128)(2,1)S(1)}, bf16[128,384]{1,0:T(8,128)(2,1)S(1)}, bf16[2,128,512]{2,1,0:T(8,128)(2,1)S(1)}) custom-call(s32[5]{0:T(128)S(1)} %stack.19.info, bf16[128,1024]{1,0:T(8,128)(2,1)S(1)} %get-tuple-element.27.xn_ref, bf16[128,1024]{1,0:T(8,128)(2,1)S(1)} %bitcast.10, ...), custom_call_target="tpu_custom_call" | custom-call | flops 400000000 | bytes 1048576 | tf_op jit(solution)/shard_map/project_qg/pallas_call | solution.py:410
  36.8 2.7 %collective-permute-start = (bf16[128,384]{1,0:T(8,128)(2,1)}, bf16[128,384]{1,0:T(8,128)(2,1)}, u32[]{:S(2)}, u32[]{:S(2)}) collective-permute-start(bf16[128,384]{1,0:T(8,128)(2,1)} %get-tuple-element.28), channel_id=1, source_target_pairs={{0,0},{4,32},{8,8},{12,40},{16,16},{20,48},{24,24},{28,56},{32,4},... | collective-permute-start | bytes 294920 | tf_op jit(solution)/shard_map/ppermute | solution.py:374
  39.7 2.2 %copy-done.1 = bf16[1024,2048]{1,0:T(8,128)(2,1)S(1)} copy-done((bf16[1024,2048]{1,0:T(8,128)(2,1)S(1)}, bf16[1024,2048]{1,0:T(8,128)(2,1)}, u32[]{:S(2)}) %copy-start.1) | copy-done | bytes 4194328
  41.9 2.7 %project_cand.1 = (bf16[16,128,128]{2,1,0:T(8,128)(2,1)}, bf16[256,512]{1,0:T(8,128)(2,1)S(1)}) custom-call(s32[256,1]{1,0:T(8,128)S(1)} %copy.11.ids_ref, bf16[256,1024]{1,0:T(8,128)(2,1)S(1)} %copy-done.6, bf16[1024,2048]{1,0:T(8,128)(2,1)S(1)} %copy-done.1), custom_call_target="tpu_custom_call" | custom-call | flops 700000000 | bytes 1048576 | tf_op jit(solution)/shard_map/project_cand/pallas_call | solution.py:419
  44.6 4.5 %all-to-all-start = ((bf16[16,128,128]{2,1,0:T(8,128)(2,1)}), bf16[16,128,128]{2,1,0:T(8,128)(2,1)S(1)}, u32[]{:S(2)}, u32[]{:S(2)}) async-start(bf16[16,128,128]{2,1,0:T(8,128)(2,1)} %get-tuple-element.50), calls=%async_computation | async-start | bytes 1048576 | tf_op jit(solution)/shard_map/all_to_all | solution.py:426
  49.1 5.6 %collective-permute-start.1 = (bf16[128,384]{1,0:T(8,128)(2,1)}, bf16[128,384]{1,0:T(8,128)(2,1)S(1)}, u32[]{:S(2)}, u32[]{:S(2)}) collective-permute-start(bf16[128,384]{1,0:T(8,128)(2,1)} %copy-done.31), channel_id=1, source_target_pairs={{0,8},{4,40},{8,16},{12,48},{16,24},{20,56},{24,0},{28,32},{32,12}... | collective-permute-start | bytes 294920 | tf_op jit(solution)/shard_map/ppermute | solution.py:374
  55.7 6.2 %collective-permute-done.1.p1 = bf16[128,384]{1,0:T(8,128)(2,1)S(1)} collective-permute-done((bf16[128,384]{1,0:T(8,128)(2,1)}, bf16[128,384]{1,0:T(8,128)(2,1)S(1)}, u32[]{:S(2)}, u32[]{:S(2)}) %collective-permute-start.1) | collective-permute-done | bytes 98336 | tf_op jit(solution)/shard_map/ppermute | solution.py:374
  61.9 1.5 collective-permute-start.2
  63.4 6.6 %collective-permute-done.2.p2 = bf16[128,384]{1,0:T(8,128)(2,1)S(1)} collective-permute-done((bf16[128,384]{1,0:T(8,128)(2,1)}, bf16[128,384]{1,0:T(8,128)(2,1)S(1)}, u32[]{:S(2)}, u32[]{:S(2)}) %collective-permute-start.2) | collective-permute-done | bytes 98336 | tf_op jit(solution)/shard_map/ppermute | solution.py:374
  70.1 1.5 collective-permute-start.3
  72.3 4.4 %collective-permute-done.3.p3 = bf16[128,384]{1,0:T(8,128)(2,1)S(1)} collective-permute-done((bf16[128,384]{1,0:T(8,128)(2,1)}, bf16[128,384]{1,0:T(8,128)(2,1)S(1)}, u32[]{:S(2)}, u32[]{:S(2)}) %collective-permute-start.3) | collective-permute-done | bytes 98336 | tf_op jit(solution)/shard_map/ppermute | solution.py:374
  76.7 1.2 arrange.3
  78.9 2.3 %collective-permute-start.24 = (bf16[512,128]{1,0:T(8,128)(2,1)}, bf16[512,128]{1,0:T(8,128)(2,1)}, u32[]{:S(2)}, u32[]{:S(2)}) collective-permute-start(bf16[512,128]{1,0:T(8,128)(2,1)} %bitcast.6.q_in.refs_0_), channel_id=1, source_target_pairs={{0,3},{1,0},{2,1},{3,2},{4,7},{5,4},{6,5},{7,6},{8,11},{9,8},{10,9... | collective-permute-start | bytes 393224 | tf_op jit(solution)/shard_map/ppermute | solution.py:365
  81.2 5.4 %hist_forward.1 = (f32[512,128]{1,0:T(8,128)S(1)}, f32[8,512]{1,0:T(8,128)}) custom-call(s32[5]{0:T(128)S(1)} %stack.19.info, bf16[128,384]{1,0:T(8,128)(2,1)} %collective-permute-done.p0, bf16[128,384]{1,0:T(8,128)(2,1)S(1)} %collective-permute-done.1.p1, bf16[128,384]{1,0:T(8,128)(2,1)S(1)} %collective-permute-done.2.p2, ...), custom_call_target="tpu_custom_call" | custom-call | flops 1400000000 | bytes 1048576 | tf_op jit(solution)/shard_map/hist_forward/pallas_call | solution.py:441
  87.3 3.0 %collective-permute-start.16 = (f32[8,512]{1,0:T(8,128)}, f32[8,512]{1,0:T(8,128)}, u32[]{:S(2)}, u32[]{:S(2)}) collective-permute-start(f32[8,512]{1,0:T(8,128)} %get-tuple-element.37.s0), channel_id=1, source_target_pairs={{0,16},{8,24},{16,0},{24,8},{1,17},{9,25},{17,1},{25,9},{2,18},{10... | collective-permute-start | bytes 49160 | tf_op jit(solution)/shard_map/ppermute | solution.py:365
  91.5 0.9 copy-done.21
  93.5 0.9 copy-done.27
  94.4 8.8 %cand_attend.2 = bf16[8,128,128]{2,1,0:T(8,128)(2,1)S(1)} custom-call(bf16[16,128,128]{2,1,0:T(8,128)(2,1)S(1)} %all-to-all-done.q_ref, bf16[4,128,256]{2,1,0:T(8,128)(2,1)S(1)} %arrange.2.refs_0_.kv_ref, bf16[4,128,256]{2,1,0:T(8,128)(2,1)} %collective-permute-done.8.refs_1_, bf16[4,128,256]{2,1,0:T(8,128)(2,1)} %collective-permute-done.9.refs_2_, ...), custom_call_target="tpu_custom_call" | custom-call | flops 4300000256 | bytes 1048576 | tf_op jit(solution)/shard_map/cand_attend/pallas_call | solution.py:450
  103.2 1.0 collective-permute-start.26
  104.4 2.2 %normed_grads.1 = (bf16[512,128]{1,0:T(8,128)(2,1)}, bf16[128,256]{1,0:T(8,128)(2,1)S(1)}, bf16[128,256]{1,0:T(8,128)(2,1)S(1)}, bf16[128,256]{1,0:T(8,128)(2,1)S(1)}, bf16[128,256]{1,0:T(8,128)(2,1)S(1)}) custom-call(s32[5]{0:T(128)S(1)} %stack.19.info, bf16[128,384]{1,0:T(8,128)(2,1)} %collective-permute-done.p0, bf16[128,384]{1,0:T(8,128)(2,1)S(1)} %copy-done.11, ...), custom_call_target="tpu_custom_call" | custom-call | flops 1000000 | bytes 1048576 | tf_op jit(solution)/shard_map/normed_grads/pallas_call | solution.py:462
  109.2 1.8 collective-permute-start.30
  111.1 1.9 %collective-permute-start.31 = (bf16[512,128]{1,0:T(8,128)(2,1)}, bf16[512,128]{1,0:T(8,128)(2,1)}, u32[]{:S(2)}, u32[]{:S(2)}) collective-permute-start(bf16[512,128]{1,0:T(8,128)(2,1)} %get-tuple-element.44.ga_ref.refs_8_), channel_id=1, source_target_pairs={{0,3},{1,0},{2,1},{3,2},{4,7},{5,4},{6,5},{7,6},{8,11},{9,8},{10,9... | collective-permute-start | bytes 393224 | tf_op jit(solution)/shard_map/ppermute | solution.py:365
  113.0 8.7 %cand_attend.3 = bf16[8,128,128]{2,1,0:T(8,128)(2,1)S(1)} custom-call(bf16[16,128,128]{2,1,0:T(8,128)(2,1)S(1)} %all-to-all-done.q_ref, bf16[4,128,256]{2,1,0:T(8,128)(2,1)S(1)} %arrange.2.refs_0_.kv_ref, bf16[4,128,256]{2,1,0:T(8,128)(2,1)} %collective-permute-done.8.refs_1_, bf16[4,128,256]{2,1,0:T(8,128)(2,1)} %collective-permute-done.9.refs_2_, ...), custom_call_target="tpu_custom_call" | custom-call | flops 4300000256 | bytes 1048576 | tf_op jit(solution)/shard_map/cand_attend/pallas_call | solution.py:450
  122.5 5.1 %all-to-all-start.1 = ((bf16[16,128,128]{2,1,0:T(8,128)(2,1)}), bf16[16,128,128]{2,1,0:T(8,128)(2,1)S(1)}, u32[]{:S(2)}, u32[]{:S(2)}) async-start(bf16[16,128,128]{2,1,0:T(8,128)(2,1)} %pad_maximum_fusion), calls=%async_computation.1 | async-start | bytes 1048576 | tf_op jit(solution)/shard_map/all_to_all | solution.py:457
  127.7 1.6 collective-permute-start.28
  134.1 6.4 %hist_dq.1.dq_ref = bf16[512,128]{1,0:T(8,128)(2,1)S(1)} custom-call(s32[5]{0:T(128)S(1)} %stack.19.info, bf16[512,128]{1,0:T(8,128)(2,1)} %bitcast.6.q_in.refs_0_, bf16[512,128]{1,0:T(8,128)(2,1)} %get-tuple-element.44.ga_ref.refs_8_, bf16[4,128,256]{2,1,0:T(8,128)(2,1)S(1)} %arrange.2.refs_0_.kv_ref, bf16[4,128,256]{2,1,0:T(8,128)(2,1)} %collective-permute-done.8.refs_1_, ...), custom_call_target="tpu_custom_call" | custom-call | flops 2000000000 | bytes 1048576 | tf_op jit(solution)/shard_map/hist_dq/pallas_call | solution.py:471
  140.6 5.0 %collective-permute-start.18 = (bf16[128,256]{1,0:T(8,128)(2,1)S(1)}, bf16[128,256]{1,0:T(8,128)(2,1)S(1)}, u32[]{:S(2)}, u32[]{:S(2)}) collective-permute-start(bf16[128,256]{1,0:T(8,128)(2,1)S(1)} %copy-done.39), channel_id=1, source_target_pairs={{0,0},{4,32},{8,8},{12,40},{16,16},{20,48},{24,24},{28,56},{32,4},... | collective-permute-start | bytes 196616 | tf_op jit(solution)/shard_map/ppermute | solution.py:374
  145.7 1.6 collective-permute-start.19
  147.2 5.1 %collective-permute-start.20 = (bf16[128,256]{1,0:T(8,128)(2,1)S(1)}, bf16[128,256]{1,0:T(8,128)(2,1)S(1)}, u32[]{:S(2)}, u32[]{:S(2)}) collective-permute-start(bf16[128,256]{1,0:T(8,128)(2,1)S(1)} %copy-done.35), channel_id=1, source_target_pairs={{0,16},{4,48},{8,24},{12,56},{16,0},{20,32},{24,8},{28,40},{32,20}... | collective-permute-start | bytes 196616 | tf_op jit(solution)/shard_map/ppermute | solution.py:374
  152.3 8.0 %hist_dkv.1 = (bf16[128,384]{1,0:T(8,128)(2,1)S(1)}, bf16[128,384]{1,0:T(8,128)(2,1)S(1)}, bf16[128,384]{1,0:T(8,128)(2,1)S(1)}, bf16[128,384]{1,0:T(8,128)(2,1)S(1)}) custom-call(s32[5]{0:T(128)S(1)} %stack.19.info, bf16[512,128]{1,0:T(8,128)(2,1)S(1)} %hist_dq.1.dq_ref, bf16[4,128,256]{2,1,0:T(8,128)(2,1)S(1)} %arrange.2.refs_0_.kv_ref, ...), custom_call_target="tpu_custom_call" | custom-call | flops 2800000000 | bytes 1048576 | tf_op jit(solution)/shard_map/hist_dkv/pallas_call | solution.py:475
  160.3 2.5 %collective-permute-start.36 = (bf16[128,384]{1,0:T(8,128)(2,1)S(1)}, bf16[128,384]{1,0:T(8,128)(2,1)S(1)}, u32[]{:S(2)}, u32[]{:S(2)}) collective-permute-start(bf16[128,384]{1,0:T(8,128)(2,1)S(1)} %get-tuple-element.45), channel_id=1, source_target_pairs={{0,0},{4,32},{8,8},{12,40},{16,16},{20,48},{24,24},{28,56},{32,4},... | collective-permute-start | bytes 294920 | tf_op jit(solution)/shard_map/ppermute | solution.py:374
  162.8 2.1 %collective-permute-start.37 = (bf16[128,384]{1,0:T(8,128)(2,1)S(1)}, bf16[128,384]{1,0:T(8,128)(2,1)S(1)}, u32[]{:S(2)}, u32[]{:S(2)}) collective-permute-start(bf16[128,384]{1,0:T(8,128)(2,1)S(1)} %get-tuple-element.46), channel_id=1, source_target_pairs={{0,8},{4,40},{8,16},{12,48},{16,24},{20,56},{24,0},{28,32},{32,12}... | collective-permute-start | bytes 294920 | tf_op jit(solution)/shard_map/ppermute | solution.py:374
  164.9 3.0 %collective-permute-start.38 = (bf16[128,384]{1,0:T(8,128)(2,1)S(1)}, bf16[128,384]{1,0:T(8,128)(2,1)S(1)}, u32[]{:S(2)}, u32[]{:S(2)}) collective-permute-start(bf16[128,384]{1,0:T(8,128)(2,1)S(1)} %get-tuple-element.47), channel_id=1, source_target_pairs={{0,16},{4,48},{8,24},{12,56},{16,0},{20,32},{24,8},{28,40},{32,20}... | collective-permute-start | bytes 294920 | tf_op jit(solution)/shard_map/ppermute | solution.py:374
  167.9 2.7 %collective-permute-start.39 = (bf16[128,384]{1,0:T(8,128)(2,1)S(1)}, bf16[128,384]{1,0:T(8,128)(2,1)S(1)}, u32[]{:S(2)}, u32[]{:S(2)}) collective-permute-start(bf16[128,384]{1,0:T(8,128)(2,1)S(1)} %get-tuple-element.48), channel_id=1, source_target_pairs={{0,24},{4,56},{8,0},{12,32},{16,8},{20,40},{24,16},{28,48},{32,28}... | collective-permute-start | bytes 294920 | tf_op jit(solution)/shard_map/ppermute | solution.py:374
  171.3 5.4 %collective-permute-done.21.b3.refs_3_ = bf16[128,256]{1,0:T(8,128)(2,1)S(1)} collective-permute-done((bf16[128,256]{1,0:T(8,128)(2,1)S(1)}, bf16[128,256]{1,0:T(8,128)(2,1)S(1)}, u32[]{:S(2)}, u32[]{:S(2)}) %collective-permute-start.21) | collective-permute-done | bytes 65568 | tf_op jit(solution)/shard_map/ppermute | solution.py:374
  176.7 1.6 hist_close.1
  178.3 4.2 %grad_close.1 = bf16[1,128,1024]{2,1,0:T(8,128)(2,1)} custom-call(s32[5]{0:T(128)S(1)} %stack.19.info, bf16[128,1024]{1,0:T(8,128)(2,1)S(1)} %bitcast.9, bf16[128,1024]{1,0:T(8,128)(2,1)S(1)} %bitcast.11, bf16[2,128,512]{2,1,0:T(8,128)(2,1)S(1)} %get-tuple-element.42.skv_ref, bf16[2,128,512]{2,1,0:T(8,128)(2,1)S(1)} %get-tuple-element.43.sqg_ref, ...), custom_call_target="tpu_custom_call" | custom-call | flops 550000000 | bytes 1048576 | tf_op jit(solution)/shard_map/grad_close/pallas_call | solution.py:494
  182.5 2.1 %cand_close.1 = bf16[256,1024]{1,0:T(8,128)(2,1)} custom-call(s32[256,1]{1,0:T(8,128)S(1)} %copy.11.ids_ref, bf16[256,1024]{1,0:T(8,128)(2,1)S(1)} %copy-done.6, bf16[256,512]{1,0:T(8,128)(2,1)S(1)} %get-tuple-element.49.gate_ref, bf16[512,1024]{1,0:T(8,128)(2,1)S(1)} %copy-done.3, bf16[16,128,128]{2,1,0:T(8,128)(2,1)S(1)} %all-to-all-done.1.ret_ref), custom_call_target="tpu_custom_call" | custom-call | flops 400000000 | bytes 1048576 | tf_op jit(solution)/shard_map/cand_close/pallas_call | solution.py:481
  (139 shorter events, 19.1 us)
Async XLA Ops:
  4.5 27.1 %copy-start.7 = (bf16[1,128,1024]{2,1,0:T(8,128)(2,1)S(1)}, bf16[1,128,1024]{2,1,0:T(8,128)(2,1)}, u32[]{:S(2)}) copy-start(bf16[1,128,1024]{2,1,0:T(8,128)(2,1)} %param.8) | copy-start | bytes 786436
  6.3 33.2 %copy-start.40 = (s32[256,1]{0,1:T(1,128)S(1)}, s32[256,1]{0,1:T(1,128)}, u32[]{:S(2)}) copy-start(s32[256,1]{0,1:T(1,128)} %param.10) | copy-start | bytes 3076
  6.3 33.3 %copy-start.6 = (bf16[256,1024]{1,0:T(8,128)(2,1)S(1)}, bf16[256,1024]{1,0:T(8,128)(2,1)}, u32[]{:S(2)}) copy-start(bf16[256,1024]{1,0:T(8,128)(2,1)} %x_ref.3) | copy-start | bytes 1572868
  6.4 13.7 %collective-permute-start.4 = (bf16[128,256]{1,0:T(8,128)(2,1)S(1)}, bf16[128,256]{1,0:T(8,128)(2,1)S(1)}, u32[]{:S(2)}, u32[]{:S(2)}) collective-permute-start(bf16[128,256]{1,0:T(8,128)(2,1)S(1)} %get-tuple-element.32), channel_id=1, source_target_pairs={{0,0},{4,32},{8,8},{12,40},{16,16},{20,48},{24,24},{28,56},{32,4},... | collective-permute-start | bytes 196616 | tf_op jit(solution)/shard_map/ppermute | solution.py:374
  12.5 7.5 %collective-permute-start.5 = (bf16[128,256]{1,0:T(8,128)(2,1)S(1)}, bf16[128,256]{1,0:T(8,128)(2,1)S(1)}, u32[]{:S(2)}, u32[]{:S(2)}) collective-permute-start(bf16[128,256]{1,0:T(8,128)(2,1)S(1)} %get-tuple-element.33), channel_id=1, source_target_pairs={{0,8},{4,40},{8,16},{12,48},{16,24},{20,56},{24,0},{28,32},{32,12}... | collective-permute-start | bytes 196616 | tf_op jit(solution)/shard_map/ppermute | solution.py:374
  13.6 8.2 %collective-permute-start.6 = (bf16[128,256]{1,0:T(8,128)(2,1)S(1)}, bf16[128,256]{1,0:T(8,128)(2,1)S(1)}, u32[]{:S(2)}, u32[]{:S(2)}) collective-permute-start(bf16[128,256]{1,0:T(8,128)(2,1)S(1)} %get-tuple-element.34), channel_id=1, source_target_pairs={{0,16},{4,48},{8,24},{12,56},{16,0},{20,32},{24,8},{28,40},{32,20}... | collective-permute-start | bytes 196616 | tf_op jit(solution)/shard_map/ppermute | solution.py:374
  19.2 6.1 %collective-permute-start.7 = (bf16[128,256]{1,0:T(8,128)(2,1)S(1)}, bf16[128,256]{1,0:T(8,128)(2,1)S(1)}, u32[]{:S(2)}, u32[]{:S(2)}) collective-permute-start(bf16[128,256]{1,0:T(8,128)(2,1)S(1)} %get-tuple-element.35), channel_id=1, source_target_pairs={{0,24},{4,56},{8,0},{12,32},{16,8},{20,40},{24,16},{28,48},{32,28}... | collective-permute-start | bytes 196616 | tf_op jit(solution)/shard_map/ppermute | solution.py:374
  25.9 28.8 %collective-permute-start.8 = (bf16[4,128,256]{2,1,0:T(8,128)(2,1)S(1)}, bf16[4,128,256]{2,1,0:T(8,128)(2,1)}, u32[]{:S(2)}, u32[]{:S(2)}) collective-permute-start(bf16[4,128,256]{2,1,0:T(8,128)(2,1)S(1)} %arrange.2.refs_0_.kv_ref), channel_id=1, source_target_pairs={{0,1},{1,2},{2,3},{3,0},{4,5},{5,6},{6,7},{7,4},{8,9},{9,10},{10,1... | collective-permute-start | bytes 786440 | tf_op jit(solution)/shard_map/ppermute | solution.py:365
  27.6 27.6 %collective-permute-start.9 = (bf16[4,128,256]{2,1,0:T(8,128)(2,1)S(1)}, bf16[4,128,256]{2,1,0:T(8,128)(2,1)}, u32[]{:S(2)}, u32[]{:S(2)}) collective-permute-start(bf16[4,128,256]{2,1,0:T(8,128)(2,1)S(1)} %arrange.2.refs_0_.kv_ref), channel_id=1, source_target_pairs={{0,2},{1,3},{2,0},{3,1},{4,6},{5,7},{6,4},{7,5},{8,10},{9,11},{10,... | collective-permute-start | bytes 786440 | tf_op jit(solution)/shard_map/ppermute | solution.py:365
  30.9 24.4 %collective-permute-start.10 = (bf16[4,128,256]{2,1,0:T(8,128)(2,1)S(1)}, bf16[4,128,256]{2,1,0:T(8,128)(2,1)}, u32[]{:S(2)}, u32[]{:S(2)}) collective-permute-start(bf16[4,128,256]{2,1,0:T(8,128)(2,1)S(1)} %arrange.2.refs_0_.kv_ref), channel_id=1, source_target_pairs={{0,3},{1,0},{2,1},{3,2},{4,7},{5,4},{6,5},{7,6},{8,11},{9,8},{10,9... | collective-permute-start | bytes 786440 | tf_op jit(solution)/shard_map/ppermute | solution.py:365
  36.8 17.9 %collective-permute-start = (bf16[128,384]{1,0:T(8,128)(2,1)}, bf16[128,384]{1,0:T(8,128)(2,1)}, u32[]{:S(2)}, u32[]{:S(2)}) collective-permute-start(bf16[128,384]{1,0:T(8,128)(2,1)} %get-tuple-element.28), channel_id=1, source_target_pairs={{0,0},{4,32},{8,8},{12,40},{16,16},{20,48},{24,24},{28,56},{32,4},... | collective-permute-start | bytes 294920 | tf_op jit(solution)/shard_map/ppermute | solution.py:374
  44.6 46.0 %all-to-all-start = ((bf16[16,128,128]{2,1,0:T(8,128)(2,1)}), bf16[16,128,128]{2,1,0:T(8,128)(2,1)S(1)}, u32[]{:S(2)}, u32[]{:S(2)}) async-start(bf16[16,128,128]{2,1,0:T(8,128)(2,1)} %get-tuple-element.50), calls=%async_computation | async-start | bytes 1048576 | tf_op jit(solution)/shard_map/all_to_all | solution.py:426
  49.1 12.8 %collective-permute-start.1 = (bf16[128,384]{1,0:T(8,128)(2,1)}, bf16[128,384]{1,0:T(8,128)(2,1)S(1)}, u32[]{:S(2)}, u32[]{:S(2)}) collective-permute-start(bf16[128,384]{1,0:T(8,128)(2,1)} %copy-done.31), channel_id=1, source_target_pairs={{0,8},{4,40},{8,16},{12,48},{16,24},{20,56},{24,0},{28,32},{32,12}... | collective-permute-start | bytes 294920 | tf_op jit(solution)/shard_map/ppermute | solution.py:374
  54.7 24.0 %collective-permute-start.11 = (bf16[4,128,256]{2,1,0:T(8,128)(2,1)S(1)}, bf16[4,128,256]{2,1,0:T(8,128)(2,1)S(1)}, u32[]{:S(2)}, u32[]{:S(2)}) collective-permute-start(bf16[4,128,256]{2,1,0:T(8,128)(2,1)S(1)} %arrange.2.refs_0_.kv_ref), channel_id=1, source_target_pairs={{0,32},{32,0},{1,33},{33,1},{2,34},{34,2},{3,35},{35,3},{4,36},{36... | collective-permute-start | bytes 786440 | tf_op jit(solution)/shard_map/ppermute | solution.py:365
  54.7 24.2 %collective-permute-start.12 = (bf16[4,128,256]{2,1,0:T(8,128)(2,1)}, bf16[4,128,256]{2,1,0:T(8,128)(2,1)S(1)}, u32[]{:S(2)}, u32[]{:S(2)}) collective-permute-start(bf16[4,128,256]{2,1,0:T(8,128)(2,1)} %collective-permute-done.8.refs_1_), channel_id=1, source_target_pairs={{0,32},{32,0},{1,33},{33,1},{2,34},{34,2},{3,35},{35,3},{4,36},{36... | collective-permute-start | bytes 786440 | tf_op jit(solution)/shard_map/ppermute | solution.py:365
  55.2 26.0 %collective-permute-start.13 = (bf16[4,128,256]{2,1,0:T(8,128)(2,1)}, bf16[4,128,256]{2,1,0:T(8,128)(2,1)S(1)}, u32[]{:S(2)}, u32[]{:S(2)}) collective-permute-start(bf16[4,128,256]{2,1,0:T(8,128)(2,1)} %collective-permute-done.9.refs_2_), channel_id=1, source_target_pairs={{0,32},{32,0},{1,33},{33,1},{2,34},{34,2},{3,35},{35,3},{4,36},{36... | collective-permute-start | bytes 786440 | tf_op jit(solution)/shard_map/ppermute | solution.py:365
  55.3 25.9 %collective-permute-start.14 = (bf16[4,128,256]{2,1,0:T(8,128)(2,1)}, bf16[4,128,256]{2,1,0:T(8,128)(2,1)S(1)}, u32[]{:S(2)}, u32[]{:S(2)}) collective-permute-start(bf16[4,128,256]{2,1,0:T(8,128)(2,1)} %collective-permute-done.10.refs_3_), channel_id=1, source_target_pairs={{0,32},{32,0},{1,33},{33,1},{2,34},{34,2},{3,35},{35,3},{4,36},{36... | collective-permute-start | bytes 786440 | tf_op jit(solution)/shard_map/ppermute | solution.py:365
  61.9 28.4 %copy-start.10 = (bf16[128,384]{1,0:T(8,128)(2,1)}, bf16[128,384]{1,0:T(8,128)(2,1)S(1)}, u32[]{:S(2)}) copy-start(bf16[128,384]{1,0:T(8,128)(2,1)S(1)} %collective-permute-done.1.p1) | copy-start | bytes 294916
  61.9 8.2 %collective-permute-start.2 = (bf16[128,384]{1,0:T(8,128)(2,1)}, bf16[128,384]{1,0:T(8,128)(2,1)S(1)}, u32[]{:S(2)}, u32[]{:S(2)}) collective-permute-start(bf16[128,384]{1,0:T(8,128)(2,1)} %copy-done.30), channel_id=1, source_target_pairs={{0,16},{4,48},{8,24},{12,56},{16,0},{20,32},{24,8},{28,40},{32,20}... | collective-permute-start | bytes 294920 | tf_op jit(solution)/shard_map/ppermute | solution.py:374
  70.1 6.7 %collective-permute-start.3 = (bf16[128,384]{1,0:T(8,128)(2,1)}, bf16[128,384]{1,0:T(8,128)(2,1)S(1)}, u32[]{:S(2)}, u32[]{:S(2)}) collective-permute-start(bf16[128,384]{1,0:T(8,128)(2,1)} %copy-done.29), channel_id=1, source_target_pairs={{0,24},{4,56},{8,0},{12,32},{16,8},{20,40},{24,16},{28,48},{32,28}... | collective-permute-start | bytes 294920 | tf_op jit(solution)/shard_map/ppermute | solution.py:374
  77.9 9.4 %collective-permute-start.22 = (bf16[512,128]{1,0:T(8,128)(2,1)}, bf16[512,128]{1,0:T(8,128)(2,1)}, u32[]{:S(2)}, u32[]{:S(2)}) collective-permute-start(bf16[512,128]{1,0:T(8,128)(2,1)} %bitcast.6.q_in.refs_0_), channel_id=1, source_target_pairs={{0,1},{1,2},{2,3},{3,0},{4,5},{5,6},{6,7},{7,4},{8,9},{9,10},{10,1... | collective-permute-start | bytes 393224 | tf_op jit(solution)/shard_map/ppermute | solution.py:365
  78.7 11.6 %collective-permute-start.23 = (bf16[512,128]{1,0:T(8,128)(2,1)}, bf16[512,128]{1,0:T(8,128)(2,1)}, u32[]{:S(2)}, u32[]{:S(2)}) collective-permute-start(bf16[512,128]{1,0:T(8,128)(2,1)} %bitcast.6.q_in.refs_0_), channel_id=1, source_target_pairs={{0,2},{1,3},{2,0},{3,1},{4,6},{5,7},{6,4},{7,5},{8,10},{9,11},{10,... | collective-permute-start | bytes 393224 | tf_op jit(solution)/shard_map/ppermute | solution.py:365
  78.9 30.3 %collective-permute-start.24 = (bf16[512,128]{1,0:T(8,128)(2,1)}, bf16[512,128]{1,0:T(8,128)(2,1)}, u32[]{:S(2)}, u32[]{:S(2)}) collective-permute-start(bf16[512,128]{1,0:T(8,128)(2,1)} %bitcast.6.q_in.refs_0_), channel_id=1, source_target_pairs={{0,3},{1,0},{2,1},{3,2},{4,7},{5,4},{6,5},{7,6},{8,11},{9,8},{10,9... | collective-permute-start | bytes 393224 | tf_op jit(solution)/shard_map/ppermute | solution.py:365
  81.2 29.9 %collective-permute-start.25 = (bf16[512,128]{1,0:T(8,128)(2,1)}, bf16[512,128]{1,0:T(8,128)(2,1)}, u32[]{:S(2)}, u32[]{:S(2)}) collective-permute-start(bf16[512,128]{1,0:T(8,128)(2,1)} %bitcast.6.q_in.refs_0_), channel_id=1, source_target_pairs={{0,32},{32,0},{1,33},{33,1},{2,34},{34,2},{3,35},{35,3},{4,36},{36... | collective-permute-start | bytes 393224 | tf_op jit(solution)/shard_map/ppermute | solution.py:365
  87.3 15.9 %collective-permute-start.15 = (f32[8,512]{1,0:T(8,128)}, f32[8,512]{1,0:T(8,128)}, u32[]{:S(2)}, u32[]{:S(2)}) collective-permute-start(f32[8,512]{1,0:T(8,128)} %get-tuple-element.37.s0), channel_id=1, source_target_pairs={{0,8},{8,16},{16,24},{24,0},{1,9},{9,17},{17,25},{25,1},{2,10},{10... | collective-permute-start | bytes 49160 | tf_op jit(solution)/shard_map/ppermute | solution.py:365
  87.3 17.0 %collective-permute-start.16 = (f32[8,512]{1,0:T(8,128)}, f32[8,512]{1,0:T(8,128)}, u32[]{:S(2)}, u32[]{:S(2)}) collective-permute-start(f32[8,512]{1,0:T(8,128)} %get-tuple-element.37.s0), channel_id=1, source_target_pairs={{0,16},{8,24},{16,0},{24,8},{1,17},{9,25},{17,1},{25,9},{2,18},{10... | collective-permute-start | bytes 49160 | tf_op jit(solution)/shard_map/ppermute | solution.py:365
  90.3 14.0 %collective-permute-start.17 = (f32[8,512]{1,0:T(8,128)}, f32[8,512]{1,0:T(8,128)}, u32[]{:S(2)}, u32[]{:S(2)}) collective-permute-start(f32[8,512]{1,0:T(8,128)} %get-tuple-element.37.s0), channel_id=1, source_target_pairs={{0,24},{8,0},{16,8},{24,16},{1,25},{9,1},{17,9},{25,17},{2,26},{10... | collective-permute-start | bytes 49160 | tf_op jit(solution)/shard_map/ppermute | solution.py:365
  103.2 24.5 %collective-permute-start.26 = (bf16[512,128]{1,0:T(8,128)(2,1)}, bf16[512,128]{1,0:T(8,128)(2,1)}, u32[]{:S(2)}, u32[]{:S(2)}) collective-permute-start(bf16[512,128]{1,0:T(8,128)(2,1)} %collective-permute-done.22.refs_1_), channel_id=1, source_target_pairs={{0,32},{32,0},{1,33},{33,1},{2,34},{34,2},{3,35},{35,3},{4,36},{36... | collective-permute-start | bytes 393224 | tf_op jit(solution)/shard_map/ppermute | solution.py:365
  104.3 25.0 %collective-permute-start.27 = (bf16[512,128]{1,0:T(8,128)(2,1)}, bf16[512,128]{1,0:T(8,128)(2,1)}, u32[]{:S(2)}, u32[]{:S(2)}) collective-permute-start(bf16[512,128]{1,0:T(8,128)(2,1)} %collective-permute-done.23.refs_2_), channel_id=1, source_target_pairs={{0,32},{32,0},{1,33},{33,1},{2,34},{34,2},{3,35},{35,3},{4,36},{36... | collective-permute-start | bytes 393224 | tf_op jit(solution)/shard_map/ppermute | solution.py:365
  109.1 20.3 %collective-permute-start.29 = (bf16[512,128]{1,0:T(8,128)(2,1)}, bf16[512,128]{1,0:T(8,128)(2,1)}, u32[]{:S(2)}, u32[]{:S(2)}) collective-permute-start(bf16[512,128]{1,0:T(8,128)(2,1)} %get-tuple-element.44.ga_ref.refs_8_), channel_id=1, source_target_pairs={{0,1},{1,2},{2,3},{3,0},{4,5},{5,6},{6,7},{7,4},{8,9},{9,10},{10,1... | collective-permute-start | bytes 393224 | tf_op jit(solution)/shard_map/ppermute | solution.py:365
  109.2 20.6 %collective-permute-start.30 = (bf16[512,128]{1,0:T(8,128)(2,1)}, bf16[512,128]{1,0:T(8,128)(2,1)}, u32[]{:S(2)}, u32[]{:S(2)}) collective-permute-start(bf16[512,128]{1,0:T(8,128)(2,1)} %get-tuple-element.44.ga_ref.refs_8_), channel_id=1, source_target_pairs={{0,2},{1,3},{2,0},{3,1},{4,6},{5,7},{6,4},{7,5},{8,10},{9,11},{10,... | collective-permute-start | bytes 393224 | tf_op jit(solution)/shard_map/ppermute | solution.py:365
  111.1 18.9 %collective-permute-start.31 = (bf16[512,128]{1,0:T(8,128)(2,1)}, bf16[512,128]{1,0:T(8,128)(2,1)}, u32[]{:S(2)}, u32[]{:S(2)}) collective-permute-start(bf16[512,128]{1,0:T(8,128)(2,1)} %get-tuple-element.44.ga_ref.refs_8_), channel_id=1, source_target_pairs={{0,3},{1,0},{2,1},{3,2},{4,7},{5,4},{6,5},{7,6},{8,11},{9,8},{10,9... | collective-permute-start | bytes 393224 | tf_op jit(solution)/shard_map/ppermute | solution.py:365
  122.5 60.0 %all-to-all-start.1 = ((bf16[16,128,128]{2,1,0:T(8,128)(2,1)}), bf16[16,128,128]{2,1,0:T(8,128)(2,1)S(1)}, u32[]{:S(2)}, u32[]{:S(2)}) async-start(bf16[16,128,128]{2,1,0:T(8,128)(2,1)} %pad_maximum_fusion), calls=%async_computation.1 | async-start | bytes 1048576 | tf_op jit(solution)/shard_map/all_to_all | solution.py:457
  127.7 12.9 %collective-permute-start.28 = (bf16[512,128]{1,0:T(8,128)(2,1)}, bf16[512,128]{1,0:T(8,128)(2,1)S(1)}, u32[]{:S(2)}, u32[]{:S(2)}) collective-permute-start(bf16[512,128]{1,0:T(8,128)(2,1)} %collective-permute-done.24.refs_3_), channel_id=1, source_target_pairs={{0,32},{32,0},{1,33},{33,1},{2,34},{34,2},{3,35},{35,3},{4,36},{36... | collective-permute-start | bytes 393224 | tf_op jit(solution)/shard_map/ppermute | solution.py:365
  129.3 16.3 %collective-permute-start.32 = (bf16[512,128]{1,0:T(8,128)(2,1)}, bf16[512,128]{1,0:T(8,128)(2,1)S(1)}, u32[]{:S(2)}, u32[]{:S(2)}) collective-permute-start(bf16[512,128]{1,0:T(8,128)(2,1)} %get-tuple-element.44.ga_ref.refs_8_), channel_id=1, source_target_pairs={{0,32},{32,0},{1,33},{33,1},{2,34},{34,2},{3,35},{35,3},{4,36},{36... | collective-permute-start | bytes 393224 | tf_op jit(solution)/shard_map/ppermute | solution.py:365
  129.4 17.8 %collective-permute-start.33 = (bf16[512,128]{1,0:T(8,128)(2,1)}, bf16[512,128]{1,0:T(8,128)(2,1)S(1)}, u32[]{:S(2)}, u32[]{:S(2)}) collective-permute-start(bf16[512,128]{1,0:T(8,128)(2,1)} %collective-permute-done.29.refs_9_), channel_id=1, source_target_pairs={{0,32},{32,0},{1,33},{33,1},{2,34},{34,2},{3,35},{35,3},{4,36},{36... | collective-permute-start | bytes 393224 | tf_op jit(solution)/shard_map/ppermute | solution.py:365
  129.8 22.5 %collective-permute-start.34 = (bf16[512,128]{1,0:T(8,128)(2,1)}, bf16[512,128]{1,0:T(8,128)(2,1)S(1)}, u32[]{:S(2)}, u32[]{:S(2)}) collective-permute-start(bf16[512,128]{1,0:T(8,128)(2,1)} %collective-permute-done.30.refs_10_), channel_id=1, source_target_pairs={{0,32},{32,0},{1,33},{33,1},{2,34},{34,2},{3,35},{35,3},{4,36},{36... | collective-permute-start | bytes 393224 | tf_op jit(solution)/shard_map/ppermute | solution.py:365
  129.9 22.4 %collective-permute-start.35 = (bf16[512,128]{1,0:T(8,128)(2,1)}, bf16[512,128]{1,0:T(8,128)(2,1)S(1)}, u32[]{:S(2)}, u32[]{:S(2)}) collective-permute-start(bf16[512,128]{1,0:T(8,128)(2,1)} %collective-permute-done.31.refs_11_), channel_id=1, source_target_pairs={{0,32},{32,0},{1,33},{33,1},{2,34},{34,2},{3,35},{35,3},{4,36},{36... | collective-permute-start | bytes 393224 | tf_op jit(solution)/shard_map/ppermute | solution.py:365
  140.6 24.3 %collective-permute-start.18 = (bf16[128,256]{1,0:T(8,128)(2,1)S(1)}, bf16[128,256]{1,0:T(8,128)(2,1)S(1)}, u32[]{:S(2)}, u32[]{:S(2)}) collective-permute-start(bf16[128,256]{1,0:T(8,128)(2,1)S(1)} %copy-done.39), channel_id=1, source_target_pairs={{0,0},{4,32},{8,8},{12,40},{16,16},{20,48},{24,24},{28,56},{32,4},... | collective-permute-start | bytes 196616 | tf_op jit(solution)/shard_map/ppermute | solution.py:374
  145.7 22.2 %collective-permute-start.19 = (bf16[128,256]{1,0:T(8,128)(2,1)S(1)}, bf16[128,256]{1,0:T(8,128)(2,1)S(1)}, u32[]{:S(2)}, u32[]{:S(2)}) collective-permute-start(bf16[128,256]{1,0:T(8,128)(2,1)S(1)} %copy-done.37), channel_id=1, source_target_pairs={{0,8},{4,40},{8,16},{12,48},{16,24},{20,56},{24,0},{28,32},{32,12}... | collective-permute-start | bytes 196616 | tf_op jit(solution)/shard_map/ppermute | solution.py:374
  147.2 29.5 %copy-start.5 = (bf16[1,128,1024]{2,1,0:T(8,128)(2,1)S(1)}, bf16[1,128,1024]{2,1,0:T(8,128)(2,1)}, u32[]{:S(2)}) copy-start(bf16[1,128,1024]{2,1,0:T(8,128)(2,1)} %param.7) | copy-start | bytes 786436
  147.2 31.0 %copy-start.2 = (bf16[1024,2048]{1,0:T(8,128)(2,1)S(1)}, bf16[1024,2048]{1,0:T(8,128)(2,1)}, u32[]{:S(2)}) copy-start(bf16[1024,2048]{1,0:T(8,128)(2,1)} %w_ref.7) | copy-start | bytes 12582916
  147.2 23.3 %collective-permute-start.20 = (bf16[128,256]{1,0:T(8,128)(2,1)S(1)}, bf16[128,256]{1,0:T(8,128)(2,1)S(1)}, u32[]{:S(2)}, u32[]{:S(2)}) collective-permute-start(bf16[128,256]{1,0:T(8,128)(2,1)S(1)} %copy-done.35), channel_id=1, source_target_pairs={{0,16},{4,48},{8,24},{12,56},{16,0},{20,32},{24,8},{28,40},{32,20}... | collective-permute-start | bytes 196616 | tf_op jit(solution)/shard_map/ppermute | solution.py:374
  160.3 17.9 %collective-permute-start.36 = (bf16[128,384]{1,0:T(8,128)(2,1)S(1)}, bf16[128,384]{1,0:T(8,128)(2,1)S(1)}, u32[]{:S(2)}, u32[]{:S(2)}) collective-permute-start(bf16[128,384]{1,0:T(8,128)(2,1)S(1)} %get-tuple-element.45), channel_id=1, source_target_pairs={{0,0},{4,32},{8,8},{12,40},{16,16},{20,48},{24,24},{28,56},{32,4},... | collective-permute-start | bytes 294920 | tf_op jit(solution)/shard_map/ppermute | solution.py:374
  162.8 15.5 %collective-permute-start.37 = (bf16[128,384]{1,0:T(8,128)(2,1)S(1)}, bf16[128,384]{1,0:T(8,128)(2,1)S(1)}, u32[]{:S(2)}, u32[]{:S(2)}) collective-permute-start(bf16[128,384]{1,0:T(8,128)(2,1)S(1)} %get-tuple-element.46), channel_id=1, source_target_pairs={{0,8},{4,40},{8,16},{12,48},{16,24},{20,56},{24,0},{28,32},{32,12}... | collective-permute-start | bytes 294920 | tf_op jit(solution)/shard_map/ppermute | solution.py:374
  164.9 13.3 %collective-permute-start.38 = (bf16[128,384]{1,0:T(8,128)(2,1)S(1)}, bf16[128,384]{1,0:T(8,128)(2,1)S(1)}, u32[]{:S(2)}, u32[]{:S(2)}) collective-permute-start(bf16[128,384]{1,0:T(8,128)(2,1)S(1)} %get-tuple-element.47), channel_id=1, source_target_pairs={{0,16},{4,48},{8,24},{12,56},{16,0},{20,32},{24,8},{28,40},{32,20}... | collective-permute-start | bytes 294920 | tf_op jit(solution)/shard_map/ppermute | solution.py:374
  167.9 10.4 %collective-permute-start.39 = (bf16[128,384]{1,0:T(8,128)(2,1)S(1)}, bf16[128,384]{1,0:T(8,128)(2,1)S(1)}, u32[]{:S(2)}, u32[]{:S(2)}) collective-permute-start(bf16[128,384]{1,0:T(8,128)(2,1)S(1)} %get-tuple-element.48), channel_id=1, source_target_pairs={{0,24},{4,56},{8,0},{12,32},{16,8},{20,40},{24,16},{28,48},{32,28}... | collective-permute-start | bytes 294920 | tf_op jit(solution)/shard_map/ppermute | solution.py:374
  170.6 6.1 %collective-permute-start.21 = (bf16[128,256]{1,0:T(8,128)(2,1)S(1)}, bf16[128,256]{1,0:T(8,128)(2,1)S(1)}, u32[]{:S(2)}, u32[]{:S(2)}) collective-permute-start(bf16[128,256]{1,0:T(8,128)(2,1)S(1)} %copy-done.33), channel_id=1, source_target_pairs={{0,24},{4,56},{8,0},{12,32},{16,8},{20,40},{24,16},{28,48},{32,28}... | collective-permute-start | bytes 196616 | tf_op jit(solution)/shard_map/ppermute | solution.py:374
  (35 other events, 233.0 us)

commit v2 on v1

v2 whole, which is shorter than its diff:
```python
import functools

import jax
import jax.numpy as jnp
from jax import lax
from jax.experimental import pallas as pl
from jax.experimental.pallas import tpu as pltpu
from jax.sharding import Mesh, PartitionSpec as P

HS = 128
CAP = 128
HEADS = 4
EPS = 1e-05
SCALE = HS ** (-0.5)
BF = jnp.bfloat16
F32 = jnp.float32

NN = (((1,), (0,)), ((), ()))
NT = (((1,), (1,)), ((), ()))
SMEM = pl.BlockSpec(memory_space=pltpu.SMEM)


def dot(a, b, dims=NN):
    return lax.dot_general(a, b, dims, preferred_element_type=F32)


def whole(shape):
    return pl.BlockSpec(memory_space=pltpu.VMEM)


def call(body, name, grid, in_specs, outs, out_specs, scratch, flops, after=(), limit=12):
    count = len(in_specs)

    def without(*refs):
        return body(*refs[:count], *refs[count + len(after) :])

    made = pl.pallas_call(
        without if after else body,
        out_shape=outs,
        grid=grid,
        in_specs=list(in_specs) + [pl.BlockSpec(memory_space=pl.ANY)] * len(after),
        out_specs=out_specs,
        scratch_shapes=scratch,
        compiler_params=pltpu.CompilerParams(vmem_limit_bytes=limit * 1024 * 1024),
        cost_estimate=pl.CostEstimate(flops=flops, transcendentals=0, bytes_accessed=1 << 20),
        name=name,
    )
    def run(*args):
        pinned = []
        for arg, spec in zip(args, in_specs):
            if spec is not SMEM:
                space = spec.memory_space or pltpu.VMEM
                arg = pltpu.with_memory_space_constraint(arg, space)
            pinned.append(arg)
        return made(*pinned, *[pltpu.with_memory_space_constraint(t, pltpu.VMEM) for t in after])

    return run


def shaped(shape, dtype=BF):
    return pltpu.VMEM(shape, dtype)


def normalize(values):
    center = values - jnp.mean(values, axis=-1, keepdims=True)
    spread = lax.rsqrt(jnp.mean(center * center, axis=-1, keepdims=True) + EPS)
    return center * spread, spread


def silu_parts(pre):
    half = 0.5 * pre
    sig = 0.5 + 0.5 * jnp.tanh(half)
    act = pre * sig
    return act, sig + act * (1.0 - sig)


def columns(w_ref, buf, sems, picks):
    copies = []
    for slot, pick in enumerate(picks):
        copy = pltpu.make_async_copy(w_ref.at[:, pl.ds(512 * pick, 512)], buf.at[slot], sems.at[slot])
        copy.start()
        copies.append(copy)
    return copies


def slot_ids(ids_ref):
    col = ids_ref[...]
    first = lax.broadcasted_iota(jnp.int32, (256, 256), 0)
    second = lax.broadcasted_iota(jnp.int32, (256, 256), 1)
    row = jnp.sum(jnp.where(first == second, col, 0), axis=0, keepdims=True)
    return col, row, first, second


def project_all(info, x_ref, cot_ref, wo_ref, w_ref, k0, k1, k2, k3, slope_ref, xn_ref, act_ref, buf, sems):
    copies = columns(w_ref, buf, sems, (3, 1, 2, 0))
    normed, _ = normalize(x_ref[...].astype(F32))
    xn_ref[...] = normed.astype(BF)
    rows = info[1] + lax.broadcasted_iota(jnp.int32, (128, 1), 0)
    inside = jnp.where(rows < info[0], 1.0, 0.0)
    length = jnp.full((128, 1), info[0], jnp.int32).astype(F32)

    def put(values, part):
        act_ref[...] = values.astype(BF)
        for k, out in enumerate((k0, k1, k2, k3)):
            lane = pl.multiple_of(((info[2] + k) & 3) * HS, HS)
            out[:, part * HS : (part + 1) * HS] = act_ref[:, pl.ds(lane, HS)]

    put(dot(cot_ref[...], wo_ref[...], NT), 4)
    for part in range(4):
        copies[part].wait()
        act, slope = silu_parts(dot(xn_ref[...], buf[part]))
        slope_ref[part] = slope.astype(BF)
        put(act * (inside, inside / length, 0.5 * SCALE, 1.0)[part], part)


def arrange(info, a0, a1, a2, a3, out_ref):
    for k, a in enumerate((a0, a1, a2, a3)):
        out_ref[(info[2] - k) & 3] = a[:, : 3 * HS]


def project_cand(ids_ref, x_ref, w_ref, sent_ref, gate_ref, xn_ref, buf, sems):
    copies = columns(w_ref, buf, sems, (2, 0))
    xn_ref[...] = normalize(x_ref[...].astype(F32))[0].astype(BF)
    col, row, first, second = slot_ids(ids_ref)
    rank = jnp.sum(jnp.where((col == row) & (first < second), 1, 0), axis=0, keepdims=True)
    slot = row * CAP + rank
    hits = (lax.broadcasted_iota(jnp.int32, (4 * CAP, 256), 0) == slot).astype(F32).astype(BF)
    copies[0].wait()
    act, _ = silu_parts(dot(xn_ref[...], buf[0]))
    placed = dot(hits, (act * (0.5 * SCALE)).astype(BF)).astype(BF)
    for u in range(4):
        for h in range(HEADS):
            sent_ref[u * HEADS + h] = placed[u * CAP : (u + 1) * CAP, h * HS : (h + 1) * HS]
    copies[1].wait()
    act, _ = silu_parts(dot(xn_ref[...], buf[1]))
    gate_ref[...] = act.astype(BF)


def pack(one_ref, two_ref, out_ref):
    out_ref[0] = one_ref[...]
    out_ref[1] = two_ref[...]


def unpack(pair_ref, out_ref):
    out_ref[...] = pair_ref[0]


def blocks_of(refs):
    pair, first, second, third, fourth = refs
    out = [pair.at[0], pair.at[1], first.at[0], first.at[1], second.at[0], second.at[1], third, fourth]
    return out


def order_of(info):
    c, z = info[3], info[4]
    o = 1 - c
    side = 1 - 2 * c
    near, far = (z - side) & 3, (z + side) & 3
    across = (z + 2) & 3
    spots = [(c, z), (o, z), (c, near), (o, near), (o, far), (c, far), (c, across), (o, across)]
    return [4 * core + spot for core, spot in spots]


def corner_masks(info, backward):
    order = order_of(info)
    first = lax.broadcasted_iota(jnp.int32, (128, 128), 0)
    second = lax.broadcasted_iota(jnp.int32, (128, 128), 1)
    masks = []
    for o in order:
        ahead = o > order[0] if backward else o < order[0]
        lead = jnp.where(ahead, 128, jnp.where(o == order[0], 0, -128))
        keep = first <= second + lead if backward else second <= first + lead
        masks.append(keep.astype(F32).astype(BF))
    return masks


def cand_attend(count, begin, end, *refs):
    q_ref, kvs, rest = refs[0], refs[1 : 1 + count], refs[1 + count :]
    q = q_ref[...].reshape(4 * CAP, HS)
    total = None if begin else rest[0][...]
    for kv in kvs:
        pieces = [kv] if len(kv.shape) == 2 else [kv.at[0], kv.at[1]]
        for block in pieces:
            half = dot(q, block[:, :HS], NT).astype(BF)
            probs = half + half * jnp.tanh(half)
            more = dot(probs, block[:, HS : 2 * HS])
            total = more if total is None else total + more
    if end:
        rest[-1][...] = total.astype(BF).reshape(4, CAP, HS)
    else:
        rest[-1][...] = total


def hist_forward(info, p0, p1, p2, p3, *refs):
    blocks, (att_ref, stat_ref, g_ref) = blocks_of(refs[:5]), refs[5:]
    masks = corner_masks(info, False)
    for k, part in enumerate((p0, p1, p2, p3)):
        rows = pl.ds(pl.multiple_of(((info[2] - k) & 3) * 128, 128), 128)
        g_ref[rows, :] = part[:, 3 * HS : 4 * HS].astype(F32) * part[:, 4 * HS :].astype(F32)
    for y in range(4):
        q = blocks[0][y * 128 : (y + 1) * 128, 2 * HS :]
        total = None
        for block, mask in zip(blocks, masks):
            half = dot(q, block[: 128 * (y + 1), :HS], NT).astype(BF)
            probs = half + half * jnp.tanh(half)
            last = probs[:, 128 * y :] * mask
            probs = last if y == 0 else jnp.concatenate([probs[:, : 128 * y], last], axis=1)
            more = dot(probs, block[: 128 * (y + 1), HS : 2 * HS])
            total = more if total is None else total + more
        att_ref[y * 128 : (y + 1) * 128, :] = total
    att = att_ref[...]
    g = g_ref[...]
    mean = jnp.mean(att, axis=1, keepdims=True)
    center = att - mean
    lane = lax.broadcasted_iota(jnp.int32, (512, 128), 1)
    stats = jnp.where(lane == 0, mean, 0.0)
    stats = jnp.where(lane == 1, jnp.sum(center * center, axis=1, keepdims=True), stats)
    stats = jnp.where(lane == 2, jnp.sum(g, axis=1, keepdims=True), stats)
    stats = jnp.where(lane == 3, jnp.sum(g * center, axis=1, keepdims=True), stats)
    stat_ref[...] = jnp.transpose(stats)[:8]


def normed_grads(info, p0, p1, p2, p3, att_ref, s0, s1, s2, s3, ga_ref, mg_ref, gate_ref, gm_ref):
    for k, part in enumerate((p0, p1, p2, p3)):
        y = (info[2] - k) & 3
        rows = pl.ds(pl.multiple_of(y * 128, 128), 128)
        gate_ref[rows, :] = part[:, 3 * HS : 4 * HS].astype(F32)
        gm_ref[rows, :] = part[:, 4 * HS :].astype(F32)
    stats = [s[...] for s in (s0, s1, s2, s3)]
    mean = sum(s[0:1] for s in stats) * 0.25
    squares = sum(s[1:2] + HS * (s[0:1] - mean) * (s[0:1] - mean) for s in stats)
    spread = lax.rsqrt(squares * (1.0 / (HEADS * HS)) + EPS)
    g_mean = sum(s[2:3] for s in stats) * (1.0 / (HEADS * HS))
    ga_sum = sum(s[3:4] + s[2:3] * (s[0:1] - mean) for s in stats)
    ga_mean = ga_sum * spread * (1.0 / (HEADS * HS))
    line = lax.broadcasted_iota(jnp.int32, (128, 512), 0)
    packed = jnp.where(line == 0, mean, 0.0)
    packed = jnp.where(line == 1, spread, packed)
    packed = jnp.where(line == 2, g_mean, packed)
    packed = jnp.where(line == 3, ga_mean, packed)
    cols = jnp.transpose(packed)
    spread_c = cols[:, 1:2]
    normed = (att_ref[...] - cols[:, 0:1]) * spread_c
    gate = gate_ref[...]
    gm = gm_ref[...]
    ga_ref[...] = (spread_c * (gate * gm - cols[:, 2:3] - normed * cols[:, 3:4])).astype(BF)
    mg_ref[:, :HS] = (normed * gate).astype(BF)
    mg_ref[:, HS:] = (normed * gm).astype(BF)


def slope_times(half, grads):
    t = jnp.tanh(half)
    probs = half + half * t
    slope = (1.0 + t + probs * (1.0 - t)).astype(BF)
    return probs, grads * slope


def hist_dq(info, ga_ref, *refs):
    blocks, dq_ref = blocks_of(refs[:5]), refs[5]
    masks = corner_masks(info, False)
    for y in range(4):
        q = blocks[0][y * 128 : (y + 1) * 128, 2 * HS :]
        ga = ga_ref[y * 128 : (y + 1) * 128, :]
        total = None
        for block, mask in zip(blocks, masks):
            key = block[: 128 * (y + 1), :HS]
            half = dot(q, key, NT).astype(BF)
            _, ds = slope_times(half, dot(ga, block[: 128 * (y + 1), HS : 2 * HS], NT).astype(BF))
            last = ds[:, 128 * y :] * mask
            ds = last if y == 0 else jnp.concatenate([ds[:, : 128 * y], last], axis=1)
            more = dot(ds, key)
            total = more if total is None else total + more
        dq_ref[y] = (total * (0.5 * SCALE)).astype(BF)


def hist_dkv(info, dq_ref, mg_ref, *refs):
    blocks, gas, outs, all_ref = blocks_of(refs[:5]), blocks_of(refs[5:10]), refs[10:14], refs[14]
    masks = corner_masks(info, True)
    for y in range(4):
        key = blocks[0][y * 128 : (y + 1) * 128, :HS]
        value = blocks[0][y * 128 : (y + 1) * 128, HS : 2 * HS]
        dk = dv = None
        for block, ga_block, mask in zip(blocks, gas, masks):
            q = block[128 * y :, 2 * HS :]
            ga = ga_block[128 * y :, :]
            half = dot(key, q, NT).astype(BF)
            probs, ds = slope_times(half, dot(value, ga, NT).astype(BF))
            p_first = probs[:, :128] * mask
            d_first = ds[:, :128] * mask
            if y < 3:
                probs = jnp.concatenate([p_first, probs[:, 128:]], axis=1)
                ds = jnp.concatenate([d_first, ds[:, 128:]], axis=1)
            else:
                probs, ds = p_first, d_first
            more_k = dot(ds, q)
            more_v = dot(probs, ga)
            dk = more_k if dk is None else dk + more_k
            dv = more_v if dv is None else dv + more_v
        all_ref[y, :, HS : 2 * HS] = dk.astype(BF)
        all_ref[y, :, 2 * HS : 3 * HS] = dv.astype(BF)
        all_ref[y, :, :HS] = dq_ref[y]
        all_ref[y, :, 3 * HS :] = mg_ref[y * 128 : (y + 1) * 128, :]
    for k in range(4):
        outs[k][...] = all_ref[(info[2] + k) & 3]


def hist_close(info, x_ref, wo_ref, b0, b1, b2, b3, out_ref, mixed_ref):
    for k, b in enumerate((b0, b1, b2, b3)):
        lane = pl.multiple_of(((info[2] - k) & 3) * HS, HS)
        mixed_ref[:, pl.ds(lane, HS)] = b[:, 3 * HS : 4 * HS]
    out_ref[0] = (x_ref[...].astype(F32) + dot(mixed_ref[...], wo_ref[...])).astype(BF)


def grad_close(info, x_ref, cot_ref, slope_ref, w_ref, b0, b1, b2, b3, out_ref, hid_ref, buf, sems):
    copies = columns(w_ref, buf, sems, (0, 1, 2, 3))
    length = jnp.full((128, 1), info[0], jnp.int32).astype(F32)
    for k, b in enumerate((b0, b1, b2, b3)):
        lanes = pl.ds(pl.multiple_of(((info[2] - k) & 3) * HS, HS), HS)

        def put(part, grads, which):
            hid_ref[part, :, lanes] = (grads * slope_ref[which, :, lanes].astype(F32)).astype(BF)

        put(0, b[:, 4 * HS :].astype(F32), 3)
        put(1, b[:, 2 * HS : 3 * HS].astype(F32) / length, 1)
        put(2, b[:, :HS].astype(F32), 2)
        put(3, b[:, HS : 2 * HS].astype(F32), 0)
    e = None
    for part in range(4):
        copies[part].wait()
        more = dot(hid_ref[part], buf[part], NT)
        e = more if e is None else e + more
    normed, spread = normalize(x_ref[...].astype(F32))
    back = spread * (
        e - jnp.mean(e, axis=-1, keepdims=True) - normed * jnp.mean(e * normed, axis=-1, keepdims=True)
    )
    out_ref[0] = (cot_ref[...].astype(F32) + back).astype(BF)


def relay(value_ref, out_ref):
    out_ref[...] = value_ref[...]


def cand_close(ids_ref, x_ref, gate_ref, wo_ref, ret_ref, out_ref):
    col, row, first, second = slot_ids(ids_ref)
    rank = jnp.sum(jnp.where((col == row) & (second < first), 1, 0), axis=1, keepdims=True)
    slot = col * CAP + rank
    hits = (lax.broadcasted_iota(jnp.int32, (256, 4 * CAP), 1) == slot).astype(F32).astype(BF)
    heads = []
    for h in range(HEADS):
        rows = jnp.concatenate([ret_ref[u * HEADS + h] for u in range(4)], axis=0)
        heads.append(dot(hits, rows))
    normed, _ = normalize(jnp.concatenate(heads, axis=1))
    mixed = (normed * gate_ref[...].astype(F32)).astype(BF)
    out_ref[...] = (x_ref[...].astype(F32) + dot(mixed, wo_ref[...])).astype(BF)


def turned(value, axis, size, steps):
    return lax.ppermute(value, axis, [(i, (i + steps) % size) for i in range(size)])


def crossed(value, steps):
    pairs = []
    for c in range(2):
        for y in range(4):
            for xh in range(2):
                pairs.append(((c * 4 + y) * 2 + xh, (xh * 4 + (y + steps) % 4) * 2 + c))
    return lax.ppermute(value, ("c", "y", "xh"), pairs)


def across(value):
    return lax.ppermute(value, "c", [(0, 1), (1, 0)])


def along(value):
    pairs = []
    for z in range(4):
        pairs.append((z, (z + 1) % 4))
        pairs.append((4 + z, 4 + (z + 3) % 4))
    return lax.ppermute(value, ("c", "z"), pairs)


def per_device(hist_x, hist_cot, cand_x, cand_loop, hist_len, w_proj, w_out):
    y, xh, z, c = (lax.axis_index(n) for n in ("y", "xh", "z", "c"))
    x_rows = hist_x.reshape(128, 1024)
    cot = hist_cot.reshape(128, 1024)
    info = jnp.stack([hist_len[0], (y * 8 + xh * 4 + z) * 128, y, c, z]).astype(jnp.int32)
    held = pl.BlockSpec(memory_space=pltpu.VMEM)
    far = pl.BlockSpec(memory_space=pltpu.HBM)

    def weights(count):
        return [pltpu.VMEM((count, 1024, 512), BF), pltpu.SemaphoreType.DMA((count,))]

    def packed(one, two, after=()):
        return call(
            pack, "pack", (1,), [held] * 2, shaped((2,) + one.shape), held, [], 1_000_000, after
        )(one, two)

    def unpacked(pair, after=()):
        return call(unpack, "unpack", (1,), [held], shaped(pair.shape[1:]), held, [], 1_000_000, after)(pair)

    *sent, slope = call(
        project_all, "project_all", (1,), [SMEM, held, held, held, far],
        [shaped((128, 640))] * 4 + [shaped((4, 128, 512))], [held] * 5,
        [pltpu.VMEM((128, 1024), BF), pltpu.VMEM((128, 512), BF)] + weights(4), 700_000_000,
    )(info, x_rows, cot, w_out, w_proj)
    parts = [crossed(v, k) for k, v in enumerate(sent)]

    sent_cand, cand_gate = call(
        project_cand, "project_cand", (1,), [held, held, far],
        [shaped((16, 128, 128)), shaped((256, 512))], [held] * 2,
        [pltpu.VMEM((256, 1024), BF)] + weights(2), 700_000_000, (slope,),
    )(cand_loop, cand_x, w_proj)

    own = call(
        arrange, "arrange", (1,), [SMEM] + [held] * 4, shaped((4, 128, 384)), held, [], 1_000_000,
        (cand_gate,),
    )(info, *parts).reshape(512, 384)
    pair = packed(own, across(own))
    near = along(pair)
    arrived = lax.all_to_all(sent_cand, ("xl", "xh", "y"), 0, 0, tiled=True)
    passing = unpacked(near, (arrived,))
    third = along(passing)
    kvq = [pair, near, across(near), third, across(third)]

    q_spec = pl.BlockSpec((4, 128, 128), lambda i: (i, 0, 0))
    acc_spec = pl.BlockSpec((512, 128), lambda i: (i, 0))

    def cand_part(kvs, total, end, after):
        begin = total is None
        return call(
            functools.partial(cand_attend, len(kvs), begin, end), "cand_attend", (4,),
            [q_spec] + [held] * len(kvs) + ([] if begin else [acc_spec]),
            shaped((16, 128, 128)) if end else shaped((2048, 128), F32),
            q_spec if end else acc_spec, [], 1_000_000_000 * len(kvs), after,
        )(arrived, *kvs, *([] if begin else [total]))

    total = cand_part(kvq[:1], None, False, (passing,))
    att, stats = call(
        hist_forward, "hist_forward", (1,), [SMEM] + [held] * 9,
        [shaped((512, 128), F32), shaped((8, 512), F32)], [held] * 2,
        [pltpu.VMEM((512, 128), F32)], 1_400_000_000, (total,),
    )(info, *parts, *kvq)
    all_stats = [stats] + [turned(stats, "y", 4, k) for k in (1, 2, 3)]
    total = cand_part(kvq[1:3], total, False, (stats,))
    ga, mg = call(
        normed_grads, "normed_grads", (1,), [SMEM] + [held] * 9,
        [shaped((512, 128)), shaped((512, 256))], [held] * 2,
        [pltpu.VMEM((512, 128), F32)] * 2, 1_000_000, (total,),
    )(info, *parts, att, *all_stats)

    ga_pair = packed(ga, across(ga))
    ga_near = along(ga_pair)
    dq = call(
        hist_dq, "hist_dq", (1,), [SMEM] + [held] * 6,
        shaped((4, 128, 128)), held, [], 2_000_000_000, (ga_pair,),
    )(info, ga, *kvq)
    ga_passing = unpacked(ga_near, (dq,))
    ga_third = along(ga_passing)
    gas = [ga_pair, ga_near, across(ga_near), ga_third, across(ga_third)]
    weighed = cand_part(kvq[3:], total, True, (ga_passing,))

    grads = call(
        hist_dkv, "hist_dkv", (1,), [SMEM] + [held] * 12,
        [shaped((128, 640))] * 4, [held] * 4, [pltpu.VMEM((4, 128, 640), BF)], 2_800_000_000,
        (weighed,),
    )(info, dq, mg, *kvq, *gas)
    back = [crossed(v, k) for k, v in enumerate(grads)]

    leaving = call(
        relay, "relay", (1,), [held], shaped((16, 128, 128)), held, [], 1_000_000, tuple(grads[:1])
    )(weighed)
    returned = lax.all_to_all(leaving, ("xl", "xh", "y"), 0, 0, tiled=True)

    hist_grad = call(
        grad_close, "grad_close", (1,), [SMEM] + [held] * 3 + [far] + [held] * 4,
        shaped((1, 128, 1024)), held, [pltpu.VMEM((4, 128, 512), BF)] + weights(4), 550_000_000,
        (leaving,),
    )(info, x_rows, cot, slope, w_proj, *back)
    hist_out = call(
        hist_close, "hist_close", (1,), [SMEM] + [held] * 6,
        shaped((1, 128, 1024)), held, [pltpu.VMEM((128, 512), BF)], 140_000_000, (hist_grad,),
    )(info, x_rows, w_out, *back)
    cand_out = call(
        cand_close, "cand_close", (1,), [held] * 5,
        shaped((256, 1024)), held, [], 400_000_000, (hist_out,),
    )(cand_loop, cand_x, cand_gate, w_out, returned)
    return hist_out, hist_grad, cand_out


def solution(mesh):
    split = Mesh(mesh.devices.reshape(2, 2, 4, 2, 4), ("xl", "c", "y", "xh", "z"))
    users, rows = ("xl", "c"), ("y", "xh", "z")
    hist = P(users, rows, None)
    cand = P(users + rows, None)
    return jax.shard_map(
        per_device,
        mesh=split,
        in_specs=(hist, hist, cand, cand, P(users), P(), P()),
        out_specs=(hist, hist, cand),
        check_vma=False,
    )
```

time: 186 us -> 139 us (0.75)
  starting transfers between devices: 78.2 us -> 47.6 us
  blocking collectives: 0 us -> 14.7 us
  Pallas kernels: 56.8 us -> 44.9 us
  local copies, waits for them, and re-layouts: 19.1 us -> 8.21 us
  waiting for transfers between devices: 28 us -> 21.4 us
    ppermute x16 -> x8, starting transfers between devices: 47.7 us -> 26 us  [crossed(): return lax.ppermute(value, ('c', 'y', 'xh'), pairs)]
    ppermute x24 -> x3, starting transfers between devices: 20.9 us -> 2.78 us  [turned(): lax.ppermute(value, axis, [(i, (i + steps) % size) for i in range(size)])]
    ppermute x16 -> x8, waiting for transfers between devices: 27.9 us -> 10 us  [crossed(): return lax.ppermute(value, ('c', 'y', 'xh'), pairs)]
    all_to_all x0 -> x1, blocking collectives: none -> 14.7 us  [per_device(): arrived = lax.all_to_all(sent_cand, ('xl', 'xh', 'y'), 0, 0, tiled=True)]
    ppermute x0 -> x10, starting transfers between devices: none -> 13.4 us  [the longest x6 8.28 us: across(): return lax.ppermute(value, 'c', [(0, 1), (1, 0)])]
    pallas_call x14 -> x18, Pallas kernels: 56.8 us -> 44.9 us  [run(): made(*pinned, *[pltpu.with_memory_space_constraint(t, pltpu.VMEM) for t i...]
    ppermute x0 -> x10, waiting for transfers between devices: none -> 11.4 us  [the longest x4 8.68 us: along(): return lax.ppermute(value, ('c', 'z'), pairs)]
    unnamed x83 -> x28, local copies, waits for them, and re-layouts: 18.2 us -> 8.13 us
  transfers between devices with their start and end apart: 42 -> 22, of which waited for: 6 -> 10; matrix products, arithmetic and copies ran while one was open for 1% -> 1% of each run, Pallas kernels for 28% -> 19%
where the time goes in v2:
time: 139 us; the launch traced here: 138 us
  starting transfers between devices  47.6 us (34%)
  Pallas kernels  44.9 us (32%)
  waiting for transfers between devices  21.4 us (15%)
  blocking collectives  14.7 us (11%)
  local copies, waits for them, and re-layouts  8.21 us (6%)
  between operations  1.6 us (1%)
    pallas_call x18, Pallas kernels, run(): made(*pinned, *[pltpu.with_memory_space_constraint(t, pltpu.VMEM) for t i...  44.9 us
    ppermute x8, starting transfers between devices, crossed(): return lax.ppermute(value, ('c', 'y', 'xh'), pairs)  26 us
    all_to_all x1, blocking collectives, per_device(): arrived = lax.all_to_all(sent_cand, ('xl', 'xh', 'y'), 0, 0, tiled=True)  14.7 us
    ppermute x8, waiting for transfers between devices, crossed(): return lax.ppermute(value, ('c', 'y', 'xh'), pairs)  10 us
    ppermute x4, waiting for transfers between devices, along(): return lax.ppermute(value, ('c', 'z'), pairs)  8.68 us
    ppermute x6, starting transfers between devices, across(): return lax.ppermute(value, 'c', [(0, 1), (1, 0)])  8.28 us
    unnamed x28, local copies, waits for them, and re-layouts  8.13 us
    all_to_all x1, starting transfers between devices, per_device(): returned = lax.all_to_all(leaving, ('xl', 'xh', 'y'), 0, 0, tiled=True)  5.4 us
  transfers between devices with their start and end apart: 22, of which 10 were waited for; matrix products, arithmetic and copies ran while one was open for 1% of the time, Pallas kernels for 19%

profile of v2, /device:TPU:1, one launch (start us, length us, event | category | flops | bytes accessed | tf_op | source)
XLA Modules:
  0.0 138.4 jit_solution(3917617451148070304)
XLA Ops:
  1.4 1.2 copy-done
  2.6 0.9 copy-done.2
  3.6 0.9 copy-done.5
  4.5 3.8 %project_all.1 = (bf16[128,640]{1,0:T(8,128)(2,1)S(1)}, bf16[128,640]{1,0:T(8,128)(2,1)S(1)}, bf16[128,640]{1,0:T(8,128)(2,1)S(1)}, bf16[128,640]{1,0:T(8,128)(2,1)S(1)}, bf16[4,128,512]{2,1,0:T(8,128)(2,1)S(1)}) custom-call(s32[5]{0:T(128)S(1)} %stack.19.info.refs_0_, bf16[128,1024]{1,0:T(8,128)(2,1)S(1)} %bitcast.7, bf16[128,1024]{1,0:T(8,128)(2,1)S(1)} %bitcast.12, ...), custom_call_target="tpu_custom_call" | custom-call | flops 700000000 | bytes 1048576 | tf_op jit(solution)/shard_map/project_all/pallas_call | solution.py:55
  8.4 6.0 %collective-permute-start = (bf16[128,640]{1,0:T(8,128)(2,1)S(1)}, bf16[128,640]{1,0:T(8,128)(2,1)S(1)}, u32[]{:S(2)}, u32[]{:S(2)}) collective-permute-start(bf16[128,640]{1,0:T(8,128)(2,1)S(1)} %get-tuple-element.18), channel_id=1, source_target_pairs={{0,0},{4,32},{8,8},{12,40},{16,16},{20,48},{24,24},{28,56},{32,4},... | collective-permute-start | bytes 491528 | tf_op jit(solution)/shard_map/ppermute | solution.py:367
  14.4 1.1 collective-permute-start.1
  15.5 5.6 %collective-permute-start.2 = (bf16[128,640]{1,0:T(8,128)(2,1)S(1)}, bf16[128,640]{1,0:T(8,128)(2,1)S(1)}, u32[]{:S(2)}, u32[]{:S(2)}) collective-permute-start(bf16[128,640]{1,0:T(8,128)(2,1)S(1)} %get-tuple-element.20), channel_id=1, source_target_pairs={{0,16},{4,48},{8,24},{12,56},{16,0},{20,32},{24,8},{28,40},{32,20}... | collective-permute-start | bytes 491528 | tf_op jit(solution)/shard_map/ppermute | solution.py:367
  21.1 0.8 collective-permute-start.3
  22.1 2.5 %project_cand.1 = (bf16[16,128,128]{2,1,0:T(8,128)(2,1)S(1)}, bf16[256,512]{1,0:T(8,128)(2,1)S(1)}) custom-call(s32[256,1]{1,0:T(8,128)S(1)} %copy.10.refs_0_, bf16[256,1024]{1,0:T(8,128)(2,1)S(1)} %copy-done.4, bf16[1024,2048]{1,0:T(8,128)(2,1)} %refs_4_.1, bf16[4,128,512]{2,1,0:T(8,128)(2,1)S(1)} %get-tuple-element.22.refs_3_), custom_call_target="tpu_custom_call" | custom-call | flops 700000000 | bytes 1048576 | tf_op jit(solution)/shard_map/project_cand/pallas_call | solution.py:55
  24.6 1.3 collective-permute-done.2.refs_3_
  25.9 2.4 %collective-permute-done.3.refs_4_ = bf16[128,640]{1,0:T(8,128)(2,1)S(1)} collective-permute-done((bf16[128,640]{1,0:T(8,128)(2,1)S(1)}, bf16[128,640]{1,0:T(8,128)(2,1)S(1)}, u32[]{:S(2)}, u32[]{:S(2)}) %collective-permute-start.3) | collective-permute-done | bytes 163872 | tf_op jit(solution)/shard_map/ppermute | solution.py:367
  28.9 1.7 %collective-permute-done.4.two_ref = bf16[512,384]{1,0:T(8,128)(2,1)S(1)} collective-permute-done((bf16[512,384]{1,0:T(8,128)(2,1)S(1)}, bf16[512,384]{1,0:T(8,128)(2,1)S(1)}, u32[]{:S(2)}, u32[]{:S(2)}) %collective-permute-start.4) | collective-permute-done | bytes 393248 | tf_op jit(solution)/shard_map/ppermute | solution.py:371
  30.7 3.8 %collective-permute-start.5 = (bf16[2,512,384]{2,1,0:T(8,128)(2,1)S(1)}, bf16[2,512,384]{2,1,0:T(8,128)(2,1)S(1)}, u32[]{:S(2)}, u32[]{:S(2)}) collective-permute-start(bf16[2,512,384]{2,1,0:T(8,128)(2,1)S(1)} %pack.2.refs_1_.refs_5_.refs_2_.refs_3_), channel_id=1, source_target_pairs={{0,1},{32,35},{1,2},{33,32},{2,3},{34,33},{3,0},{35,34},{4,5},{36,... | collective-permute-start | bytes 2359304 | tf_op jit(solution)/shard_map/ppermute | solution.py:379
  34.6 14.7 %all_to_all.10.refs_1_.refs_0_ = bf16[16,128,128]{2,1,0:T(8,128)(2,1)S(1)} all-to-all(bf16[16,128,128]{2,1,0:T(8,128)(2,1)S(1)} %get-tuple-element.24), channel_id=1, replica_groups=mesh['xl'=2,'c'=2,'y'=4,'xh'=2,'z'=4] {'xl','xh','y'}, dimensions={0} | all-to-all | bytes 1048576 | tf_op jit(solution)/shard_map/all_to_all | solution.py:420
  49.5 6.8 %collective-permute-done.7.refs_8_.refs_5_.refs_1_.refs_6_ = bf16[512,384]{1,0:T(8,128)(2,1)S(1)} collective-permute-done((bf16[512,384]{1,0:T(8,128)(2,1)S(1)}, bf16[512,384]{1,0:T(8,128)(2,1)S(1)}, u32[]{:S(2)}, u32[]{:S(2)}) %collective-permute-start.7) | collective-permute-done | bytes 393248 | tf_op jit(solution)/shard_map/ppermute | solution.py:379
  56.3 1.7 %collective-permute-start.8 = (bf16[512,384]{1,0:T(8,128)(2,1)S(1)}, bf16[512,384]{1,0:T(8,128)(2,1)S(1)}, u32[]{:S(2)}, u32[]{:S(2)}) collective-permute-start(bf16[512,384]{1,0:T(8,128)(2,1)S(1)} %collective-permute-done.7.refs_8_.refs_5_.refs_1_.refs_6_), channel_id=1, source_target_pairs={{0,32},{32,0},{1,33},{33,1},{2,34},{34,2},{3,35},{35,3},{4,36},{36... | collective-permute-start | bytes 1179656 | tf_op jit(solution)/shard_map/ppermute | solution.py:371
  58.0 4.4 %cand_attend.3.refs_10_.refs_3_ = f32[2048,128]{1,0:T(8,128)S(1)} custom-call(bf16[16,128,128]{2,1,0:T(8,128)(2,1)S(1)} %all_to_all.10.refs_1_.refs_0_, bf16[2,512,384]{2,1,0:T(8,128)(2,1)S(1)} %pack.2.refs_1_.refs_5_.refs_2_.refs_3_, bf16[512,384]{1,0:T(8,128)(2,1)S(1)} %unpack.2.refs_2_), custom_call_target="tpu_custom_call" | custom-call | flops 1000000000 | bytes 1048576 | tf_op jit(solution)/shard_map/cand_attend/pallas_call | solution.py:55
  62.4 4.0 %hist_forward.1 = (f32[512,128]{1,0:T(8,128)S(1)}, f32[8,512]{1,0:T(8,128)S(1)}) custom-call(s32[5]{0:T(128)S(1)} %stack.19.info.refs_0_, bf16[128,640]{1,0:T(8,128)(2,1)S(1)} %collective-permute-done.refs_1_, bf16[128,640]{1,0:T(8,128)(2,1)S(1)} %collective-permute-done.1.refs_2_, bf16[128,640]{1,0:T(8,128)(2,1)S(1)} %collective-permute-done.2.refs_3_, ...), custom_call_target="tpu_custom_call" | custom-call | flops 1400000000 | bytes 1048576 | tf_op jit(solution)/shard_map/hist_forward/pallas_call | solution.py:55
  66.4 1.3 collective-permute-start.11
  67.8 0.7 collective-permute-start.10
  68.4 0.8 collective-permute-start.9
  69.2 5.5 %cand_attend.4.refs_10_.refs_3_ = f32[2048,128]{1,0:T(8,128)S(1)} custom-call(bf16[16,128,128]{2,1,0:T(8,128)(2,1)S(1)} %all_to_all.10.refs_1_.refs_0_, bf16[2,512,384]{2,1,0:T(8,128)(2,1)S(1)} %collective-permute-done.5.refs_0_.refs_6_.refs_1_.refs_3_.refs_4_, bf16[2,512,384]{2,1,0:T(8,128)(2,1)S(1)} %collective-permute-done.6.refs_7_.refs_2_.refs_4_.refs_5_, ...), custom_call_target="tpu_custom_call" | custom-call | flops 2000000000 | bytes 1048576 | tf_op jit(solution)/shard_map/cand_attend/pallas_call | solution.py:55
  74.7 1.1 normed_grads.1
  75.8 0.9 collective-permute-start.12
  76.7 1.0 collective-permute-done.12.two_ref
  78.1 5.7 %hist_dq.1.refs_1_ = bf16[4,128,128]{2,1,0:T(8,128)(2,1)S(1)} custom-call(s32[5]{0:T(128)S(1)} %stack.19.info.refs_0_, bf16[512,128]{1,0:T(8,128)(2,1)S(1)} %get-tuple-element.27.one_ref.refs_1_, bf16[2,512,384]{2,1,0:T(8,128)(2,1)S(1)} %pack.2.refs_1_.refs_5_.refs_2_.refs_3_, ...), custom_call_target="tpu_custom_call" | custom-call | flops 2000000000 | bytes 1048576 | tf_op jit(solution)/shard_map/hist_dq/pallas_call | solution.py:55
  83.9 0.8 collective-permute-start.15
  84.7 1.2 collective-permute-start.14
  85.9 1.9 %collective-permute-done.15.refs_11_ = bf16[512,128]{1,0:T(8,128)(2,1)S(1)} collective-permute-done((bf16[512,128]{1,0:T(8,128)(2,1)S(1)}, bf16[512,128]{1,0:T(8,128)(2,1)S(1)}, u32[]{:S(2)}, u32[]{:S(2)}) %collective-permute-start.15) | collective-permute-done | bytes 131104 | tf_op jit(solution)/shard_map/ppermute | solution.py:379
  87.8 4.2 %collective-permute-start.16 = (bf16[512,128]{1,0:T(8,128)(2,1)S(1)}, bf16[512,128]{1,0:T(8,128)(2,1)S(1)}, u32[]{:S(2)}, u32[]{:S(2)}) collective-permute-start(bf16[512,128]{1,0:T(8,128)(2,1)S(1)} %collective-permute-done.15.refs_11_), channel_id=1, source_target_pairs={{0,32},{32,0},{1,33},{33,1},{2,34},{34,2},{3,35},{35,3},{4,36},{36... | collective-permute-start | bytes 393224 | tf_op jit(solution)/shard_map/ppermute | solution.py:371
  92.0 3.3 %cand_attend.5.refs_13_.refs_0_ = bf16[16,128,128]{2,1,0:T(8,128)(2,1)S(1)} custom-call(bf16[16,128,128]{2,1,0:T(8,128)(2,1)S(1)} %all_to_all.10.refs_1_.refs_0_, bf16[512,384]{1,0:T(8,128)(2,1)S(1)} %collective-permute-done.7.refs_8_.refs_5_.refs_1_.refs_6_, bf16[512,384]{1,0:T(8,128)(2,1)S(1)} %collective-permute-done.8.refs_9_.refs_6_.refs_2_.refs_7_, ...), custom_call_target="tpu_custom_call" | custom-call | flops 2000000000 | bytes 1048576 | tf_op jit(solution)/shard_map/cand_attend/pallas_call | solution.py:55
  95.3 7.1 %hist_dkv.1 = (bf16[128,640]{1,0:T(8,128)(2,1)S(1)}, bf16[128,640]{1,0:T(8,128)(2,1)S(1)}, bf16[128,640]{1,0:T(8,128)(2,1)S(1)}, bf16[128,640]{1,0:T(8,128)(2,1)S(1)}) custom-call(s32[5]{0:T(128)S(1)} %stack.19.info.refs_0_, bf16[4,128,128]{2,1,0:T(8,128)(2,1)S(1)} %hist_dq.1.refs_1_, bf16[512,256]{1,0:T(8,128)(2,1)S(1)} %get-tuple-element.28.refs_2_, ...), custom_call_target="tpu_custom_call" | custom-call | flops 2800000000 | bytes 1048576 | tf_op jit(solution)/shard_map/hist_dkv/pallas_call | solution.py:55
  103.8 0.7 copy-done.10
  104.4 0.8 relay.1.refs_9_
  105.9 5.4 %all-to-all-start.1 = ((bf16[16,128,128]{2,1,0:T(8,128)(2,1)}), bf16[16,128,128]{2,1,0:T(8,128)(2,1)S(1)}, u32[]{:S(2)}, u32[]{:S(2)}) async-start(bf16[16,128,128]{2,1,0:T(8,128)(2,1)} %relay.1.refs_9_), calls=%async_computation.1 | async-start | bytes 1048576 | tf_op jit(solution)/shard_map/all_to_all | solution.py:472
  111.3 4.2 %collective-permute-start.18 = (bf16[128,640]{1,0:T(8,128)(2,1)}, bf16[128,640]{1,0:T(8,128)(2,1)S(1)}, u32[]{:S(2)}, u32[]{:S(2)}) collective-permute-start(bf16[128,640]{1,0:T(8,128)(2,1)} %copy-done.10), channel_id=1, source_target_pairs={{0,8},{4,40},{8,16},{12,48},{16,24},{20,56},{24,0},{28,32},{32,12}... | collective-permute-start | bytes 491528 | tf_op jit(solution)/shard_map/ppermute | solution.py:367
  115.6 2.2 %collective-permute-start.19 = (bf16[128,640]{1,0:T(8,128)(2,1)}, bf16[128,640]{1,0:T(8,128)(2,1)S(1)}, u32[]{:S(2)}, u32[]{:S(2)}) collective-permute-start(bf16[128,640]{1,0:T(8,128)(2,1)} %copy-done.9), channel_id=1, source_target_pairs={{0,16},{4,48},{8,24},{12,56},{16,0},{20,32},{24,8},{28,40},{32,20}... | collective-permute-start | bytes 491528 | tf_op jit(solution)/shard_map/ppermute | solution.py:367
  117.8 4.0 %collective-permute-start.20 = (bf16[128,640]{1,0:T(8,128)(2,1)}, bf16[128,640]{1,0:T(8,128)(2,1)S(1)}, u32[]{:S(2)}, u32[]{:S(2)}) collective-permute-start(bf16[128,640]{1,0:T(8,128)(2,1)} %copy-done.8), channel_id=1, source_target_pairs={{0,24},{4,56},{8,0},{12,32},{16,8},{20,40},{24,16},{28,48},{32,28}... | collective-permute-start | bytes 491528 | tf_op jit(solution)/shard_map/ppermute | solution.py:367
  121.8 2.0 %collective-permute-start.17 = (bf16[128,640]{1,0:T(8,128)(2,1)}, bf16[128,640]{1,0:T(8,128)(2,1)S(1)}, u32[]{:S(2)}, u32[]{:S(2)}) collective-permute-start(bf16[128,640]{1,0:T(8,128)(2,1)} %copy-done.7), channel_id=1, source_target_pairs={{0,0},{4,32},{8,8},{12,40},{16,16},{20,48},{24,24},{28,56},{32,4},... | collective-permute-start | bytes 491528 | tf_op jit(solution)/shard_map/ppermute | solution.py:367
  123.8 1.1 collective-permute-done.18.refs_6_.refs_4_
  125.0 1.9 %collective-permute-done.19.refs_7_.refs_5_ = bf16[128,640]{1,0:T(8,128)(2,1)S(1)} collective-permute-done((bf16[128,640]{1,0:T(8,128)(2,1)}, bf16[128,640]{1,0:T(8,128)(2,1)S(1)}, u32[]{:S(2)}, u32[]{:S(2)}) %collective-permute-start.19) | collective-permute-done | bytes 163872 | tf_op jit(solution)/shard_map/ppermute | solution.py:367
  127.3 2.9 %collective-permute-done.17.refs_5_.refs_3_ = bf16[128,640]{1,0:T(8,128)(2,1)S(1)} collective-permute-done((bf16[128,640]{1,0:T(8,128)(2,1)}, bf16[128,640]{1,0:T(8,128)(2,1)S(1)}, u32[]{:S(2)}, u32[]{:S(2)}) %collective-permute-start.17) | collective-permute-done | bytes 163872 | tf_op jit(solution)/shard_map/ppermute | solution.py:367
  130.2 3.9 %grad_close.1.refs_7_ = bf16[1,128,1024]{2,1,0:T(8,128)(2,1)S(1)} custom-call(s32[5]{0:T(128)S(1)} %stack.19.info.refs_0_, bf16[128,1024]{1,0:T(8,128)(2,1)S(1)} %bitcast.8, bf16[128,1024]{1,0:T(8,128)(2,1)S(1)} %bitcast.13, bf16[4,128,512]{2,1,0:T(8,128)(2,1)S(1)} %get-tuple-element.22.refs_3_, bf16[1024,2048]{1,0:T(8,128)(2,1)} %refs_4_.1, ...), custom_call_target="tpu_custom_call" | custom-call | flops 550000000 | bytes 1048576 | tf_op jit(solution)/shard_map/grad_close/pallas_call | solution.py:55
  134.0 0.7 copy.13
  134.7 0.9 hist_close.1.refs_5_
  135.6 0.7 copy.12
  136.3 1.3 cand_close.1
  137.6 0.8 copy.14
  (44 shorter events, 4.0 us)
Async XLA Ops:
  0.6 21.3 %copy-start.11 = (s32[256,1]{0,1:T(1,128)S(1)}, s32[256,1]{0,1:T(1,128)}, u32[]{:S(2)}) copy-start(s32[256,1]{0,1:T(1,128)} %param.10) | copy-start | bytes 3076
  1.4 1.2 copy-start
  2.6 0.9 copy-start.2
  3.6 0.9 copy-start.5
  4.5 17.6 %copy-start.4 = (bf16[256,1024]{1,0:T(8,128)(2,1)S(1)}, bf16[256,1024]{1,0:T(8,128)(2,1)}, u32[]{:S(2)}) copy-start(bf16[256,1024]{1,0:T(8,128)(2,1)} %refs_1_.3) | copy-start | bytes 1572868
  8.4 16.2 %collective-permute-start = (bf16[128,640]{1,0:T(8,128)(2,1)S(1)}, bf16[128,640]{1,0:T(8,128)(2,1)S(1)}, u32[]{:S(2)}, u32[]{:S(2)}) collective-permute-start(bf16[128,640]{1,0:T(8,128)(2,1)S(1)} %get-tuple-element.18), channel_id=1, source_target_pairs={{0,0},{4,32},{8,8},{12,40},{16,16},{20,48},{24,24},{28,56},{32,4},... | collective-permute-start | bytes 491528 | tf_op jit(solution)/shard_map/ppermute | solution.py:367
  14.4 10.2 %collective-permute-start.1 = (bf16[128,640]{1,0:T(8,128)(2,1)S(1)}, bf16[128,640]{1,0:T(8,128)(2,1)S(1)}, u32[]{:S(2)}, u32[]{:S(2)}) collective-permute-start(bf16[128,640]{1,0:T(8,128)(2,1)S(1)} %get-tuple-element.19), channel_id=1, source_target_pairs={{0,8},{4,40},{8,16},{12,48},{16,24},{20,56},{24,0},{28,32},{32,12}... | collective-permute-start | bytes 491528 | tf_op jit(solution)/shard_map/ppermute | solution.py:367
  15.5 10.3 %collective-permute-start.2 = (bf16[128,640]{1,0:T(8,128)(2,1)S(1)}, bf16[128,640]{1,0:T(8,128)(2,1)S(1)}, u32[]{:S(2)}, u32[]{:S(2)}) collective-permute-start(bf16[128,640]{1,0:T(8,128)(2,1)S(1)} %get-tuple-element.20), channel_id=1, source_target_pairs={{0,16},{4,48},{8,24},{12,56},{16,0},{20,32},{24,8},{28,40},{32,20}... | collective-permute-start | bytes 491528 | tf_op jit(solution)/shard_map/ppermute | solution.py:367
  21.1 7.1 %collective-permute-start.3 = (bf16[128,640]{1,0:T(8,128)(2,1)S(1)}, bf16[128,640]{1,0:T(8,128)(2,1)S(1)}, u32[]{:S(2)}, u32[]{:S(2)}) collective-permute-start(bf16[128,640]{1,0:T(8,128)(2,1)S(1)} %get-tuple-element.21), channel_id=1, source_target_pairs={{0,24},{4,56},{8,0},{12,32},{16,8},{20,40},{24,16},{28,48},{32,28}... | collective-permute-start | bytes 491528 | tf_op jit(solution)/shard_map/ppermute | solution.py:367
  28.8 1.8 %collective-permute-start.4 = (bf16[512,384]{1,0:T(8,128)(2,1)S(1)}, bf16[512,384]{1,0:T(8,128)(2,1)S(1)}, u32[]{:S(2)}, u32[]{:S(2)}) collective-permute-start(bf16[512,384]{1,0:T(8,128)(2,1)S(1)} %bitcast.10), channel_id=1, source_target_pairs={{0,32},{32,0},{1,33},{33,1},{2,34},{34,2},{3,35},{35,3},{4,36},{36... | collective-permute-start | bytes 1179656 | tf_op jit(solution)/shard_map/ppermute | solution.py:371
  30.7 18.6 %collective-permute-start.5 = (bf16[2,512,384]{2,1,0:T(8,128)(2,1)S(1)}, bf16[2,512,384]{2,1,0:T(8,128)(2,1)S(1)}, u32[]{:S(2)}, u32[]{:S(2)}) collective-permute-start(bf16[2,512,384]{2,1,0:T(8,128)(2,1)S(1)} %pack.2.refs_1_.refs_5_.refs_2_.refs_3_), channel_id=1, source_target_pairs={{0,1},{32,35},{1,2},{33,32},{2,3},{34,33},{3,0},{35,34},{4,5},{36,... | collective-permute-start | bytes 2359304 | tf_op jit(solution)/shard_map/ppermute | solution.py:379
  49.3 7.0 %collective-permute-start.7 = (bf16[512,384]{1,0:T(8,128)(2,1)S(1)}, bf16[512,384]{1,0:T(8,128)(2,1)S(1)}, u32[]{:S(2)}, u32[]{:S(2)}) collective-permute-start(bf16[512,384]{1,0:T(8,128)(2,1)S(1)} %unpack.2.refs_2_), channel_id=1, source_target_pairs={{0,1},{32,35},{1,2},{33,32},{2,3},{34,33},{3,0},{35,34},{4,5},{36,... | collective-permute-start | bytes 1179656 | tf_op jit(solution)/shard_map/ppermute | solution.py:379
  49.4 13.0 %collective-permute-start.6 = (bf16[2,512,384]{2,1,0:T(8,128)(2,1)S(1)}, bf16[2,512,384]{2,1,0:T(8,128)(2,1)S(1)}, u32[]{:S(2)}, u32[]{:S(2)}) collective-permute-start(bf16[2,512,384]{2,1,0:T(8,128)(2,1)S(1)} %collective-permute-done.5.refs_0_.refs_6_.refs_1_.refs_3_.refs_4_), channel_id=1, source_target_pairs={{0,32},{32,0},{1,33},{33,1},{2,34},{34,2},{3,35},{35,3},{4,36},{36... | collective-permute-start | bytes 2359304 | tf_op jit(solution)/shard_map/ppermute | solution.py:371
  56.3 6.1 %collective-permute-start.8 = (bf16[512,384]{1,0:T(8,128)(2,1)S(1)}, bf16[512,384]{1,0:T(8,128)(2,1)S(1)}, u32[]{:S(2)}, u32[]{:S(2)}) collective-permute-start(bf16[512,384]{1,0:T(8,128)(2,1)S(1)} %collective-permute-done.7.refs_8_.refs_5_.refs_1_.refs_6_), channel_id=1, source_target_pairs={{0,32},{32,0},{1,33},{33,1},{2,34},{34,2},{3,35},{35,3},{4,36},{36... | collective-permute-start | bytes 1179656 | tf_op jit(solution)/shard_map/ppermute | solution.py:371
  66.4 8.3 %collective-permute-start.11 = (f32[8,512]{1,0:T(8,128)S(1)}, f32[8,512]{1,0:T(8,128)S(1)}, u32[]{:S(2)}, u32[]{:S(2)}) collective-permute-start(f32[8,512]{1,0:T(8,128)S(1)} %get-tuple-element.26.refs_4_.refs_6_), channel_id=1, source_target_pairs={{0,24},{8,0},{16,8},{24,16},{1,25},{9,1},{17,9},{25,17},{2,26},{10... | collective-permute-start | bytes 49160 | tf_op jit(solution)/shard_map/ppermute | solution.py:358
  67.8 6.9 %collective-permute-start.10 = (f32[8,512]{1,0:T(8,128)S(1)}, f32[8,512]{1,0:T(8,128)S(1)}, u32[]{:S(2)}, u32[]{:S(2)}) collective-permute-start(f32[8,512]{1,0:T(8,128)S(1)} %get-tuple-element.26.refs_4_.refs_6_), channel_id=1, source_target_pairs={{0,16},{8,24},{16,0},{24,8},{1,17},{9,25},{17,1},{25,9},{2,18},{10... | collective-permute-start | bytes 49160 | tf_op jit(solution)/shard_map/ppermute | solution.py:358
  68.4 6.3 %collective-permute-start.9 = (f32[8,512]{1,0:T(8,128)S(1)}, f32[8,512]{1,0:T(8,128)S(1)}, u32[]{:S(2)}, u32[]{:S(2)}) collective-permute-start(f32[8,512]{1,0:T(8,128)S(1)} %get-tuple-element.26.refs_4_.refs_6_), channel_id=1, source_target_pairs={{0,8},{8,16},{16,24},{24,0},{1,9},{9,17},{17,25},{25,1},{2,10},{10... | collective-permute-start | bytes 49160 | tf_op jit(solution)/shard_map/ppermute | solution.py:358
  75.8 1.9 %collective-permute-start.12 = (bf16[512,128]{1,0:T(8,128)(2,1)S(1)}, bf16[512,128]{1,0:T(8,128)(2,1)S(1)}, u32[]{:S(2)}, u32[]{:S(2)}) collective-permute-start(bf16[512,128]{1,0:T(8,128)(2,1)S(1)} %get-tuple-element.27.one_ref.refs_1_), channel_id=1, source_target_pairs={{0,32},{32,0},{1,33},{33,1},{2,34},{34,2},{3,35},{35,3},{4,36},{36... | collective-permute-start | bytes 393224 | tf_op jit(solution)/shard_map/ppermute | solution.py:371
  77.7 6.1 %collective-permute-start.13 = (bf16[2,512,128]{2,1,0:T(8,128)(2,1)S(1)}, bf16[2,512,128]{2,1,0:T(8,128)(2,1)S(1)}, u32[]{:S(2)}, u32[]{:S(2)}) collective-permute-start(bf16[2,512,128]{2,1,0:T(8,128)(2,1)S(1)} %pack.3.refs_7_.refs_8_), channel_id=1, source_target_pairs={{0,1},{32,35},{1,2},{33,32},{2,3},{34,33},{3,0},{35,34},{4,5},{36,... | collective-permute-start | bytes 786440 | tf_op jit(solution)/shard_map/ppermute | solution.py:379
  83.9 3.9 %collective-permute-start.15 = (bf16[512,128]{1,0:T(8,128)(2,1)S(1)}, bf16[512,128]{1,0:T(8,128)(2,1)S(1)}, u32[]{:S(2)}, u32[]{:S(2)}) collective-permute-start(bf16[512,128]{1,0:T(8,128)(2,1)S(1)} %unpack.3.refs_4_), channel_id=1, source_target_pairs={{0,1},{32,35},{1,2},{33,32},{2,3},{34,33},{3,0},{35,34},{4,5},{36,... | collective-permute-start | bytes 393224 | tf_op jit(solution)/shard_map/ppermute | solution.py:379
  84.7 10.6 %collective-permute-start.14 = (bf16[2,512,128]{2,1,0:T(8,128)(2,1)S(1)}, bf16[2,512,128]{2,1,0:T(8,128)(2,1)S(1)}, u32[]{:S(2)}, u32[]{:S(2)}) collective-permute-start(bf16[2,512,128]{2,1,0:T(8,128)(2,1)S(1)} %collective-permute-done.13.refs_0_.refs_9_), channel_id=1, source_target_pairs={{0,32},{32,0},{1,33},{33,1},{2,34},{34,2},{3,35},{35,3},{4,36},{36... | collective-permute-start | bytes 786440 | tf_op jit(solution)/shard_map/ppermute | solution.py:371
  87.8 7.5 %collective-permute-start.16 = (bf16[512,128]{1,0:T(8,128)(2,1)S(1)}, bf16[512,128]{1,0:T(8,128)(2,1)S(1)}, u32[]{:S(2)}, u32[]{:S(2)}) collective-permute-start(bf16[512,128]{1,0:T(8,128)(2,1)S(1)} %collective-permute-done.15.refs_11_), channel_id=1, source_target_pairs={{0,32},{32,0},{1,33},{33,1},{2,34},{34,2},{3,35},{35,3},{4,36},{36... | collective-permute-start | bytes 393224 | tf_op jit(solution)/shard_map/ppermute | solution.py:371
  95.3 34.8 %copy-start.3 = (bf16[1,128,1024]{2,1,0:T(8,128)(2,1)S(1)}, bf16[1,128,1024]{2,1,0:T(8,128)(2,1)}, u32[]{:S(2)}) copy-start(bf16[1,128,1024]{2,1,0:T(8,128)(2,1)} %param.7) | copy-start | bytes 786436
  95.3 34.8 %copy-start.6 = (bf16[1,128,1024]{2,1,0:T(8,128)(2,1)S(1)}, bf16[1,128,1024]{2,1,0:T(8,128)(2,1)}, u32[]{:S(2)}) copy-start(bf16[1,128,1024]{2,1,0:T(8,128)(2,1)} %param.8) | copy-start | bytes 786436
  102.5 0.7 copy-start.8
  103.1 0.7 copy-start.9
  103.8 0.7 copy-start.10
  105.3 0.7 copy-start.7
  105.9 28.8 %copy-start.1 = (bf16[512,1024]{1,0:T(8,128)(2,1)S(1)}, bf16[512,1024]{1,0:T(8,128)(2,1)}, u32[]{:S(2)}) copy-start(bf16[512,1024]{1,0:T(8,128)(2,1)} %refs_3_.1) | copy-start | bytes 3145732
  105.9 30.4 %all-to-all-start.1 = ((bf16[16,128,128]{2,1,0:T(8,128)(2,1)}), bf16[16,128,128]{2,1,0:T(8,128)(2,1)S(1)}, u32[]{:S(2)}, u32[]{:S(2)}) async-start(bf16[16,128,128]{2,1,0:T(8,128)(2,1)} %relay.1.refs_9_), calls=%async_computation.1 | async-start | bytes 1048576 | tf_op jit(solution)/shard_map/all_to_all | solution.py:472
  111.3 13.6 %collective-permute-start.18 = (bf16[128,640]{1,0:T(8,128)(2,1)}, bf16[128,640]{1,0:T(8,128)(2,1)S(1)}, u32[]{:S(2)}, u32[]{:S(2)}) collective-permute-start(bf16[128,640]{1,0:T(8,128)(2,1)} %copy-done.10), channel_id=1, source_target_pairs={{0,8},{4,40},{8,16},{12,48},{16,24},{20,56},{24,0},{28,32},{32,12}... | collective-permute-start | bytes 491528 | tf_op jit(solution)/shard_map/ppermute | solution.py:367
  115.6 11.3 %collective-permute-start.19 = (bf16[128,640]{1,0:T(8,128)(2,1)}, bf16[128,640]{1,0:T(8,128)(2,1)S(1)}, u32[]{:S(2)}, u32[]{:S(2)}) collective-permute-start(bf16[128,640]{1,0:T(8,128)(2,1)} %copy-done.9), channel_id=1, source_target_pairs={{0,16},{4,48},{8,24},{12,56},{16,0},{20,32},{24,8},{28,40},{32,20}... | collective-permute-start | bytes 491528 | tf_op jit(solution)/shard_map/ppermute | solution.py:367
  117.8 9.5 %collective-permute-start.20 = (bf16[128,640]{1,0:T(8,128)(2,1)}, bf16[128,640]{1,0:T(8,128)(2,1)S(1)}, u32[]{:S(2)}, u32[]{:S(2)}) collective-permute-start(bf16[128,640]{1,0:T(8,128)(2,1)} %copy-done.8), channel_id=1, source_target_pairs={{0,24},{4,56},{8,0},{12,32},{16,8},{20,40},{24,16},{28,48},{32,28}... | collective-permute-start | bytes 491528 | tf_op jit(solution)/shard_map/ppermute | solution.py:367
  121.8 8.3 %collective-permute-start.17 = (bf16[128,640]{1,0:T(8,128)(2,1)}, bf16[128,640]{1,0:T(8,128)(2,1)S(1)}, u32[]{:S(2)}, u32[]{:S(2)}) collective-permute-start(bf16[128,640]{1,0:T(8,128)(2,1)} %copy-done.7), channel_id=1, source_target_pairs={{0,0},{4,32},{8,8},{12,40},{16,16},{20,48},{24,24},{28,56},{32,4},... | collective-permute-start | bytes 491528 | tf_op jit(solution)/shard_map/ppermute | solution.py:367

commit v3 on v2

v3 whole, which is shorter than its diff:
```python
import functools

import jax
import jax.numpy as jnp
from jax import lax
from jax.experimental import pallas as pl
from jax.experimental.pallas import tpu as pltpu
from jax.sharding import Mesh, PartitionSpec as P

HS = 128
CAP = 128
HEADS = 4
EPS = 1e-05
SCALE = HS ** (-0.5)
BF = jnp.bfloat16
F32 = jnp.float32

NN = (((1,), (0,)), ((), ()))
NT = (((1,), (1,)), ((), ()))
SMEM = pl.BlockSpec(memory_space=pltpu.SMEM)


def dot(a, b, dims=NN):
    return lax.dot_general(a, b, dims, preferred_element_type=F32)


def whole(shape):
    return pl.BlockSpec(memory_space=pltpu.VMEM)


def call(body, name, grid, in_specs, outs, out_specs, scratch, flops, after=(), limit=12, carry=()):
    count, extra = len(in_specs), len(after) + len(carry)
    single = not isinstance(outs, (list, tuple))
    outs = [outs] if single else list(outs)
    out_specs = [out_specs] if single else list(out_specs)
    kept = len(outs)
    anywhere = pl.BlockSpec(memory_space=pl.ANY)

    def without(*refs):
        first = count + extra
        return body(*refs[:count], *refs[first : first + kept], *refs[first + kept + len(carry) :])

    made = pl.pallas_call(
        without,
        out_shape=outs + [jax.ShapeDtypeStruct(v.shape, v.dtype) for v in carry],
        grid=grid,
        in_specs=list(in_specs) + [anywhere] * extra,
        out_specs=out_specs + [anywhere] * len(carry),
        input_output_aliases={count + len(after) + n: kept + n for n in range(len(carry))},
        scratch_shapes=scratch,
        compiler_params=pltpu.CompilerParams(vmem_limit_bytes=limit * 1024 * 1024),
        cost_estimate=pl.CostEstimate(flops=flops, transcendentals=0, bytes_accessed=1 << 20),
        name=name,
    )

    def run(*args):
        pinned = []
        for arg, spec in zip(args, in_specs):
            if spec is not SMEM:
                space = spec.memory_space or pltpu.VMEM
                arg = pltpu.with_memory_space_constraint(arg, space)
            pinned.append(arg)
        got = made(*pinned, *after, *carry)
        return got[0] if len(got) == 1 and single else got

    return run


def shaped(shape, dtype=BF):
    return pltpu.VMEM(shape, dtype)


def normalize(values):
    center = values - jnp.mean(values, axis=-1, keepdims=True)
    spread = lax.rsqrt(jnp.mean(center * center, axis=-1, keepdims=True) + EPS)
    return center * spread, spread


def silu_parts(pre):
    half = 0.5 * pre
    sig = 0.5 + 0.5 * jnp.tanh(half)
    act = pre * sig
    return act, sig + act * (1.0 - sig)


def columns(w_ref, buf, sems, picks):
    copies = []
    for slot, pick in enumerate(picks):
        copy = pltpu.make_async_copy(w_ref.at[:, pl.ds(512 * pick, 512)], buf.at[slot], sems.at[slot])
        copy.start()
        copies.append(copy)
    return copies


def slot_ids(ids_ref):
    col = ids_ref[...]
    first = lax.broadcasted_iota(jnp.int32, (256, 256), 0)
    second = lax.broadcasted_iota(jnp.int32, (256, 256), 1)
    row = jnp.sum(jnp.where(first == second, col, 0), axis=0, keepdims=True)
    return col, row, first, second


def fetched(pairs, sems):
    copies = []
    for slot, (source, target) in enumerate(pairs):
        copy = pltpu.make_async_copy(source, target, sems.at[slot])
        copy.start()
        copies.append(copy)
    return copies


def project_all(
    info, x_far, cot_far, wo_far, w_ref, k0, k1, k2, k3, slope_ref,
    xn_ref, act_ref, x_ref, cot_ref, wo_ref, few, buf, sems,
):
    (got_x,) = fetched([(x_far, x_ref)], few)
    copies = columns(w_ref, buf, sems, (3, 1, 2, 0))
    rest = fetched([(cot_far, cot_ref), (wo_far, wo_ref)], few.at[pl.ds(1, 2)])
    got_x.wait()
    normed, _ = normalize(x_ref[...].astype(F32))
    xn_ref[...] = normed.astype(BF)
    rows = info[1] + lax.broadcasted_iota(jnp.int32, (128, 1), 0)
    inside = jnp.where(rows < info[0], 1.0, 0.0)
    length = jnp.full((128, 1), info[0], jnp.int32).astype(F32)

    def put(values, part):
        act_ref[...] = values.astype(BF)
        for k, out in enumerate((k0, k1, k2, k3)):
            lane = pl.multiple_of(((info[2] + k) & 3) * HS, HS)
            out[:, part * HS : (part + 1) * HS] = act_ref[:, pl.ds(lane, HS)]

    for part in range(4):
        copies[part].wait()
        act, slope = silu_parts(dot(xn_ref[...], buf[part]))
        slope_ref[part] = slope.astype(BF)
        put(act * (inside, inside / length, 0.5 * SCALE, 1.0)[part], part)
    for copy in rest:
        copy.wait()
    put(dot(cot_ref[...], wo_ref[...], NT), 4)


def arrange(info, a0, a1, a2, a3, out_ref):
    for k, a in enumerate((a0, a1, a2, a3)):
        out_ref[(info[2] - k) & 3] = a[:, : 3 * HS]


def project_cand(ids_ref, x_ref, w_ref, sent_ref, gate_ref, xn_ref, buf, sems):
    copies = columns(w_ref, buf, sems, (2, 0))
    xn_ref[...] = normalize(x_ref[...].astype(F32))[0].astype(BF)
    col, row, first, second = slot_ids(ids_ref)
    rank = jnp.sum(jnp.where((col == row) & (first < second), 1, 0), axis=0, keepdims=True)
    slot = row * CAP + rank
    hits = (lax.broadcasted_iota(jnp.int32, (4 * CAP, 256), 0) == slot).astype(F32).astype(BF)
    copies[0].wait()
    act, _ = silu_parts(dot(xn_ref[...], buf[0]))
    placed = dot(hits, (act * (0.5 * SCALE)).astype(BF)).astype(BF)
    for u in range(4):
        for h in range(HEADS):
            sent_ref[u * HEADS + h] = placed[u * CAP : (u + 1) * CAP, h * HS : (h + 1) * HS]
    copies[1].wait()
    act, _ = silu_parts(dot(xn_ref[...], buf[1]))
    gate_ref[...] = act.astype(BF)


def nothing(*refs):
    del refs


def order_of(info):
    c, z = info[3], info[4]
    o = 1 - c
    side = 1 - 2 * c
    near, far = (z - side) & 3, (z + side) & 3
    across = (z + 2) & 3
    spots = [(c, z), (o, z), (c, near), (o, far), (c, far), (o, near), (c, across), (o, across)]
    return [4 * core + spot for core, spot in spots]


def corner_masks(info, backward):
    order = order_of(info)
    first = lax.broadcasted_iota(jnp.int32, (128, 128), 0)
    second = lax.broadcasted_iota(jnp.int32, (128, 128), 1)
    masks = []
    for o in order:
        ahead = o > order[0] if backward else o < order[0]
        lead = jnp.where(ahead, 128, jnp.where(o == order[0], 0, -128))
        keep = first <= second + lead if backward else second <= first + lead
        masks.append(keep.astype(F32).astype(BF))
    return masks


def cand_attend(count, begin, end, *refs):
    q_ref, kvs, rest = refs[0], refs[1 : 1 + count], refs[1 + count :]
    q = q_ref[...].reshape(4 * CAP, HS)
    total = None if begin else rest[0][...]
    for block in kvs:
        half = dot(q, block[:, :HS], NT).astype(BF)
        probs = half + half * jnp.tanh(half)
        more = dot(probs, block[:, HS : 2 * HS])
        total = more if total is None else total + more
    if end:
        rest[-1][...] = total.astype(BF).reshape(4, CAP, HS)
    else:
        rest[-1][...] = total


def attend_rows(q_ref, blocks, masks, old_ref, att_ref):
    for y in range(4):
        rows = slice(y * 128, (y + 1) * 128)
        q = q_ref[rows, 2 * HS :]
        total = None if old_ref is None else old_ref[rows, :]
        for block, mask in zip(blocks, masks):
            half = dot(q, block[: 128 * (y + 1), :HS], NT).astype(BF)
            probs = half + half * jnp.tanh(half)
            last = probs[:, 128 * y :] * mask
            probs = last if y == 0 else jnp.concatenate([probs[:, : 128 * y], last], axis=1)
            more = dot(probs, block[: 128 * (y + 1), HS : 2 * HS])
            total = more if total is None else total + more
        att_ref[rows, :] = total


def hist_begin(info, *refs):
    attend_rows(refs[0], refs[:6], corner_masks(info, False)[:6], None, refs[6])


def hist_end(info, p0, p1, p2, p3, own_ref, b0, b1, old_ref, att_ref, stat_ref, g_ref):
    for k, part in enumerate((p0, p1, p2, p3)):
        rows = pl.ds(pl.multiple_of(((info[2] - k) & 3) * 128, 128), 128)
        g_ref[rows, :] = part[:, 3 * HS : 4 * HS].astype(F32) * part[:, 4 * HS :].astype(F32)
    attend_rows(own_ref, (b0, b1), corner_masks(info, False)[6:], old_ref, att_ref)
    att = att_ref[...]
    g = g_ref[...]
    mean = jnp.mean(att, axis=1, keepdims=True)
    center = att - mean
    lane = lax.broadcasted_iota(jnp.int32, (512, 128), 1)
    stats = jnp.where(lane == 0, mean, 0.0)
    stats = jnp.where(lane == 1, jnp.sum(center * center, axis=1, keepdims=True), stats)
    stats = jnp.where(lane == 2, jnp.sum(g, axis=1, keepdims=True), stats)
    stats = jnp.where(lane == 3, jnp.sum(g * center, axis=1, keepdims=True), stats)
    stat_ref[...] = jnp.transpose(stats)[:8]


def normed_grads(info, p0, p1, p2, p3, att_ref, s0, s1, s2, s3, ga_ref, mg_ref, gate_ref, gm_ref):
    for k, part in enumerate((p0, p1, p2, p3)):
        y = (info[2] - k) & 3
        rows = pl.ds(pl.multiple_of(y * 128, 128), 128)
        gate_ref[rows, :] = part[:, 3 * HS : 4 * HS].astype(F32)
        gm_ref[rows, :] = part[:, 4 * HS :].astype(F32)
    stats = [s[...] for s in (s0, s1, s2, s3)]
    mean = sum(s[0:1] for s in stats) * 0.25
    squares = sum(s[1:2] + HS * (s[0:1] - mean) * (s[0:1] - mean) for s in stats)
    spread = lax.rsqrt(squares * (1.0 / (HEADS * HS)) + EPS)
    g_mean = sum(s[2:3] for s in stats) * (1.0 / (HEADS * HS))
    ga_sum = sum(s[3:4] + s[2:3] * (s[0:1] - mean) for s in stats)
    ga_mean = ga_sum * spread * (1.0 / (HEADS * HS))
    line = lax.broadcasted_iota(jnp.int32, (128, 512), 0)
    packed = jnp.where(line == 0, mean, 0.0)
    packed = jnp.where(line == 1, spread, packed)
    packed = jnp.where(line == 2, g_mean, packed)
    packed = jnp.where(line == 3, ga_mean, packed)
    cols = jnp.transpose(packed)
    spread_c = cols[:, 1:2]
    normed = (att_ref[...] - cols[:, 0:1]) * spread_c
    gate = gate_ref[...]
    gm = gm_ref[...]
    ga_ref[...] = (spread_c * (gate * gm - cols[:, 2:3] - normed * cols[:, 3:4])).astype(BF)
    mg_ref[:, :HS] = (normed * gate).astype(BF)
    mg_ref[:, HS:] = (normed * gm).astype(BF)


def slope_times(half, grads):
    t = jnp.tanh(half)
    probs = half + half * t
    slope = (1.0 + t + probs * (1.0 - t)).astype(BF)
    return probs, grads * slope


def hist_dq(info, ga_ref, *refs):
    blocks, dq_ref = refs[:8], refs[8]
    masks = corner_masks(info, False)
    for y in range(4):
        q = blocks[0][y * 128 : (y + 1) * 128, 2 * HS :]
        ga = ga_ref[y * 128 : (y + 1) * 128, :]
        total = None
        for block, mask in zip(blocks, masks):
            key = block[: 128 * (y + 1), :HS]
            half = dot(q, key, NT).astype(BF)
            _, ds = slope_times(half, dot(ga, block[: 128 * (y + 1), HS : 2 * HS], NT).astype(BF))
            last = ds[:, 128 * y :] * mask
            ds = last if y == 0 else jnp.concatenate([ds[:, : 128 * y], last], axis=1)
            more = dot(ds, key)
            total = more if total is None else total + more
        dq_ref[y] = (total * (0.5 * SCALE)).astype(BF)


def key_grads(own_ref, blocks, gas, masks, y, dk, dv):
    key = own_ref[y * 128 : (y + 1) * 128, :HS]
    value = own_ref[y * 128 : (y + 1) * 128, HS : 2 * HS]
    for block, ga_block, mask in zip(blocks, gas, masks):
        q = block[128 * y :, 2 * HS :]
        ga = ga_block[128 * y :, :]
        half = dot(key, q, NT).astype(BF)
        probs, ds = slope_times(half, dot(value, ga, NT).astype(BF))
        p_first = probs[:, :128] * mask
        d_first = ds[:, :128] * mask
        if y < 3:
            probs = jnp.concatenate([p_first, probs[:, 128:]], axis=1)
            ds = jnp.concatenate([d_first, ds[:, 128:]], axis=1)
        else:
            probs, ds = p_first, d_first
        more_k = dot(ds, q)
        more_v = dot(probs, ga)
        dk = more_k if dk is None else dk + more_k
        dv = more_v if dv is None else dv + more_v
    return dk, dv


def hist_dkv_begin(info, *refs):
    masks = corner_masks(info, True)[:6]
    for y in range(4):
        dk, dv = key_grads(refs[0], refs[:6], refs[6:12], masks, y, None, None)
        refs[12][y, :, :HS] = dk
        refs[12][y, :, HS:] = dv


def hist_dkv_end(info, dq_ref, mg_ref, own_ref, b0, b1, g0, g1, old_ref, k0, k1, k2, k3, all_ref):
    masks = corner_masks(info, True)[6:]
    for y in range(4):
        dk, dv = key_grads(own_ref, (b0, b1), (g0, g1), masks, y, old_ref[y, :, :HS], old_ref[y, :, HS:])
        all_ref[y, :, :HS] = dq_ref[y]
        all_ref[y, :, HS : 2 * HS] = dk.astype(BF)
        all_ref[y, :, 2 * HS : 3 * HS] = dv.astype(BF)
        all_ref[y, :, 3 * HS :] = mg_ref[y * 128 : (y + 1) * 128, :]
    for k, out in enumerate((k0, k1, k2, k3)):
        out[...] = all_ref[(info[2] + k) & 3]


def hist_close(
    info, x_far, cot_far, slope_far, wo_far, w_ref, b0, b1, b2, b3, out_far, grad_far,
    mixed_ref, hid_ref, out_ref, grad_ref, x_ref, cot_ref, slope_ref, wo_ref, most, few, buf, sems,
):
    got = fetched([(slope_far, slope_ref), (wo_far, wo_ref), (x_far, x_ref)], most)
    copies = columns(w_ref, buf, sems, (0, 1, 2, 3))
    got += fetched([(cot_far, cot_ref)], most.at[pl.ds(3, 1)])
    length = jnp.full((128, 1), info[0], jnp.int32).astype(F32)
    got[0].wait()
    for k, b in enumerate((b0, b1, b2, b3)):
        lanes = pl.ds(pl.multiple_of(((info[2] - k) & 3) * HS, HS), HS)

        def put(part, grads, which):
            hid_ref[part, :, lanes] = (grads * slope_ref[which, :, lanes].astype(F32)).astype(BF)

        put(0, b[:, 4 * HS :].astype(F32), 3)
        put(1, b[:, 2 * HS : 3 * HS].astype(F32) / length, 1)
        put(2, b[:, :HS].astype(F32), 2)
        put(3, b[:, HS : 2 * HS].astype(F32), 0)
        mixed_ref[:, lanes] = b[:, 3 * HS : 4 * HS]
    got[1].wait()
    got[2].wait()
    x = x_ref[...].astype(F32)
    out_ref[...] = (x + dot(mixed_ref[...], wo_ref[...])).astype(BF)
    done = fetched([(out_ref, out_far.at[0])], few)
    e = None
    for part in range(4):
        copies[part].wait()
        more = dot(hid_ref[part], buf[part], NT)
        e = more if e is None else e + more
    normed, spread = normalize(x)
    back = spread * (
        e - jnp.mean(e, axis=-1, keepdims=True) - normed * jnp.mean(e * normed, axis=-1, keepdims=True)
    )
    got[3].wait()
    grad_ref[...] = (cot_ref[...].astype(F32) + back).astype(BF)
    done += fetched([(grad_ref, grad_far.at[0])], few.at[pl.ds(1, 1)])
    for copy in done:
        copy.wait()


def cand_close(ids_ref, gate_far, ret_ref, x_far, wo_far, out_ref, gate_ref, x_ref, wo_ref, few):
    copies = fetched([(gate_far, gate_ref), (wo_far, wo_ref), (x_far, x_ref)], few)
    col, row, first, second = slot_ids(ids_ref)
    rank = jnp.sum(jnp.where((col == row) & (second < first), 1, 0), axis=1, keepdims=True)
    slot = col * CAP + rank
    hits = (lax.broadcasted_iota(jnp.int32, (256, 4 * CAP), 1) == slot).astype(F32).astype(BF)
    heads = []
    for h in range(HEADS):
        rows = jnp.concatenate([ret_ref[u * HEADS + h] for u in range(4)], axis=0)
        heads.append(dot(hits, rows))
    normed, _ = normalize(jnp.concatenate(heads, axis=1))
    copies[0].wait()
    mixed = (normed * gate_ref[...].astype(F32)).astype(BF)
    copies[1].wait()
    more = dot(mixed, wo_ref[...])
    copies[2].wait()
    out_ref[...] = (x_ref[...].astype(F32) + more).astype(BF)


def turned(value, axis, size, steps):
    return lax.ppermute(value, axis, [(i, (i + steps) % size) for i in range(size)])


def crossed(value, steps):
    pairs = []
    for c in range(2):
        for y in range(4):
            for xh in range(2):
                pairs.append(((c * 4 + y) * 2 + xh, (xh * 4 + (y + steps) % 4) * 2 + c))
    return lax.ppermute(value, ("c", "y", "xh"), pairs)


def across(value):
    return lax.ppermute(value, "c", [(0, 1), (1, 0)])


def along(value, way, cross):
    pairs = []
    for c in range(2):
        step = way if c == 0 else -way
        for z in range(4):
            pairs.append((4 * c + z, 4 * (c ^ cross) + (z + step) % 4))
    return lax.ppermute(value, ("c", "z"), pairs)


def per_device(hist_x, hist_cot, cand_x, cand_loop, hist_len, w_proj, w_out):
    y, xh, z, c = (lax.axis_index(n) for n in ("y", "xh", "z", "c"))
    x_rows = hist_x.reshape(128, 1024)
    cot = hist_cot.reshape(128, 1024)
    info = jnp.stack([hist_len[0], (y * 8 + xh * 4 + z) * 128, y, c, z]).astype(jnp.int32)
    held = pl.BlockSpec(memory_space=pltpu.VMEM)
    far = pl.BlockSpec(memory_space=pltpu.HBM)

    def weights(count):
        return [pltpu.VMEM((count, 1024, 512), BF), pltpu.SemaphoreType.DMA((count,))]

    def relayed(values, after):
        return call(nothing, "relay", (1,), [], [], [], [], 1_000, after, carry=values)()

    *sent, slope = call(
        project_all, "project_all", (1,), [SMEM, far, far, far, far],
        [shaped((128, 640))] * 4 + [shaped((4, 128, 512))], [held] * 5,
        [
            pltpu.VMEM((128, 1024), BF), pltpu.VMEM((128, 512), BF), pltpu.VMEM((128, 1024), BF),
            pltpu.VMEM((128, 1024), BF), pltpu.VMEM((512, 1024), BF), pltpu.SemaphoreType.DMA((3,)),
        ] + weights(4), 700_000_000, (), 16,
    )(info, x_rows, cot, w_out, w_proj)
    parts = [crossed(v, k) for k, v in enumerate(sent)]

    sent_cand, cand_gate = call(
        project_cand, "project_cand", (1,), [held, held, far],
        [shaped((16, 128, 128)), shaped((256, 512))], [held] * 2,
        [pltpu.VMEM((256, 1024), BF)] + weights(2), 700_000_000, (slope,),
    )(cand_loop, cand_x, w_proj)

    own, sent_cand = call(
        arrange, "arrange", (1,), [SMEM] + [held] * 4, shaped((4, 128, 384)), held, [], 1_000_000,
        (cand_gate,), carry=(sent_cand,),
    )(info, *parts)
    own = own.reshape(512, 384)
    own_pair = across(own)
    plus, minus = along(own, 1, 0), along(own, -1, 0)
    arrived = lax.all_to_all(sent_cand, ("xl", "xh", "y"), 0, 0, tiled=True)
    last = [along(plus, 1, 0), along(plus, 1, 1)]
    kvq = [own, own_pair, plus, across(plus), minus, across(minus)]

    q_spec = pl.BlockSpec((4, 128, 128), lambda i: (i, 0, 0))
    acc_spec = pl.BlockSpec((512, 128), lambda i: (i, 0))

    def cand_part(kvs, total, end, after):
        begin = total is None
        return call(
            functools.partial(cand_attend, len(kvs), begin, end), "cand_attend", (4,),
            [q_spec] + [held] * len(kvs) + ([] if begin else [acc_spec]),
            shaped((16, 128, 128)) if end else shaped((2048, 128), F32),
            q_spec if end else acc_spec, [], 600_000_000 * len(kvs), after,
        )(arrived, *kvs, *([] if begin else [total]))

    total = cand_part(kvq, None, False, ())
    att = call(
        hist_begin, "hist_begin", (1,), [SMEM] + [held] * 6,
        shaped((512, 128), F32), held, [], 1_400_000_000, (total,),
    )(info, *kvq)
    att, stats = call(
        hist_end, "hist_end", (1,), [SMEM] + [held] * 8,
        [shaped((512, 128), F32), shaped((8, 512), F32)], [held] * 2,
        [pltpu.VMEM((512, 128), F32)], 400_000_000,
    )(info, *parts, own, *last, att)
    all_stats = [stats] + [turned(stats, "y", 4, k) for k in (1, 2, 3)]
    weighed = cand_part(last, total, True, (stats,))
    ga, mg = call(
        normed_grads, "normed_grads", (1,), [SMEM] + [held] * 9,
        [shaped((512, 128)), shaped((512, 256))], [held] * 2,
        [pltpu.VMEM((512, 128), F32)] * 2, 1_000_000, (weighed,),
    )(info, *parts, att, *all_stats)

    ga_plus, ga_minus = along(ga, 1, 0), along(ga, -1, 0)
    dq = call(
        hist_dq, "hist_dq", (1,), [SMEM] + [held] * 9,
        shaped((4, 128, 128)), held, [], 2_000_000_000,
    )(info, ga, *kvq, *last)
    ga_plus, ga_minus = relayed([ga_plus, ga_minus], (dq,))
    ga_last = [along(ga_plus, 1, 0), along(ga_plus, 1, 1)]
    gas = [ga, across(ga), ga_plus, across(ga_plus), ga_minus, across(ga_minus)]
    key_sums = call(
        hist_dkv_begin, "hist_dkv_begin", (1,), [SMEM] + [held] * 12,
        shaped((4, 128, 256), F32), held, [], 2_000_000_000,
    )(info, *kvq, *gas)
    (leaving,) = relayed([weighed], (key_sums,))
    returned = lax.all_to_all(leaving, ("xl", "xh", "y"), 0, 0, tiled=True)
    grads = call(
        hist_dkv_end, "hist_dkv_end", (1,), [SMEM] + [held] * 8,
        [shaped((128, 640))] * 4, [held] * 4, [pltpu.VMEM((4, 128, 640), BF)], 800_000_000,
    )(info, dq, mg, own, *last, *ga_last, key_sums)
    back = [crossed(v, k) for k, v in enumerate(grads)]

    cand_out = call(
        cand_close, "cand_close", (1,), [held, far, held, far, far],
        pltpu.HBM((256, 1024), BF), pl.BlockSpec((256, 1024), lambda i: (0, 0)),
        [
            pltpu.VMEM((256, 512), BF), pltpu.VMEM((256, 1024), BF), pltpu.VMEM((512, 1024), BF),
            pltpu.SemaphoreType.DMA((3,)),
        ], 400_000_000, (grads[0],),
    )(cand_loop, cand_gate, returned, cand_x, w_out)
    final = pltpu.HBM((1, 128, 1024), BF)
    hist_out, hist_grad = call(
        hist_close, "hist_close", (1,), [SMEM] + [far] * 5 + [held] * 4,
        [final] * 2, [far] * 2,
        [
            pltpu.VMEM((128, 512), BF), pltpu.VMEM((4, 128, 512), BF), pltpu.VMEM((128, 1024), BF),
            pltpu.VMEM((128, 1024), BF), pltpu.VMEM((128, 1024), BF), pltpu.VMEM((128, 1024), BF),
            pltpu.VMEM((4, 128, 512), BF), pltpu.VMEM((512, 1024), BF), pltpu.SemaphoreType.DMA((4,)),
            pltpu.SemaphoreType.DMA((2,)),
        ] + weights(4), 700_000_000, (pltpu.with_memory_space_constraint(cand_out, pltpu.HBM),), 16,
    )(info, x_rows, cot, slope, w_out, w_proj, *back)
    return hist_out, hist_grad, cand_out


def solution(mesh):
    split = Mesh(mesh.devices.reshape(2, 2, 4, 2, 4), ("xl", "c", "y", "xh", "z"))
    users, rows = ("xl", "c"), ("y", "xh", "z")
    hist = P(users, rows, None)
    cand = P(users + rows, None)
    return jax.shard_map(
        per_device,
        mesh=split,
        in_specs=(hist, hist, cand, cand, P(users), P(), P()),
        out_specs=(hist, hist, cand),
        check_vma=False,
    )
```

time: 139 us -> 129 us (0.928)
  blocking collectives: 14.7 us -> 0 us
  starting transfers between devices: 47.6 us -> 56.5 us
  Pallas kernels: 44.9 us -> 53.4 us
  waiting for transfers between devices: 21.4 us -> 14.7 us
  local copies, waits for them, and re-layouts: 8.21 us -> 2.01 us
    all_to_all x1 -> x0, blocking collectives: 14.7 us -> none  [per_device(): arrived = lax.all_to_all(sent_cand, ('xl', 'xh', 'y'), 0, 0, tiled=True)]
    pallas_call x18 -> x15, Pallas kernels: 44.9 us -> 53.4 us  [run(): got = made(*pinned, *after, *carry)]
    ppermute x4 -> x8, starting transfers between devices: 5.11 us -> 12.5 us  [along(): return lax.ppermute(value, ('c', 'z'), pairs)]
    unnamed x28 -> x15, local copies, waits for them, and re-layouts: 8.13 us -> 1.92 us
    ppermute x4 -> x8, waiting for transfers between devices: 8.68 us -> 4.13 us  [along(): return lax.ppermute(value, ('c', 'z'), pairs)]
    ppermute x8, waiting for transfers between devices: 10 us -> 6.01 us  [crossed(): return lax.ppermute(value, ('c', 'y', 'xh'), pairs)]
    all_to_all x0 -> x1, starting transfers between devices: none -> 3.68 us  [per_device(): arrived = lax.all_to_all(sent_cand, ('xl', 'xh', 'y'), 0, 0, tiled=True)]
    all_to_all x0 -> x1, waiting for transfers between devices: none -> 3.49 us  [per_device(): arrived = lax.all_to_all(sent_cand, ('xl', 'xh', 'y'), 0, 0, tiled=True)]
  transfers between devices with their start and end apart: 22 -> 27, of which waited for: 10 -> 8; matrix products, arithmetic and copies ran while one was open for 1% -> 0% of each run, Pallas kernels for 19% -> 26%
where the time goes in v3:
time: 129 us; the launch traced here: 128 us
  starting transfers between devices  56.5 us (44%)
  Pallas kernels  53.4 us (41%)
  waiting for transfers between devices  14.7 us (11%)
  local copies, waits for them, and re-layouts  2.01 us (2%)
  between operations  1.82 us (1%)
    pallas_call x15, Pallas kernels, run(): got = made(*pinned, *after, *carry)  53.4 us
    ppermute x8, starting transfers between devices, crossed(): return lax.ppermute(value, ('c', 'y', 'xh'), pairs)  26.2 us
    ppermute x8, starting transfers between devices, along(): return lax.ppermute(value, ('c', 'z'), pairs)  12.5 us
    ppermute x6, starting transfers between devices, across(): return lax.ppermute(value, 'c', [(0, 1), (1, 0)])  6.33 us
    ppermute x8, waiting for transfers between devices, crossed(): return lax.ppermute(value, ('c', 'y', 'xh'), pairs)  6.01 us
    all_to_all x1, starting transfers between devices, per_device(): returned = lax.all_to_all(leaving, ('xl', 'xh', 'y'), 0, 0, tiled=True)  4.91 us
    ppermute x8, waiting for transfers between devices, along(): return lax.ppermute(value, ('c', 'z'), pairs)  4.13 us
    all_to_all x1, starting transfers between devices, per_device(): arrived = lax.all_to_all(sent_cand, ('xl', 'xh', 'y'), 0, 0, tiled=True)  3.68 us
  transfers between devices with their start and end apart: 27, of which 8 were waited for; matrix products, arithmetic and copies ran while one was open for 0% of the time, Pallas kernels for 26%

profile of v3, /device:TPU:1, one launch (start us, length us, event | category | flops | bytes accessed | tf_op | source)
XLA Modules:
  0.0 128.4 jit_solution(706098894086130520)
XLA Ops:
  1.4 4.3 %project_all.1 = (bf16[128,640]{1,0:T(8,128)(2,1)S(1)}, bf16[128,640]{1,0:T(8,128)(2,1)S(1)}, bf16[128,640]{1,0:T(8,128)(2,1)S(1)}, bf16[128,640]{1,0:T(8,128)(2,1)S(1)}, bf16[4,128,512]{2,1,0:T(8,128)(2,1)S(1)}) custom-call(s32[5]{0:T(128)S(1)} %stack.19.refs_0_, bf16[128,1024]{1,0:T(8,128)(2,1)} %bitcast.16, bf16[128,1024]{1,0:T(8,128)(2,1)} %bitcast.18, ...), custom_call_target="tpu_custom_call" | custom-call | flops 700000000 | bytes 1048576 | tf_op jit(solution)/shard_map/project_all/pallas_call | solution.py:63
  5.8 6.0 %collective-permute-start = (bf16[128,640]{1,0:T(8,128)(2,1)S(1)}, bf16[128,640]{1,0:T(8,128)(2,1)S(1)}, u32[]{:S(2)}, u32[]{:S(2)}) collective-permute-start(bf16[128,640]{1,0:T(8,128)(2,1)S(1)} %get-tuple-element.25), channel_id=1, source_target_pairs={{0,0},{4,32},{8,8},{12,40},{16,16},{20,48},{24,24},{28,56},{32,4},... | collective-permute-start | bytes 491528 | tf_op jit(solution)/shard_map/ppermute | solution.py:408
  11.9 1.1 collective-permute-start.1
  13.0 5.6 %collective-permute-start.2 = (bf16[128,640]{1,0:T(8,128)(2,1)S(1)}, bf16[128,640]{1,0:T(8,128)(2,1)S(1)}, u32[]{:S(2)}, u32[]{:S(2)}) collective-permute-start(bf16[128,640]{1,0:T(8,128)(2,1)S(1)} %get-tuple-element.27), channel_id=1, source_target_pairs={{0,16},{4,48},{8,24},{12,56},{16,0},{20,32},{24,8},{28,40},{32,20}... | collective-permute-start | bytes 491528 | tf_op jit(solution)/shard_map/ppermute | solution.py:408
  18.6 0.8 collective-permute-start.3
  19.4 0.1 copy.14.refs_0_
  19.5 3.1 %project_cand.1 = (bf16[16,128,128]{2,1,0:T(8,128)(2,1)}, bf16[256,512]{1,0:T(8,128)(2,1)S(1)}) custom-call(s32[256,1]{1,0:T(8,128)S(1)} %copy.14.refs_0_, bf16[256,1024]{1,0:T(8,128)(2,1)S(1)} %copy-done, bf16[1024,2048]{1,0:T(8,128)(2,1)} %refs_5_.1, bf16[4,128,512]{2,1,0:T(8,128)(2,1)S(1)} %get-tuple-element.24.refs_3_), custom_call_target="tpu_custom_call" | custom-call | flops 700000000 | bytes 1048576 | tf_op jit(solution)/shard_map/project_cand/pallas_call | solution.py:63
  22.7 0.6 collective-permute-done.2.refs_3_
  23.3 2.4 %collective-permute-done.3.refs_4_ = bf16[128,640]{1,0:T(8,128)(2,1)S(1)} collective-permute-done((bf16[128,640]{1,0:T(8,128)(2,1)S(1)}, bf16[128,640]{1,0:T(8,128)(2,1)S(1)}, u32[]{:S(2)}, u32[]{:S(2)}) %collective-permute-start.3) | collective-permute-done | bytes 163872 | tf_op jit(solution)/shard_map/ppermute | solution.py:408
  25.7 0.6 arrange.1
  26.3 1.7 %collective-permute-start.9 = (bf16[512,384]{1,0:T(8,128)(2,1)S(1)}, bf16[512,384]{1,0:T(8,128)(2,1)}, u32[]{:S(2)}, u32[]{:S(2)}) collective-permute-start(bf16[512,384]{1,0:T(8,128)(2,1)S(1)} %bitcast.7), channel_id=1, source_target_pairs={{0,3},{1,0},{2,1},{3,2},{32,33},{33,34},{34,35},{35,32},{4,7},{5,4... | collective-permute-start | bytes 1179656 | tf_op jit(solution)/shard_map/ppermute | solution.py:421
  28.0 2.2 %collective-permute-start.4 = (bf16[512,384]{1,0:T(8,128)(2,1)S(1)}, bf16[512,384]{1,0:T(8,128)(2,1)}, u32[]{:S(2)}, u32[]{:S(2)}) collective-permute-start(bf16[512,384]{1,0:T(8,128)(2,1)S(1)} %bitcast.8), channel_id=1, source_target_pairs={{0,1},{1,2},{2,3},{3,0},{32,35},{33,32},{34,33},{35,34},{4,5},{5,6... | collective-permute-start | bytes 1179656 | tf_op jit(solution)/shard_map/ppermute | solution.py:421
  30.2 3.7 %all-to-all-start = ((bf16[16,128,128]{2,1,0:T(8,128)(2,1)}), bf16[16,128,128]{2,1,0:T(8,128)(2,1)S(1)}, u32[]{:S(2)}, u32[]{:S(2)}) async-start(bf16[16,128,128]{2,1,0:T(8,128)(2,1)} %get-tuple-element.32), calls=%async_computation | async-start | bytes 1048576 | tf_op jit(solution)/shard_map/all_to_all | solution.py:461
  33.9 1.5 %collective-permute-start.7 = (bf16[512,384]{1,0:T(8,128)(2,1)S(1)}, bf16[512,384]{1,0:T(8,128)(2,1)S(1)}, u32[]{:S(2)}, u32[]{:S(2)}) collective-permute-start(bf16[512,384]{1,0:T(8,128)(2,1)S(1)} %bitcast.9), channel_id=1, source_target_pairs={{0,32},{32,0},{1,33},{33,1},{2,34},{34,2},{3,35},{35,3},{4,36},{36... | collective-permute-start | bytes 1179656 | tf_op jit(solution)/shard_map/ppermute | solution.py:412
  35.4 0.1 collective-permute-start.10
  35.5 0.4 collective-permute-start.8
  36.0 2.9 %collective-permute-start.6 = (bf16[512,384]{1,0:T(8,128)(2,1)}, bf16[512,384]{1,0:T(8,128)(2,1)S(1)}, u32[]{:S(2)}, u32[]{:S(2)}) collective-permute-start(bf16[512,384]{1,0:T(8,128)(2,1)} %collective-permute-done.4.refs_3_.refs_4_), channel_id=1, source_target_pairs={{0,33},{1,34},{2,35},{3,32},{32,3},{33,0},{34,1},{35,2},{4,37},{5,... | collective-permute-start | bytes 1179656 | tf_op jit(solution)/shard_map/ppermute | solution.py:421
  38.9 0.8 copy-done.3
  39.7 3.5 %all-to-all-done.refs_0_ = bf16[16,128,128]{2,1,0:T(8,128)(2,1)S(1)} async-done(((bf16[16,128,128]{2,1,0:T(8,128)(2,1)}), bf16[16,128,128]{2,1,0:T(8,128)(2,1)S(1)}, u32[]{:S(2)}, u32[]{:S(2)}) %all-to-all-start) | async-done | bytes 524320 | tf_op jit(solution)/shard_map/all_to_all | solution.py:461
  43.2 1.0 copy-done.4
  44.2 10.2 %cand_attend.2.refs_7_.refs_3_ = f32[2048,128]{1,0:T(8,128)S(1)} custom-call(bf16[16,128,128]{2,1,0:T(8,128)(2,1)S(1)} %all-to-all-done.refs_0_, bf16[512,384]{1,0:T(8,128)(2,1)S(1)} %bitcast.10, bf16[512,384]{1,0:T(8,128)(2,1)S(1)} %copy-done.4, bf16[512,384]{1,0:T(8,128)(2,1)} %collective-permute-done.4.refs_3_.refs_4_, ...), custom_call_target="tpu_custom_call" | custom-call | flops 3600000000 | bytes 1048576 | tf_op jit(solution)/shard_map/cand_attend/pallas_call | solution.py:63
  54.4 3.9 %hist_begin.1.refs_8_ = f32[512,128]{1,0:T(8,128)S(1)} custom-call(s32[5]{0:T(128)S(1)} %stack.19.refs_0_, bf16[512,384]{1,0:T(8,128)(2,1)S(1)} %bitcast.11, bf16[512,384]{1,0:T(8,128)(2,1)S(1)} %copy-done.5, bf16[512,384]{1,0:T(8,128)(2,1)} %collective-permute-done.4.refs_3_.refs_4_, bf16[512,384]{1,0:T(8,128)(2,1)} %collective-permute-done.8.refs_4_.refs_5_, ...), custom_call_target="tpu_custom_call" | custom-call | flops 1400000000 | bytes 1048576 | tf_op jit(solution)/shard_map/hist_begin/pallas_call | solution.py:63
  58.4 1.8 %hist_end.1 = (f32[512,128]{1,0:T(8,128)S(1)}, f32[8,512]{1,0:T(8,128)S(1)}) custom-call(s32[5]{0:T(128)S(1)} %stack.19.refs_0_, bf16[128,640]{1,0:T(8,128)(2,1)S(1)} %collective-permute-done.refs_1_, bf16[128,640]{1,0:T(8,128)(2,1)S(1)} %collective-permute-done.1.refs_2_, bf16[128,640]{1,0:T(8,128)(2,1)S(1)} %collective-permute-done.2.refs_3_, ...), custom_call_target="tpu_custom_call" | custom-call | flops 400000000 | bytes 1048576 | tf_op jit(solution)/shard_map/hist_end/pallas_call | solution.py:63
  60.2 1.3 %collective-permute-start.13 = (f32[8,512]{1,0:T(8,128)S(1)}, f32[8,512]{1,0:T(8,128)S(1)}, u32[]{:S(2)}, u32[]{:S(2)}) collective-permute-start(f32[8,512]{1,0:T(8,128)S(1)} %get-tuple-element.34.refs_4_.refs_6_), channel_id=1, source_target_pairs={{0,24},{8,0},{16,8},{24,16},{1,25},{9,1},{17,9},{25,17},{2,26},{10... | collective-permute-start | bytes 49160 | tf_op jit(solution)/shard_map/ppermute | solution.py:399
  61.5 0.9 collective-permute-start.12
  62.4 0.6 collective-permute-start.11
  63.0 4.0 %cand_attend.3.refs_10_.refs_1_ = bf16[16,128,128]{2,1,0:T(8,128)(2,1)} custom-call(bf16[16,128,128]{2,1,0:T(8,128)(2,1)S(1)} %all-to-all-done.refs_0_, bf16[512,384]{1,0:T(8,128)(2,1)S(1)} %collective-permute-done.5.refs_6_.refs_1_.refs_8_.refs_4_, bf16[512,384]{1,0:T(8,128)(2,1)S(1)} %collective-permute-done.6.refs_7_.refs_2_.refs_9_.refs_5_, ...), custom_call_target="tpu_custom_call" | custom-call | flops 1200000000 | bytes 1048576 | tf_op jit(solution)/shard_map/cand_attend/pallas_call | solution.py:63
  67.0 1.1 normed_grads.1
  68.1 3.7 %collective-permute-start.18 = (bf16[512,128]{1,0:T(8,128)(2,1)S(1)}, bf16[512,128]{1,0:T(8,128)(2,1)S(1)}, u32[]{:S(2)}, u32[]{:S(2)}) collective-permute-start(bf16[512,128]{1,0:T(8,128)(2,1)S(1)} %get-tuple-element.35.refs_1_.refs_7_), channel_id=1, source_target_pairs={{0,32},{32,0},{1,33},{33,1},{2,34},{34,2},{3,35},{35,3},{4,36},{36... | collective-permute-start | bytes 393224 | tf_op jit(solution)/shard_map/ppermute | solution.py:412
  71.8 2.7 %collective-permute-start.14 = (bf16[512,128]{1,0:T(8,128)(2,1)S(1)}, bf16[512,128]{1,0:T(8,128)(2,1)S(1)}, u32[]{:S(2)}, u32[]{:S(2)}) collective-permute-start(bf16[512,128]{1,0:T(8,128)(2,1)S(1)} %get-tuple-element.35.refs_1_.refs_7_), channel_id=1, source_target_pairs={{0,1},{1,2},{2,3},{3,0},{32,35},{33,32},{34,33},{35,34},{4,5},{5,6... | collective-permute-start | bytes 393224 | tf_op jit(solution)/shard_map/ppermute | solution.py:421
  74.4 6.5 %hist_dq.1.refs_0_.refs_1_ = bf16[4,128,128]{2,1,0:T(8,128)(2,1)S(1)} custom-call(s32[5]{0:T(128)S(1)} %stack.19.refs_0_, bf16[512,128]{1,0:T(8,128)(2,1)S(1)} %get-tuple-element.35.refs_1_.refs_7_, bf16[512,384]{1,0:T(8,128)(2,1)S(1)} %bitcast.13, bf16[512,384]{1,0:T(8,128)(2,1)S(1)} %copy-done.5, bf16[512,384]{1,0:T(8,128)(2,1)} %collective-permute-done.4.refs_3_.refs_4_, ...), custom_call_target="tpu_custom_call" | custom-call | flops 2000000000 | bytes 1048576 | tf_op jit(solution)/shard_map/hist_dq/pallas_call | solution.py:63
  81.0 0.1 collective-permute-start.20
  81.1 0.5 collective-permute-start.19
  81.6 0.8 collective-permute-done.20.refs_12_
  82.4 0.2 collective-permute-done.19.refs_10_
  82.6 6.1 %hist_dkv_begin.1.refs_8_.refs_0_ = f32[4,128,256]{2,1,0:T(8,128)S(1)} custom-call(s32[5]{0:T(128)S(1)} %stack.19.refs_0_, bf16[512,384]{1,0:T(8,128)(2,1)S(1)} %bitcast.14, bf16[512,384]{1,0:T(8,128)(2,1)S(1)} %copy-done.5, bf16[512,384]{1,0:T(8,128)(2,1)} %collective-permute-done.4.refs_3_.refs_4_, ...), custom_call_target="tpu_custom_call" | custom-call | flops 2000000000 | bytes 1048576 | tf_op jit(solution)/shard_map/hist_dkv_begin/pallas_call | solution.py:63
  88.7 4.9 %all-to-all-start.1 = ((bf16[16,128,128]{2,1,0:T(8,128)(2,1)}), bf16[16,128,128]{2,1,0:T(8,128)(2,1)S(1)}, u32[]{:S(2)}, u32[]{:S(2)}) async-start(bf16[16,128,128]{2,1,0:T(8,128)(2,1)} %relay.3), calls=%async_computation.1 | async-start | bytes 1048576 | tf_op jit(solution)/shard_map/all_to_all | solution.py:508
  93.7 2.9 %collective-permute-start.17 = (bf16[512,128]{1,0:T(8,128)(2,1)S(1)}, bf16[512,128]{1,0:T(8,128)(2,1)S(1)}, u32[]{:S(2)}, u32[]{:S(2)}) collective-permute-start(bf16[512,128]{1,0:T(8,128)(2,1)S(1)} %get-tuple-element.37.refs_9_), channel_id=1, source_target_pairs={{0,33},{1,34},{2,35},{3,32},{32,3},{33,0},{34,1},{35,2},{4,37},{5,... | collective-permute-start | bytes 393224 | tf_op jit(solution)/shard_map/ppermute | solution.py:421
  96.6 3.0 %collective-permute-done.17.refs_7_ = bf16[512,128]{1,0:T(8,128)(2,1)S(1)} collective-permute-done((bf16[512,128]{1,0:T(8,128)(2,1)S(1)}, bf16[512,128]{1,0:T(8,128)(2,1)S(1)}, u32[]{:S(2)}, u32[]{:S(2)}) %collective-permute-start.17) | collective-permute-done | bytes 131104 | tf_op jit(solution)/shard_map/ppermute | solution.py:421
  99.6 1.1 collective-permute-done.16.refs_6_
  100.7 3.1 %hist_dkv_end.1 = (bf16[128,640]{1,0:T(8,128)(2,1)S(1)}, bf16[128,640]{1,0:T(8,128)(2,1)}, bf16[128,640]{1,0:T(8,128)(2,1)S(1)}, bf16[128,640]{1,0:T(8,128)(2,1)S(1)}) custom-call(s32[5]{0:T(128)S(1)} %stack.19.refs_0_, bf16[4,128,128]{2,1,0:T(8,128)(2,1)S(1)} %hist_dq.1.refs_0_.refs_1_, bf16[512,256]{1,0:T(8,128)(2,1)S(1)} %get-tuple-element.36.refs_2_, ...), custom_call_target="tpu_custom_call" | custom-call | flops 800000000 | bytes 1048576 | tf_op jit(solution)/shard_map/hist_dkv_end/pallas_call | solution.py:63
  103.8 4.5 %collective-permute-start.22 = (bf16[128,640]{1,0:T(8,128)(2,1)}, bf16[128,640]{1,0:T(8,128)(2,1)S(1)}, u32[]{:S(2)}, u32[]{:S(2)}) collective-permute-start(bf16[128,640]{1,0:T(8,128)(2,1)} %get-tuple-element.40), channel_id=1, source_target_pairs={{0,8},{4,40},{8,16},{12,48},{16,24},{20,56},{24,0},{28,32},{32,12}... | collective-permute-start | bytes 491528 | tf_op jit(solution)/shard_map/ppermute | solution.py:408
  108.3 2.2 %collective-permute-start.23 = (bf16[128,640]{1,0:T(8,128)(2,1)S(1)}, bf16[128,640]{1,0:T(8,128)(2,1)S(1)}, u32[]{:S(2)}, u32[]{:S(2)}) collective-permute-start(bf16[128,640]{1,0:T(8,128)(2,1)S(1)} %get-tuple-element.41), channel_id=1, source_target_pairs={{0,16},{4,48},{8,24},{12,56},{16,0},{20,32},{24,8},{28,40},{32,20}... | collective-permute-start | bytes 491528 | tf_op jit(solution)/shard_map/ppermute | solution.py:408
  110.5 4.1 %collective-permute-start.24 = (bf16[128,640]{1,0:T(8,128)(2,1)S(1)}, bf16[128,640]{1,0:T(8,128)(2,1)S(1)}, u32[]{:S(2)}, u32[]{:S(2)}) collective-permute-start(bf16[128,640]{1,0:T(8,128)(2,1)S(1)} %get-tuple-element.42), channel_id=1, source_target_pairs={{0,24},{4,56},{8,0},{12,32},{16,8},{20,40},{24,16},{28,48},{32,28}... | collective-permute-start | bytes 491528 | tf_op jit(solution)/shard_map/ppermute | solution.py:408
  114.6 1.9 %collective-permute-start.21 = (bf16[128,640]{1,0:T(8,128)(2,1)S(1)}, bf16[128,640]{1,0:T(8,128)(2,1)S(1)}, u32[]{:S(2)}, u32[]{:S(2)}) collective-permute-start(bf16[128,640]{1,0:T(8,128)(2,1)S(1)} %get-tuple-element.39.refs_5_), channel_id=1, source_target_pairs={{0,0},{4,32},{8,8},{12,40},{16,16},{20,48},{24,24},{28,56},{32,4},... | collective-permute-start | bytes 491528 | tf_op jit(solution)/shard_map/ppermute | solution.py:408
  116.5 3.1 %cand_close.1.refs_10_ = bf16[256,1024]{1,0:T(8,128)(2,1)} custom-call(s32[256,1]{1,0:T(8,128)S(1)} %copy.14.refs_0_, bf16[256,512]{1,0:T(8,128)(2,1)} %copy-done.2, bf16[16,128,128]{2,1,0:T(8,128)(2,1)S(1)} %all-to-all-done.1.refs_2_, bf16[256,1024]{1,0:T(8,128)(2,1)} %refs_3_.3, bf16[512,1024]{1,0:T(8,128)(2,1)} %refs_4_.5, ...), custom_call_target="tpu_custom_call" | custom-call | flops 400000000 | bytes 1048576 | tf_op jit(solution)/shard_map/cand_close/pallas_call | solution.py:63
  119.7 3.0 %collective-permute-done.21.refs_6_ = bf16[128,640]{1,0:T(8,128)(2,1)S(1)} collective-permute-done((bf16[128,640]{1,0:T(8,128)(2,1)S(1)}, bf16[128,640]{1,0:T(8,128)(2,1)S(1)}, u32[]{:S(2)}, u32[]{:S(2)}) %collective-permute-start.21) | collective-permute-done | bytes 163872 | tf_op jit(solution)/shard_map/ppermute | solution.py:408
  122.7 5.5 %hist_close.1 = (bf16[1,128,1024]{2,1,0:T(8,128)(2,1)}, bf16[1,128,1024]{2,1,0:T(8,128)(2,1)}) custom-call(s32[5]{0:T(128)S(1)} %stack.19.refs_0_, bf16[128,1024]{1,0:T(8,128)(2,1)} %bitcast.17, bf16[128,1024]{1,0:T(8,128)(2,1)} %bitcast.19, bf16[4,128,512]{2,1,0:T(8,128)(2,1)} %copy-done.1, bf16[512,1024]{1,0:T(8,128)(2,1)} %refs_4_.5, ...), custom_call_target="tpu_custom_call" | custom-call | flops 700000000 | bytes 1048576 | tf_op jit(solution)/shard_map/hist_close/pallas_call | solution.py:63
  (37 shorter events, 0.2 us)
Async XLA Ops:
  0.6 18.7 %copy-start.6 = (s32[256,1]{0,1:T(1,128)S(1)}, s32[256,1]{0,1:T(1,128)}, u32[]{:S(2)}) copy-start(s32[256,1]{0,1:T(1,128)} %param.10) | copy-start | bytes 3076
  0.6 18.9 %copy-start = (bf16[256,1024]{1,0:T(8,128)(2,1)S(1)}, bf16[256,1024]{1,0:T(8,128)(2,1)}, u32[]{:S(2)}) copy-start(bf16[256,1024]{1,0:T(8,128)(2,1)} %refs_3_.3) | copy-start | bytes 1572868
  5.8 48.6 %copy-start.1 = (bf16[4,128,512]{2,1,0:T(8,128)(2,1)}, bf16[4,128,512]{2,1,0:T(8,128)(2,1)S(1)}, u32[]{:S(2)}) copy-start(bf16[4,128,512]{2,1,0:T(8,128)(2,1)S(1)} %get-tuple-element.24.refs_3_) | copy-start | bytes 1572868
  5.8 16.9 %collective-permute-start = (bf16[128,640]{1,0:T(8,128)(2,1)S(1)}, bf16[128,640]{1,0:T(8,128)(2,1)S(1)}, u32[]{:S(2)}, u32[]{:S(2)}) collective-permute-start(bf16[128,640]{1,0:T(8,128)(2,1)S(1)} %get-tuple-element.25), channel_id=1, source_target_pairs={{0,0},{4,32},{8,8},{12,40},{16,16},{20,48},{24,24},{28,56},{32,4},... | collective-permute-start | bytes 491528 | tf_op jit(solution)/shard_map/ppermute | solution.py:408
  11.9 10.8 %collective-permute-start.1 = (bf16[128,640]{1,0:T(8,128)(2,1)S(1)}, bf16[128,640]{1,0:T(8,128)(2,1)S(1)}, u32[]{:S(2)}, u32[]{:S(2)}) collective-permute-start(bf16[128,640]{1,0:T(8,128)(2,1)S(1)} %get-tuple-element.26), channel_id=1, source_target_pairs={{0,8},{4,40},{8,16},{12,48},{16,24},{20,56},{24,0},{28,32},{32,12}... | collective-permute-start | bytes 491528 | tf_op jit(solution)/shard_map/ppermute | solution.py:408
  13.0 10.3 %collective-permute-start.2 = (bf16[128,640]{1,0:T(8,128)(2,1)S(1)}, bf16[128,640]{1,0:T(8,128)(2,1)S(1)}, u32[]{:S(2)}, u32[]{:S(2)}) collective-permute-start(bf16[128,640]{1,0:T(8,128)(2,1)S(1)} %get-tuple-element.27), channel_id=1, source_target_pairs={{0,16},{4,48},{8,24},{12,56},{16,0},{20,32},{24,8},{28,40},{32,20}... | collective-permute-start | bytes 491528 | tf_op jit(solution)/shard_map/ppermute | solution.py:408
  18.6 7.1 %collective-permute-start.3 = (bf16[128,640]{1,0:T(8,128)(2,1)S(1)}, bf16[128,640]{1,0:T(8,128)(2,1)S(1)}, u32[]{:S(2)}, u32[]{:S(2)}) collective-permute-start(bf16[128,640]{1,0:T(8,128)(2,1)S(1)} %get-tuple-element.28), channel_id=1, source_target_pairs={{0,24},{4,56},{8,0},{12,32},{16,8},{20,40},{24,16},{28,48},{32,28}... | collective-permute-start | bytes 491528 | tf_op jit(solution)/shard_map/ppermute | solution.py:408
  22.7 31.7 %copy-start.2 = (bf16[256,512]{1,0:T(8,128)(2,1)}, bf16[256,512]{1,0:T(8,128)(2,1)S(1)}, u32[]{:S(2)}) copy-start(bf16[256,512]{1,0:T(8,128)(2,1)S(1)} %get-tuple-element.29.refs_5_.refs_1_) | copy-start | bytes 786436
  26.3 9.1 %collective-permute-start.9 = (bf16[512,384]{1,0:T(8,128)(2,1)S(1)}, bf16[512,384]{1,0:T(8,128)(2,1)}, u32[]{:S(2)}, u32[]{:S(2)}) collective-permute-start(bf16[512,384]{1,0:T(8,128)(2,1)S(1)} %bitcast.7), channel_id=1, source_target_pairs={{0,3},{1,0},{2,1},{3,2},{32,33},{33,34},{34,35},{35,32},{4,7},{5,4... | collective-permute-start | bytes 1179656 | tf_op jit(solution)/shard_map/ppermute | solution.py:421
  28.0 7.5 %collective-permute-start.4 = (bf16[512,384]{1,0:T(8,128)(2,1)S(1)}, bf16[512,384]{1,0:T(8,128)(2,1)}, u32[]{:S(2)}, u32[]{:S(2)}) collective-permute-start(bf16[512,384]{1,0:T(8,128)(2,1)S(1)} %bitcast.8), channel_id=1, source_target_pairs={{0,1},{1,2},{2,3},{3,0},{32,35},{33,32},{34,33},{35,34},{4,5},{5,6... | collective-permute-start | bytes 1179656 | tf_op jit(solution)/shard_map/ppermute | solution.py:421
  30.2 13.0 %all-to-all-start = ((bf16[16,128,128]{2,1,0:T(8,128)(2,1)}), bf16[16,128,128]{2,1,0:T(8,128)(2,1)S(1)}, u32[]{:S(2)}, u32[]{:S(2)}) async-start(bf16[16,128,128]{2,1,0:T(8,128)(2,1)} %get-tuple-element.32), calls=%async_computation | async-start | bytes 1048576 | tf_op jit(solution)/shard_map/all_to_all | solution.py:461
  33.9 5.0 %collective-permute-start.7 = (bf16[512,384]{1,0:T(8,128)(2,1)S(1)}, bf16[512,384]{1,0:T(8,128)(2,1)S(1)}, u32[]{:S(2)}, u32[]{:S(2)}) collective-permute-start(bf16[512,384]{1,0:T(8,128)(2,1)S(1)} %bitcast.9), channel_id=1, source_target_pairs={{0,32},{32,0},{1,33},{33,1},{2,34},{34,2},{3,35},{35,3},{4,36},{36... | collective-permute-start | bytes 1179656 | tf_op jit(solution)/shard_map/ppermute | solution.py:412
  35.4 7.8 %collective-permute-start.10 = (bf16[512,384]{1,0:T(8,128)(2,1)}, bf16[512,384]{1,0:T(8,128)(2,1)}, u32[]{:S(2)}, u32[]{:S(2)}) collective-permute-start(bf16[512,384]{1,0:T(8,128)(2,1)} %collective-permute-done.9.refs_5_.refs_6_), channel_id=1, source_target_pairs={{0,32},{32,0},{1,33},{33,1},{2,34},{34,2},{3,35},{35,3},{4,36},{36... | collective-permute-start | bytes 1179656 | tf_op jit(solution)/shard_map/ppermute | solution.py:412
  35.5 7.7 %collective-permute-start.8 = (bf16[512,384]{1,0:T(8,128)(2,1)}, bf16[512,384]{1,0:T(8,128)(2,1)}, u32[]{:S(2)}, u32[]{:S(2)}) collective-permute-start(bf16[512,384]{1,0:T(8,128)(2,1)} %collective-permute-done.4.refs_3_.refs_4_), channel_id=1, source_target_pairs={{0,32},{32,0},{1,33},{33,1},{2,34},{34,2},{3,35},{35,3},{4,36},{36... | collective-permute-start | bytes 1179656 | tf_op jit(solution)/shard_map/ppermute | solution.py:412
  36.0 22.4 %collective-permute-start.6 = (bf16[512,384]{1,0:T(8,128)(2,1)}, bf16[512,384]{1,0:T(8,128)(2,1)S(1)}, u32[]{:S(2)}, u32[]{:S(2)}) collective-permute-start(bf16[512,384]{1,0:T(8,128)(2,1)} %collective-permute-done.4.refs_3_.refs_4_), channel_id=1, source_target_pairs={{0,33},{1,34},{2,35},{3,32},{32,3},{33,0},{34,1},{35,2},{4,37},{5,... | collective-permute-start | bytes 1179656 | tf_op jit(solution)/shard_map/ppermute | solution.py:421
  38.9 19.5 %collective-permute-start.5 = (bf16[512,384]{1,0:T(8,128)(2,1)}, bf16[512,384]{1,0:T(8,128)(2,1)S(1)}, u32[]{:S(2)}, u32[]{:S(2)}) collective-permute-start(bf16[512,384]{1,0:T(8,128)(2,1)} %collective-permute-done.4.refs_3_.refs_4_), channel_id=1, source_target_pairs={{0,1},{1,2},{2,3},{3,0},{32,35},{33,32},{34,33},{35,34},{4,5},{5,6... | collective-permute-start | bytes 1179656 | tf_op jit(solution)/shard_map/ppermute | solution.py:421
  38.9 0.8 copy-start.3
  43.2 1.0 copy-start.4
  44.2 10.2 %copy-start.5 = (bf16[512,384]{1,0:T(8,128)(2,1)S(1)}, bf16[512,384]{1,0:T(8,128)(2,1)}, u32[]{:S(2)}) copy-start(bf16[512,384]{1,0:T(8,128)(2,1)} %copy-done.3) | copy-start | bytes 1179652
  60.2 6.8 %collective-permute-start.13 = (f32[8,512]{1,0:T(8,128)S(1)}, f32[8,512]{1,0:T(8,128)S(1)}, u32[]{:S(2)}, u32[]{:S(2)}) collective-permute-start(f32[8,512]{1,0:T(8,128)S(1)} %get-tuple-element.34.refs_4_.refs_6_), channel_id=1, source_target_pairs={{0,24},{8,0},{16,8},{24,16},{1,25},{9,1},{17,9},{25,17},{2,26},{10... | collective-permute-start | bytes 49160 | tf_op jit(solution)/shard_map/ppermute | solution.py:399
  61.5 5.5 %collective-permute-start.12 = (f32[8,512]{1,0:T(8,128)S(1)}, f32[8,512]{1,0:T(8,128)S(1)}, u32[]{:S(2)}, u32[]{:S(2)}) collective-permute-start(f32[8,512]{1,0:T(8,128)S(1)} %get-tuple-element.34.refs_4_.refs_6_), channel_id=1, source_target_pairs={{0,16},{8,24},{16,0},{24,8},{1,17},{9,25},{17,1},{25,9},{2,18},{10... | collective-permute-start | bytes 49160 | tf_op jit(solution)/shard_map/ppermute | solution.py:399
  62.4 4.6 %collective-permute-start.11 = (f32[8,512]{1,0:T(8,128)S(1)}, f32[8,512]{1,0:T(8,128)S(1)}, u32[]{:S(2)}, u32[]{:S(2)}) collective-permute-start(f32[8,512]{1,0:T(8,128)S(1)} %get-tuple-element.34.refs_4_.refs_6_), channel_id=1, source_target_pairs={{0,8},{8,16},{16,24},{24,0},{1,9},{9,17},{17,25},{25,1},{2,10},{10... | collective-permute-start | bytes 49160 | tf_op jit(solution)/shard_map/ppermute | solution.py:399
  68.1 13.5 %collective-permute-start.18 = (bf16[512,128]{1,0:T(8,128)(2,1)S(1)}, bf16[512,128]{1,0:T(8,128)(2,1)S(1)}, u32[]{:S(2)}, u32[]{:S(2)}) collective-permute-start(bf16[512,128]{1,0:T(8,128)(2,1)S(1)} %get-tuple-element.35.refs_1_.refs_7_), channel_id=1, source_target_pairs={{0,32},{32,0},{1,33},{33,1},{2,34},{34,2},{3,35},{35,3},{4,36},{36... | collective-permute-start | bytes 393224 | tf_op jit(solution)/shard_map/ppermute | solution.py:412
  71.8 9.2 %collective-permute-start.15 = (bf16[512,128]{1,0:T(8,128)(2,1)S(1)}, bf16[512,128]{1,0:T(8,128)(2,1)S(1)}, u32[]{:S(2)}, u32[]{:S(2)}) collective-permute-start(bf16[512,128]{1,0:T(8,128)(2,1)S(1)} %get-tuple-element.35.refs_1_.refs_7_), channel_id=1, source_target_pairs={{0,3},{1,0},{2,1},{3,2},{32,33},{33,34},{34,35},{35,32},{4,7},{5,4... | collective-permute-start | bytes 393224 | tf_op jit(solution)/shard_map/ppermute | solution.py:421
  71.8 9.2 %collective-permute-start.14 = (bf16[512,128]{1,0:T(8,128)(2,1)S(1)}, bf16[512,128]{1,0:T(8,128)(2,1)S(1)}, u32[]{:S(2)}, u32[]{:S(2)}) collective-permute-start(bf16[512,128]{1,0:T(8,128)(2,1)S(1)} %get-tuple-element.35.refs_1_.refs_7_), channel_id=1, source_target_pairs={{0,1},{1,2},{2,3},{3,0},{32,35},{33,32},{34,33},{35,34},{4,5},{5,6... | collective-permute-start | bytes 393224 | tf_op jit(solution)/shard_map/ppermute | solution.py:421
  81.0 1.4 %collective-permute-start.20 = (bf16[512,128]{1,0:T(8,128)(2,1)S(1)}, bf16[512,128]{1,0:T(8,128)(2,1)S(1)}, u32[]{:S(2)}, u32[]{:S(2)}) collective-permute-start(bf16[512,128]{1,0:T(8,128)(2,1)S(1)} %get-tuple-element.38.refs_11_), channel_id=1, source_target_pairs={{0,32},{32,0},{1,33},{33,1},{2,34},{34,2},{3,35},{35,3},{4,36},{36... | collective-permute-start | bytes 393224 | tf_op jit(solution)/shard_map/ppermute | solution.py:412
  81.1 1.5 %collective-permute-start.19 = (bf16[512,128]{1,0:T(8,128)(2,1)S(1)}, bf16[512,128]{1,0:T(8,128)(2,1)S(1)}, u32[]{:S(2)}, u32[]{:S(2)}) collective-permute-start(bf16[512,128]{1,0:T(8,128)(2,1)S(1)} %get-tuple-element.37.refs_9_), channel_id=1, source_target_pairs={{0,32},{32,0},{1,33},{33,1},{2,34},{34,2},{3,35},{35,3},{4,36},{36... | collective-permute-start | bytes 393224 | tf_op jit(solution)/shard_map/ppermute | solution.py:412
  88.7 27.8 %all-to-all-start.1 = ((bf16[16,128,128]{2,1,0:T(8,128)(2,1)}), bf16[16,128,128]{2,1,0:T(8,128)(2,1)S(1)}, u32[]{:S(2)}, u32[]{:S(2)}) async-start(bf16[16,128,128]{2,1,0:T(8,128)(2,1)} %relay.3), calls=%async_computation.1 | async-start | bytes 1048576 | tf_op jit(solution)/shard_map/all_to_all | solution.py:508
  93.7 6.0 %collective-permute-start.17 = (bf16[512,128]{1,0:T(8,128)(2,1)S(1)}, bf16[512,128]{1,0:T(8,128)(2,1)S(1)}, u32[]{:S(2)}, u32[]{:S(2)}) collective-permute-start(bf16[512,128]{1,0:T(8,128)(2,1)S(1)} %get-tuple-element.37.refs_9_), channel_id=1, source_target_pairs={{0,33},{1,34},{2,35},{3,32},{32,3},{33,0},{34,1},{35,2},{4,37},{5,... | collective-permute-start | bytes 393224 | tf_op jit(solution)/shard_map/ppermute | solution.py:421
  96.6 4.1 %collective-permute-start.16 = (bf16[512,128]{1,0:T(8,128)(2,1)S(1)}, bf16[512,128]{1,0:T(8,128)(2,1)S(1)}, u32[]{:S(2)}, u32[]{:S(2)}) collective-permute-start(bf16[512,128]{1,0:T(8,128)(2,1)S(1)} %get-tuple-element.37.refs_9_), channel_id=1, source_target_pairs={{0,1},{1,2},{2,3},{3,0},{32,35},{33,32},{34,33},{35,34},{4,5},{5,6... | collective-permute-start | bytes 393224 | tf_op jit(solution)/shard_map/ppermute | solution.py:421
  103.8 15.9 %collective-permute-start.22 = (bf16[128,640]{1,0:T(8,128)(2,1)}, bf16[128,640]{1,0:T(8,128)(2,1)S(1)}, u32[]{:S(2)}, u32[]{:S(2)}) collective-permute-start(bf16[128,640]{1,0:T(8,128)(2,1)} %get-tuple-element.40), channel_id=1, source_target_pairs={{0,8},{4,40},{8,16},{12,48},{16,24},{20,56},{24,0},{28,32},{32,12}... | collective-permute-start | bytes 491528 | tf_op jit(solution)/shard_map/ppermute | solution.py:408
  108.3 11.4 %collective-permute-start.23 = (bf16[128,640]{1,0:T(8,128)(2,1)S(1)}, bf16[128,640]{1,0:T(8,128)(2,1)S(1)}, u32[]{:S(2)}, u32[]{:S(2)}) collective-permute-start(bf16[128,640]{1,0:T(8,128)(2,1)S(1)} %get-tuple-element.41), channel_id=1, source_target_pairs={{0,16},{4,48},{8,24},{12,56},{16,0},{20,32},{24,8},{28,40},{32,20}... | collective-permute-start | bytes 491528 | tf_op jit(solution)/shard_map/ppermute | solution.py:408
  110.5 9.2 %collective-permute-start.24 = (bf16[128,640]{1,0:T(8,128)(2,1)S(1)}, bf16[128,640]{1,0:T(8,128)(2,1)S(1)}, u32[]{:S(2)}, u32[]{:S(2)}) collective-permute-start(bf16[128,640]{1,0:T(8,128)(2,1)S(1)} %get-tuple-element.42), channel_id=1, source_target_pairs={{0,24},{4,56},{8,0},{12,32},{16,8},{20,40},{24,16},{28,48},{32,28}... | collective-permute-start | bytes 491528 | tf_op jit(solution)/shard_map/ppermute | solution.py:408
  114.6 8.1 %collective-permute-start.21 = (bf16[128,640]{1,0:T(8,128)(2,1)S(1)}, bf16[128,640]{1,0:T(8,128)(2,1)S(1)}, u32[]{:S(2)}, u32[]{:S(2)}) collective-permute-start(bf16[128,640]{1,0:T(8,128)(2,1)S(1)} %get-tuple-element.39.refs_5_), channel_id=1, source_target_pairs={{0,0},{4,32},{8,8},{12,40},{16,16},{20,48},{24,24},{28,56},{32,4},... | collective-permute-start | bytes 491528 | tf_op jit(solution)/shard_map/ppermute | solution.py:408

commit v4 on v3

--- a/solution.py
+++ b/solution.py
@@ -49,7 +49,7 @@
         input_output_aliases={count + len(after) + n: kept + n for n in range(len(carry))},
         scratch_shapes=scratch,
         compiler_params=pltpu.CompilerParams(vmem_limit_bytes=limit * 1024 * 1024),
-        cost_estimate=pl.CostEstimate(flops=flops, transcendentals=0, bytes_accessed=1 << 20),
+        cost_estimate=pl.CostEstimate(flops=flops, transcendentals=0, bytes_accessed=(1 << 20) if flops > 1000 else 1000),
         name=name,
     )
 
@@ -110,7 +110,7 @@
 
 
 def project_all(
-    info, x_far, cot_far, wo_far, w_ref, k0, k1, k2, k3, slope_ref,
+    info, x_far, cot_far, wo_far, w_ref, k0, k1, k2, k3, slope_ref, gate_ref, gm_ref,
     xn_ref, act_ref, x_ref, cot_ref, wo_ref, few, buf, sems,
 ):
     (got_x,) = fetched([(x_far, x_ref)], few)
@@ -133,10 +133,14 @@
         copies[part].wait()
         act, slope = silu_parts(dot(xn_ref[...], buf[part]))
         slope_ref[part] = slope.astype(BF)
-        put(act * (inside, inside / length, 0.5 * SCALE, 1.0)[part], part)
+        if part < 3:
+            put(act * (inside, inside / length, 0.5 * SCALE)[part], part)
+    gate_ref[...] = act.astype(BF)
     for copy in rest:
         copy.wait()
-    put(dot(cot_ref[...], wo_ref[...], NT), 4)
+    gm = dot(cot_ref[...], wo_ref[...], NT)
+    gm_ref[...] = gm.astype(BF)
+    put(gm * gate_ref[...].astype(F32), 3)
 
 
 def arrange(info, a0, a1, a2, a3, out_ref):
@@ -226,7 +230,7 @@
 def hist_end(info, p0, p1, p2, p3, own_ref, b0, b1, old_ref, att_ref, stat_ref, g_ref):
     for k, part in enumerate((p0, p1, p2, p3)):
         rows = pl.ds(pl.multiple_of(((info[2] - k) & 3) * 128, 128), 128)
-        g_ref[rows, :] = part[:, 3 * HS : 4 * HS].astype(F32) * part[:, 4 * HS :].astype(F32)
+        g_ref[rows, :] = part[:, 3 * HS :].astype(F32)
     attend_rows(own_ref, (b0, b1), corner_masks(info, False)[6:], old_ref, att_ref)
     att = att_ref[...]
     g = g_ref[...]
@@ -240,12 +244,11 @@
     stat_ref[...] = jnp.transpose(stats)[:8]
 
 
-def normed_grads(info, p0, p1, p2, p3, att_ref, s0, s1, s2, s3, ga_ref, mg_ref, gate_ref, gm_ref):
+def normed_grads(info, p0, p1, p2, p3, att_ref, s0, s1, s2, s3, ga_ref, normed_ref, g_ref):
     for k, part in enumerate((p0, p1, p2, p3)):
         y = (info[2] - k) & 3
         rows = pl.ds(pl.multiple_of(y * 128, 128), 128)
-        gate_ref[rows, :] = part[:, 3 * HS : 4 * HS].astype(F32)
-        gm_ref[rows, :] = part[:, 4 * HS :].astype(F32)
+        g_ref[rows, :] = part[:, 3 * HS :].astype(F32)
     stats = [s[...] for s in (s0, s1, s2, s3)]
     mean = sum(s[0:1] for s in stats) * 0.25
     squares = sum(s[1:2] + HS * (s[0:1] - mean) * (s[0:1] - mean) for s in stats)
@@ -261,11 +264,8 @@
     cols = jnp.transpose(packed)
     spread_c = cols[:, 1:2]
     normed = (att_ref[...] - cols[:, 0:1]) * spread_c
-    gate = gate_ref[...]
-    gm = gm_ref[...]
-    ga_ref[...] = (spread_c * (gate * gm - cols[:, 2:3] - normed * cols[:, 3:4])).astype(BF)
-    mg_ref[:, :HS] = (normed * gate).astype(BF)
-    mg_ref[:, HS:] = (normed * gm).astype(BF)
+    ga_ref[...] = (spread_c * (g_ref[...] - cols[:, 2:3] - normed * cols[:, 3:4])).astype(BF)
+    normed_ref[...] = normed.astype(BF)
 
 
 def slope_times(half, grads):
@@ -323,61 +323,59 @@
         refs[12][y, :, HS:] = dv
 
 
-def hist_dkv_end(info, dq_ref, mg_ref, own_ref, b0, b1, g0, g1, old_ref, k0, k1, k2, k3, all_ref):
+def hist_dkv_end(info, dq_ref, normed_ref, own_ref, b0, b1, g0, g1, old_ref, k0, k1, k2, k3, all_ref):
     masks = corner_masks(info, True)[6:]
     for y in range(4):
         dk, dv = key_grads(own_ref, (b0, b1), (g0, g1), masks, y, old_ref[y, :, :HS], old_ref[y, :, HS:])
         all_ref[y, :, :HS] = dq_ref[y]
         all_ref[y, :, HS : 2 * HS] = dk.astype(BF)
         all_ref[y, :, 2 * HS : 3 * HS] = dv.astype(BF)
-        all_ref[y, :, 3 * HS :] = mg_ref[y * 128 : (y + 1) * 128, :]
+        all_ref[y, :, 3 * HS :] = normed_ref[y * 128 : (y + 1) * 128, :]
     for k, out in enumerate((k0, k1, k2, k3)):
         out[...] = all_ref[(info[2] + k) & 3]
 
 
 def hist_close(
-    info, x_far, cot_far, slope_far, wo_far, w_ref, b0, b1, b2, b3, out_far, grad_far,
-    mixed_ref, hid_ref, out_ref, grad_ref, x_ref, cot_ref, slope_ref, wo_ref, most, few, buf, sems,
+    info, x_ref, cot_ref, slope_ref, wo_ref, buf, gate_ref, gm_ref, b0, b1, b2, b3, out_far, grad_far,
+    mixed_ref, hid_ref, out_ref, grad_ref, few,
 ):
-    got = fetched([(slope_far, slope_ref), (wo_far, wo_ref), (x_far, x_ref)], most)
-    copies = columns(w_ref, buf, sems, (0, 1, 2, 3))
-    got += fetched([(cot_far, cot_ref)], most.at[pl.ds(3, 1)])
     length = jnp.full((128, 1), info[0], jnp.int32).astype(F32)
-    got[0].wait()
     for k, b in enumerate((b0, b1, b2, b3)):
         lanes = pl.ds(pl.multiple_of(((info[2] - k) & 3) * HS, HS), HS)
 
         def put(part, grads, which):
             hid_ref[part, :, lanes] = (grads * slope_ref[which, :, lanes].astype(F32)).astype(BF)
 
-        put(0, b[:, 4 * HS :].astype(F32), 3)
+        normed = b[:, 3 * HS :].astype(F32)
+        put(0, normed * gm_ref[:, lanes].astype(F32), 3)
         put(1, b[:, 2 * HS : 3 * HS].astype(F32) / length, 1)
         put(2, b[:, :HS].astype(F32), 2)
         put(3, b[:, HS : 2 * HS].astype(F32), 0)
-        mixed_ref[:, lanes] = b[:, 3 * HS : 4 * HS]
-    got[1].wait()
-    got[2].wait()
+        mixed_ref[:, lanes] = (normed * gate_ref[:, lanes].astype(F32)).astype(BF)
     x = x_ref[...].astype(F32)
     out_ref[...] = (x + dot(mixed_ref[...], wo_ref[...])).astype(BF)
     done = fetched([(out_ref, out_far.at[0])], few)
     e = None
     for part in range(4):
-        copies[part].wait()
         more = dot(hid_ref[part], buf[part], NT)
         e = more if e is None else e + more
     normed, spread = normalize(x)
     back = spread * (
         e - jnp.mean(e, axis=-1, keepdims=True) - normed * jnp.mean(e * normed, axis=-1, keepdims=True)
     )
-    got[3].wait()
     grad_ref[...] = (cot_ref[...].astype(F32) + back).astype(BF)
     done += fetched([(grad_ref, grad_far.at[0])], few.at[pl.ds(1, 1)])
     for copy in done:
         copy.wait()
 
 
-def cand_close(ids_ref, gate_far, ret_ref, x_far, wo_far, out_ref, gate_ref, x_ref, wo_ref, few):
+def cand_close(
+    ids_ref, gate_far, ret_ref, x_far, wo_far, w_far, hx_far, cot_far, out_ref, wo_ref, buf, hx_ref, cot_ref,
+    gate_ref, x_ref, few, sems,
+):
     copies = fetched([(gate_far, gate_ref), (wo_far, wo_ref), (x_far, x_ref)], few)
+    later = columns(w_far, buf, sems, (0, 1, 2, 3))
+    later += fetched([(hx_far, hx_ref), (cot_far, cot_ref)], few.at[pl.ds(3, 2)])
     col, row, first, second = slot_ids(ids_ref)
     rank = jnp.sum(jnp.where((col == row) & (second < first), 1, 0), axis=1, keepdims=True)
     slot = col * CAP + rank
@@ -393,6 +391,8 @@
     more = dot(mixed, wo_ref[...])
     copies[2].wait()
     out_ref[...] = (x_ref[...].astype(F32) + more).astype(BF)
+    for copy in later:
+        copy.wait()
 
 
 def turned(value, axis, size, steps):
@@ -435,9 +435,9 @@
     def relayed(values, after):
         return call(nothing, "relay", (1,), [], [], [], [], 1_000, after, carry=values)()
 
-    *sent, slope = call(
+    *sent, slope, gate, gm = call(
         project_all, "project_all", (1,), [SMEM, far, far, far, far],
-        [shaped((128, 640))] * 4 + [shaped((4, 128, 512))], [held] * 5,
+        [shaped((128, 512))] * 4 + [shaped((4, 128, 512))] + [shaped((128, 512))] * 2, [held] * 7,
         [
             pltpu.VMEM((128, 1024), BF), pltpu.VMEM((128, 512), BF), pltpu.VMEM((128, 1024), BF),
             pltpu.VMEM((128, 1024), BF), pltpu.VMEM((512, 1024), BF), pltpu.SemaphoreType.DMA((3,)),
@@ -474,22 +474,22 @@
             q_spec if end else acc_spec, [], 600_000_000 * len(kvs), after,
         )(arrived, *kvs, *([] if begin else [total]))
 
-    total = cand_part(kvq, None, False, ())
     att = call(
         hist_begin, "hist_begin", (1,), [SMEM] + [held] * 6,
-        shaped((512, 128), F32), held, [], 1_400_000_000, (total,),
+        shaped((512, 128), F32), held, [], 1_000,
     )(info, *kvq)
+    total = cand_part(kvq, None, False, (att,))
     att, stats = call(
         hist_end, "hist_end", (1,), [SMEM] + [held] * 8,
         [shaped((512, 128), F32), shaped((8, 512), F32)], [held] * 2,
-        [pltpu.VMEM((512, 128), F32)], 400_000_000,
+        [pltpu.VMEM((512, 128), F32)], 400_000_000, (total,),
     )(info, *parts, own, *last, att)
     all_stats = [stats] + [turned(stats, "y", 4, k) for k in (1, 2, 3)]
     weighed = cand_part(last, total, True, (stats,))
-    ga, mg = call(
+    ga, normed = call(
         normed_grads, "normed_grads", (1,), [SMEM] + [held] * 9,
-        [shaped((512, 128)), shaped((512, 256))], [held] * 2,
-        [pltpu.VMEM((512, 128), F32)] * 2, 1_000_000, (weighed,),
+        [shaped((512, 128))] * 2, [held] * 2,
+        [pltpu.VMEM((512, 128), F32)], 1_000_000, (weighed,),
     )(info, *parts, att, *all_stats)
 
     ga_plus, ga_minus = along(ga, 1, 0), along(ga, -1, 0)
@@ -504,33 +504,32 @@
         hist_dkv_begin, "hist_dkv_begin", (1,), [SMEM] + [held] * 12,
         shaped((4, 128, 256), F32), held, [], 2_000_000_000,
     )(info, *kvq, *gas)
-    (leaving,) = relayed([weighed], (key_sums,))
+    (leaving,) = relayed([weighed], (key_sums, *ga_last))
     returned = lax.all_to_all(leaving, ("xl", "xh", "y"), 0, 0, tiled=True)
     grads = call(
         hist_dkv_end, "hist_dkv_end", (1,), [SMEM] + [held] * 8,
-        [shaped((128, 640))] * 4, [held] * 4, [pltpu.VMEM((4, 128, 640), BF)], 800_000_000,
-    )(info, dq, mg, own, *last, *ga_last, key_sums)
+        [shaped((128, 512))] * 4, [held] * 4, [pltpu.VMEM((4, 128, 512), BF)], 800_000_000,
+    )(info, dq, normed, own, *last, *ga_last, key_sums)
     back = [crossed(v, k) for k, v in enumerate(grads)]
 
-    cand_out = call(
-        cand_close, "cand_close", (1,), [held, far, held, far, far],
-        pltpu.HBM((256, 1024), BF), pl.BlockSpec((256, 1024), lambda i: (0, 0)),
+    cand_out, wo_near, w_near, x_near, cot_near = call(
+        cand_close, "cand_close", (1,), [held, far, held] + [far] * 5,
+        [pltpu.HBM((256, 1024), BF), shaped((512, 1024)), shaped((4, 1024, 512))] + [shaped((128, 1024))] * 2,
+        [pl.BlockSpec((256, 1024), lambda i: (0, 0))] + [held] * 4,
         [
-            pltpu.VMEM((256, 512), BF), pltpu.VMEM((256, 1024), BF), pltpu.VMEM((512, 1024), BF),
-            pltpu.SemaphoreType.DMA((3,)),
+            pltpu.VMEM((256, 512), BF), pltpu.VMEM((256, 1024), BF),
+            pltpu.SemaphoreType.DMA((5,)), pltpu.SemaphoreType.DMA((4,)),
         ], 400_000_000, (grads[0],),
-    )(cand_loop, cand_gate, returned, cand_x, w_out)
+    )(cand_loop, cand_gate, returned, cand_x, w_out, w_proj, x_rows, cot)
     final = pltpu.HBM((1, 128, 1024), BF)
     hist_out, hist_grad = call(
-        hist_close, "hist_close", (1,), [SMEM] + [far] * 5 + [held] * 4,
+        hist_close, "hist_close", (1,), [SMEM] + [held] * 11,
         [final] * 2, [far] * 2,
         [
             pltpu.VMEM((128, 512), BF), pltpu.VMEM((4, 128, 512), BF), pltpu.VMEM((128, 1024), BF),
-            pltpu.VMEM((128, 1024), BF), pltpu.VMEM((128, 1024), BF), pltpu.VMEM((128, 1024), BF),
-            pltpu.VMEM((4, 128, 512), BF), pltpu.VMEM((512, 1024), BF), pltpu.SemaphoreType.DMA((4,)),
-            pltpu.SemaphoreType.DMA((2,)),
-        ] + weights(4), 700_000_000, (pltpu.with_memory_space_constraint(cand_out, pltpu.HBM),), 16,
-    )(info, x_rows, cot, slope, w_out, w_proj, *back)
+            pltpu.VMEM((128, 1024), BF), pltpu.SemaphoreType.DMA((2,)),
+        ], 700_000_000,
+    )(info, x_near, cot_near, slope, wo_near, w_near, gate, gm, *back)
     return hist_out, hist_grad, cand_out
 
 

time: 129 us -> 119 us (0.922)
  waiting for transfers between devices: 14.7 us -> 8.25 us
  starting transfers between devices: 56.5 us -> 50.8 us
  local copies, waits for them, and re-layouts: 2.01 us -> 6.79 us
  Pallas kernels: 53.4 us -> 50.7 us
    unnamed x15 -> x33, local copies, waits for them, and re-layouts: 1.92 us -> 6.7 us
    all_to_all x1, waiting for transfers between devices: 3.49 us -> 0.01 us  [per_device(): arrived = lax.all_to_all(sent_cand, ('xl', 'xh', 'y'), 0, 0, tiled=True)]
    ppermute x8, starting transfers between devices: 12.5 us -> 9.1 us  [along(): return lax.ppermute(value, ('c', 'z'), pairs)]
    pallas_call x15, Pallas kernels: 53.4 us -> 50.7 us  [run(): got = made(*pinned, *after, *carry)]
    ppermute x8, waiting for transfers between devices: 6.01 us -> 3.8 us  [crossed(): return lax.ppermute(value, ('c', 'y', 'xh'), pairs)]
    ppermute x6, starting transfers between devices: 6.33 us -> 4.27 us  [across(): return lax.ppermute(value, 'c', [(0, 1), (1, 0)])]
  transfers between devices with their start and end apart: 27 -> 27, of which waited for: 8 -> 4; matrix products, arithmetic and copies ran while one was open for 0% -> 0% of each run, Pallas kernels for 26% -> 34%
where the time goes in v4:
time: 119 us; the launch traced here: 118 us
  starting transfers between devices  50.8 us (43%)
  Pallas kernels  50.7 us (43%)
  waiting for transfers between devices  8.25 us (7%)
  local copies, waits for them, and re-layouts  6.79 us (6%)
  between operations  1.86 us (2%)
    pallas_call x15, Pallas kernels, run(): got = made(*pinned, *after, *carry)  50.7 us
    ppermute x8, starting transfers between devices, crossed(): return lax.ppermute(value, ('c', 'y', 'xh'), pairs)  26.2 us
    ppermute x8, starting transfers between devices, along(): return lax.ppermute(value, ('c', 'z'), pairs)  9.1 us
    unnamed x33, local copies, waits for them, and re-layouts  6.7 us
    ppermute x6, starting transfers between devices, across(): return lax.ppermute(value, 'c', [(0, 1), (1, 0)])  4.27 us
    all_to_all x1, starting transfers between devices, per_device(): returned = lax.all_to_all(leaving, ('xl', 'xh', 'y'), 0, 0, tiled=True)  4.08 us
    ppermute x8, waiting for transfers between devices, crossed(): return lax.ppermute(value, ('c', 'y', 'xh'), pairs)  3.8 us
    all_to_all x1, starting transfers between devices, per_device(): arrived = lax.all_to_all(sent_cand, ('xl', 'xh', 'y'), 0, 0, tiled=True)  3.69 us
  transfers between devices with their start and end apart: 27, of which 4 were waited for; matrix products, arithmetic and copies ran while one was open for 0% of the time, Pallas kernels for 34%

profile of v4, /device:TPU:1, one launch (start us, length us, event | category | flops | bytes accessed | tf_op | source)
XLA Modules:
  0.0 118.4 jit_solution(14648219228478390681)
XLA Ops:
  1.4 4.3 %project_all.1 = (bf16[128,512]{1,0:T(8,128)(2,1)S(1)}, bf16[128,512]{1,0:T(8,128)(2,1)S(1)}, bf16[128,512]{1,0:T(8,128)(2,1)S(1)}, bf16[128,512]{1,0:T(8,128)(2...) custom-call(s32[5]{0:T(128)S(1)} %stack.19.refs_0_, ...), custom_call_target="tpu_custom_call" | custom-call | flops 700000000 | bytes 1048576 | tf_op jit(solution)/shard_map/project_all/pallas_call | solution.py:63
  5.8 0.6 copy-done.11
  6.4 0.7 copy-done.13
  7.1 6.0 %collective-permute-start = (bf16[128,512]{1,0:T(8,128)(2,1)S(1)}, bf16[128,512]{1,0:T(8,128)(2,1)S(1)}, u32[]{:S(2)}, u32[]{:S(2)}) collective-permute-start(bf16[128,512]{1,0:T(8,128)(2,1)S(1)} %get-tuple-element.33), channel_id=1, source_target_pairs={{0,0},{4,32},{8,8},{12,40},{16,16},{20,48},{24,24},{28,56},{32,4},... | collective-permute-start | bytes 393224 | tf_op jit(solution)/shard_map/ppermute | solution.py:408
  13.1 1.1 collective-permute-start.1
  14.2 5.6 %collective-permute-start.2 = (bf16[128,512]{1,0:T(8,128)(2,1)S(1)}, bf16[128,512]{1,0:T(8,128)(2,1)S(1)}, u32[]{:S(2)}, u32[]{:S(2)}) collective-permute-start(bf16[128,512]{1,0:T(8,128)(2,1)S(1)} %get-tuple-element.35), channel_id=1, source_target_pairs={{0,16},{4,48},{8,24},{12,56},{16,0},{20,32},{24,8},{28,40},{32,20}... | collective-permute-start | bytes 393224 | tf_op jit(solution)/shard_map/ppermute | solution.py:408
  19.8 0.8 collective-permute-start.3
  20.6 0.1 copy.15.refs_0_
  20.7 3.1 %project_cand.1 = (bf16[16,128,128]{2,1,0:T(8,128)(2,1)}, bf16[256,512]{1,0:T(8,128)(2,1)S(1)}) custom-call(s32[256,1]{1,0:T(8,128)S(1)} %copy.15.refs_0_, bf16[256,1024]{1,0:T(8,128)(2,1)S(1)} %copy-done, bf16[1024,2048]{1,0:T(8,128)(2,1)} %refs_5_.1, bf16[4,128,512]{2,1,0:T(8,128)(2,1)S(1)} %get-tuple-element.31.refs_3_), custom_call_target="tpu_custom_call" | custom-call | flops 700000000 | bytes 1048576 | tf_op jit(solution)/shard_map/project_cand/pallas_call | solution.py:63
  23.9 2.6 %collective-permute-done.3.refs_4_ = bf16[128,512]{1,0:T(8,128)(2,1)S(1)} collective-permute-done((bf16[128,512]{1,0:T(8,128)(2,1)S(1)}, bf16[128,512]{1,0:T(8,128)(2,1)S(1)}, u32[]{:S(2)}, u32[]{:S(2)}) %collective-permute-start.3) | collective-permute-done | bytes 131104 | tf_op jit(solution)/shard_map/ppermute | solution.py:408
  26.6 0.6 arrange.1
  27.2 3.8 %collective-permute-start.5 = (bf16[512,384]{1,0:T(8,128)(2,1)S(1)}, bf16[512,384]{1,0:T(8,128)(2,1)}, u32[]{:S(2)}, u32[]{:S(2)}) collective-permute-start(bf16[512,384]{1,0:T(8,128)(2,1)S(1)} %bitcast.7), channel_id=1, source_target_pairs={{0,1},{1,2},{2,3},{3,0},{32,35},{33,32},{34,33},{35,34},{4,5},{5,6... | collective-permute-start | bytes 1179656 | tf_op jit(solution)/shard_map/ppermute | solution.py:421
  31.0 3.7 %all-to-all-start = ((bf16[16,128,128]{2,1,0:T(8,128)(2,1)}), bf16[16,128,128]{2,1,0:T(8,128)(2,1)S(1)}, u32[]{:S(2)}, u32[]{:S(2)}) async-start(bf16[16,128,128]{2,1,0:T(8,128)(2,1)} %get-tuple-element.39), calls=%async_computation | async-start | bytes 1048576 | tf_op jit(solution)/shard_map/all_to_all | solution.py:461
  34.7 1.1 collective-permute-start.4
  35.9 0.1 collective-permute-start.6
  36.0 3.0 %collective-permute-done.7.refs_5_.refs_6_ = bf16[512,384]{1,0:T(8,128)(2,1)} collective-permute-done((bf16[512,384]{1,0:T(8,128)(2,1)S(1)}, bf16[512,384]{1,0:T(8,128)(2,1)}, u32[]{:S(2)}, u32[]{:S(2)}) %collective-permute-start.7) | collective-permute-done | bytes 393248 | tf_op jit(solution)/shard_map/ppermute | solution.py:421
  39.0 0.4 collective-permute-start.10
  39.4 0.1 collective-permute-start.9
  39.5 1.4 %collective-permute-done.8.refs_6_.refs_7_ = bf16[512,384]{1,0:T(8,128)(2,1)S(1)} collective-permute-done((bf16[512,384]{1,0:T(8,128)(2,1)}, bf16[512,384]{1,0:T(8,128)(2,1)S(1)}, u32[]{:S(2)}, u32[]{:S(2)}) %collective-permute-start.8) | collective-permute-done | bytes 393248 | tf_op jit(solution)/shard_map/ppermute | solution.py:412
  40.9 3.7 %hist_begin.1.refs_7_.refs_8_ = f32[512,128]{1,0:T(8,128)S(1)} custom-call(s32[5]{0:T(128)S(1)} %stack.19.refs_0_, bf16[512,384]{1,0:T(8,128)(2,1)S(1)} %bitcast.10, bf16[512,384]{1,0:T(8,128)(2,1)S(1)} %collective-permute-done.4.refs_2_.refs_3_, bf16[512,384]{1,0:T(8,128)(2,1)} %collective-permute-done.5.refs_3_.refs_4_, ...), custom_call_target="tpu_custom_call" | custom-call | flops 1000 | bytes 1000 | tf_op jit(solution)/shard_map/hist_begin/pallas_call | solution.py:63
  44.6 0.7 copy-done.2
  45.3 0.8 copy-done.5
  46.1 0.7 copy-done.8
  46.9 1.0 copy-done.3
  47.9 1.0 copy-done.6
  48.9 1.0 copy-done.9
  49.9 9.9 %cand_attend.2.refs_9_.refs_3_ = f32[2048,128]{1,0:T(8,128)S(1)} custom-call(bf16[16,128,128]{2,1,0:T(8,128)(2,1)S(1)} %all-to-all-done.refs_0_, bf16[512,384]{1,0:T(8,128)(2,1)S(1)} %bitcast.11, bf16[512,384]{1,0:T(8,128)(2,1)S(1)} %copy-done.3, bf16[512,384]{1,0:T(8,128)(2,1)} %collective-permute-done.5.refs_3_.refs_4_, bf16[512,384]{1,0:T(8,128)(2,1)S(1)} %copy-done.6, ...), custom_call_target="tpu_custom_call" | custom-call | flops 3600000000 | bytes 1048576 | tf_op jit(solution)/shard_map/cand_attend/pallas_call | solution.py:63
  59.8 1.8 %hist_end.1 = (f32[512,128]{1,0:T(8,128)S(1)}, f32[8,512]{1,0:T(8,128)S(1)}) custom-call(s32[5]{0:T(128)S(1)} %stack.19.refs_0_, bf16[128,512]{1,0:T(8,128)(2,1)S(1)} %collective-permute-done.refs_1_, bf16[128,512]{1,0:T(8,128)(2,1)S(1)} %collective-permute-done.1.refs_2_, bf16[128,512]{1,0:T(8,128)(2,1)S(1)} %collective-permute-done.2.refs_3_, ...), custom_call_target="tpu_custom_call" | custom-call | flops 400000000 | bytes 1048576 | tf_op jit(solution)/shard_map/hist_end/pallas_call | solution.py:63
  61.7 3.5 %collective-permute-start.12 = (f32[8,512]{1,0:T(8,128)S(1)}, f32[8,512]{1,0:T(8,128)S(1)}, u32[]{:S(2)}, u32[]{:S(2)}) collective-permute-start(f32[8,512]{1,0:T(8,128)S(1)} %get-tuple-element.41.refs_4_.refs_6_), channel_id=1, source_target_pairs={{0,16},{8,24},{16,0},{24,8},{1,17},{9,25},{17,1},{25,9},{2,18},{10... | collective-permute-start | bytes 49160 | tf_op jit(solution)/shard_map/ppermute | solution.py:399
  65.1 4.0 %cand_attend.3.refs_10_.refs_3_ = bf16[16,128,128]{2,1,0:T(8,128)(2,1)} custom-call(bf16[16,128,128]{2,1,0:T(8,128)(2,1)S(1)} %all-to-all-done.refs_0_, bf16[512,384]{1,0:T(8,128)(2,1)S(1)} %collective-permute-done.9.refs_6_.refs_1_.refs_8_.refs_4_, bf16[512,384]{1,0:T(8,128)(2,1)S(1)} %collective-permute-done.10.refs_7_.refs_2_.refs_9_.refs_5_, ...), custom_call_target="tpu_custom_call" | custom-call | flops 1200000000 | bytes 1048576 | tf_op jit(solution)/shard_map/cand_attend/pallas_call | solution.py:63
  69.1 1.0 normed_grads.1
  70.1 1.8 %collective-permute-start.15 = (bf16[512,128]{1,0:T(8,128)(2,1)S(1)}, bf16[512,128]{1,0:T(8,128)(2,1)S(1)}, u32[]{:S(2)}, u32[]{:S(2)}) collective-permute-start(bf16[512,128]{1,0:T(8,128)(2,1)S(1)} %get-tuple-element.42.refs_1_.refs_7_), channel_id=1, source_target_pairs={{0,1},{1,2},{2,3},{3,0},{32,35},{33,32},{34,33},{35,34},{4,5},{5,6... | collective-permute-start | bytes 393224 | tf_op jit(solution)/shard_map/ppermute | solution.py:421
  72.0 2.4 %collective-permute-start.14 = (bf16[512,128]{1,0:T(8,128)(2,1)S(1)}, bf16[512,128]{1,0:T(8,128)(2,1)S(1)}, u32[]{:S(2)}, u32[]{:S(2)}) collective-permute-start(bf16[512,128]{1,0:T(8,128)(2,1)S(1)} %get-tuple-element.42.refs_1_.refs_7_), channel_id=1, source_target_pairs={{0,32},{32,0},{1,33},{33,1},{2,34},{34,2},{3,35},{35,3},{4,36},{36... | collective-permute-start | bytes 393224 | tf_op jit(solution)/shard_map/ppermute | solution.py:412
  74.4 6.3 %hist_dq.1.refs_0_.refs_1_ = bf16[4,128,128]{2,1,0:T(8,128)(2,1)S(1)} custom-call(s32[5]{0:T(128)S(1)} %stack.19.refs_0_, bf16[512,128]{1,0:T(8,128)(2,1)S(1)} %get-tuple-element.42.refs_1_.refs_7_, bf16[512,384]{1,0:T(8,128)(2,1)S(1)} %bitcast.13, bf16[512,384]{1,0:T(8,128)(2,1)S(1)} %copy-done.4, bf16[512,384]{1,0:T(8,128)(2,1)} %collective-permute-done.5.refs_3_.refs_4_, ...), custom_call_target="tpu_custom_call" | custom-call | flops 2000000000 | bytes 1048576 | tf_op jit(solution)/shard_map/hist_dq/pallas_call | solution.py:63
  80.7 0.1 collective-permute-start.17
  80.8 0.5 collective-permute-start.18
  81.3 1.4 %collective-permute-start.19 = (bf16[512,128]{1,0:T(8,128)(2,1)S(1)}, bf16[512,128]{1,0:T(8,128)(2,1)S(1)}, u32[]{:S(2)}, u32[]{:S(2)}) collective-permute-start(bf16[512,128]{1,0:T(8,128)(2,1)S(1)} %get-tuple-element.43.refs_9_), channel_id=1, source_target_pairs={{0,1},{1,2},{2,3},{3,0},{32,35},{33,32},{34,33},{35,34},{4,5},{5,6... | collective-permute-start | bytes 393224 | tf_op jit(solution)/shard_map/ppermute | solution.py:421
  82.8 1.5 %collective-permute-start.20 = (bf16[512,128]{1,0:T(8,128)(2,1)S(1)}, bf16[512,128]{1,0:T(8,128)(2,1)S(1)}, u32[]{:S(2)}, u32[]{:S(2)}) collective-permute-start(bf16[512,128]{1,0:T(8,128)(2,1)S(1)} %get-tuple-element.43.refs_9_), channel_id=1, source_target_pairs={{0,33},{1,34},{2,35},{3,32},{32,3},{33,0},{34,1},{35,2},{4,37},{5,... | collective-permute-start | bytes 393224 | tf_op jit(solution)/shard_map/ppermute | solution.py:421
  84.3 5.9 %hist_dkv_begin.1.refs_0_.refs_8_ = f32[4,128,256]{2,1,0:T(8,128)S(1)} custom-call(s32[5]{0:T(128)S(1)} %stack.19.refs_0_, bf16[512,384]{1,0:T(8,128)(2,1)S(1)} %bitcast.14, bf16[512,384]{1,0:T(8,128)(2,1)S(1)} %copy-done.4, bf16[512,384]{1,0:T(8,128)(2,1)} %collective-permute-done.5.refs_3_.refs_4_, bf16[512,384]{1,0:T(8,128)(2,1)S(1)} %copy-done.7, ...), custom_call_target="tpu_custom_call" | custom-call | flops 2000000000 | bytes 1048576 | tf_op jit(solution)/shard_map/hist_dkv_begin/pallas_call | solution.py:63
  90.3 4.1 %all-to-all-start.1 = ((bf16[16,128,128]{2,1,0:T(8,128)(2,1)}), bf16[16,128,128]{2,1,0:T(8,128)(2,1)S(1)}, u32[]{:S(2)}, u32[]{:S(2)}) async-start(bf16[16,128,128]{2,1,0:T(8,128)(2,1)} %relay.3), calls=%async_computation.1 | async-start | bytes 1048576 | tf_op jit(solution)/shard_map/all_to_all | solution.py:508
  94.3 3.1 %hist_dkv_end.1 = (bf16[128,512]{1,0:T(8,128)(2,1)S(1)}, bf16[128,512]{1,0:T(8,128)(2,1)}, bf16[128,512]{1,0:T(8,128)(2,1)}, bf16[128,512]{1,0:T(8,128)(2,1)}) custom-call(s32[5]{0:T(128)S(1)} %stack.19.refs_0_, bf16[4,128,128]{2,1,0:T(8,128)(2,1)S(1)} %hist_dq.1.refs_0_.refs_1_, bf16[512,128]{1,0:T(8,128)(2,1)S(1)} %get-tuple-element.45.refs_2_, ...), custom_call_target="tpu_custom_call" | custom-call | flops 800000000 | bytes 1048576 | tf_op jit(solution)/shard_map/hist_dkv_end/pallas_call | solution.py:63
  97.5 4.3 %collective-permute-start.21 = (bf16[128,512]{1,0:T(8,128)(2,1)S(1)}, bf16[128,512]{1,0:T(8,128)(2,1)S(1)}, u32[]{:S(2)}, u32[]{:S(2)}) collective-permute-start(bf16[128,512]{1,0:T(8,128)(2,1)S(1)} %get-tuple-element.46.refs_8_), channel_id=1, source_target_pairs={{0,0},{4,32},{8,8},{12,40},{16,16},{20,48},{24,24},{28,56},{32,4},... | collective-permute-start | bytes 393224 | tf_op jit(solution)/shard_map/ppermute | solution.py:408
  101.8 2.1 %collective-permute-start.22 = (bf16[128,512]{1,0:T(8,128)(2,1)}, bf16[128,512]{1,0:T(8,128)(2,1)S(1)}, u32[]{:S(2)}, u32[]{:S(2)}) collective-permute-start(bf16[128,512]{1,0:T(8,128)(2,1)} %get-tuple-element.53), channel_id=1, source_target_pairs={{0,8},{4,40},{8,16},{12,48},{16,24},{20,56},{24,0},{28,32},{32,12}... | collective-permute-start | bytes 393224 | tf_op jit(solution)/shard_map/ppermute | solution.py:408
  103.9 4.2 %collective-permute-start.23 = (bf16[128,512]{1,0:T(8,128)(2,1)}, bf16[128,512]{1,0:T(8,128)(2,1)S(1)}, u32[]{:S(2)}, u32[]{:S(2)}) collective-permute-start(bf16[128,512]{1,0:T(8,128)(2,1)} %get-tuple-element.54), channel_id=1, source_target_pairs={{0,16},{4,48},{8,24},{12,56},{16,0},{20,32},{24,8},{28,40},{32,20}... | collective-permute-start | bytes 393224 | tf_op jit(solution)/shard_map/ppermute | solution.py:408
  108.1 2.1 %collective-permute-start.24 = (bf16[128,512]{1,0:T(8,128)(2,1)}, bf16[128,512]{1,0:T(8,128)(2,1)S(1)}, u32[]{:S(2)}, u32[]{:S(2)}) collective-permute-start(bf16[128,512]{1,0:T(8,128)(2,1)} %get-tuple-element.55), channel_id=1, source_target_pairs={{0,24},{4,56},{8,0},{12,32},{16,8},{20,40},{24,16},{28,48},{32,28}... | collective-permute-start | bytes 393224 | tf_op jit(solution)/shard_map/ppermute | solution.py:408
  110.2 3.8 %cand_close.1 = (bf16[256,1024]{1,0:T(8,128)(2,1)}, bf16[512,1024]{1,0:T(8,128)(2,1)S(1)}, bf16[4,1024,512]{2,1,0:T(8,128)(2,1)S(1)}, bf16[128,1024]{1,0:T(8,128)(2,1)S(1)}, bf16[128,1024]{1,0:T(8,128)(2,1)S(1)}) custom-call(s32[256,1]{1,0:T(8,128)S(1)} %copy.15.refs_0_, bf16[256,512]{1,0:T(8,128)(2,1)} %copy-done.1, ...), custom_call_target="tpu_custom_call" | custom-call | flops 400000000 | bytes 1048576 | tf_op jit(solution)/shard_map/cand_close/pallas_call | solution.py:63
  114.0 1.1 collective-permute-done.24.refs_11_
  115.1 3.1 %hist_close.1 = (bf16[1,128,1024]{2,1,0:T(8,128)(2,1)}, bf16[1,128,1024]{2,1,0:T(8,128)(2,1)}) custom-call(s32[5]{0:T(128)S(1)} %stack.19.refs_0_, bf16[128,1024]{1,0:T(8,128)(2,1)S(1)} %get-tuple-element.47.refs_1_, bf16[128,1024]{1,0:T(8,128)(2,1)S(1)} %get-tuple-element.48.refs_2_, bf16[4,128,512]{2,1,0:T(8,128)(2,1)S(1)} %get-tuple-element.31.refs_3_, ...), custom_call_target="tpu_custom_call" | custom-call | flops 700000000 | bytes 1048576 | tf_op jit(solution)/shard_map/hist_close/pallas_call | solution.py:63
  (55 shorter events, 0.3 us)
Async XLA Ops:
  0.6 20.0 %copy-start.15 = (s32[256,1]{0,1:T(1,128)S(1)}, s32[256,1]{0,1:T(1,128)}, u32[]{:S(2)}) copy-start(s32[256,1]{0,1:T(1,128)} %param.10) | copy-start | bytes 3076
  0.6 20.1 %copy-start = (bf16[256,1024]{1,0:T(8,128)(2,1)S(1)}, bf16[256,1024]{1,0:T(8,128)(2,1)}, u32[]{:S(2)}) copy-start(bf16[256,1024]{1,0:T(8,128)(2,1)} %refs_3_.3) | copy-start | bytes 1572868
  5.8 0.6 copy-start.11
  6.4 0.7 copy-start.13
  7.1 16.8 %collective-permute-start = (bf16[128,512]{1,0:T(8,128)(2,1)S(1)}, bf16[128,512]{1,0:T(8,128)(2,1)S(1)}, u32[]{:S(2)}, u32[]{:S(2)}) collective-permute-start(bf16[128,512]{1,0:T(8,128)(2,1)S(1)} %get-tuple-element.33), channel_id=1, source_target_pairs={{0,0},{4,32},{8,8},{12,40},{16,16},{20,48},{24,24},{28,56},{32,4},... | collective-permute-start | bytes 393224 | tf_op jit(solution)/shard_map/ppermute | solution.py:408
  13.1 10.8 %collective-permute-start.1 = (bf16[128,512]{1,0:T(8,128)(2,1)S(1)}, bf16[128,512]{1,0:T(8,128)(2,1)S(1)}, u32[]{:S(2)}, u32[]{:S(2)}) collective-permute-start(bf16[128,512]{1,0:T(8,128)(2,1)S(1)} %get-tuple-element.34), channel_id=1, source_target_pairs={{0,8},{4,40},{8,16},{12,48},{16,24},{20,56},{24,0},{28,32},{32,12}... | collective-permute-start | bytes 393224 | tf_op jit(solution)/shard_map/ppermute | solution.py:408
  14.2 9.7 %collective-permute-start.2 = (bf16[128,512]{1,0:T(8,128)(2,1)S(1)}, bf16[128,512]{1,0:T(8,128)(2,1)S(1)}, u32[]{:S(2)}, u32[]{:S(2)}) collective-permute-start(bf16[128,512]{1,0:T(8,128)(2,1)S(1)} %get-tuple-element.35), channel_id=1, source_target_pairs={{0,16},{4,48},{8,24},{12,56},{16,0},{20,32},{24,8},{28,40},{32,20}... | collective-permute-start | bytes 393224 | tf_op jit(solution)/shard_map/ppermute | solution.py:408
  19.8 6.8 %collective-permute-start.3 = (bf16[128,512]{1,0:T(8,128)(2,1)S(1)}, bf16[128,512]{1,0:T(8,128)(2,1)S(1)}, u32[]{:S(2)}, u32[]{:S(2)}) collective-permute-start(bf16[128,512]{1,0:T(8,128)(2,1)S(1)} %get-tuple-element.36), channel_id=1, source_target_pairs={{0,24},{4,56},{8,0},{12,32},{16,8},{20,40},{24,16},{28,48},{32,28}... | collective-permute-start | bytes 393224 | tf_op jit(solution)/shard_map/ppermute | solution.py:408
  23.9 35.8 %copy-start.1 = (bf16[256,512]{1,0:T(8,128)(2,1)}, bf16[256,512]{1,0:T(8,128)(2,1)S(1)}, u32[]{:S(2)}) copy-start(bf16[256,512]{1,0:T(8,128)(2,1)S(1)} %get-tuple-element.32.refs_5_.refs_1_) | copy-start | bytes 786436
  27.2 8.7 %collective-permute-start.5 = (bf16[512,384]{1,0:T(8,128)(2,1)S(1)}, bf16[512,384]{1,0:T(8,128)(2,1)}, u32[]{:S(2)}, u32[]{:S(2)}) collective-permute-start(bf16[512,384]{1,0:T(8,128)(2,1)S(1)} %bitcast.7), channel_id=1, source_target_pairs={{0,1},{1,2},{2,3},{3,0},{32,35},{33,32},{34,33},{35,34},{4,5},{5,6... | collective-permute-start | bytes 1179656 | tf_op jit(solution)/shard_map/ppermute | solution.py:421
  31.0 7.9 %collective-permute-start.7 = (bf16[512,384]{1,0:T(8,128)(2,1)S(1)}, bf16[512,384]{1,0:T(8,128)(2,1)}, u32[]{:S(2)}, u32[]{:S(2)}) collective-permute-start(bf16[512,384]{1,0:T(8,128)(2,1)S(1)} %bitcast.8), channel_id=1, source_target_pairs={{0,3},{1,0},{2,1},{3,2},{32,33},{33,34},{34,35},{35,32},{4,7},{5,4... | collective-permute-start | bytes 1179656 | tf_op jit(solution)/shard_map/ppermute | solution.py:421
  31.0 15.9 %all-to-all-start = ((bf16[16,128,128]{2,1,0:T(8,128)(2,1)}), bf16[16,128,128]{2,1,0:T(8,128)(2,1)S(1)}, u32[]{:S(2)}, u32[]{:S(2)}) async-start(bf16[16,128,128]{2,1,0:T(8,128)(2,1)} %get-tuple-element.39), calls=%async_computation | async-start | bytes 1048576 | tf_op jit(solution)/shard_map/all_to_all | solution.py:461
  34.7 4.8 %collective-permute-start.4 = (bf16[512,384]{1,0:T(8,128)(2,1)S(1)}, bf16[512,384]{1,0:T(8,128)(2,1)S(1)}, u32[]{:S(2)}, u32[]{:S(2)}) collective-permute-start(bf16[512,384]{1,0:T(8,128)(2,1)S(1)} %bitcast.9), channel_id=1, source_target_pairs={{0,32},{32,0},{1,33},{33,1},{2,34},{34,2},{3,35},{35,3},{4,36},{36... | collective-permute-start | bytes 1179656 | tf_op jit(solution)/shard_map/ppermute | solution.py:412
  35.9 3.6 %collective-permute-start.6 = (bf16[512,384]{1,0:T(8,128)(2,1)}, bf16[512,384]{1,0:T(8,128)(2,1)S(1)}, u32[]{:S(2)}, u32[]{:S(2)}) collective-permute-start(bf16[512,384]{1,0:T(8,128)(2,1)} %collective-permute-done.5.refs_3_.refs_4_), channel_id=1, source_target_pairs={{0,32},{32,0},{1,33},{33,1},{2,34},{34,2},{3,35},{35,3},{4,36},{36... | collective-permute-start | bytes 1179656 | tf_op jit(solution)/shard_map/ppermute | solution.py:412
  39.0 1.9 %collective-permute-start.8 = (bf16[512,384]{1,0:T(8,128)(2,1)}, bf16[512,384]{1,0:T(8,128)(2,1)S(1)}, u32[]{:S(2)}, u32[]{:S(2)}) collective-permute-start(bf16[512,384]{1,0:T(8,128)(2,1)} %collective-permute-done.7.refs_5_.refs_6_), channel_id=1, source_target_pairs={{0,32},{32,0},{1,33},{33,1},{2,34},{34,2},{3,35},{35,3},{4,36},{36... | collective-permute-start | bytes 1179656 | tf_op jit(solution)/shard_map/ppermute | solution.py:412
  39.0 20.8 %collective-permute-start.10 = (bf16[512,384]{1,0:T(8,128)(2,1)}, bf16[512,384]{1,0:T(8,128)(2,1)S(1)}, u32[]{:S(2)}, u32[]{:S(2)}) collective-permute-start(bf16[512,384]{1,0:T(8,128)(2,1)} %collective-permute-done.5.refs_3_.refs_4_), channel_id=1, source_target_pairs={{0,33},{1,34},{2,35},{3,32},{32,3},{33,0},{34,1},{35,2},{4,37},{5,... | collective-permute-start | bytes 1179656 | tf_op jit(solution)/shard_map/ppermute | solution.py:421
  39.4 20.4 %collective-permute-start.9 = (bf16[512,384]{1,0:T(8,128)(2,1)}, bf16[512,384]{1,0:T(8,128)(2,1)S(1)}, u32[]{:S(2)}, u32[]{:S(2)}) collective-permute-start(bf16[512,384]{1,0:T(8,128)(2,1)} %collective-permute-done.5.refs_3_.refs_4_), channel_id=1, source_target_pairs={{0,1},{1,2},{2,3},{3,0},{32,35},{33,32},{34,33},{35,34},{4,5},{5,6... | collective-permute-start | bytes 1179656 | tf_op jit(solution)/shard_map/ppermute | solution.py:421
  44.6 0.7 copy-start.2
  45.3 0.8 copy-start.5
  46.1 0.7 copy-start.8
  46.9 1.0 copy-start.3
  47.9 1.0 copy-start.6
  48.9 1.0 copy-start.9
  59.7 14.7 %copy-start.4 = (bf16[512,384]{1,0:T(8,128)(2,1)S(1)}, bf16[512,384]{1,0:T(8,128)(2,1)}, u32[]{:S(2)}) copy-start(bf16[512,384]{1,0:T(8,128)(2,1)} %copy-done.2) | copy-start | bytes 1179652
  59.8 14.7 %copy-start.7 = (bf16[512,384]{1,0:T(8,128)(2,1)S(1)}, bf16[512,384]{1,0:T(8,128)(2,1)}, u32[]{:S(2)}) copy-start(bf16[512,384]{1,0:T(8,128)(2,1)} %copy-done.5) | copy-start | bytes 1179652
  59.8 14.7 %copy-start.10 = (bf16[512,384]{1,0:T(8,128)(2,1)S(1)}, bf16[512,384]{1,0:T(8,128)(2,1)}, u32[]{:S(2)}) copy-start(bf16[512,384]{1,0:T(8,128)(2,1)} %copy-done.8) | copy-start | bytes 1179652
  61.6 7.5 %collective-permute-start.11 = (f32[8,512]{1,0:T(8,128)S(1)}, f32[8,512]{1,0:T(8,128)S(1)}, u32[]{:S(2)}, u32[]{:S(2)}) collective-permute-start(f32[8,512]{1,0:T(8,128)S(1)} %get-tuple-element.41.refs_4_.refs_6_), channel_id=1, source_target_pairs={{0,8},{8,16},{16,24},{24,0},{1,9},{9,17},{17,25},{25,1},{2,10},{10... | collective-permute-start | bytes 49160 | tf_op jit(solution)/shard_map/ppermute | solution.py:399
  61.7 7.4 %collective-permute-start.12 = (f32[8,512]{1,0:T(8,128)S(1)}, f32[8,512]{1,0:T(8,128)S(1)}, u32[]{:S(2)}, u32[]{:S(2)}) collective-permute-start(f32[8,512]{1,0:T(8,128)S(1)} %get-tuple-element.41.refs_4_.refs_6_), channel_id=1, source_target_pairs={{0,16},{8,24},{16,0},{24,8},{1,17},{9,25},{17,1},{25,9},{2,18},{10... | collective-permute-start | bytes 49160 | tf_op jit(solution)/shard_map/ppermute | solution.py:399
  65.1 4.0 %collective-permute-start.13 = (f32[8,512]{1,0:T(8,128)S(1)}, f32[8,512]{1,0:T(8,128)S(1)}, u32[]{:S(2)}, u32[]{:S(2)}) collective-permute-start(f32[8,512]{1,0:T(8,128)S(1)} %get-tuple-element.41.refs_4_.refs_6_), channel_id=1, source_target_pairs={{0,24},{8,0},{16,8},{24,16},{1,25},{9,1},{17,9},{25,17},{2,26},{10... | collective-permute-start | bytes 49160 | tf_op jit(solution)/shard_map/ppermute | solution.py:399
  70.1 10.6 %collective-permute-start.15 = (bf16[512,128]{1,0:T(8,128)(2,1)S(1)}, bf16[512,128]{1,0:T(8,128)(2,1)S(1)}, u32[]{:S(2)}, u32[]{:S(2)}) collective-permute-start(bf16[512,128]{1,0:T(8,128)(2,1)S(1)} %get-tuple-element.42.refs_1_.refs_7_), channel_id=1, source_target_pairs={{0,1},{1,2},{2,3},{3,0},{32,35},{33,32},{34,33},{35,34},{4,5},{5,6... | collective-permute-start | bytes 393224 | tf_op jit(solution)/shard_map/ppermute | solution.py:421
  72.0 8.8 %collective-permute-start.16 = (bf16[512,128]{1,0:T(8,128)(2,1)S(1)}, bf16[512,128]{1,0:T(8,128)(2,1)S(1)}, u32[]{:S(2)}, u32[]{:S(2)}) collective-permute-start(bf16[512,128]{1,0:T(8,128)(2,1)S(1)} %get-tuple-element.42.refs_1_.refs_7_), channel_id=1, source_target_pairs={{0,3},{1,0},{2,1},{3,2},{32,33},{33,34},{34,35},{35,32},{4,7},{5,4... | collective-permute-start | bytes 393224 | tf_op jit(solution)/shard_map/ppermute | solution.py:421
  72.0 12.3 %collective-permute-start.14 = (bf16[512,128]{1,0:T(8,128)(2,1)S(1)}, bf16[512,128]{1,0:T(8,128)(2,1)S(1)}, u32[]{:S(2)}, u32[]{:S(2)}) collective-permute-start(bf16[512,128]{1,0:T(8,128)(2,1)S(1)} %get-tuple-element.42.refs_1_.refs_7_), channel_id=1, source_target_pairs={{0,32},{32,0},{1,33},{33,1},{2,34},{34,2},{3,35},{35,3},{4,36},{36... | collective-permute-start | bytes 393224 | tf_op jit(solution)/shard_map/ppermute | solution.py:412
  80.7 3.5 %collective-permute-start.17 = (bf16[512,128]{1,0:T(8,128)(2,1)S(1)}, bf16[512,128]{1,0:T(8,128)(2,1)S(1)}, u32[]{:S(2)}, u32[]{:S(2)}) collective-permute-start(bf16[512,128]{1,0:T(8,128)(2,1)S(1)} %get-tuple-element.43.refs_9_), channel_id=1, source_target_pairs={{0,32},{32,0},{1,33},{33,1},{2,34},{34,2},{3,35},{35,3},{4,36},{36... | collective-permute-start | bytes 393224 | tf_op jit(solution)/shard_map/ppermute | solution.py:412
  80.8 3.4 %collective-permute-start.18 = (bf16[512,128]{1,0:T(8,128)(2,1)S(1)}, bf16[512,128]{1,0:T(8,128)(2,1)S(1)}, u32[]{:S(2)}, u32[]{:S(2)}) collective-permute-start(bf16[512,128]{1,0:T(8,128)(2,1)S(1)} %get-tuple-element.44.refs_11_), channel_id=1, source_target_pairs={{0,32},{32,0},{1,33},{33,1},{2,34},{34,2},{3,35},{35,3},{4,36},{36... | collective-permute-start | bytes 393224 | tf_op jit(solution)/shard_map/ppermute | solution.py:412
  81.3 8.9 %collective-permute-start.19 = (bf16[512,128]{1,0:T(8,128)(2,1)S(1)}, bf16[512,128]{1,0:T(8,128)(2,1)S(1)}, u32[]{:S(2)}, u32[]{:S(2)}) collective-permute-start(bf16[512,128]{1,0:T(8,128)(2,1)S(1)} %get-tuple-element.43.refs_9_), channel_id=1, source_target_pairs={{0,1},{1,2},{2,3},{3,0},{32,35},{33,32},{34,33},{35,34},{4,5},{5,6... | collective-permute-start | bytes 393224 | tf_op jit(solution)/shard_map/ppermute | solution.py:421
  82.8 7.5 %collective-permute-start.20 = (bf16[512,128]{1,0:T(8,128)(2,1)S(1)}, bf16[512,128]{1,0:T(8,128)(2,1)S(1)}, u32[]{:S(2)}, u32[]{:S(2)}) collective-permute-start(bf16[512,128]{1,0:T(8,128)(2,1)S(1)} %get-tuple-element.43.refs_9_), channel_id=1, source_target_pairs={{0,33},{1,34},{2,35},{3,32},{32,3},{33,0},{34,1},{35,2},{4,37},{5,... | collective-permute-start | bytes 393224 | tf_op jit(solution)/shard_map/ppermute | solution.py:421
  90.3 19.9 %all-to-all-start.1 = ((bf16[16,128,128]{2,1,0:T(8,128)(2,1)}), bf16[16,128,128]{2,1,0:T(8,128)(2,1)S(1)}, u32[]{:S(2)}, u32[]{:S(2)}) async-start(bf16[16,128,128]{2,1,0:T(8,128)(2,1)} %relay.3), calls=%async_computation.1 | async-start | bytes 1048576 | tf_op jit(solution)/shard_map/all_to_all | solution.py:508
  97.5 17.6 %copy-start.12 = (bf16[128,512]{1,0:T(8,128)(2,1)S(1)}, bf16[128,512]{1,0:T(8,128)(2,1)}, u32[]{:S(2)}) copy-start(bf16[128,512]{1,0:T(8,128)(2,1)} %copy-done.11) | copy-start | bytes 393220
  97.5 17.6 %copy-start.14 = (bf16[128,512]{1,0:T(8,128)(2,1)S(1)}, bf16[128,512]{1,0:T(8,128)(2,1)}, u32[]{:S(2)}) copy-start(bf16[128,512]{1,0:T(8,128)(2,1)} %copy-done.13) | copy-start | bytes 393220
  97.5 16.5 %collective-permute-start.21 = (bf16[128,512]{1,0:T(8,128)(2,1)S(1)}, bf16[128,512]{1,0:T(8,128)(2,1)S(1)}, u32[]{:S(2)}, u32[]{:S(2)}) collective-permute-start(bf16[128,512]{1,0:T(8,128)(2,1)S(1)} %get-tuple-element.46.refs_8_), channel_id=1, source_target_pairs={{0,0},{4,32},{8,8},{12,40},{16,16},{20,48},{24,24},{28,56},{32,4},... | collective-permute-start | bytes 393224 | tf_op jit(solution)/shard_map/ppermute | solution.py:408
  101.8 12.2 %collective-permute-start.22 = (bf16[128,512]{1,0:T(8,128)(2,1)}, bf16[128,512]{1,0:T(8,128)(2,1)S(1)}, u32[]{:S(2)}, u32[]{:S(2)}) collective-permute-start(bf16[128,512]{1,0:T(8,128)(2,1)} %get-tuple-element.53), channel_id=1, source_target_pairs={{0,8},{4,40},{8,16},{12,48},{16,24},{20,56},{24,0},{28,32},{32,12}... | collective-permute-start | bytes 393224 | tf_op jit(solution)/shard_map/ppermute | solution.py:408
  103.9 10.0 %collective-permute-start.23 = (bf16[128,512]{1,0:T(8,128)(2,1)}, bf16[128,512]{1,0:T(8,128)(2,1)S(1)}, u32[]{:S(2)}, u32[]{:S(2)}) collective-permute-start(bf16[128,512]{1,0:T(8,128)(2,1)} %get-tuple-element.54), channel_id=1, source_target_pairs={{0,16},{4,48},{8,24},{12,56},{16,0},{20,32},{24,8},{28,40},{32,20}... | collective-permute-start | bytes 393224 | tf_op jit(solution)/shard_map/ppermute | solution.py:408
  108.1 7.0 %collective-permute-start.24 = (bf16[128,512]{1,0:T(8,128)(2,1)}, bf16[128,512]{1,0:T(8,128)(2,1)S(1)}, u32[]{:S(2)}, u32[]{:S(2)}) collective-permute-start(bf16[128,512]{1,0:T(8,128)(2,1)} %get-tuple-element.55), channel_id=1, source_target_pairs={{0,24},{4,56},{8,0},{12,32},{16,8},{20,40},{24,16},{28,48},{32,28}... | collective-permute-start | bytes 393224 | tf_op jit(solution)/shard_map/ppermute | solution.py:408

commit v5 on v4

--- a/solution.py
+++ b/solution.py
@@ -182,20 +182,23 @@
 
 def corner_masks(info, backward):
     order = order_of(info)
-    first = lax.broadcasted_iota(jnp.int32, (128, 128), 0)
-    second = lax.broadcasted_iota(jnp.int32, (128, 128), 1)
+    first = lax.broadcasted_iota(jnp.int32, (256, 256), 0)
+    second = lax.broadcasted_iota(jnp.int32, (256, 256), 1)
+    early, late = (first, second) if backward else (second, first)
+    below = (early >> 7) < (late >> 7)
+    gap = jnp.where((early >> 7) == (late >> 7), early - late, 512)
+    gap = jnp.where(below, -512, gap)
     masks = []
     for o in order:
         ahead = o > order[0] if backward else o < order[0]
         lead = jnp.where(ahead, 128, jnp.where(o == order[0], 0, -128))
-        keep = first <= second + lead if backward else second <= first + lead
-        masks.append(keep.astype(F32).astype(BF))
+        masks.append((gap <= lead).astype(F32).astype(BF))
     return masks
 
 
 def cand_attend(count, begin, end, *refs):
     q_ref, kvs, rest = refs[0], refs[1 : 1 + count], refs[1 + count :]
-    q = q_ref[...].reshape(4 * CAP, HS)
+    q = q_ref[...].reshape(8 * CAP, HS)
     total = None if begin else rest[0][...]
     for block in kvs:
         half = dot(q, block[:, :HS], NT).astype(BF)
@@ -203,22 +206,22 @@
         more = dot(probs, block[:, HS : 2 * HS])
         total = more if total is None else total + more
     if end:
-        rest[-1][...] = total.astype(BF).reshape(4, CAP, HS)
+        rest[-1][...] = total.astype(BF).reshape(8, CAP, HS)
     else:
         rest[-1][...] = total
 
 
 def attend_rows(q_ref, blocks, masks, old_ref, att_ref):
-    for y in range(4):
-        rows = slice(y * 128, (y + 1) * 128)
+    for y in range(2):
+        rows = slice(y * 256, (y + 1) * 256)
         q = q_ref[rows, 2 * HS :]
         total = None if old_ref is None else old_ref[rows, :]
         for block, mask in zip(blocks, masks):
-            half = dot(q, block[: 128 * (y + 1), :HS], NT).astype(BF)
+            half = dot(q, block[: 256 * (y + 1), :HS], NT).astype(BF)
             probs = half + half * jnp.tanh(half)
-            last = probs[:, 128 * y :] * mask
-            probs = last if y == 0 else jnp.concatenate([probs[:, : 128 * y], last], axis=1)
-            more = dot(probs, block[: 128 * (y + 1), HS : 2 * HS])
+            last = probs[:, 256 * y :] * mask
+            probs = last if y == 0 else jnp.concatenate([probs[:, : 256 * y], last], axis=1)
+            more = dot(probs, block[: 256 * (y + 1), HS : 2 * HS])
             total = more if total is None else total + more
         att_ref[rows, :] = total
 
@@ -278,34 +281,34 @@
 def hist_dq(info, ga_ref, *refs):
     blocks, dq_ref = refs[:8], refs[8]
     masks = corner_masks(info, False)
-    for y in range(4):
-        q = blocks[0][y * 128 : (y + 1) * 128, 2 * HS :]
-        ga = ga_ref[y * 128 : (y + 1) * 128, :]
+    for y in range(2):
+        q = blocks[0][y * 256 : (y + 1) * 256, 2 * HS :]
+        ga = ga_ref[y * 256 : (y + 1) * 256, :]
         total = None
         for block, mask in zip(blocks, masks):
-            key = block[: 128 * (y + 1), :HS]
+            key = block[: 256 * (y + 1), :HS]
             half = dot(q, key, NT).astype(BF)
-            _, ds = slope_times(half, dot(ga, block[: 128 * (y + 1), HS : 2 * HS], NT).astype(BF))
-            last = ds[:, 128 * y :] * mask
-            ds = last if y == 0 else jnp.concatenate([ds[:, : 128 * y], last], axis=1)
+            _, ds = slope_times(half, dot(ga, block[: 256 * (y + 1), HS : 2 * HS], NT).astype(BF))
+            last = ds[:, 256 * y :] * mask
+            ds = last if y == 0 else jnp.concatenate([ds[:, : 256 * y], last], axis=1)
             more = dot(ds, key)
             total = more if total is None else total + more
-        dq_ref[y] = (total * (0.5 * SCALE)).astype(BF)
+        dq_ref[2 * y : 2 * y + 2] = (total * (0.5 * SCALE)).astype(BF).reshape(2, 128, HS)
 
 
 def key_grads(own_ref, blocks, gas, masks, y, dk, dv):
-    key = own_ref[y * 128 : (y + 1) * 128, :HS]
-    value = own_ref[y * 128 : (y + 1) * 128, HS : 2 * HS]
+    key = own_ref[y * 256 : (y + 1) * 256, :HS]
+    value = own_ref[y * 256 : (y + 1) * 256, HS : 2 * HS]
     for block, ga_block, mask in zip(blocks, gas, masks):
-        q = block[128 * y :, 2 * HS :]
-        ga = ga_block[128 * y :, :]
+        q = block[256 * y :, 2 * HS :]
+        ga = ga_block[256 * y :, :]
         half = dot(key, q, NT).astype(BF)
         probs, ds = slope_times(half, dot(value, ga, NT).astype(BF))
-        p_first = probs[:, :128] * mask
-        d_first = ds[:, :128] * mask
-        if y < 3:
-            probs = jnp.concatenate([p_first, probs[:, 128:]], axis=1)
-            ds = jnp.concatenate([d_first, ds[:, 128:]], axis=1)
+        p_first = probs[:, :256] * mask
+        d_first = ds[:, :256] * mask
+        if y < 1:
+            probs = jnp.concatenate([p_first, probs[:, 256:]], axis=1)
+            ds = jnp.concatenate([d_first, ds[:, 256:]], axis=1)
         else:
             probs, ds = p_first, d_first
         more_k = dot(ds, q)
@@ -317,7 +320,7 @@
 
 def hist_dkv_begin(info, *refs):
     masks = corner_masks(info, True)[:6]
-    for y in range(4):
+    for y in range(2):
         dk, dv = key_grads(refs[0], refs[:6], refs[6:12], masks, y, None, None)
         refs[12][y, :, :HS] = dk
         refs[12][y, :, HS:] = dv
@@ -325,11 +328,12 @@
 
 def hist_dkv_end(info, dq_ref, normed_ref, own_ref, b0, b1, g0, g1, old_ref, k0, k1, k2, k3, all_ref):
     masks = corner_masks(info, True)[6:]
+    for y in range(2):
+        dk, dv = key_grads(own_ref, (b0, b1), (g0, g1), masks, y, old_ref[y, :, :HS], old_ref[y, :, HS:])
+        all_ref[2 * y : 2 * y + 2, :, HS : 2 * HS] = dk.astype(BF).reshape(2, 128, HS)
+        all_ref[2 * y : 2 * y + 2, :, 2 * HS : 3 * HS] = dv.astype(BF).reshape(2, 128, HS)
     for y in range(4):
-        dk, dv = key_grads(own_ref, (b0, b1), (g0, g1), masks, y, old_ref[y, :, :HS], old_ref[y, :, HS:])
         all_ref[y, :, :HS] = dq_ref[y]
-        all_ref[y, :, HS : 2 * HS] = dk.astype(BF)
-        all_ref[y, :, 2 * HS : 3 * HS] = dv.astype(BF)
         all_ref[y, :, 3 * HS :] = normed_ref[y * 128 : (y + 1) * 128, :]
     for k, out in enumerate((k0, k1, k2, k3)):
         out[...] = all_ref[(info[2] + k) & 3]
@@ -437,7 +441,8 @@
 
     *sent, slope, gate, gm = call(
         project_all, "project_all", (1,), [SMEM, far, far, far, far],
-        [shaped((128, 512))] * 4 + [shaped((4, 128, 512))] + [shaped((128, 512))] * 2, [held] * 7,
+        [shaped((128, 512))] * 4 + [shaped((4, 128, 512))] + [pltpu.HBM((128, 512), BF)] * 2,
+        [held] * 5 + [pl.BlockSpec((128, 512), lambda i: (0, 0))] * 2,
         [
             pltpu.VMEM((128, 1024), BF), pltpu.VMEM((128, 512), BF), pltpu.VMEM((128, 1024), BF),
             pltpu.VMEM((128, 1024), BF), pltpu.VMEM((512, 1024), BF), pltpu.SemaphoreType.DMA((3,)),
@@ -462,13 +467,13 @@
     last = [along(plus, 1, 0), along(plus, 1, 1)]
     kvq = [own, own_pair, plus, across(plus), minus, across(minus)]
 
-    q_spec = pl.BlockSpec((4, 128, 128), lambda i: (i, 0, 0))
-    acc_spec = pl.BlockSpec((512, 128), lambda i: (i, 0))
+    q_spec = pl.BlockSpec((8, 128, 128), lambda i: (i, 0, 0))
+    acc_spec = pl.BlockSpec((1024, 128), lambda i: (i, 0))
 
     def cand_part(kvs, total, end, after):
         begin = total is None
         return call(
-            functools.partial(cand_attend, len(kvs), begin, end), "cand_attend", (4,),
+            functools.partial(cand_attend, len(kvs), begin, end), "cand_attend", (2,),
             [q_spec] + [held] * len(kvs) + ([] if begin else [acc_spec]),
             shaped((16, 128, 128)) if end else shaped((2048, 128), F32),
             q_spec if end else acc_spec, [], 600_000_000 * len(kvs), after,
@@ -502,7 +507,7 @@
     gas = [ga, across(ga), ga_plus, across(ga_plus), ga_minus, across(ga_minus)]
     key_sums = call(
         hist_dkv_begin, "hist_dkv_begin", (1,), [SMEM] + [held] * 12,
-        shaped((4, 128, 256), F32), held, [], 2_000_000_000,
+        shaped((2, 256, 256), F32), held, [], 2_000_000_000,
     )(info, *kvq, *gas)
     (leaving,) = relayed([weighed], (key_sums, *ga_last))
     returned = lax.all_to_all(leaving, ("xl", "xh", "y"), 0, 0, tiled=True)

time: 119 us -> 114 us (0.958)
  Pallas kernels: 50.7 us -> 46.2 us
  local copies, waits for them, and re-layouts: 6.79 us -> 5.52 us
    pallas_call x15, Pallas kernels: 50.7 us -> 46.2 us  [run(): got = made(*pinned, *after, *carry)]
    unnamed x33 -> x29, local copies, waits for them, and re-layouts: 6.7 us -> 5.43 us
  transfers between devices with their start and end apart: 27 -> 27, of which waited for: 4 -> 4; matrix products, arithmetic and copies ran while one was open for 0% -> 0% of each run, Pallas kernels for 34% -> 31%
where the time goes in v5:
time: 114 us; the launch traced here: 113 us
  starting transfers between devices  51.4 us (45%)
  Pallas kernels  46.2 us (41%)
  waiting for transfers between devices  8.21 us (7%)
  local copies, waits for them, and re-layouts  5.52 us (5%)
  between operations  1.85 us (2%)
    pallas_call x15, Pallas kernels, run(): got = made(*pinned, *after, *carry)  46.2 us
    ppermute x8, starting transfers between devices, crossed(): return lax.ppermute(value, ('c', 'y', 'xh'), pairs)  26.2 us
    ppermute x8, starting transfers between devices, along(): return lax.ppermute(value, ('c', 'z'), pairs)  9.71 us
    unnamed x29, local copies, waits for them, and re-layouts  5.43 us
    ppermute x6, starting transfers between devices, across(): return lax.ppermute(value, 'c', [(0, 1), (1, 0)])  4.29 us
    all_to_all x1, starting transfers between devices, per_device(): returned = lax.all_to_all(leaving, ('xl', 'xh', 'y'), 0, 0, tiled=True)  4.02 us
    ppermute x8, waiting for transfers between devices, crossed(): return lax.ppermute(value, ('c', 'y', 'xh'), pairs)  3.76 us
    all_to_all x1, starting transfers between devices, per_device(): arrived = lax.all_to_all(sent_cand, ('xl', 'xh', 'y'), 0, 0, tiled=True)  3.69 us
  transfers between devices with their start and end apart: 27, of which 4 were waited for; matrix products, arithmetic and copies ran while one was open for 0% of the time, Pallas kernels for 31%

profile of v5, /device:TPU:1, one launch (start us, length us, event | category | flops | bytes accessed | tf_op | source)
XLA Modules:
  0.0 113.2 jit_solution(14944543626141157347)
XLA Ops:
  1.4 0.1 stack.19.refs_0_
  1.4 5.0 %project_all.1 = (bf16[128,512]{1,0:T(8,128)(2,1)S(1)}, bf16[128,512]{1,0:T(8,128)(2,1)S(1)}, bf16[128,512]{1,0:T(8,128)(2,1)S(1)}, bf16[128,512]{1,0:T(8,128)(2...) custom-call(s32[5]{0:T(128)S(1)} %stack.19.refs_0_, ...), custom_call_target="tpu_custom_call" | custom-call | flops 700000000 | bytes 1048576 | tf_op jit(solution)/shard_map/project_all/pallas_call | solution.py:63
  6.4 6.0 %collective-permute-start = (bf16[128,512]{1,0:T(8,128)(2,1)S(1)}, bf16[128,512]{1,0:T(8,128)(2,1)S(1)}, u32[]{:S(2)}, u32[]{:S(2)}) collective-permute-start(bf16[128,512]{1,0:T(8,128)(2,1)S(1)} %get-tuple-element.33), channel_id=1, source_target_pairs={{0,0},{4,32},{8,8},{12,40},{16,16},{20,48},{24,24},{28,56},{32,4},... | collective-permute-start | bytes 393224 | tf_op jit(solution)/shard_map/ppermute | solution.py:412
  12.5 1.1 collective-permute-start.1
  13.6 5.6 %collective-permute-start.2 = (bf16[128,512]{1,0:T(8,128)(2,1)S(1)}, bf16[128,512]{1,0:T(8,128)(2,1)S(1)}, u32[]{:S(2)}, u32[]{:S(2)}) collective-permute-start(bf16[128,512]{1,0:T(8,128)(2,1)S(1)} %get-tuple-element.35), channel_id=1, source_target_pairs={{0,16},{4,48},{8,24},{12,56},{16,0},{20,32},{24,8},{28,40},{32,20}... | collective-permute-start | bytes 393224 | tf_op jit(solution)/shard_map/ppermute | solution.py:412
  19.1 0.8 collective-permute-start.3
  20.0 0.1 copy.15.refs_0_
  20.1 3.1 %project_cand.1 = (bf16[16,128,128]{2,1,0:T(8,128)(2,1)}, bf16[256,512]{1,0:T(8,128)(2,1)S(1)}) custom-call(s32[256,1]{1,0:T(8,128)S(1)} %copy.15.refs_0_, bf16[256,1024]{1,0:T(8,128)(2,1)S(1)} %copy-done, bf16[1024,2048]{1,0:T(8,128)(2,1)} %refs_5_.1, bf16[4,128,512]{2,1,0:T(8,128)(2,1)S(1)} %get-tuple-element.31.refs_3_), custom_call_target="tpu_custom_call" | custom-call | flops 700000000 | bytes 1048576 | tf_op jit(solution)/shard_map/project_cand/pallas_call | solution.py:63
  23.3 2.6 %collective-permute-done.3.refs_4_ = bf16[128,512]{1,0:T(8,128)(2,1)S(1)} collective-permute-done((bf16[128,512]{1,0:T(8,128)(2,1)S(1)}, bf16[128,512]{1,0:T(8,128)(2,1)S(1)}, u32[]{:S(2)}, u32[]{:S(2)}) %collective-permute-start.3) | collective-permute-done | bytes 131104 | tf_op jit(solution)/shard_map/ppermute | solution.py:412
  25.9 0.6 arrange.1
  26.5 3.8 %collective-permute-start.5 = (bf16[512,384]{1,0:T(8,128)(2,1)S(1)}, bf16[512,384]{1,0:T(8,128)(2,1)}, u32[]{:S(2)}, u32[]{:S(2)}) collective-permute-start(bf16[512,384]{1,0:T(8,128)(2,1)S(1)} %bitcast.7), channel_id=1, source_target_pairs={{0,1},{1,2},{2,3},{3,0},{32,35},{33,32},{34,33},{35,34},{4,5},{5,6... | collective-permute-start | bytes 1179656 | tf_op jit(solution)/shard_map/ppermute | solution.py:425
  30.4 3.7 %all-to-all-start = ((bf16[16,128,128]{2,1,0:T(8,128)(2,1)}), bf16[16,128,128]{2,1,0:T(8,128)(2,1)S(1)}, u32[]{:S(2)}, u32[]{:S(2)}) async-start(bf16[16,128,128]{2,1,0:T(8,128)(2,1)} %get-tuple-element.39), calls=%async_computation | async-start | bytes 1048576 | tf_op jit(solution)/shard_map/all_to_all | solution.py:466
  34.1 1.1 %collective-permute-start.4 = (bf16[512,384]{1,0:T(8,128)(2,1)S(1)}, bf16[512,384]{1,0:T(8,128)(2,1)S(1)}, u32[]{:S(2)}, u32[]{:S(2)}) collective-permute-start(bf16[512,384]{1,0:T(8,128)(2,1)S(1)} %bitcast.9), channel_id=1, source_target_pairs={{0,32},{32,0},{1,33},{33,1},{2,34},{34,2},{3,35},{35,3},{4,36},{36... | collective-permute-start | bytes 1179656 | tf_op jit(solution)/shard_map/ppermute | solution.py:416
  35.2 0.1 collective-permute-start.6
  35.3 3.0 %collective-permute-done.7.refs_5_.refs_6_ = bf16[512,384]{1,0:T(8,128)(2,1)} collective-permute-done((bf16[512,384]{1,0:T(8,128)(2,1)S(1)}, bf16[512,384]{1,0:T(8,128)(2,1)}, u32[]{:S(2)}, u32[]{:S(2)}) %collective-permute-start.7) | collective-permute-done | bytes 393248 | tf_op jit(solution)/shard_map/ppermute | solution.py:425
  38.3 0.4 collective-permute-start.10
  38.7 0.1 collective-permute-start.9
  38.8 1.4 %collective-permute-done.8.refs_6_.refs_7_ = bf16[512,384]{1,0:T(8,128)(2,1)S(1)} collective-permute-done((bf16[512,384]{1,0:T(8,128)(2,1)}, bf16[512,384]{1,0:T(8,128)(2,1)S(1)}, u32[]{:S(2)}, u32[]{:S(2)}) %collective-permute-start.8) | collective-permute-done | bytes 393248 | tf_op jit(solution)/shard_map/ppermute | solution.py:416
  40.2 3.1 %hist_begin.1.refs_7_.refs_8_ = f32[512,128]{1,0:T(8,128)S(1)} custom-call(s32[5]{0:T(128)S(1)} %stack.19.refs_0_, bf16[512,384]{1,0:T(8,128)(2,1)S(1)} %bitcast.10, bf16[512,384]{1,0:T(8,128)(2,1)S(1)} %collective-permute-done.4.refs_2_.refs_3_, bf16[512,384]{1,0:T(8,128)(2,1)} %collective-permute-done.5.refs_3_.refs_4_, ...), custom_call_target="tpu_custom_call" | custom-call | flops 1000 | bytes 1000 | tf_op jit(solution)/shard_map/hist_begin/pallas_call | solution.py:63
  43.3 0.7 copy-done.2
  44.1 0.8 copy-done.5
  44.8 0.7 copy-done.8
  45.6 1.0 copy-done.3
  46.6 1.0 copy-done.6
  47.6 1.0 copy-done.9
  48.6 9.3 %cand_attend.2.refs_9_.refs_3_ = f32[2048,128]{1,0:T(8,128)S(1)} custom-call(bf16[16,128,128]{2,1,0:T(8,128)(2,1)S(1)} %all-to-all-done.refs_0_, bf16[512,384]{1,0:T(8,128)(2,1)S(1)} %bitcast.11, bf16[512,384]{1,0:T(8,128)(2,1)S(1)} %copy-done.3, bf16[512,384]{1,0:T(8,128)(2,1)} %collective-permute-done.5.refs_3_.refs_4_, bf16[512,384]{1,0:T(8,128)(2,1)S(1)} %copy-done.6, ...), custom_call_target="tpu_custom_call" | custom-call | flops 3600000000 | bytes 1048576 | tf_op jit(solution)/shard_map/cand_attend/pallas_call | solution.py:63
  57.9 1.7 %hist_end.1 = (f32[512,128]{1,0:T(8,128)S(1)}, f32[8,512]{1,0:T(8,128)S(1)}) custom-call(s32[5]{0:T(128)S(1)} %stack.19.refs_0_, bf16[128,512]{1,0:T(8,128)(2,1)S(1)} %collective-permute-done.refs_1_, bf16[128,512]{1,0:T(8,128)(2,1)S(1)} %collective-permute-done.1.refs_2_, bf16[128,512]{1,0:T(8,128)(2,1)S(1)} %collective-permute-done.2.refs_3_, ...), custom_call_target="tpu_custom_call" | custom-call | flops 400000000 | bytes 1048576 | tf_op jit(solution)/shard_map/hist_end/pallas_call | solution.py:63
  59.6 0.0 collective-permute-start.11
  59.7 3.5 %collective-permute-start.12 = (f32[8,512]{1,0:T(8,128)S(1)}, f32[8,512]{1,0:T(8,128)S(1)}, u32[]{:S(2)}, u32[]{:S(2)}) collective-permute-start(f32[8,512]{1,0:T(8,128)S(1)} %get-tuple-element.41.refs_4_.refs_6_), channel_id=1, source_target_pairs={{0,16},{8,24},{16,0},{24,8},{1,17},{9,25},{17,1},{25,9},{2,18},{10... | collective-permute-start | bytes 49160 | tf_op jit(solution)/shard_map/ppermute | solution.py:403
  63.1 3.4 %cand_attend.3.refs_10_.refs_3_ = bf16[16,128,128]{2,1,0:T(8,128)(2,1)} custom-call(bf16[16,128,128]{2,1,0:T(8,128)(2,1)S(1)} %all-to-all-done.refs_0_, bf16[512,384]{1,0:T(8,128)(2,1)S(1)} %collective-permute-done.9.refs_6_.refs_1_.refs_8_.refs_4_, bf16[512,384]{1,0:T(8,128)(2,1)S(1)} %collective-permute-done.10.refs_7_.refs_2_.refs_9_.refs_5_, ...), custom_call_target="tpu_custom_call" | custom-call | flops 1200000000 | bytes 1048576 | tf_op jit(solution)/shard_map/cand_attend/pallas_call | solution.py:63
  66.6 1.0 normed_grads.1
  67.6 2.4 %collective-permute-start.15 = (bf16[512,128]{1,0:T(8,128)(2,1)S(1)}, bf16[512,128]{1,0:T(8,128)(2,1)S(1)}, u32[]{:S(2)}, u32[]{:S(2)}) collective-permute-start(bf16[512,128]{1,0:T(8,128)(2,1)S(1)} %get-tuple-element.42.refs_1_.refs_7_), channel_id=1, source_target_pairs={{0,1},{1,2},{2,3},{3,0},{32,35},{33,32},{34,33},{35,34},{4,5},{5,6... | collective-permute-start | bytes 393224 | tf_op jit(solution)/shard_map/ppermute | solution.py:425
  70.1 2.5 %collective-permute-start.14 = (bf16[512,128]{1,0:T(8,128)(2,1)S(1)}, bf16[512,128]{1,0:T(8,128)(2,1)S(1)}, u32[]{:S(2)}, u32[]{:S(2)}) collective-permute-start(bf16[512,128]{1,0:T(8,128)(2,1)S(1)} %get-tuple-element.42.refs_1_.refs_7_), channel_id=1, source_target_pairs={{0,32},{32,0},{1,33},{33,1},{2,34},{34,2},{3,35},{35,3},{4,36},{36... | collective-permute-start | bytes 393224 | tf_op jit(solution)/shard_map/ppermute | solution.py:416
  72.5 4.8 %hist_dq.1.refs_0_.refs_1_ = bf16[4,128,128]{2,1,0:T(8,128)(2,1)S(1)} custom-call(s32[5]{0:T(128)S(1)} %stack.19.refs_0_, bf16[512,128]{1,0:T(8,128)(2,1)S(1)} %get-tuple-element.42.refs_1_.refs_7_, bf16[512,384]{1,0:T(8,128)(2,1)S(1)} %bitcast.13, bf16[512,384]{1,0:T(8,128)(2,1)S(1)} %copy-done.4, bf16[512,384]{1,0:T(8,128)(2,1)} %collective-permute-done.5.refs_3_.refs_4_, ...), custom_call_target="tpu_custom_call" | custom-call | flops 2000000000 | bytes 1048576 | tf_op jit(solution)/shard_map/hist_dq/pallas_call | solution.py:63
  77.4 0.1 collective-permute-start.17
  77.5 0.5 collective-permute-start.18
  78.0 1.4 %collective-permute-start.19 = (bf16[512,128]{1,0:T(8,128)(2,1)S(1)}, bf16[512,128]{1,0:T(8,128)(2,1)S(1)}, u32[]{:S(2)}, u32[]{:S(2)}) collective-permute-start(bf16[512,128]{1,0:T(8,128)(2,1)S(1)} %get-tuple-element.43.refs_9_), channel_id=1, source_target_pairs={{0,1},{1,2},{2,3},{3,0},{32,35},{33,32},{34,33},{35,34},{4,5},{5,6... | collective-permute-start | bytes 393224 | tf_op jit(solution)/shard_map/ppermute | solution.py:425
  79.4 1.5 %collective-permute-start.20 = (bf16[512,128]{1,0:T(8,128)(2,1)S(1)}, bf16[512,128]{1,0:T(8,128)(2,1)S(1)}, u32[]{:S(2)}, u32[]{:S(2)}) collective-permute-start(bf16[512,128]{1,0:T(8,128)(2,1)S(1)} %get-tuple-element.43.refs_9_), channel_id=1, source_target_pairs={{0,33},{1,34},{2,35},{3,32},{32,3},{33,0},{34,1},{35,2},{4,37},{5,... | collective-permute-start | bytes 393224 | tf_op jit(solution)/shard_map/ppermute | solution.py:425
  80.9 4.6 %hist_dkv_begin.1.refs_0_.refs_8_ = f32[2,256,256]{2,1,0:T(8,128)S(1)} custom-call(s32[5]{0:T(128)S(1)} %stack.19.refs_0_, bf16[512,384]{1,0:T(8,128)(2,1)S(1)} %bitcast.14, bf16[512,384]{1,0:T(8,128)(2,1)S(1)} %copy-done.4, bf16[512,384]{1,0:T(8,128)(2,1)} %collective-permute-done.5.refs_3_.refs_4_, bf16[512,384]{1,0:T(8,128)(2,1)S(1)} %copy-done.7, ...), custom_call_target="tpu_custom_call" | custom-call | flops 2000000000 | bytes 1048576 | tf_op jit(solution)/shard_map/hist_dkv_begin/pallas_call | solution.py:63
  85.6 4.0 %all-to-all-start.1 = ((bf16[16,128,128]{2,1,0:T(8,128)(2,1)}), bf16[16,128,128]{2,1,0:T(8,128)(2,1)S(1)}, u32[]{:S(2)}, u32[]{:S(2)}) async-start(bf16[16,128,128]{2,1,0:T(8,128)(2,1)} %relay.3), calls=%async_computation.1 | async-start | bytes 1048576 | tf_op jit(solution)/shard_map/all_to_all | solution.py:513
  89.6 2.7 %hist_dkv_end.1 = (bf16[128,512]{1,0:T(8,128)(2,1)S(1)}, bf16[128,512]{1,0:T(8,128)(2,1)}, bf16[128,512]{1,0:T(8,128)(2,1)}, bf16[128,512]{1,0:T(8,128)(2,1)}) custom-call(s32[5]{0:T(128)S(1)} %stack.19.refs_0_, bf16[4,128,128]{2,1,0:T(8,128)(2,1)S(1)} %hist_dq.1.refs_0_.refs_1_, bf16[512,128]{1,0:T(8,128)(2,1)S(1)} %get-tuple-element.45.refs_2_, ...), custom_call_target="tpu_custom_call" | custom-call | flops 800000000 | bytes 1048576 | tf_op jit(solution)/shard_map/hist_dkv_end/pallas_call | solution.py:63
  92.3 4.3 %collective-permute-start.21 = (bf16[128,512]{1,0:T(8,128)(2,1)S(1)}, bf16[128,512]{1,0:T(8,128)(2,1)S(1)}, u32[]{:S(2)}, u32[]{:S(2)}) collective-permute-start(bf16[128,512]{1,0:T(8,128)(2,1)S(1)} %get-tuple-element.46.refs_8_), channel_id=1, source_target_pairs={{0,0},{4,32},{8,8},{12,40},{16,16},{20,48},{24,24},{28,56},{32,4},... | collective-permute-start | bytes 393224 | tf_op jit(solution)/shard_map/ppermute | solution.py:412
  96.6 2.2 %collective-permute-start.22 = (bf16[128,512]{1,0:T(8,128)(2,1)}, bf16[128,512]{1,0:T(8,128)(2,1)S(1)}, u32[]{:S(2)}, u32[]{:S(2)}) collective-permute-start(bf16[128,512]{1,0:T(8,128)(2,1)} %get-tuple-element.53), channel_id=1, source_target_pairs={{0,8},{4,40},{8,16},{12,48},{16,24},{20,56},{24,0},{28,32},{32,12}... | collective-permute-start | bytes 393224 | tf_op jit(solution)/shard_map/ppermute | solution.py:412
  98.7 4.2 %collective-permute-start.23 = (bf16[128,512]{1,0:T(8,128)(2,1)}, bf16[128,512]{1,0:T(8,128)(2,1)S(1)}, u32[]{:S(2)}, u32[]{:S(2)}) collective-permute-start(bf16[128,512]{1,0:T(8,128)(2,1)} %get-tuple-element.54), channel_id=1, source_target_pairs={{0,16},{4,48},{8,24},{12,56},{16,0},{20,32},{24,8},{28,40},{32,20}... | collective-permute-start | bytes 393224 | tf_op jit(solution)/shard_map/ppermute | solution.py:412
  102.9 2.1 %collective-permute-start.24 = (bf16[128,512]{1,0:T(8,128)(2,1)}, bf16[128,512]{1,0:T(8,128)(2,1)S(1)}, u32[]{:S(2)}, u32[]{:S(2)}) collective-permute-start(bf16[128,512]{1,0:T(8,128)(2,1)} %get-tuple-element.55), channel_id=1, source_target_pairs={{0,24},{4,56},{8,0},{12,32},{16,8},{20,40},{24,16},{28,48},{32,28}... | collective-permute-start | bytes 393224 | tf_op jit(solution)/shard_map/ppermute | solution.py:412
  105.0 3.8 %cand_close.1 = (bf16[256,1024]{1,0:T(8,128)(2,1)}, bf16[512,1024]{1,0:T(8,128)(2,1)S(1)}, bf16[4,1024,512]{2,1,0:T(8,128)(2,1)S(1)}, bf16[128,1024]{1,0:T(8,128)(2,1)S(1)}, bf16[128,1024]{1,0:T(8,128)(2,1)S(1)}) custom-call(s32[256,1]{1,0:T(8,128)S(1)} %copy.15.refs_0_, bf16[256,512]{1,0:T(8,128)(2,1)} %copy-done.1, ...), custom_call_target="tpu_custom_call" | custom-call | flops 400000000 | bytes 1048576 | tf_op jit(solution)/shard_map/cand_close/pallas_call | solution.py:63
  108.8 1.1 collective-permute-done.24.refs_11_
  109.9 3.1 %hist_close.1 = (bf16[1,128,1024]{2,1,0:T(8,128)(2,1)}, bf16[1,128,1024]{2,1,0:T(8,128)(2,1)}) custom-call(s32[5]{0:T(128)S(1)} %stack.19.refs_0_, bf16[128,1024]{1,0:T(8,128)(2,1)S(1)} %get-tuple-element.47.refs_1_, bf16[128,1024]{1,0:T(8,128)(2,1)S(1)} %get-tuple-element.48.refs_2_, bf16[4,128,512]{2,1,0:T(8,128)(2,1)S(1)} %get-tuple-element.31.refs_3_, ...), custom_call_target="tpu_custom_call" | custom-call | flops 700000000 | bytes 1048576 | tf_op jit(solution)/shard_map/hist_close/pallas_call | solution.py:63
  (51 shorter events, 0.1 us)
Async XLA Ops:
  0.6 19.3 %copy-start.13 = (s32[256,1]{0,1:T(1,128)S(1)}, s32[256,1]{0,1:T(1,128)}, u32[]{:S(2)}) copy-start(s32[256,1]{0,1:T(1,128)} %param.10) | copy-start | bytes 3076
  0.6 19.5 %copy-start = (bf16[256,1024]{1,0:T(8,128)(2,1)S(1)}, bf16[256,1024]{1,0:T(8,128)(2,1)}, u32[]{:S(2)}) copy-start(bf16[256,1024]{1,0:T(8,128)(2,1)} %refs_3_.3) | copy-start | bytes 1572868
  6.4 16.9 %collective-permute-start = (bf16[128,512]{1,0:T(8,128)(2,1)S(1)}, bf16[128,512]{1,0:T(8,128)(2,1)S(1)}, u32[]{:S(2)}, u32[]{:S(2)}) collective-permute-start(bf16[128,512]{1,0:T(8,128)(2,1)S(1)} %get-tuple-element.33), channel_id=1, source_target_pairs={{0,0},{4,32},{8,8},{12,40},{16,16},{20,48},{24,24},{28,56},{32,4},... | collective-permute-start | bytes 393224 | tf_op jit(solution)/shard_map/ppermute | solution.py:412
  12.5 10.8 %collective-permute-start.1 = (bf16[128,512]{1,0:T(8,128)(2,1)S(1)}, bf16[128,512]{1,0:T(8,128)(2,1)S(1)}, u32[]{:S(2)}, u32[]{:S(2)}) collective-permute-start(bf16[128,512]{1,0:T(8,128)(2,1)S(1)} %get-tuple-element.34), channel_id=1, source_target_pairs={{0,8},{4,40},{8,16},{12,48},{16,24},{20,56},{24,0},{28,32},{32,12}... | collective-permute-start | bytes 393224 | tf_op jit(solution)/shard_map/ppermute | solution.py:412
  13.6 9.7 %collective-permute-start.2 = (bf16[128,512]{1,0:T(8,128)(2,1)S(1)}, bf16[128,512]{1,0:T(8,128)(2,1)S(1)}, u32[]{:S(2)}, u32[]{:S(2)}) collective-permute-start(bf16[128,512]{1,0:T(8,128)(2,1)S(1)} %get-tuple-element.35), channel_id=1, source_target_pairs={{0,16},{4,48},{8,24},{12,56},{16,0},{20,32},{24,8},{28,40},{32,20}... | collective-permute-start | bytes 393224 | tf_op jit(solution)/shard_map/ppermute | solution.py:412
  19.1 6.8 %collective-permute-start.3 = (bf16[128,512]{1,0:T(8,128)(2,1)S(1)}, bf16[128,512]{1,0:T(8,128)(2,1)S(1)}, u32[]{:S(2)}, u32[]{:S(2)}) collective-permute-start(bf16[128,512]{1,0:T(8,128)(2,1)S(1)} %get-tuple-element.36), channel_id=1, source_target_pairs={{0,24},{4,56},{8,0},{12,32},{16,8},{20,40},{24,16},{28,48},{32,28}... | collective-permute-start | bytes 393224 | tf_op jit(solution)/shard_map/ppermute | solution.py:412
  23.3 34.6 %copy-start.1 = (bf16[256,512]{1,0:T(8,128)(2,1)}, bf16[256,512]{1,0:T(8,128)(2,1)S(1)}, u32[]{:S(2)}) copy-start(bf16[256,512]{1,0:T(8,128)(2,1)S(1)} %get-tuple-element.32.refs_5_.refs_1_) | copy-start | bytes 786436
  26.5 8.7 %collective-permute-start.5 = (bf16[512,384]{1,0:T(8,128)(2,1)S(1)}, bf16[512,384]{1,0:T(8,128)(2,1)}, u32[]{:S(2)}, u32[]{:S(2)}) collective-permute-start(bf16[512,384]{1,0:T(8,128)(2,1)S(1)} %bitcast.7), channel_id=1, source_target_pairs={{0,1},{1,2},{2,3},{3,0},{32,35},{33,32},{34,33},{35,34},{4,5},{5,6... | collective-permute-start | bytes 1179656 | tf_op jit(solution)/shard_map/ppermute | solution.py:425
  30.4 7.9 %collective-permute-start.7 = (bf16[512,384]{1,0:T(8,128)(2,1)S(1)}, bf16[512,384]{1,0:T(8,128)(2,1)}, u32[]{:S(2)}, u32[]{:S(2)}) collective-permute-start(bf16[512,384]{1,0:T(8,128)(2,1)S(1)} %bitcast.8), channel_id=1, source_target_pairs={{0,3},{1,0},{2,1},{3,2},{32,33},{33,34},{34,35},{35,32},{4,7},{5,4... | collective-permute-start | bytes 1179656 | tf_op jit(solution)/shard_map/ppermute | solution.py:425
  30.4 15.2 %all-to-all-start = ((bf16[16,128,128]{2,1,0:T(8,128)(2,1)}), bf16[16,128,128]{2,1,0:T(8,128)(2,1)S(1)}, u32[]{:S(2)}, u32[]{:S(2)}) async-start(bf16[16,128,128]{2,1,0:T(8,128)(2,1)} %get-tuple-element.39), calls=%async_computation | async-start | bytes 1048576 | tf_op jit(solution)/shard_map/all_to_all | solution.py:466
  34.1 4.8 %collective-permute-start.4 = (bf16[512,384]{1,0:T(8,128)(2,1)S(1)}, bf16[512,384]{1,0:T(8,128)(2,1)S(1)}, u32[]{:S(2)}, u32[]{:S(2)}) collective-permute-start(bf16[512,384]{1,0:T(8,128)(2,1)S(1)} %bitcast.9), channel_id=1, source_target_pairs={{0,32},{32,0},{1,33},{33,1},{2,34},{34,2},{3,35},{35,3},{4,36},{36... | collective-permute-start | bytes 1179656 | tf_op jit(solution)/shard_map/ppermute | solution.py:416
  35.2 3.6 %collective-permute-start.6 = (bf16[512,384]{1,0:T(8,128)(2,1)}, bf16[512,384]{1,0:T(8,128)(2,1)S(1)}, u32[]{:S(2)}, u32[]{:S(2)}) collective-permute-start(bf16[512,384]{1,0:T(8,128)(2,1)} %collective-permute-done.5.refs_3_.refs_4_), channel_id=1, source_target_pairs={{0,32},{32,0},{1,33},{33,1},{2,34},{34,2},{3,35},{35,3},{4,36},{36... | collective-permute-start | bytes 1179656 | tf_op jit(solution)/shard_map/ppermute | solution.py:416
  38.3 1.9 %collective-permute-start.8 = (bf16[512,384]{1,0:T(8,128)(2,1)}, bf16[512,384]{1,0:T(8,128)(2,1)S(1)}, u32[]{:S(2)}, u32[]{:S(2)}) collective-permute-start(bf16[512,384]{1,0:T(8,128)(2,1)} %collective-permute-done.7.refs_5_.refs_6_), channel_id=1, source_target_pairs={{0,32},{32,0},{1,33},{33,1},{2,34},{34,2},{3,35},{35,3},{4,36},{36... | collective-permute-start | bytes 1179656 | tf_op jit(solution)/shard_map/ppermute | solution.py:416
  38.3 19.6 %collective-permute-start.10 = (bf16[512,384]{1,0:T(8,128)(2,1)}, bf16[512,384]{1,0:T(8,128)(2,1)S(1)}, u32[]{:S(2)}, u32[]{:S(2)}) collective-permute-start(bf16[512,384]{1,0:T(8,128)(2,1)} %collective-permute-done.5.refs_3_.refs_4_), channel_id=1, source_target_pairs={{0,33},{1,34},{2,35},{3,32},{32,3},{33,0},{34,1},{35,2},{4,37},{5,... | collective-permute-start | bytes 1179656 | tf_op jit(solution)/shard_map/ppermute | solution.py:425
  38.7 19.2 %collective-permute-start.9 = (bf16[512,384]{1,0:T(8,128)(2,1)}, bf16[512,384]{1,0:T(8,128)(2,1)S(1)}, u32[]{:S(2)}, u32[]{:S(2)}) collective-permute-start(bf16[512,384]{1,0:T(8,128)(2,1)} %collective-permute-done.5.refs_3_.refs_4_), channel_id=1, source_target_pairs={{0,1},{1,2},{2,3},{3,0},{32,35},{33,32},{34,33},{35,34},{4,5},{5,6... | collective-permute-start | bytes 1179656 | tf_op jit(solution)/shard_map/ppermute | solution.py:425
  43.3 0.8 copy-start.2
  44.1 0.8 copy-start.5
  44.8 0.7 copy-start.8
  45.6 1.0 copy-start.3
  46.6 1.0 copy-start.6
  47.6 1.0 copy-start.9
  57.9 14.7 %copy-start.4 = (bf16[512,384]{1,0:T(8,128)(2,1)S(1)}, bf16[512,384]{1,0:T(8,128)(2,1)}, u32[]{:S(2)}) copy-start(bf16[512,384]{1,0:T(8,128)(2,1)} %copy-done.2) | copy-start | bytes 1179652
  57.9 14.7 %copy-start.7 = (bf16[512,384]{1,0:T(8,128)(2,1)S(1)}, bf16[512,384]{1,0:T(8,128)(2,1)}, u32[]{:S(2)}) copy-start(bf16[512,384]{1,0:T(8,128)(2,1)} %copy-done.5) | copy-start | bytes 1179652
  57.9 14.7 %copy-start.10 = (bf16[512,384]{1,0:T(8,128)(2,1)S(1)}, bf16[512,384]{1,0:T(8,128)(2,1)}, u32[]{:S(2)}) copy-start(bf16[512,384]{1,0:T(8,128)(2,1)} %copy-done.8) | copy-start | bytes 1179652
  59.6 7.0 %collective-permute-start.11 = (f32[8,512]{1,0:T(8,128)S(1)}, f32[8,512]{1,0:T(8,128)S(1)}, u32[]{:S(2)}, u32[]{:S(2)}) collective-permute-start(f32[8,512]{1,0:T(8,128)S(1)} %get-tuple-element.41.refs_4_.refs_6_), channel_id=1, source_target_pairs={{0,8},{8,16},{16,24},{24,0},{1,9},{9,17},{17,25},{25,1},{2,10},{10... | collective-permute-start | bytes 49160 | tf_op jit(solution)/shard_map/ppermute | solution.py:403
  59.7 6.9 %collective-permute-start.12 = (f32[8,512]{1,0:T(8,128)S(1)}, f32[8,512]{1,0:T(8,128)S(1)}, u32[]{:S(2)}, u32[]{:S(2)}) collective-permute-start(f32[8,512]{1,0:T(8,128)S(1)} %get-tuple-element.41.refs_4_.refs_6_), channel_id=1, source_target_pairs={{0,16},{8,24},{16,0},{24,8},{1,17},{9,25},{17,1},{25,9},{2,18},{10... | collective-permute-start | bytes 49160 | tf_op jit(solution)/shard_map/ppermute | solution.py:403
  63.1 3.5 %collective-permute-start.13 = (f32[8,512]{1,0:T(8,128)S(1)}, f32[8,512]{1,0:T(8,128)S(1)}, u32[]{:S(2)}, u32[]{:S(2)}) collective-permute-start(f32[8,512]{1,0:T(8,128)S(1)} %get-tuple-element.41.refs_4_.refs_6_), channel_id=1, source_target_pairs={{0,24},{8,0},{16,8},{24,16},{1,25},{9,1},{17,9},{25,17},{2,26},{10... | collective-permute-start | bytes 49160 | tf_op jit(solution)/shard_map/ppermute | solution.py:403
  67.6 9.7 %collective-permute-start.15 = (bf16[512,128]{1,0:T(8,128)(2,1)S(1)}, bf16[512,128]{1,0:T(8,128)(2,1)S(1)}, u32[]{:S(2)}, u32[]{:S(2)}) collective-permute-start(bf16[512,128]{1,0:T(8,128)(2,1)S(1)} %get-tuple-element.42.refs_1_.refs_7_), channel_id=1, source_target_pairs={{0,1},{1,2},{2,3},{3,0},{32,35},{33,32},{34,33},{35,34},{4,5},{5,6... | collective-permute-start | bytes 393224 | tf_op jit(solution)/shard_map/ppermute | solution.py:425
  70.1 7.3 %collective-permute-start.16 = (bf16[512,128]{1,0:T(8,128)(2,1)S(1)}, bf16[512,128]{1,0:T(8,128)(2,1)S(1)}, u32[]{:S(2)}, u32[]{:S(2)}) collective-permute-start(bf16[512,128]{1,0:T(8,128)(2,1)S(1)} %get-tuple-element.42.refs_1_.refs_7_), channel_id=1, source_target_pairs={{0,3},{1,0},{2,1},{3,2},{32,33},{33,34},{34,35},{35,32},{4,7},{5,4... | collective-permute-start | bytes 393224 | tf_op jit(solution)/shard_map/ppermute | solution.py:425
  70.1 10.8 %collective-permute-start.14 = (bf16[512,128]{1,0:T(8,128)(2,1)S(1)}, bf16[512,128]{1,0:T(8,128)(2,1)S(1)}, u32[]{:S(2)}, u32[]{:S(2)}) collective-permute-start(bf16[512,128]{1,0:T(8,128)(2,1)S(1)} %get-tuple-element.42.refs_1_.refs_7_), channel_id=1, source_target_pairs={{0,32},{32,0},{1,33},{33,1},{2,34},{34,2},{3,35},{35,3},{4,36},{36... | collective-permute-start | bytes 393224 | tf_op jit(solution)/shard_map/ppermute | solution.py:416
  77.4 3.5 %collective-permute-start.17 = (bf16[512,128]{1,0:T(8,128)(2,1)S(1)}, bf16[512,128]{1,0:T(8,128)(2,1)S(1)}, u32[]{:S(2)}, u32[]{:S(2)}) collective-permute-start(bf16[512,128]{1,0:T(8,128)(2,1)S(1)} %get-tuple-element.43.refs_9_), channel_id=1, source_target_pairs={{0,32},{32,0},{1,33},{33,1},{2,34},{34,2},{3,35},{35,3},{4,36},{36... | collective-permute-start | bytes 393224 | tf_op jit(solution)/shard_map/ppermute | solution.py:416
  77.5 3.4 %collective-permute-start.18 = (bf16[512,128]{1,0:T(8,128)(2,1)S(1)}, bf16[512,128]{1,0:T(8,128)(2,1)S(1)}, u32[]{:S(2)}, u32[]{:S(2)}) collective-permute-start(bf16[512,128]{1,0:T(8,128)(2,1)S(1)} %get-tuple-element.44.refs_11_), channel_id=1, source_target_pairs={{0,32},{32,0},{1,33},{33,1},{2,34},{34,2},{3,35},{35,3},{4,36},{36... | collective-permute-start | bytes 393224 | tf_op jit(solution)/shard_map/ppermute | solution.py:416
  78.0 7.6 %collective-permute-start.19 = (bf16[512,128]{1,0:T(8,128)(2,1)S(1)}, bf16[512,128]{1,0:T(8,128)(2,1)S(1)}, u32[]{:S(2)}, u32[]{:S(2)}) collective-permute-start(bf16[512,128]{1,0:T(8,128)(2,1)S(1)} %get-tuple-element.43.refs_9_), channel_id=1, source_target_pairs={{0,1},{1,2},{2,3},{3,0},{32,35},{33,32},{34,33},{35,34},{4,5},{5,6... | collective-permute-start | bytes 393224 | tf_op jit(solution)/shard_map/ppermute | solution.py:425
  79.4 6.2 %collective-permute-start.20 = (bf16[512,128]{1,0:T(8,128)(2,1)S(1)}, bf16[512,128]{1,0:T(8,128)(2,1)S(1)}, u32[]{:S(2)}, u32[]{:S(2)}) collective-permute-start(bf16[512,128]{1,0:T(8,128)(2,1)S(1)} %get-tuple-element.43.refs_9_), channel_id=1, source_target_pairs={{0,33},{1,34},{2,35},{3,32},{32,3},{33,0},{34,1},{35,2},{4,37},{5,... | collective-permute-start | bytes 393224 | tf_op jit(solution)/shard_map/ppermute | solution.py:425
  85.6 19.4 %all-to-all-start.1 = ((bf16[16,128,128]{2,1,0:T(8,128)(2,1)}), bf16[16,128,128]{2,1,0:T(8,128)(2,1)S(1)}, u32[]{:S(2)}, u32[]{:S(2)}) async-start(bf16[16,128,128]{2,1,0:T(8,128)(2,1)} %relay.3), calls=%async_computation.1 | async-start | bytes 1048576 | tf_op jit(solution)/shard_map/all_to_all | solution.py:513
  92.3 17.6 %copy-start.11 = (bf16[128,512]{1,0:T(8,128)(2,1)S(1)}, bf16[128,512]{1,0:T(8,128)(2,1)}, u32[]{:S(2)}) copy-start(bf16[128,512]{1,0:T(8,128)(2,1)} %get-tuple-element.51.refs_6_) | copy-start | bytes 393220
  92.3 17.6 %copy-start.12 = (bf16[128,512]{1,0:T(8,128)(2,1)S(1)}, bf16[128,512]{1,0:T(8,128)(2,1)}, u32[]{:S(2)}) copy-start(bf16[128,512]{1,0:T(8,128)(2,1)} %get-tuple-element.52.refs_7_) | copy-start | bytes 393220
  92.3 16.5 %collective-permute-start.21 = (bf16[128,512]{1,0:T(8,128)(2,1)S(1)}, bf16[128,512]{1,0:T(8,128)(2,1)S(1)}, u32[]{:S(2)}, u32[]{:S(2)}) collective-permute-start(bf16[128,512]{1,0:T(8,128)(2,1)S(1)} %get-tuple-element.46.refs_8_), channel_id=1, source_target_pairs={{0,0},{4,32},{8,8},{12,40},{16,16},{20,48},{24,24},{28,56},{32,4},... | collective-permute-start | bytes 393224 | tf_op jit(solution)/shard_map/ppermute | solution.py:412
  96.6 12.2 %collective-permute-start.22 = (bf16[128,512]{1,0:T(8,128)(2,1)}, bf16[128,512]{1,0:T(8,128)(2,1)S(1)}, u32[]{:S(2)}, u32[]{:S(2)}) collective-permute-start(bf16[128,512]{1,0:T(8,128)(2,1)} %get-tuple-element.53), channel_id=1, source_target_pairs={{0,8},{4,40},{8,16},{12,48},{16,24},{20,56},{24,0},{28,32},{32,12}... | collective-permute-start | bytes 393224 | tf_op jit(solution)/shard_map/ppermute | solution.py:412
  98.7 10.1 %collective-permute-start.23 = (bf16[128,512]{1,0:T(8,128)(2,1)}, bf16[128,512]{1,0:T(8,128)(2,1)S(1)}, u32[]{:S(2)}, u32[]{:S(2)}) collective-permute-start(bf16[128,512]{1,0:T(8,128)(2,1)} %get-tuple-element.54), channel_id=1, source_target_pairs={{0,16},{4,48},{8,24},{12,56},{16,0},{20,32},{24,8},{28,40},{32,20}... | collective-permute-start | bytes 393224 | tf_op jit(solution)/shard_map/ppermute | solution.py:412
  102.9 7.0 %collective-permute-start.24 = (bf16[128,512]{1,0:T(8,128)(2,1)}, bf16[128,512]{1,0:T(8,128)(2,1)S(1)}, u32[]{:S(2)}, u32[]{:S(2)}) collective-permute-start(bf16[128,512]{1,0:T(8,128)(2,1)} %get-tuple-element.55), channel_id=1, source_target_pairs={{0,24},{4,56},{8,0},{12,32},{16,8},{20,40},{24,16},{28,48},{32,28}... | collective-permute-start | bytes 393224 | tf_op jit(solution)/shard_map/ppermute | solution.py:412

commit v6 on v5

--- a/solution.py
+++ b/solution.py
@@ -198,7 +198,7 @@
 
 def cand_attend(count, begin, end, *refs):
     q_ref, kvs, rest = refs[0], refs[1 : 1 + count], refs[1 + count :]
-    q = q_ref[...].reshape(8 * CAP, HS)
+    q = q_ref[...].reshape(16 * CAP, HS)
     total = None if begin else rest[0][...]
     for block in kvs:
         half = dot(q, block[:, :HS], NT).astype(BF)
@@ -206,7 +206,7 @@
         more = dot(probs, block[:, HS : 2 * HS])
         total = more if total is None else total + more
     if end:
-        rest[-1][...] = total.astype(BF).reshape(8, CAP, HS)
+        rest[-1][...] = total.astype(BF).reshape(16, CAP, HS)
     else:
         rest[-1][...] = total
 
@@ -467,16 +467,16 @@
     last = [along(plus, 1, 0), along(plus, 1, 1)]
     kvq = [own, own_pair, plus, across(plus), minus, across(minus)]
 
-    q_spec = pl.BlockSpec((8, 128, 128), lambda i: (i, 0, 0))
-    acc_spec = pl.BlockSpec((1024, 128), lambda i: (i, 0))
+    q_spec = held
+    acc_spec = held
 
     def cand_part(kvs, total, end, after):
         begin = total is None
         return call(
-            functools.partial(cand_attend, len(kvs), begin, end), "cand_attend", (2,),
+            functools.partial(cand_attend, len(kvs), begin, end), "cand_attend", (1,),
             [q_spec] + [held] * len(kvs) + ([] if begin else [acc_spec]),
             shaped((16, 128, 128)) if end else shaped((2048, 128), F32),
-            q_spec if end else acc_spec, [], 600_000_000 * len(kvs), after,
+            q_spec if end else acc_spec, [], 600_000_000 * len(kvs), after, 20,
         )(arrived, *kvs, *([] if begin else [total]))
 
     att = call(

time: 114 us -> 114 us (level)
    unnamed x29 -> x23, local copies, waits for them, and re-layouts: 5.43 us -> 5.41 us
  transfers between devices with their start and end apart: 27 -> 27, of which waited for: 4 -> 4; matrix products, arithmetic and copies ran while one was open for 0% -> 0% of each run, Pallas kernels for 31% -> 30%
where the time goes in v6:
time: 114 us; the launch traced here: 113 us
  starting transfers between devices  51.6 us (45%)
  Pallas kernels  45.8 us (40%)
  waiting for transfers between devices  8.25 us (7%)
  local copies, waits for them, and re-layouts  5.49 us (5%)
  between operations  1.85 us (2%)
    pallas_call x15, Pallas kernels, run(): got = made(*pinned, *after, *carry)  45.8 us
    ppermute x8, starting transfers between devices, crossed(): return lax.ppermute(value, ('c', 'y', 'xh'), pairs)  26.2 us
    ppermute x8, starting transfers between devices, along(): return lax.ppermute(value, ('c', 'z'), pairs)  9.73 us
    unnamed x23, local copies, waits for them, and re-layouts  5.41 us
    ppermute x6, starting transfers between devices, across(): return lax.ppermute(value, 'c', [(0, 1), (1, 0)])  4.27 us
    all_to_all x1, starting transfers between devices, per_device(): returned = lax.all_to_all(leaving, ('xl', 'xh', 'y'), 0, 0, tiled=True)  4.17 us
    ppermute x8, waiting for transfers between devices, crossed(): return lax.ppermute(value, ('c', 'y', 'xh'), pairs)  3.8 us
    all_to_all x1, starting transfers between devices, per_device(): arrived = lax.all_to_all(sent_cand, ('xl', 'xh', 'y'), 0, 0, tiled=True)  3.69 us
  transfers between devices with their start and end apart: 27, of which 4 were waited for; matrix products, arithmetic and copies ran while one was open for 0% of the time, Pallas kernels for 30%

profile of v6, /device:TPU:1, one launch (start us, length us, event | category | flops | bytes accessed | tf_op | source)
XLA Modules:
  0.0 112.9 jit_solution(1059048166218922540)
XLA Ops:
  1.4 0.1 stack.19.refs_0_
  1.4 4.9 %project_all.1 = (bf16[128,512]{1,0:T(8,128)(2,1)S(1)}, bf16[128,512]{1,0:T(8,128)(2,1)S(1)}, bf16[128,512]{1,0:T(8,128)(2,1)S(1)}, bf16[128,512]{1,0:T(8,128)(2...) custom-call(s32[5]{0:T(128)S(1)} %stack.19.refs_0_, ...), custom_call_target="tpu_custom_call" | custom-call | flops 700000000 | bytes 1048576 | tf_op jit(solution)/shard_map/project_all/pallas_call | solution.py:63
  6.4 6.0 %collective-permute-start = (bf16[128,512]{1,0:T(8,128)(2,1)S(1)}, bf16[128,512]{1,0:T(8,128)(2,1)S(1)}, u32[]{:S(2)}, u32[]{:S(2)}) collective-permute-start(bf16[128,512]{1,0:T(8,128)(2,1)S(1)} %get-tuple-element.33), channel_id=1, source_target_pairs={{0,0},{4,32},{8,8},{12,40},{16,16},{20,48},{24,24},{28,56},{32,4},... | collective-permute-start | bytes 393224 | tf_op jit(solution)/shard_map/ppermute | solution.py:412
  12.5 1.1 collective-permute-start.1
  13.6 5.6 %collective-permute-start.2 = (bf16[128,512]{1,0:T(8,128)(2,1)S(1)}, bf16[128,512]{1,0:T(8,128)(2,1)S(1)}, u32[]{:S(2)}, u32[]{:S(2)}) collective-permute-start(bf16[128,512]{1,0:T(8,128)(2,1)S(1)} %get-tuple-element.35), channel_id=1, source_target_pairs={{0,16},{4,48},{8,24},{12,56},{16,0},{20,32},{24,8},{28,40},{32,20}... | collective-permute-start | bytes 393224 | tf_op jit(solution)/shard_map/ppermute | solution.py:412
  19.1 0.8 collective-permute-start.3
  19.9 0.1 copy.15.refs_0_
  20.1 3.1 %project_cand.1 = (bf16[16,128,128]{2,1,0:T(8,128)(2,1)}, bf16[256,512]{1,0:T(8,128)(2,1)S(1)}) custom-call(s32[256,1]{1,0:T(8,128)S(1)} %copy.15.refs_0_, bf16[256,1024]{1,0:T(8,128)(2,1)S(1)} %copy-done, bf16[1024,2048]{1,0:T(8,128)(2,1)} %refs_5_.1, bf16[4,128,512]{2,1,0:T(8,128)(2,1)S(1)} %get-tuple-element.31.refs_3_), custom_call_target="tpu_custom_call" | custom-call | flops 700000000 | bytes 1048576 | tf_op jit(solution)/shard_map/project_cand/pallas_call | solution.py:63
  23.3 2.6 %collective-permute-done.3.refs_4_ = bf16[128,512]{1,0:T(8,128)(2,1)S(1)} collective-permute-done((bf16[128,512]{1,0:T(8,128)(2,1)S(1)}, bf16[128,512]{1,0:T(8,128)(2,1)S(1)}, u32[]{:S(2)}, u32[]{:S(2)}) %collective-permute-start.3) | collective-permute-done | bytes 131104 | tf_op jit(solution)/shard_map/ppermute | solution.py:412
  25.9 0.6 arrange.1
  26.5 3.8 %collective-permute-start.5 = (bf16[512,384]{1,0:T(8,128)(2,1)S(1)}, bf16[512,384]{1,0:T(8,128)(2,1)}, u32[]{:S(2)}, u32[]{:S(2)}) collective-permute-start(bf16[512,384]{1,0:T(8,128)(2,1)S(1)} %bitcast.7), channel_id=1, source_target_pairs={{0,1},{1,2},{2,3},{3,0},{32,35},{33,32},{34,33},{35,34},{4,5},{5,6... | collective-permute-start | bytes 1179656 | tf_op jit(solution)/shard_map/ppermute | solution.py:425
  30.4 3.7 %all-to-all-start = ((bf16[16,128,128]{2,1,0:T(8,128)(2,1)}), bf16[16,128,128]{2,1,0:T(8,128)(2,1)S(1)}, u32[]{:S(2)}, u32[]{:S(2)}) async-start(bf16[16,128,128]{2,1,0:T(8,128)(2,1)} %get-tuple-element.39), calls=%async_computation | async-start | bytes 1048576 | tf_op jit(solution)/shard_map/all_to_all | solution.py:466
  34.0 1.1 %collective-permute-start.4 = (bf16[512,384]{1,0:T(8,128)(2,1)S(1)}, bf16[512,384]{1,0:T(8,128)(2,1)S(1)}, u32[]{:S(2)}, u32[]{:S(2)}) collective-permute-start(bf16[512,384]{1,0:T(8,128)(2,1)S(1)} %bitcast.9), channel_id=1, source_target_pairs={{0,32},{32,0},{1,33},{33,1},{2,34},{34,2},{3,35},{35,3},{4,36},{36... | collective-permute-start | bytes 1179656 | tf_op jit(solution)/shard_map/ppermute | solution.py:416
  35.2 0.1 collective-permute-start.6
  35.3 3.0 %collective-permute-done.7.refs_5_.refs_6_ = bf16[512,384]{1,0:T(8,128)(2,1)} collective-permute-done((bf16[512,384]{1,0:T(8,128)(2,1)S(1)}, bf16[512,384]{1,0:T(8,128)(2,1)}, u32[]{:S(2)}, u32[]{:S(2)}) %collective-permute-start.7) | collective-permute-done | bytes 393248 | tf_op jit(solution)/shard_map/ppermute | solution.py:425
  38.3 0.4 collective-permute-start.10
  38.7 0.1 collective-permute-start.9
  38.8 1.4 %collective-permute-done.8.refs_6_.refs_7_ = bf16[512,384]{1,0:T(8,128)(2,1)S(1)} collective-permute-done((bf16[512,384]{1,0:T(8,128)(2,1)}, bf16[512,384]{1,0:T(8,128)(2,1)S(1)}, u32[]{:S(2)}, u32[]{:S(2)}) %collective-permute-start.8) | collective-permute-done | bytes 393248 | tf_op jit(solution)/shard_map/ppermute | solution.py:416
  40.2 3.1 %hist_begin.1.refs_7_.refs_8_ = f32[512,128]{1,0:T(8,128)S(1)} custom-call(s32[5]{0:T(128)S(1)} %stack.19.refs_0_, bf16[512,384]{1,0:T(8,128)(2,1)S(1)} %bitcast.10, bf16[512,384]{1,0:T(8,128)(2,1)S(1)} %collective-permute-done.4.refs_2_.refs_3_, bf16[512,384]{1,0:T(8,128)(2,1)} %collective-permute-done.5.refs_3_.refs_4_, ...), custom_call_target="tpu_custom_call" | custom-call | flops 1000 | bytes 1000 | tf_op jit(solution)/shard_map/hist_begin/pallas_call | solution.py:63
  43.3 0.7 copy-done.2
  44.0 0.8 copy-done.4
  44.8 0.7 copy-done.6
  45.6 1.0 copy-done.3
  46.6 1.0 copy-done.5
  47.6 1.0 copy-done.7
  48.6 9.0 %cand_attend.2.refs_9_.refs_3_ = f32[2048,128]{1,0:T(8,128)S(1)} custom-call(bf16[16,128,128]{2,1,0:T(8,128)(2,1)S(1)} %all-to-all-done.refs_0_, bf16[512,384]{1,0:T(8,128)(2,1)S(1)} %bitcast.11, bf16[512,384]{1,0:T(8,128)(2,1)S(1)} %copy-done.3, bf16[512,384]{1,0:T(8,128)(2,1)} %collective-permute-done.5.refs_3_.refs_4_, bf16[512,384]{1,0:T(8,128)(2,1)S(1)} %copy-done.5, ...), custom_call_target="tpu_custom_call" | custom-call | flops 3600000000 | bytes 1048576 | tf_op jit(solution)/shard_map/cand_attend/pallas_call | solution.py:63
  57.6 1.7 %hist_end.1 = (f32[512,128]{1,0:T(8,128)S(1)}, f32[8,512]{1,0:T(8,128)S(1)}) custom-call(s32[5]{0:T(128)S(1)} %stack.19.refs_0_, bf16[128,512]{1,0:T(8,128)(2,1)S(1)} %collective-permute-done.refs_1_, bf16[128,512]{1,0:T(8,128)(2,1)S(1)} %collective-permute-done.1.refs_2_, bf16[128,512]{1,0:T(8,128)(2,1)S(1)} %collective-permute-done.2.refs_3_, ...), custom_call_target="tpu_custom_call" | custom-call | flops 400000000 | bytes 1048576 | tf_op jit(solution)/shard_map/hist_end/pallas_call | solution.py:63
  59.3 0.0 collective-permute-start.11
  59.4 3.4 %collective-permute-start.12 = (f32[8,512]{1,0:T(8,128)S(1)}, f32[8,512]{1,0:T(8,128)S(1)}, u32[]{:S(2)}, u32[]{:S(2)}) collective-permute-start(f32[8,512]{1,0:T(8,128)S(1)} %get-tuple-element.41.refs_4_.refs_6_), channel_id=1, source_target_pairs={{0,16},{8,24},{16,0},{24,8},{1,17},{9,25},{17,1},{25,9},{2,18},{10... | collective-permute-start | bytes 49160 | tf_op jit(solution)/shard_map/ppermute | solution.py:403
  62.8 3.3 %cand_attend.3.refs_10_.refs_3_ = bf16[16,128,128]{2,1,0:T(8,128)(2,1)} custom-call(bf16[16,128,128]{2,1,0:T(8,128)(2,1)S(1)} %all-to-all-done.refs_0_, bf16[512,384]{1,0:T(8,128)(2,1)S(1)} %collective-permute-done.9.refs_6_.refs_1_.refs_8_.refs_4_, bf16[512,384]{1,0:T(8,128)(2,1)S(1)} %collective-permute-done.10.refs_7_.refs_2_.refs_9_.refs_5_, ...), custom_call_target="tpu_custom_call" | custom-call | flops 1200000000 | bytes 1048576 | tf_op jit(solution)/shard_map/cand_attend/pallas_call | solution.py:63
  66.1 1.0 normed_grads.1
  67.2 2.4 %collective-permute-start.15 = (bf16[512,128]{1,0:T(8,128)(2,1)S(1)}, bf16[512,128]{1,0:T(8,128)(2,1)S(1)}, u32[]{:S(2)}, u32[]{:S(2)}) collective-permute-start(bf16[512,128]{1,0:T(8,128)(2,1)S(1)} %get-tuple-element.42.refs_1_.refs_7_), channel_id=1, source_target_pairs={{0,1},{1,2},{2,3},{3,0},{32,35},{33,32},{34,33},{35,34},{4,5},{5,6... | collective-permute-start | bytes 393224 | tf_op jit(solution)/shard_map/ppermute | solution.py:425
  69.6 2.4 %collective-permute-start.14 = (bf16[512,128]{1,0:T(8,128)(2,1)S(1)}, bf16[512,128]{1,0:T(8,128)(2,1)S(1)}, u32[]{:S(2)}, u32[]{:S(2)}) collective-permute-start(bf16[512,128]{1,0:T(8,128)(2,1)S(1)} %get-tuple-element.42.refs_1_.refs_7_), channel_id=1, source_target_pairs={{0,32},{32,0},{1,33},{33,1},{2,34},{34,2},{3,35},{35,3},{4,36},{36... | collective-permute-start | bytes 393224 | tf_op jit(solution)/shard_map/ppermute | solution.py:416
  72.1 4.8 %hist_dq.1.refs_0_.refs_1_ = bf16[4,128,128]{2,1,0:T(8,128)(2,1)S(1)} custom-call(s32[5]{0:T(128)S(1)} %stack.19.refs_0_, bf16[512,128]{1,0:T(8,128)(2,1)S(1)} %get-tuple-element.42.refs_1_.refs_7_, bf16[512,384]{1,0:T(8,128)(2,1)S(1)} %bitcast.13, bf16[512,384]{1,0:T(8,128)(2,1)S(1)} %copy-done.3, bf16[512,384]{1,0:T(8,128)(2,1)} %collective-permute-done.5.refs_3_.refs_4_, ...), custom_call_target="tpu_custom_call" | custom-call | flops 2000000000 | bytes 1048576 | tf_op jit(solution)/shard_map/hist_dq/pallas_call | solution.py:63
  76.9 0.1 collective-permute-start.17
  77.0 0.5 collective-permute-start.18
  77.5 1.4 %collective-permute-start.19 = (bf16[512,128]{1,0:T(8,128)(2,1)S(1)}, bf16[512,128]{1,0:T(8,128)(2,1)S(1)}, u32[]{:S(2)}, u32[]{:S(2)}) collective-permute-start(bf16[512,128]{1,0:T(8,128)(2,1)S(1)} %get-tuple-element.43.refs_9_), channel_id=1, source_target_pairs={{0,1},{1,2},{2,3},{3,0},{32,35},{33,32},{34,33},{35,34},{4,5},{5,6... | collective-permute-start | bytes 393224 | tf_op jit(solution)/shard_map/ppermute | solution.py:425
  78.9 1.5 %collective-permute-start.20 = (bf16[512,128]{1,0:T(8,128)(2,1)S(1)}, bf16[512,128]{1,0:T(8,128)(2,1)S(1)}, u32[]{:S(2)}, u32[]{:S(2)}) collective-permute-start(bf16[512,128]{1,0:T(8,128)(2,1)S(1)} %get-tuple-element.43.refs_9_), channel_id=1, source_target_pairs={{0,33},{1,34},{2,35},{3,32},{32,3},{33,0},{34,1},{35,2},{4,37},{5,... | collective-permute-start | bytes 393224 | tf_op jit(solution)/shard_map/ppermute | solution.py:425
  80.4 4.6 %hist_dkv_begin.1.refs_0_.refs_8_ = f32[2,256,256]{2,1,0:T(8,128)S(1)} custom-call(s32[5]{0:T(128)S(1)} %stack.19.refs_0_, bf16[512,384]{1,0:T(8,128)(2,1)S(1)} %bitcast.14, bf16[512,384]{1,0:T(8,128)(2,1)S(1)} %copy-done.3, bf16[512,384]{1,0:T(8,128)(2,1)} %collective-permute-done.5.refs_3_.refs_4_, bf16[512,384]{1,0:T(8,128)(2,1)S(1)} %copy-done.5, ...), custom_call_target="tpu_custom_call" | custom-call | flops 2000000000 | bytes 1048576 | tf_op jit(solution)/shard_map/hist_dkv_begin/pallas_call | solution.py:63
  85.1 4.2 %all-to-all-start.1 = ((bf16[16,128,128]{2,1,0:T(8,128)(2,1)}), bf16[16,128,128]{2,1,0:T(8,128)(2,1)S(1)}, u32[]{:S(2)}, u32[]{:S(2)}) async-start(bf16[16,128,128]{2,1,0:T(8,128)(2,1)} %relay.3), calls=%async_computation.1 | async-start | bytes 1048576 | tf_op jit(solution)/shard_map/all_to_all | solution.py:513
  89.3 2.7 %hist_dkv_end.1 = (bf16[128,512]{1,0:T(8,128)(2,1)S(1)}, bf16[128,512]{1,0:T(8,128)(2,1)}, bf16[128,512]{1,0:T(8,128)(2,1)}, bf16[128,512]{1,0:T(8,128)(2,1)}) custom-call(s32[5]{0:T(128)S(1)} %stack.19.refs_0_, bf16[4,128,128]{2,1,0:T(8,128)(2,1)S(1)} %hist_dq.1.refs_0_.refs_1_, bf16[512,128]{1,0:T(8,128)(2,1)S(1)} %get-tuple-element.45.refs_2_, ...), custom_call_target="tpu_custom_call" | custom-call | flops 800000000 | bytes 1048576 | tf_op jit(solution)/shard_map/hist_dkv_end/pallas_call | solution.py:63
  92.0 4.3 %collective-permute-start.21 = (bf16[128,512]{1,0:T(8,128)(2,1)S(1)}, bf16[128,512]{1,0:T(8,128)(2,1)S(1)}, u32[]{:S(2)}, u32[]{:S(2)}) collective-permute-start(bf16[128,512]{1,0:T(8,128)(2,1)S(1)} %get-tuple-element.46.refs_8_), channel_id=1, source_target_pairs={{0,0},{4,32},{8,8},{12,40},{16,16},{20,48},{24,24},{28,56},{32,4},... | collective-permute-start | bytes 393224 | tf_op jit(solution)/shard_map/ppermute | solution.py:412
  96.3 2.1 %collective-permute-start.22 = (bf16[128,512]{1,0:T(8,128)(2,1)}, bf16[128,512]{1,0:T(8,128)(2,1)S(1)}, u32[]{:S(2)}, u32[]{:S(2)}) collective-permute-start(bf16[128,512]{1,0:T(8,128)(2,1)} %get-tuple-element.53), channel_id=1, source_target_pairs={{0,8},{4,40},{8,16},{12,48},{16,24},{20,56},{24,0},{28,32},{32,12}... | collective-permute-start | bytes 393224 | tf_op jit(solution)/shard_map/ppermute | solution.py:412
  98.4 4.2 %collective-permute-start.23 = (bf16[128,512]{1,0:T(8,128)(2,1)}, bf16[128,512]{1,0:T(8,128)(2,1)S(1)}, u32[]{:S(2)}, u32[]{:S(2)}) collective-permute-start(bf16[128,512]{1,0:T(8,128)(2,1)} %get-tuple-element.54), channel_id=1, source_target_pairs={{0,16},{4,48},{8,24},{12,56},{16,0},{20,32},{24,8},{28,40},{32,20}... | collective-permute-start | bytes 393224 | tf_op jit(solution)/shard_map/ppermute | solution.py:412
  102.6 2.1 %collective-permute-start.24 = (bf16[128,512]{1,0:T(8,128)(2,1)}, bf16[128,512]{1,0:T(8,128)(2,1)S(1)}, u32[]{:S(2)}, u32[]{:S(2)}) collective-permute-start(bf16[128,512]{1,0:T(8,128)(2,1)} %get-tuple-element.55), channel_id=1, source_target_pairs={{0,24},{4,56},{8,0},{12,32},{16,8},{20,40},{24,16},{28,48},{32,28}... | collective-permute-start | bytes 393224 | tf_op jit(solution)/shard_map/ppermute | solution.py:412
  104.6 3.8 %cand_close.1 = (bf16[256,1024]{1,0:T(8,128)(2,1)}, bf16[512,1024]{1,0:T(8,128)(2,1)S(1)}, bf16[4,1024,512]{2,1,0:T(8,128)(2,1)S(1)}, bf16[128,1024]{1,0:T(8,128)(2,1)S(1)}, bf16[128,1024]{1,0:T(8,128)(2,1)S(1)}) custom-call(s32[256,1]{1,0:T(8,128)S(1)} %copy.15.refs_0_, bf16[256,512]{1,0:T(8,128)(2,1)} %copy-done.1, ...), custom_call_target="tpu_custom_call" | custom-call | flops 400000000 | bytes 1048576 | tf_op jit(solution)/shard_map/cand_close/pallas_call | solution.py:63
  108.5 1.1 %collective-permute-done.24.refs_11_ = bf16[128,512]{1,0:T(8,128)(2,1)S(1)} collective-permute-done((bf16[128,512]{1,0:T(8,128)(2,1)}, bf16[128,512]{1,0:T(8,128)(2,1)S(1)}, u32[]{:S(2)}, u32[]{:S(2)}) %collective-permute-start.24) | collective-permute-done | bytes 131104 | tf_op jit(solution)/shard_map/ppermute | solution.py:412
  109.6 3.1 %hist_close.1 = (bf16[1,128,1024]{2,1,0:T(8,128)(2,1)}, bf16[1,128,1024]{2,1,0:T(8,128)(2,1)}) custom-call(s32[5]{0:T(128)S(1)} %stack.19.refs_0_, bf16[128,1024]{1,0:T(8,128)(2,1)S(1)} %get-tuple-element.47.refs_1_, bf16[128,1024]{1,0:T(8,128)(2,1)S(1)} %get-tuple-element.48.refs_2_, bf16[4,128,512]{2,1,0:T(8,128)(2,1)S(1)} %get-tuple-element.31.refs_3_, ...), custom_call_target="tpu_custom_call" | custom-call | flops 700000000 | bytes 1048576 | tf_op jit(solution)/shard_map/hist_close/pallas_call | solution.py:63
  (45 shorter events, 0.1 us)
Async XLA Ops:
  0.6 19.3 %copy-start.10 = (s32[256,1]{0,1:T(1,128)S(1)}, s32[256,1]{0,1:T(1,128)}, u32[]{:S(2)}) copy-start(s32[256,1]{0,1:T(1,128)} %param.10) | copy-start | bytes 3076
  0.6 19.4 %copy-start = (bf16[256,1024]{1,0:T(8,128)(2,1)S(1)}, bf16[256,1024]{1,0:T(8,128)(2,1)}, u32[]{:S(2)}) copy-start(bf16[256,1024]{1,0:T(8,128)(2,1)} %refs_3_.3) | copy-start | bytes 1572868
  6.4 16.9 %collective-permute-start = (bf16[128,512]{1,0:T(8,128)(2,1)S(1)}, bf16[128,512]{1,0:T(8,128)(2,1)S(1)}, u32[]{:S(2)}, u32[]{:S(2)}) collective-permute-start(bf16[128,512]{1,0:T(8,128)(2,1)S(1)} %get-tuple-element.33), channel_id=1, source_target_pairs={{0,0},{4,32},{8,8},{12,40},{16,16},{20,48},{24,24},{28,56},{32,4},... | collective-permute-start | bytes 393224 | tf_op jit(solution)/shard_map/ppermute | solution.py:412
  12.5 10.8 %collective-permute-start.1 = (bf16[128,512]{1,0:T(8,128)(2,1)S(1)}, bf16[128,512]{1,0:T(8,128)(2,1)S(1)}, u32[]{:S(2)}, u32[]{:S(2)}) collective-permute-start(bf16[128,512]{1,0:T(8,128)(2,1)S(1)} %get-tuple-element.34), channel_id=1, source_target_pairs={{0,8},{4,40},{8,16},{12,48},{16,24},{20,56},{24,0},{28,32},{32,12}... | collective-permute-start | bytes 393224 | tf_op jit(solution)/shard_map/ppermute | solution.py:412
  13.6 9.7 %collective-permute-start.2 = (bf16[128,512]{1,0:T(8,128)(2,1)S(1)}, bf16[128,512]{1,0:T(8,128)(2,1)S(1)}, u32[]{:S(2)}, u32[]{:S(2)}) collective-permute-start(bf16[128,512]{1,0:T(8,128)(2,1)S(1)} %get-tuple-element.35), channel_id=1, source_target_pairs={{0,16},{4,48},{8,24},{12,56},{16,0},{20,32},{24,8},{28,40},{32,20}... | collective-permute-start | bytes 393224 | tf_op jit(solution)/shard_map/ppermute | solution.py:412
  19.1 6.8 %collective-permute-start.3 = (bf16[128,512]{1,0:T(8,128)(2,1)S(1)}, bf16[128,512]{1,0:T(8,128)(2,1)S(1)}, u32[]{:S(2)}, u32[]{:S(2)}) collective-permute-start(bf16[128,512]{1,0:T(8,128)(2,1)S(1)} %get-tuple-element.36), channel_id=1, source_target_pairs={{0,24},{4,56},{8,0},{12,32},{16,8},{20,40},{24,16},{28,48},{32,28}... | collective-permute-start | bytes 393224 | tf_op jit(solution)/shard_map/ppermute | solution.py:412
  23.2 34.3 %copy-start.1 = (bf16[256,512]{1,0:T(8,128)(2,1)}, bf16[256,512]{1,0:T(8,128)(2,1)S(1)}, u32[]{:S(2)}) copy-start(bf16[256,512]{1,0:T(8,128)(2,1)S(1)} %get-tuple-element.32.refs_5_.refs_1_) | copy-start | bytes 786436
  26.5 8.7 %collective-permute-start.5 = (bf16[512,384]{1,0:T(8,128)(2,1)S(1)}, bf16[512,384]{1,0:T(8,128)(2,1)}, u32[]{:S(2)}, u32[]{:S(2)}) collective-permute-start(bf16[512,384]{1,0:T(8,128)(2,1)S(1)} %bitcast.7), channel_id=1, source_target_pairs={{0,1},{1,2},{2,3},{3,0},{32,35},{33,32},{34,33},{35,34},{4,5},{5,6... | collective-permute-start | bytes 1179656 | tf_op jit(solution)/shard_map/ppermute | solution.py:425
  30.4 7.9 %collective-permute-start.7 = (bf16[512,384]{1,0:T(8,128)(2,1)S(1)}, bf16[512,384]{1,0:T(8,128)(2,1)}, u32[]{:S(2)}, u32[]{:S(2)}) collective-permute-start(bf16[512,384]{1,0:T(8,128)(2,1)S(1)} %bitcast.8), channel_id=1, source_target_pairs={{0,3},{1,0},{2,1},{3,2},{32,33},{33,34},{34,35},{35,32},{4,7},{5,4... | collective-permute-start | bytes 1179656 | tf_op jit(solution)/shard_map/ppermute | solution.py:425
  30.4 15.2 %all-to-all-start = ((bf16[16,128,128]{2,1,0:T(8,128)(2,1)}), bf16[16,128,128]{2,1,0:T(8,128)(2,1)S(1)}, u32[]{:S(2)}, u32[]{:S(2)}) async-start(bf16[16,128,128]{2,1,0:T(8,128)(2,1)} %get-tuple-element.39), calls=%async_computation | async-start | bytes 1048576 | tf_op jit(solution)/shard_map/all_to_all | solution.py:466
  34.0 4.8 %collective-permute-start.4 = (bf16[512,384]{1,0:T(8,128)(2,1)S(1)}, bf16[512,384]{1,0:T(8,128)(2,1)S(1)}, u32[]{:S(2)}, u32[]{:S(2)}) collective-permute-start(bf16[512,384]{1,0:T(8,128)(2,1)S(1)} %bitcast.9), channel_id=1, source_target_pairs={{0,32},{32,0},{1,33},{33,1},{2,34},{34,2},{3,35},{35,3},{4,36},{36... | collective-permute-start | bytes 1179656 | tf_op jit(solution)/shard_map/ppermute | solution.py:416
  35.2 3.6 %collective-permute-start.6 = (bf16[512,384]{1,0:T(8,128)(2,1)}, bf16[512,384]{1,0:T(8,128)(2,1)S(1)}, u32[]{:S(2)}, u32[]{:S(2)}) collective-permute-start(bf16[512,384]{1,0:T(8,128)(2,1)} %collective-permute-done.5.refs_3_.refs_4_), channel_id=1, source_target_pairs={{0,32},{32,0},{1,33},{33,1},{2,34},{34,2},{3,35},{35,3},{4,36},{36... | collective-permute-start | bytes 1179656 | tf_op jit(solution)/shard_map/ppermute | solution.py:416
  38.3 1.9 %collective-permute-start.8 = (bf16[512,384]{1,0:T(8,128)(2,1)}, bf16[512,384]{1,0:T(8,128)(2,1)S(1)}, u32[]{:S(2)}, u32[]{:S(2)}) collective-permute-start(bf16[512,384]{1,0:T(8,128)(2,1)} %collective-permute-done.7.refs_5_.refs_6_), channel_id=1, source_target_pairs={{0,32},{32,0},{1,33},{33,1},{2,34},{34,2},{3,35},{35,3},{4,36},{36... | collective-permute-start | bytes 1179656 | tf_op jit(solution)/shard_map/ppermute | solution.py:416
  38.3 19.3 %collective-permute-start.10 = (bf16[512,384]{1,0:T(8,128)(2,1)}, bf16[512,384]{1,0:T(8,128)(2,1)S(1)}, u32[]{:S(2)}, u32[]{:S(2)}) collective-permute-start(bf16[512,384]{1,0:T(8,128)(2,1)} %collective-permute-done.5.refs_3_.refs_4_), channel_id=1, source_target_pairs={{0,33},{1,34},{2,35},{3,32},{32,3},{33,0},{34,1},{35,2},{4,37},{5,... | collective-permute-start | bytes 1179656 | tf_op jit(solution)/shard_map/ppermute | solution.py:425
  38.7 18.9 %collective-permute-start.9 = (bf16[512,384]{1,0:T(8,128)(2,1)}, bf16[512,384]{1,0:T(8,128)(2,1)S(1)}, u32[]{:S(2)}, u32[]{:S(2)}) collective-permute-start(bf16[512,384]{1,0:T(8,128)(2,1)} %collective-permute-done.5.refs_3_.refs_4_), channel_id=1, source_target_pairs={{0,1},{1,2},{2,3},{3,0},{32,35},{33,32},{34,33},{35,34},{4,5},{5,6... | collective-permute-start | bytes 1179656 | tf_op jit(solution)/shard_map/ppermute | solution.py:425
  43.3 0.7 copy-start.2
  44.0 0.8 copy-start.4
  44.8 0.7 copy-start.6
  45.6 1.0 copy-start.3
  46.6 1.0 copy-start.5
  47.6 1.0 copy-start.7
  59.3 6.8 %collective-permute-start.11 = (f32[8,512]{1,0:T(8,128)S(1)}, f32[8,512]{1,0:T(8,128)S(1)}, u32[]{:S(2)}, u32[]{:S(2)}) collective-permute-start(f32[8,512]{1,0:T(8,128)S(1)} %get-tuple-element.41.refs_4_.refs_6_), channel_id=1, source_target_pairs={{0,8},{8,16},{16,24},{24,0},{1,9},{9,17},{17,25},{25,1},{2,10},{10... | collective-permute-start | bytes 49160 | tf_op jit(solution)/shard_map/ppermute | solution.py:403
  59.4 6.7 %collective-permute-start.12 = (f32[8,512]{1,0:T(8,128)S(1)}, f32[8,512]{1,0:T(8,128)S(1)}, u32[]{:S(2)}, u32[]{:S(2)}) collective-permute-start(f32[8,512]{1,0:T(8,128)S(1)} %get-tuple-element.41.refs_4_.refs_6_), channel_id=1, source_target_pairs={{0,16},{8,24},{16,0},{24,8},{1,17},{9,25},{17,1},{25,9},{2,18},{10... | collective-permute-start | bytes 49160 | tf_op jit(solution)/shard_map/ppermute | solution.py:403
  62.8 3.3 %collective-permute-start.13 = (f32[8,512]{1,0:T(8,128)S(1)}, f32[8,512]{1,0:T(8,128)S(1)}, u32[]{:S(2)}, u32[]{:S(2)}) collective-permute-start(f32[8,512]{1,0:T(8,128)S(1)} %get-tuple-element.41.refs_4_.refs_6_), channel_id=1, source_target_pairs={{0,24},{8,0},{16,8},{24,16},{1,25},{9,1},{17,9},{25,17},{2,26},{10... | collective-permute-start | bytes 49160 | tf_op jit(solution)/shard_map/ppermute | solution.py:403
  67.2 9.7 %collective-permute-start.15 = (bf16[512,128]{1,0:T(8,128)(2,1)S(1)}, bf16[512,128]{1,0:T(8,128)(2,1)S(1)}, u32[]{:S(2)}, u32[]{:S(2)}) collective-permute-start(bf16[512,128]{1,0:T(8,128)(2,1)S(1)} %get-tuple-element.42.refs_1_.refs_7_), channel_id=1, source_target_pairs={{0,1},{1,2},{2,3},{3,0},{32,35},{33,32},{34,33},{35,34},{4,5},{5,6... | collective-permute-start | bytes 393224 | tf_op jit(solution)/shard_map/ppermute | solution.py:425
  69.6 7.3 %collective-permute-start.16 = (bf16[512,128]{1,0:T(8,128)(2,1)S(1)}, bf16[512,128]{1,0:T(8,128)(2,1)S(1)}, u32[]{:S(2)}, u32[]{:S(2)}) collective-permute-start(bf16[512,128]{1,0:T(8,128)(2,1)S(1)} %get-tuple-element.42.refs_1_.refs_7_), channel_id=1, source_target_pairs={{0,3},{1,0},{2,1},{3,2},{32,33},{33,34},{34,35},{35,32},{4,7},{5,4... | collective-permute-start | bytes 393224 | tf_op jit(solution)/shard_map/ppermute | solution.py:425
  69.6 10.8 %collective-permute-start.14 = (bf16[512,128]{1,0:T(8,128)(2,1)S(1)}, bf16[512,128]{1,0:T(8,128)(2,1)S(1)}, u32[]{:S(2)}, u32[]{:S(2)}) collective-permute-start(bf16[512,128]{1,0:T(8,128)(2,1)S(1)} %get-tuple-element.42.refs_1_.refs_7_), channel_id=1, source_target_pairs={{0,32},{32,0},{1,33},{33,1},{2,34},{34,2},{3,35},{35,3},{4,36},{36... | collective-permute-start | bytes 393224 | tf_op jit(solution)/shard_map/ppermute | solution.py:416
  76.9 3.5 %collective-permute-start.17 = (bf16[512,128]{1,0:T(8,128)(2,1)S(1)}, bf16[512,128]{1,0:T(8,128)(2,1)S(1)}, u32[]{:S(2)}, u32[]{:S(2)}) collective-permute-start(bf16[512,128]{1,0:T(8,128)(2,1)S(1)} %get-tuple-element.43.refs_9_), channel_id=1, source_target_pairs={{0,32},{32,0},{1,33},{33,1},{2,34},{34,2},{3,35},{35,3},{4,36},{36... | collective-permute-start | bytes 393224 | tf_op jit(solution)/shard_map/ppermute | solution.py:416
  77.0 3.4 %collective-permute-start.18 = (bf16[512,128]{1,0:T(8,128)(2,1)S(1)}, bf16[512,128]{1,0:T(8,128)(2,1)S(1)}, u32[]{:S(2)}, u32[]{:S(2)}) collective-permute-start(bf16[512,128]{1,0:T(8,128)(2,1)S(1)} %get-tuple-element.44.refs_11_), channel_id=1, source_target_pairs={{0,32},{32,0},{1,33},{33,1},{2,34},{34,2},{3,35},{35,3},{4,36},{36... | collective-permute-start | bytes 393224 | tf_op jit(solution)/shard_map/ppermute | solution.py:416
  77.5 7.6 %collective-permute-start.19 = (bf16[512,128]{1,0:T(8,128)(2,1)S(1)}, bf16[512,128]{1,0:T(8,128)(2,1)S(1)}, u32[]{:S(2)}, u32[]{:S(2)}) collective-permute-start(bf16[512,128]{1,0:T(8,128)(2,1)S(1)} %get-tuple-element.43.refs_9_), channel_id=1, source_target_pairs={{0,1},{1,2},{2,3},{3,0},{32,35},{33,32},{34,33},{35,34},{4,5},{5,6... | collective-permute-start | bytes 393224 | tf_op jit(solution)/shard_map/ppermute | solution.py:425
  78.9 6.2 %collective-permute-start.20 = (bf16[512,128]{1,0:T(8,128)(2,1)S(1)}, bf16[512,128]{1,0:T(8,128)(2,1)S(1)}, u32[]{:S(2)}, u32[]{:S(2)}) collective-permute-start(bf16[512,128]{1,0:T(8,128)(2,1)S(1)} %get-tuple-element.43.refs_9_), channel_id=1, source_target_pairs={{0,33},{1,34},{2,35},{3,32},{32,3},{33,0},{34,1},{35,2},{4,37},{5,... | collective-permute-start | bytes 393224 | tf_op jit(solution)/shard_map/ppermute | solution.py:425
  85.1 19.6 %all-to-all-start.1 = ((bf16[16,128,128]{2,1,0:T(8,128)(2,1)}), bf16[16,128,128]{2,1,0:T(8,128)(2,1)S(1)}, u32[]{:S(2)}, u32[]{:S(2)}) async-start(bf16[16,128,128]{2,1,0:T(8,128)(2,1)} %relay.3), calls=%async_computation.1 | async-start | bytes 1048576 | tf_op jit(solution)/shard_map/all_to_all | solution.py:513
  92.0 17.6 %copy-start.8 = (bf16[128,512]{1,0:T(8,128)(2,1)S(1)}, bf16[128,512]{1,0:T(8,128)(2,1)}, u32[]{:S(2)}) copy-start(bf16[128,512]{1,0:T(8,128)(2,1)} %get-tuple-element.51.refs_6_) | copy-start | bytes 393220
  92.0 17.6 %copy-start.9 = (bf16[128,512]{1,0:T(8,128)(2,1)S(1)}, bf16[128,512]{1,0:T(8,128)(2,1)}, u32[]{:S(2)}) copy-start(bf16[128,512]{1,0:T(8,128)(2,1)} %get-tuple-element.52.refs_7_) | copy-start | bytes 393220
  92.0 16.5 %collective-permute-start.21 = (bf16[128,512]{1,0:T(8,128)(2,1)S(1)}, bf16[128,512]{1,0:T(8,128)(2,1)S(1)}, u32[]{:S(2)}, u32[]{:S(2)}) collective-permute-start(bf16[128,512]{1,0:T(8,128)(2,1)S(1)} %get-tuple-element.46.refs_8_), channel_id=1, source_target_pairs={{0,0},{4,32},{8,8},{12,40},{16,16},{20,48},{24,24},{28,56},{32,4},... | collective-permute-start | bytes 393224 | tf_op jit(solution)/shard_map/ppermute | solution.py:412
  96.3 12.2 %collective-permute-start.22 = (bf16[128,512]{1,0:T(8,128)(2,1)}, bf16[128,512]{1,0:T(8,128)(2,1)S(1)}, u32[]{:S(2)}, u32[]{:S(2)}) collective-permute-start(bf16[128,512]{1,0:T(8,128)(2,1)} %get-tuple-element.53), channel_id=1, source_target_pairs={{0,8},{4,40},{8,16},{12,48},{16,24},{20,56},{24,0},{28,32},{32,12}... | collective-permute-start | bytes 393224 | tf_op jit(solution)/shard_map/ppermute | solution.py:412
  98.4 10.1 %collective-permute-start.23 = (bf16[128,512]{1,0:T(8,128)(2,1)}, bf16[128,512]{1,0:T(8,128)(2,1)S(1)}, u32[]{:S(2)}, u32[]{:S(2)}) collective-permute-start(bf16[128,512]{1,0:T(8,128)(2,1)} %get-tuple-element.54), channel_id=1, source_target_pairs={{0,16},{4,48},{8,24},{12,56},{16,0},{20,32},{24,8},{28,40},{32,20}... | collective-permute-start | bytes 393224 | tf_op jit(solution)/shard_map/ppermute | solution.py:412
  102.6 7.0 %collective-permute-start.24 = (bf16[128,512]{1,0:T(8,128)(2,1)}, bf16[128,512]{1,0:T(8,128)(2,1)S(1)}, u32[]{:S(2)}, u32[]{:S(2)}) collective-permute-start(bf16[128,512]{1,0:T(8,128)(2,1)} %get-tuple-element.55), channel_id=1, source_target_pairs={{0,24},{4,56},{8,0},{12,32},{16,8},{20,40},{24,16},{28,48},{32,28}... | collective-permute-start | bytes 393224 | tf_op jit(solution)/shard_map/ppermute | solution.py:412

commit v7 on v6

--- a/solution.py
+++ b/solution.py
@@ -110,12 +110,13 @@
 
 
 def project_all(
-    info, x_far, cot_far, wo_far, w_ref, k0, k1, k2, k3, slope_ref, gate_ref, gm_ref,
-    xn_ref, act_ref, x_ref, cot_ref, wo_ref, few, buf, sems,
+    info, x_far, cot_far, wo_far, w_ref, k0, k1, k2, k3, slope_ref, gate_far, gm_far,
+    gate_ref, gm_ref, xn_ref, act_ref, x_ref, cot_ref, wo_ref, few, buf, sems,
 ):
     (got_x,) = fetched([(x_far, x_ref)], few)
-    copies = columns(w_ref, buf, sems, (3, 1, 2, 0))
+    copies = columns(w_ref, buf, sems, (3, 1, 0))
     rest = fetched([(cot_far, cot_ref), (wo_far, wo_ref)], few.at[pl.ds(1, 2)])
+    copies += columns(w_ref, buf.at[pl.ds(3, 1)], sems.at[pl.ds(3, 1)], (2,))
     got_x.wait()
     normed, _ = normalize(x_ref[...].astype(F32))
     xn_ref[...] = normed.astype(BF)
@@ -129,18 +130,25 @@
             lane = pl.multiple_of(((info[2] + k) & 3) * HS, HS)
             out[:, part * HS : (part + 1) * HS] = act_ref[:, pl.ds(lane, HS)]
 
-    for part in range(4):
-        copies[part].wait()
-        act, slope = silu_parts(dot(xn_ref[...], buf[part]))
-        slope_ref[part] = slope.astype(BF)
-        if part < 3:
-            put(act * (inside, inside / length, 0.5 * SCALE)[part], part)
-    gate_ref[...] = act.astype(BF)
+    def project(slot, which):
+        copies[slot].wait()
+        act, slope = silu_parts(dot(xn_ref[...], buf[slot]))
+        slope_ref[which] = slope.astype(BF)
+        return act
+
+    put(project(0, 0) * inside, 0)
+    put(project(1, 1) * (inside / length), 1)
+    gate_ref[...] = project(2, 3).astype(BF)
+    leaving = fetched([(gate_ref, gate_far)], few.at[pl.ds(3, 1)])
     for copy in rest:
         copy.wait()
     gm = dot(cot_ref[...], wo_ref[...], NT)
     gm_ref[...] = gm.astype(BF)
+    leaving += fetched([(gm_ref, gm_far)], few.at[pl.ds(4, 1)])
     put(gm * gate_ref[...].astype(F32), 3)
+    put(project(3, 2) * (0.5 * SCALE), 2)
+    for copy in leaving:
+        copy.wait()
 
 
 def arrange(info, a0, a1, a2, a3, out_ref):
@@ -442,10 +450,11 @@
     *sent, slope, gate, gm = call(
         project_all, "project_all", (1,), [SMEM, far, far, far, far],
         [shaped((128, 512))] * 4 + [shaped((4, 128, 512))] + [pltpu.HBM((128, 512), BF)] * 2,
-        [held] * 5 + [pl.BlockSpec((128, 512), lambda i: (0, 0))] * 2,
+        [held] * 5 + [far] * 2,
         [
+            pltpu.VMEM((128, 512), BF), pltpu.VMEM((128, 512), BF),
             pltpu.VMEM((128, 1024), BF), pltpu.VMEM((128, 512), BF), pltpu.VMEM((128, 1024), BF),
-            pltpu.VMEM((128, 1024), BF), pltpu.VMEM((512, 1024), BF), pltpu.SemaphoreType.DMA((3,)),
+            pltpu.VMEM((128, 1024), BF), pltpu.VMEM((512, 1024), BF), pltpu.SemaphoreType.DMA((5,)),
         ] + weights(4), 700_000_000, (), 16,
     )(info, x_rows, cot, w_out, w_proj)
     parts = [crossed(v, k) for k, v in enumerate(sent)]

time: 114 us -> 113 us (level)
  transfers between devices with their start and end apart: 27 -> 27, of which waited for: 4 -> 4; matrix products, arithmetic and copies ran while one was open for 0% -> 0% of each run, Pallas kernels for 30% -> 31%
where the time goes in v7:
time: 113 us
  starting transfers between devices  51.5 us (46%)
  Pallas kernels  45.4 us (40%)
  waiting for transfers between devices  8.26 us (7%)
  local copies, waits for them, and re-layouts  5.49 us (5%)
  between operations  1.85 us (2%)
    pallas_call x15, Pallas kernels, run(): got = made(*pinned, *after, *carry)  45.4 us
    ppermute x8, starting transfers between devices, crossed(): return lax.ppermute(value, ('c', 'y', 'xh'), pairs)  26.2 us
    ppermute x8, starting transfers between devices, along(): return lax.ppermute(value, ('c', 'z'), pairs)  9.73 us
    unnamed x23, local copies, waits for them, and re-layouts  5.41 us
    ppermute x6, starting transfers between devices, across(): return lax.ppermute(value, 'c', [(0, 1), (1, 0)])  4.27 us
    all_to_all x1, starting transfers between devices, per_device(): returned = lax.all_to_all(leaving, ('xl', 'xh', 'y'), 0, 0, tiled=True)  4.16 us
    ppermute x8, waiting for transfers between devices, crossed(): return lax.ppermute(value, ('c', 'y', 'xh'), pairs)  3.8 us
    all_to_all x1, starting transfers between devices, per_device(): arrived = lax.all_to_all(sent_cand, ('xl', 'xh', 'y'), 0, 0, tiled=True)  3.69 us
  transfers between devices with their start and end apart: 27, of which 4 were waited for; matrix products, arithmetic and copies ran while one was open for 0% of the time, Pallas kernels for 31%

profile of v7, /device:TPU:1, one launch (start us, length us, event | category | flops | bytes accessed | tf_op | source)
XLA Modules:
  0.0 112.5 jit_solution(9992902485097364356)
XLA Ops:
  1.4 0.1 stack.19.refs_0_
  1.4 4.6 %project_all.1 = (bf16[128,512]{1,0:T(8,128)(2,1)S(1)}, bf16[128,512]{1,0:T(8,128)(2,1)S(1)}, bf16[128,512]{1,0:T(8,128)(2,1)S(1)}, bf16[128,512]{1,0:T(8,128)(2...) custom-call(s32[5]{0:T(128)S(1)} %stack.19.refs_0_, ...), custom_call_target="tpu_custom_call" | custom-call | flops 700000000 | bytes 1048576 | tf_op jit(solution)/shard_map/project_all/pallas_call | solution.py:63
  6.0 6.0 %collective-permute-start = (bf16[128,512]{1,0:T(8,128)(2,1)S(1)}, bf16[128,512]{1,0:T(8,128)(2,1)S(1)}, u32[]{:S(2)}, u32[]{:S(2)}) collective-permute-start(bf16[128,512]{1,0:T(8,128)(2,1)S(1)} %get-tuple-element.33), channel_id=1, source_target_pairs={{0,0},{4,32},{8,8},{12,40},{16,16},{20,48},{24,24},{28,56},{32,4},... | collective-permute-start | bytes 393224 | tf_op jit(solution)/shard_map/ppermute | solution.py:420
  12.1 1.1 collective-permute-start.1
  13.2 5.6 %collective-permute-start.2 = (bf16[128,512]{1,0:T(8,128)(2,1)S(1)}, bf16[128,512]{1,0:T(8,128)(2,1)S(1)}, u32[]{:S(2)}, u32[]{:S(2)}) collective-permute-start(bf16[128,512]{1,0:T(8,128)(2,1)S(1)} %get-tuple-element.35), channel_id=1, source_target_pairs={{0,16},{4,48},{8,24},{12,56},{16,0},{20,32},{24,8},{28,40},{32,20}... | collective-permute-start | bytes 393224 | tf_op jit(solution)/shard_map/ppermute | solution.py:420
  18.7 0.8 collective-permute-start.3
  19.5 0.1 copy.15.refs_0_
  19.7 3.1 %project_cand.1 = (bf16[16,128,128]{2,1,0:T(8,128)(2,1)}, bf16[256,512]{1,0:T(8,128)(2,1)S(1)}) custom-call(s32[256,1]{1,0:T(8,128)S(1)} %copy.15.refs_0_, bf16[256,1024]{1,0:T(8,128)(2,1)S(1)} %copy-done, bf16[1024,2048]{1,0:T(8,128)(2,1)} %refs_5_.1, bf16[4,128,512]{2,1,0:T(8,128)(2,1)S(1)} %get-tuple-element.31.refs_3_), custom_call_target="tpu_custom_call" | custom-call | flops 700000000 | bytes 1048576 | tf_op jit(solution)/shard_map/project_cand/pallas_call | solution.py:63
  22.9 2.6 %collective-permute-done.3.refs_4_ = bf16[128,512]{1,0:T(8,128)(2,1)S(1)} collective-permute-done((bf16[128,512]{1,0:T(8,128)(2,1)S(1)}, bf16[128,512]{1,0:T(8,128)(2,1)S(1)}, u32[]{:S(2)}, u32[]{:S(2)}) %collective-permute-start.3) | collective-permute-done | bytes 131104 | tf_op jit(solution)/shard_map/ppermute | solution.py:420
  25.5 0.6 arrange.1
  26.1 3.8 %collective-permute-start.5 = (bf16[512,384]{1,0:T(8,128)(2,1)S(1)}, bf16[512,384]{1,0:T(8,128)(2,1)}, u32[]{:S(2)}, u32[]{:S(2)}) collective-permute-start(bf16[512,384]{1,0:T(8,128)(2,1)S(1)} %bitcast.7), channel_id=1, source_target_pairs={{0,1},{1,2},{2,3},{3,0},{32,35},{33,32},{34,33},{35,34},{4,5},{5,6... | collective-permute-start | bytes 1179656 | tf_op jit(solution)/shard_map/ppermute | solution.py:433
  30.0 3.7 %all-to-all-start = ((bf16[16,128,128]{2,1,0:T(8,128)(2,1)}), bf16[16,128,128]{2,1,0:T(8,128)(2,1)S(1)}, u32[]{:S(2)}, u32[]{:S(2)}) async-start(bf16[16,128,128]{2,1,0:T(8,128)(2,1)} %get-tuple-element.39), calls=%async_computation | async-start | bytes 1048576 | tf_op jit(solution)/shard_map/all_to_all | solution.py:475
  33.7 1.1 %collective-permute-start.4 = (bf16[512,384]{1,0:T(8,128)(2,1)S(1)}, bf16[512,384]{1,0:T(8,128)(2,1)S(1)}, u32[]{:S(2)}, u32[]{:S(2)}) collective-permute-start(bf16[512,384]{1,0:T(8,128)(2,1)S(1)} %bitcast.9), channel_id=1, source_target_pairs={{0,32},{32,0},{1,33},{33,1},{2,34},{34,2},{3,35},{35,3},{4,36},{36... | collective-permute-start | bytes 1179656 | tf_op jit(solution)/shard_map/ppermute | solution.py:424
  34.8 0.1 collective-permute-start.6
  34.9 3.0 %collective-permute-done.7.refs_5_.refs_6_ = bf16[512,384]{1,0:T(8,128)(2,1)} collective-permute-done((bf16[512,384]{1,0:T(8,128)(2,1)S(1)}, bf16[512,384]{1,0:T(8,128)(2,1)}, u32[]{:S(2)}, u32[]{:S(2)}) %collective-permute-start.7) | collective-permute-done | bytes 393248 | tf_op jit(solution)/shard_map/ppermute | solution.py:433
  37.9 0.4 collective-permute-start.10
  38.3 0.1 collective-permute-start.9
  38.4 1.4 %collective-permute-done.8.refs_6_.refs_7_ = bf16[512,384]{1,0:T(8,128)(2,1)S(1)} collective-permute-done((bf16[512,384]{1,0:T(8,128)(2,1)}, bf16[512,384]{1,0:T(8,128)(2,1)S(1)}, u32[]{:S(2)}, u32[]{:S(2)}) %collective-permute-start.8) | collective-permute-done | bytes 393248 | tf_op jit(solution)/shard_map/ppermute | solution.py:424
  39.8 3.1 %hist_begin.1.refs_7_.refs_8_ = f32[512,128]{1,0:T(8,128)S(1)} custom-call(s32[5]{0:T(128)S(1)} %stack.19.refs_0_, bf16[512,384]{1,0:T(8,128)(2,1)S(1)} %bitcast.10, bf16[512,384]{1,0:T(8,128)(2,1)S(1)} %collective-permute-done.4.refs_2_.refs_3_, bf16[512,384]{1,0:T(8,128)(2,1)} %collective-permute-done.5.refs_3_.refs_4_, ...), custom_call_target="tpu_custom_call" | custom-call | flops 1000 | bytes 1000 | tf_op jit(solution)/shard_map/hist_begin/pallas_call | solution.py:63
  42.9 0.7 copy-done.2
  43.6 0.8 copy-done.4
  44.4 0.7 copy-done.6
  45.2 1.0 copy-done.3
  46.2 1.0 copy-done.5
  47.2 1.0 copy-done.7
  48.2 9.0 %cand_attend.2.refs_9_.refs_3_ = f32[2048,128]{1,0:T(8,128)S(1)} custom-call(bf16[16,128,128]{2,1,0:T(8,128)(2,1)S(1)} %all-to-all-done.refs_0_, bf16[512,384]{1,0:T(8,128)(2,1)S(1)} %bitcast.11, bf16[512,384]{1,0:T(8,128)(2,1)S(1)} %copy-done.3, bf16[512,384]{1,0:T(8,128)(2,1)} %collective-permute-done.5.refs_3_.refs_4_, bf16[512,384]{1,0:T(8,128)(2,1)S(1)} %copy-done.5, ...), custom_call_target="tpu_custom_call" | custom-call | flops 3600000000 | bytes 1048576 | tf_op jit(solution)/shard_map/cand_attend/pallas_call | solution.py:63
  57.2 1.7 %hist_end.1 = (f32[512,128]{1,0:T(8,128)S(1)}, f32[8,512]{1,0:T(8,128)S(1)}) custom-call(s32[5]{0:T(128)S(1)} %stack.19.refs_0_, bf16[128,512]{1,0:T(8,128)(2,1)S(1)} %collective-permute-done.refs_1_, bf16[128,512]{1,0:T(8,128)(2,1)S(1)} %collective-permute-done.1.refs_2_, bf16[128,512]{1,0:T(8,128)(2,1)S(1)} %collective-permute-done.2.refs_3_, ...), custom_call_target="tpu_custom_call" | custom-call | flops 400000000 | bytes 1048576 | tf_op jit(solution)/shard_map/hist_end/pallas_call | solution.py:63
  58.9 0.0 collective-permute-start.11
  59.0 3.5 %collective-permute-start.12 = (f32[8,512]{1,0:T(8,128)S(1)}, f32[8,512]{1,0:T(8,128)S(1)}, u32[]{:S(2)}, u32[]{:S(2)}) collective-permute-start(f32[8,512]{1,0:T(8,128)S(1)} %get-tuple-element.41.refs_4_.refs_6_), channel_id=1, source_target_pairs={{0,16},{8,24},{16,0},{24,8},{1,17},{9,25},{17,1},{25,9},{2,18},{10... | collective-permute-start | bytes 49160 | tf_op jit(solution)/shard_map/ppermute | solution.py:411
  62.5 3.3 %cand_attend.3.refs_10_.refs_3_ = bf16[16,128,128]{2,1,0:T(8,128)(2,1)} custom-call(bf16[16,128,128]{2,1,0:T(8,128)(2,1)S(1)} %all-to-all-done.refs_0_, bf16[512,384]{1,0:T(8,128)(2,1)S(1)} %collective-permute-done.9.refs_6_.refs_1_.refs_8_.refs_4_, bf16[512,384]{1,0:T(8,128)(2,1)S(1)} %collective-permute-done.10.refs_7_.refs_2_.refs_9_.refs_5_, ...), custom_call_target="tpu_custom_call" | custom-call | flops 1200000000 | bytes 1048576 | tf_op jit(solution)/shard_map/cand_attend/pallas_call | solution.py:63
  65.7 1.0 normed_grads.1
  66.8 2.5 %collective-permute-start.15 = (bf16[512,128]{1,0:T(8,128)(2,1)S(1)}, bf16[512,128]{1,0:T(8,128)(2,1)S(1)}, u32[]{:S(2)}, u32[]{:S(2)}) collective-permute-start(bf16[512,128]{1,0:T(8,128)(2,1)S(1)} %get-tuple-element.42.refs_1_.refs_7_), channel_id=1, source_target_pairs={{0,1},{1,2},{2,3},{3,0},{32,35},{33,32},{34,33},{35,34},{4,5},{5,6... | collective-permute-start | bytes 393224 | tf_op jit(solution)/shard_map/ppermute | solution.py:433
  69.2 2.4 %collective-permute-start.14 = (bf16[512,128]{1,0:T(8,128)(2,1)S(1)}, bf16[512,128]{1,0:T(8,128)(2,1)S(1)}, u32[]{:S(2)}, u32[]{:S(2)}) collective-permute-start(bf16[512,128]{1,0:T(8,128)(2,1)S(1)} %get-tuple-element.42.refs_1_.refs_7_), channel_id=1, source_target_pairs={{0,32},{32,0},{1,33},{33,1},{2,34},{34,2},{3,35},{35,3},{4,36},{36... | collective-permute-start | bytes 393224 | tf_op jit(solution)/shard_map/ppermute | solution.py:424
  71.7 4.8 %hist_dq.1.refs_0_.refs_1_ = bf16[4,128,128]{2,1,0:T(8,128)(2,1)S(1)} custom-call(s32[5]{0:T(128)S(1)} %stack.19.refs_0_, bf16[512,128]{1,0:T(8,128)(2,1)S(1)} %get-tuple-element.42.refs_1_.refs_7_, bf16[512,384]{1,0:T(8,128)(2,1)S(1)} %bitcast.13, bf16[512,384]{1,0:T(8,128)(2,1)S(1)} %copy-done.3, bf16[512,384]{1,0:T(8,128)(2,1)} %collective-permute-done.5.refs_3_.refs_4_, ...), custom_call_target="tpu_custom_call" | custom-call | flops 2000000000 | bytes 1048576 | tf_op jit(solution)/shard_map/hist_dq/pallas_call | solution.py:63
  76.5 0.1 collective-permute-start.17
  76.6 0.5 collective-permute-start.18
  77.1 1.4 %collective-permute-start.19 = (bf16[512,128]{1,0:T(8,128)(2,1)S(1)}, bf16[512,128]{1,0:T(8,128)(2,1)S(1)}, u32[]{:S(2)}, u32[]{:S(2)}) collective-permute-start(bf16[512,128]{1,0:T(8,128)(2,1)S(1)} %get-tuple-element.43.refs_9_), channel_id=1, source_target_pairs={{0,1},{1,2},{2,3},{3,0},{32,35},{33,32},{34,33},{35,34},{4,5},{5,6... | collective-permute-start | bytes 393224 | tf_op jit(solution)/shard_map/ppermute | solution.py:433
  78.5 1.5 %collective-permute-start.20 = (bf16[512,128]{1,0:T(8,128)(2,1)S(1)}, bf16[512,128]{1,0:T(8,128)(2,1)S(1)}, u32[]{:S(2)}, u32[]{:S(2)}) collective-permute-start(bf16[512,128]{1,0:T(8,128)(2,1)S(1)} %get-tuple-element.43.refs_9_), channel_id=1, source_target_pairs={{0,33},{1,34},{2,35},{3,32},{32,3},{33,0},{34,1},{35,2},{4,37},{5,... | collective-permute-start | bytes 393224 | tf_op jit(solution)/shard_map/ppermute | solution.py:433
  80.0 4.6 %hist_dkv_begin.1.refs_0_.refs_8_ = f32[2,256,256]{2,1,0:T(8,128)S(1)} custom-call(s32[5]{0:T(128)S(1)} %stack.19.refs_0_, bf16[512,384]{1,0:T(8,128)(2,1)S(1)} %bitcast.14, bf16[512,384]{1,0:T(8,128)(2,1)S(1)} %copy-done.3, bf16[512,384]{1,0:T(8,128)(2,1)} %collective-permute-done.5.refs_3_.refs_4_, bf16[512,384]{1,0:T(8,128)(2,1)S(1)} %copy-done.5, ...), custom_call_target="tpu_custom_call" | custom-call | flops 2000000000 | bytes 1048576 | tf_op jit(solution)/shard_map/hist_dkv_begin/pallas_call | solution.py:63
  84.7 4.2 %all-to-all-start.1 = ((bf16[16,128,128]{2,1,0:T(8,128)(2,1)}), bf16[16,128,128]{2,1,0:T(8,128)(2,1)S(1)}, u32[]{:S(2)}, u32[]{:S(2)}) async-start(bf16[16,128,128]{2,1,0:T(8,128)(2,1)} %relay.3), calls=%async_computation.1 | async-start | bytes 1048576 | tf_op jit(solution)/shard_map/all_to_all | solution.py:522
  88.9 2.7 %hist_dkv_end.1 = (bf16[128,512]{1,0:T(8,128)(2,1)S(1)}, bf16[128,512]{1,0:T(8,128)(2,1)}, bf16[128,512]{1,0:T(8,128)(2,1)}, bf16[128,512]{1,0:T(8,128)(2,1)}) custom-call(s32[5]{0:T(128)S(1)} %stack.19.refs_0_, bf16[4,128,128]{2,1,0:T(8,128)(2,1)S(1)} %hist_dq.1.refs_0_.refs_1_, bf16[512,128]{1,0:T(8,128)(2,1)S(1)} %get-tuple-element.45.refs_2_, ...), custom_call_target="tpu_custom_call" | custom-call | flops 800000000 | bytes 1048576 | tf_op jit(solution)/shard_map/hist_dkv_end/pallas_call | solution.py:63
  91.6 4.3 %collective-permute-start.21 = (bf16[128,512]{1,0:T(8,128)(2,1)S(1)}, bf16[128,512]{1,0:T(8,128)(2,1)S(1)}, u32[]{:S(2)}, u32[]{:S(2)}) collective-permute-start(bf16[128,512]{1,0:T(8,128)(2,1)S(1)} %get-tuple-element.46.refs_8_), channel_id=1, source_target_pairs={{0,0},{4,32},{8,8},{12,40},{16,16},{20,48},{24,24},{28,56},{32,4},... | collective-permute-start | bytes 393224 | tf_op jit(solution)/shard_map/ppermute | solution.py:420
  95.9 2.1 %collective-permute-start.22 = (bf16[128,512]{1,0:T(8,128)(2,1)}, bf16[128,512]{1,0:T(8,128)(2,1)S(1)}, u32[]{:S(2)}, u32[]{:S(2)}) collective-permute-start(bf16[128,512]{1,0:T(8,128)(2,1)} %get-tuple-element.53), channel_id=1, source_target_pairs={{0,8},{4,40},{8,16},{12,48},{16,24},{20,56},{24,0},{28,32},{32,12}... | collective-permute-start | bytes 393224 | tf_op jit(solution)/shard_map/ppermute | solution.py:420
  98.0 4.2 %collective-permute-start.23 = (bf16[128,512]{1,0:T(8,128)(2,1)}, bf16[128,512]{1,0:T(8,128)(2,1)S(1)}, u32[]{:S(2)}, u32[]{:S(2)}) collective-permute-start(bf16[128,512]{1,0:T(8,128)(2,1)} %get-tuple-element.54), channel_id=1, source_target_pairs={{0,16},{4,48},{8,24},{12,56},{16,0},{20,32},{24,8},{28,40},{32,20}... | collective-permute-start | bytes 393224 | tf_op jit(solution)/shard_map/ppermute | solution.py:420
  102.2 2.1 %collective-permute-start.24 = (bf16[128,512]{1,0:T(8,128)(2,1)}, bf16[128,512]{1,0:T(8,128)(2,1)S(1)}, u32[]{:S(2)}, u32[]{:S(2)}) collective-permute-start(bf16[128,512]{1,0:T(8,128)(2,1)} %get-tuple-element.55), channel_id=1, source_target_pairs={{0,24},{4,56},{8,0},{12,32},{16,8},{20,40},{24,16},{28,48},{32,28}... | collective-permute-start | bytes 393224 | tf_op jit(solution)/shard_map/ppermute | solution.py:420
  104.2 3.8 %cand_close.1 = (bf16[256,1024]{1,0:T(8,128)(2,1)}, bf16[512,1024]{1,0:T(8,128)(2,1)S(1)}, bf16[4,1024,512]{2,1,0:T(8,128)(2,1)S(1)}, bf16[128,1024]{1,0:T(8,128)(2,1)S(1)}, bf16[128,1024]{1,0:T(8,128)(2,1)S(1)}) custom-call(s32[256,1]{1,0:T(8,128)S(1)} %copy.15.refs_0_, bf16[256,512]{1,0:T(8,128)(2,1)} %copy-done.1, ...), custom_call_target="tpu_custom_call" | custom-call | flops 400000000 | bytes 1048576 | tf_op jit(solution)/shard_map/cand_close/pallas_call | solution.py:63
  108.0 1.1 %collective-permute-done.24.refs_11_ = bf16[128,512]{1,0:T(8,128)(2,1)S(1)} collective-permute-done((bf16[128,512]{1,0:T(8,128)(2,1)}, bf16[128,512]{1,0:T(8,128)(2,1)S(1)}, u32[]{:S(2)}, u32[]{:S(2)}) %collective-permute-start.24) | collective-permute-done | bytes 131104 | tf_op jit(solution)/shard_map/ppermute | solution.py:420
  109.2 3.1 %hist_close.1 = (bf16[1,128,1024]{2,1,0:T(8,128)(2,1)}, bf16[1,128,1024]{2,1,0:T(8,128)(2,1)}) custom-call(s32[5]{0:T(128)S(1)} %stack.19.refs_0_, bf16[128,1024]{1,0:T(8,128)(2,1)S(1)} %get-tuple-element.47.refs_1_, bf16[128,1024]{1,0:T(8,128)(2,1)S(1)} %get-tuple-element.48.refs_2_, bf16[4,128,512]{2,1,0:T(8,128)(2,1)S(1)} %get-tuple-element.31.refs_3_, ...), custom_call_target="tpu_custom_call" | custom-call | flops 700000000 | bytes 1048576 | tf_op jit(solution)/shard_map/hist_close/pallas_call | solution.py:63
  (45 shorter events, 0.1 us)
Async XLA Ops:
  0.6 18.9 %copy-start.10 = (s32[256,1]{0,1:T(1,128)S(1)}, s32[256,1]{0,1:T(1,128)}, u32[]{:S(2)}) copy-start(s32[256,1]{0,1:T(1,128)} %param.10) | copy-start | bytes 3076
  0.6 19.1 %copy-start = (bf16[256,1024]{1,0:T(8,128)(2,1)S(1)}, bf16[256,1024]{1,0:T(8,128)(2,1)}, u32[]{:S(2)}) copy-start(bf16[256,1024]{1,0:T(8,128)(2,1)} %refs_3_.3) | copy-start | bytes 1572868
  6.0 16.9 %collective-permute-start = (bf16[128,512]{1,0:T(8,128)(2,1)S(1)}, bf16[128,512]{1,0:T(8,128)(2,1)S(1)}, u32[]{:S(2)}, u32[]{:S(2)}) collective-permute-start(bf16[128,512]{1,0:T(8,128)(2,1)S(1)} %get-tuple-element.33), channel_id=1, source_target_pairs={{0,0},{4,32},{8,8},{12,40},{16,16},{20,48},{24,24},{28,56},{32,4},... | collective-permute-start | bytes 393224 | tf_op jit(solution)/shard_map/ppermute | solution.py:420
  12.1 10.8 %collective-permute-start.1 = (bf16[128,512]{1,0:T(8,128)(2,1)S(1)}, bf16[128,512]{1,0:T(8,128)(2,1)S(1)}, u32[]{:S(2)}, u32[]{:S(2)}) collective-permute-start(bf16[128,512]{1,0:T(8,128)(2,1)S(1)} %get-tuple-element.34), channel_id=1, source_target_pairs={{0,8},{4,40},{8,16},{12,48},{16,24},{20,56},{24,0},{28,32},{32,12}... | collective-permute-start | bytes 393224 | tf_op jit(solution)/shard_map/ppermute | solution.py:420
  13.2 9.7 %collective-permute-start.2 = (bf16[128,512]{1,0:T(8,128)(2,1)S(1)}, bf16[128,512]{1,0:T(8,128)(2,1)S(1)}, u32[]{:S(2)}, u32[]{:S(2)}) collective-permute-start(bf16[128,512]{1,0:T(8,128)(2,1)S(1)} %get-tuple-element.35), channel_id=1, source_target_pairs={{0,16},{4,48},{8,24},{12,56},{16,0},{20,32},{24,8},{28,40},{32,20}... | collective-permute-start | bytes 393224 | tf_op jit(solution)/shard_map/ppermute | solution.py:420
  18.7 6.8 %collective-permute-start.3 = (bf16[128,512]{1,0:T(8,128)(2,1)S(1)}, bf16[128,512]{1,0:T(8,128)(2,1)S(1)}, u32[]{:S(2)}, u32[]{:S(2)}) collective-permute-start(bf16[128,512]{1,0:T(8,128)(2,1)S(1)} %get-tuple-element.36), channel_id=1, source_target_pairs={{0,24},{4,56},{8,0},{12,32},{16,8},{20,40},{24,16},{28,48},{32,28}... | collective-permute-start | bytes 393224 | tf_op jit(solution)/shard_map/ppermute | solution.py:420
  22.9 34.3 %copy-start.1 = (bf16[256,512]{1,0:T(8,128)(2,1)}, bf16[256,512]{1,0:T(8,128)(2,1)S(1)}, u32[]{:S(2)}) copy-start(bf16[256,512]{1,0:T(8,128)(2,1)S(1)} %get-tuple-element.32.refs_5_.refs_1_) | copy-start | bytes 786436
  26.1 8.7 %collective-permute-start.5 = (bf16[512,384]{1,0:T(8,128)(2,1)S(1)}, bf16[512,384]{1,0:T(8,128)(2,1)}, u32[]{:S(2)}, u32[]{:S(2)}) collective-permute-start(bf16[512,384]{1,0:T(8,128)(2,1)S(1)} %bitcast.7), channel_id=1, source_target_pairs={{0,1},{1,2},{2,3},{3,0},{32,35},{33,32},{34,33},{35,34},{4,5},{5,6... | collective-permute-start | bytes 1179656 | tf_op jit(solution)/shard_map/ppermute | solution.py:433
  30.0 7.9 %collective-permute-start.7 = (bf16[512,384]{1,0:T(8,128)(2,1)S(1)}, bf16[512,384]{1,0:T(8,128)(2,1)}, u32[]{:S(2)}, u32[]{:S(2)}) collective-permute-start(bf16[512,384]{1,0:T(8,128)(2,1)S(1)} %bitcast.8), channel_id=1, source_target_pairs={{0,3},{1,0},{2,1},{3,2},{32,33},{33,34},{34,35},{35,32},{4,7},{5,4... | collective-permute-start | bytes 1179656 | tf_op jit(solution)/shard_map/ppermute | solution.py:433
  30.0 15.2 %all-to-all-start = ((bf16[16,128,128]{2,1,0:T(8,128)(2,1)}), bf16[16,128,128]{2,1,0:T(8,128)(2,1)S(1)}, u32[]{:S(2)}, u32[]{:S(2)}) async-start(bf16[16,128,128]{2,1,0:T(8,128)(2,1)} %get-tuple-element.39), calls=%async_computation | async-start | bytes 1048576 | tf_op jit(solution)/shard_map/all_to_all | solution.py:475
  33.7 4.8 %collective-permute-start.4 = (bf16[512,384]{1,0:T(8,128)(2,1)S(1)}, bf16[512,384]{1,0:T(8,128)(2,1)S(1)}, u32[]{:S(2)}, u32[]{:S(2)}) collective-permute-start(bf16[512,384]{1,0:T(8,128)(2,1)S(1)} %bitcast.9), channel_id=1, source_target_pairs={{0,32},{32,0},{1,33},{33,1},{2,34},{34,2},{3,35},{35,3},{4,36},{36... | collective-permute-start | bytes 1179656 | tf_op jit(solution)/shard_map/ppermute | solution.py:424
  34.8 3.6 %collective-permute-start.6 = (bf16[512,384]{1,0:T(8,128)(2,1)}, bf16[512,384]{1,0:T(8,128)(2,1)S(1)}, u32[]{:S(2)}, u32[]{:S(2)}) collective-permute-start(bf16[512,384]{1,0:T(8,128)(2,1)} %collective-permute-done.5.refs_3_.refs_4_), channel_id=1, source_target_pairs={{0,32},{32,0},{1,33},{33,1},{2,34},{34,2},{3,35},{35,3},{4,36},{36... | collective-permute-start | bytes 1179656 | tf_op jit(solution)/shard_map/ppermute | solution.py:424
  37.9 1.9 %collective-permute-start.8 = (bf16[512,384]{1,0:T(8,128)(2,1)}, bf16[512,384]{1,0:T(8,128)(2,1)S(1)}, u32[]{:S(2)}, u32[]{:S(2)}) collective-permute-start(bf16[512,384]{1,0:T(8,128)(2,1)} %collective-permute-done.7.refs_5_.refs_6_), channel_id=1, source_target_pairs={{0,32},{32,0},{1,33},{33,1},{2,34},{34,2},{3,35},{35,3},{4,36},{36... | collective-permute-start | bytes 1179656 | tf_op jit(solution)/shard_map/ppermute | solution.py:424
  37.9 19.3 %collective-permute-start.10 = (bf16[512,384]{1,0:T(8,128)(2,1)}, bf16[512,384]{1,0:T(8,128)(2,1)S(1)}, u32[]{:S(2)}, u32[]{:S(2)}) collective-permute-start(bf16[512,384]{1,0:T(8,128)(2,1)} %collective-permute-done.5.refs_3_.refs_4_), channel_id=1, source_target_pairs={{0,33},{1,34},{2,35},{3,32},{32,3},{33,0},{34,1},{35,2},{4,37},{5,... | collective-permute-start | bytes 1179656 | tf_op jit(solution)/shard_map/ppermute | solution.py:433
  38.3 18.9 %collective-permute-start.9 = (bf16[512,384]{1,0:T(8,128)(2,1)}, bf16[512,384]{1,0:T(8,128)(2,1)S(1)}, u32[]{:S(2)}, u32[]{:S(2)}) collective-permute-start(bf16[512,384]{1,0:T(8,128)(2,1)} %collective-permute-done.5.refs_3_.refs_4_), channel_id=1, source_target_pairs={{0,1},{1,2},{2,3},{3,0},{32,35},{33,32},{34,33},{35,34},{4,5},{5,6... | collective-permute-start | bytes 1179656 | tf_op jit(solution)/shard_map/ppermute | solution.py:433
  42.9 0.7 copy-start.2
  43.6 0.8 copy-start.4
  44.4 0.7 copy-start.6
  45.2 1.0 copy-start.3
  46.2 1.0 copy-start.5
  47.2 1.0 copy-start.7
  58.9 6.8 %collective-permute-start.11 = (f32[8,512]{1,0:T(8,128)S(1)}, f32[8,512]{1,0:T(8,128)S(1)}, u32[]{:S(2)}, u32[]{:S(2)}) collective-permute-start(f32[8,512]{1,0:T(8,128)S(1)} %get-tuple-element.41.refs_4_.refs_6_), channel_id=1, source_target_pairs={{0,8},{8,16},{16,24},{24,0},{1,9},{9,17},{17,25},{25,1},{2,10},{10... | collective-permute-start | bytes 49160 | tf_op jit(solution)/shard_map/ppermute | solution.py:411
  59.0 6.7 %collective-permute-start.12 = (f32[8,512]{1,0:T(8,128)S(1)}, f32[8,512]{1,0:T(8,128)S(1)}, u32[]{:S(2)}, u32[]{:S(2)}) collective-permute-start(f32[8,512]{1,0:T(8,128)S(1)} %get-tuple-element.41.refs_4_.refs_6_), channel_id=1, source_target_pairs={{0,16},{8,24},{16,0},{24,8},{1,17},{9,25},{17,1},{25,9},{2,18},{10... | collective-permute-start | bytes 49160 | tf_op jit(solution)/shard_map/ppermute | solution.py:411
  62.4 3.3 %collective-permute-start.13 = (f32[8,512]{1,0:T(8,128)S(1)}, f32[8,512]{1,0:T(8,128)S(1)}, u32[]{:S(2)}, u32[]{:S(2)}) collective-permute-start(f32[8,512]{1,0:T(8,128)S(1)} %get-tuple-element.41.refs_4_.refs_6_), channel_id=1, source_target_pairs={{0,24},{8,0},{16,8},{24,16},{1,25},{9,1},{17,9},{25,17},{2,26},{10... | collective-permute-start | bytes 49160 | tf_op jit(solution)/shard_map/ppermute | solution.py:411
  66.8 9.7 %collective-permute-start.15 = (bf16[512,128]{1,0:T(8,128)(2,1)S(1)}, bf16[512,128]{1,0:T(8,128)(2,1)S(1)}, u32[]{:S(2)}, u32[]{:S(2)}) collective-permute-start(bf16[512,128]{1,0:T(8,128)(2,1)S(1)} %get-tuple-element.42.refs_1_.refs_7_), channel_id=1, source_target_pairs={{0,1},{1,2},{2,3},{3,0},{32,35},{33,32},{34,33},{35,34},{4,5},{5,6... | collective-permute-start | bytes 393224 | tf_op jit(solution)/shard_map/ppermute | solution.py:433
  69.2 7.3 %collective-permute-start.16 = (bf16[512,128]{1,0:T(8,128)(2,1)S(1)}, bf16[512,128]{1,0:T(8,128)(2,1)S(1)}, u32[]{:S(2)}, u32[]{:S(2)}) collective-permute-start(bf16[512,128]{1,0:T(8,128)(2,1)S(1)} %get-tuple-element.42.refs_1_.refs_7_), channel_id=1, source_target_pairs={{0,3},{1,0},{2,1},{3,2},{32,33},{33,34},{34,35},{35,32},{4,7},{5,4... | collective-permute-start | bytes 393224 | tf_op jit(solution)/shard_map/ppermute | solution.py:433
  69.2 10.8 %collective-permute-start.14 = (bf16[512,128]{1,0:T(8,128)(2,1)S(1)}, bf16[512,128]{1,0:T(8,128)(2,1)S(1)}, u32[]{:S(2)}, u32[]{:S(2)}) collective-permute-start(bf16[512,128]{1,0:T(8,128)(2,1)S(1)} %get-tuple-element.42.refs_1_.refs_7_), channel_id=1, source_target_pairs={{0,32},{32,0},{1,33},{33,1},{2,34},{34,2},{3,35},{35,3},{4,36},{36... | collective-permute-start | bytes 393224 | tf_op jit(solution)/shard_map/ppermute | solution.py:424
  76.5 3.5 %collective-permute-start.17 = (bf16[512,128]{1,0:T(8,128)(2,1)S(1)}, bf16[512,128]{1,0:T(8,128)(2,1)S(1)}, u32[]{:S(2)}, u32[]{:S(2)}) collective-permute-start(bf16[512,128]{1,0:T(8,128)(2,1)S(1)} %get-tuple-element.43.refs_9_), channel_id=1, source_target_pairs={{0,32},{32,0},{1,33},{33,1},{2,34},{34,2},{3,35},{35,3},{4,36},{36... | collective-permute-start | bytes 393224 | tf_op jit(solution)/shard_map/ppermute | solution.py:424
  76.6 3.4 %collective-permute-start.18 = (bf16[512,128]{1,0:T(8,128)(2,1)S(1)}, bf16[512,128]{1,0:T(8,128)(2,1)S(1)}, u32[]{:S(2)}, u32[]{:S(2)}) collective-permute-start(bf16[512,128]{1,0:T(8,128)(2,1)S(1)} %get-tuple-element.44.refs_11_), channel_id=1, source_target_pairs={{0,32},{32,0},{1,33},{33,1},{2,34},{34,2},{3,35},{35,3},{4,36},{36... | collective-permute-start | bytes 393224 | tf_op jit(solution)/shard_map/ppermute | solution.py:424
  77.1 7.6 %collective-permute-start.19 = (bf16[512,128]{1,0:T(8,128)(2,1)S(1)}, bf16[512,128]{1,0:T(8,128)(2,1)S(1)}, u32[]{:S(2)}, u32[]{:S(2)}) collective-permute-start(bf16[512,128]{1,0:T(8,128)(2,1)S(1)} %get-tuple-element.43.refs_9_), channel_id=1, source_target_pairs={{0,1},{1,2},{2,3},{3,0},{32,35},{33,32},{34,33},{35,34},{4,5},{5,6... | collective-permute-start | bytes 393224 | tf_op jit(solution)/shard_map/ppermute | solution.py:433
  78.5 6.1 %collective-permute-start.20 = (bf16[512,128]{1,0:T(8,128)(2,1)S(1)}, bf16[512,128]{1,0:T(8,128)(2,1)S(1)}, u32[]{:S(2)}, u32[]{:S(2)}) collective-permute-start(bf16[512,128]{1,0:T(8,128)(2,1)S(1)} %get-tuple-element.43.refs_9_), channel_id=1, source_target_pairs={{0,33},{1,34},{2,35},{3,32},{32,3},{33,0},{34,1},{35,2},{4,37},{5,... | collective-permute-start | bytes 393224 | tf_op jit(solution)/shard_map/ppermute | solution.py:433
  84.7 19.6 %all-to-all-start.1 = ((bf16[16,128,128]{2,1,0:T(8,128)(2,1)}), bf16[16,128,128]{2,1,0:T(8,128)(2,1)S(1)}, u32[]{:S(2)}, u32[]{:S(2)}) async-start(bf16[16,128,128]{2,1,0:T(8,128)(2,1)} %relay.3), calls=%async_computation.1 | async-start | bytes 1048576 | tf_op jit(solution)/shard_map/all_to_all | solution.py:522
  91.6 17.6 %copy-start.8 = (bf16[128,512]{1,0:T(8,128)(2,1)S(1)}, bf16[128,512]{1,0:T(8,128)(2,1)}, u32[]{:S(2)}) copy-start(bf16[128,512]{1,0:T(8,128)(2,1)} %get-tuple-element.51.refs_6_) | copy-start | bytes 393220
  91.6 17.6 %copy-start.9 = (bf16[128,512]{1,0:T(8,128)(2,1)S(1)}, bf16[128,512]{1,0:T(8,128)(2,1)}, u32[]{:S(2)}) copy-start(bf16[128,512]{1,0:T(8,128)(2,1)} %get-tuple-element.52.refs_7_) | copy-start | bytes 393220
  91.6 16.5 %collective-permute-start.21 = (bf16[128,512]{1,0:T(8,128)(2,1)S(1)}, bf16[128,512]{1,0:T(8,128)(2,1)S(1)}, u32[]{:S(2)}, u32[]{:S(2)}) collective-permute-start(bf16[128,512]{1,0:T(8,128)(2,1)S(1)} %get-tuple-element.46.refs_8_), channel_id=1, source_target_pairs={{0,0},{4,32},{8,8},{12,40},{16,16},{20,48},{24,24},{28,56},{32,4},... | collective-permute-start | bytes 393224 | tf_op jit(solution)/shard_map/ppermute | solution.py:420
  95.9 12.2 %collective-permute-start.22 = (bf16[128,512]{1,0:T(8,128)(2,1)}, bf16[128,512]{1,0:T(8,128)(2,1)S(1)}, u32[]{:S(2)}, u32[]{:S(2)}) collective-permute-start(bf16[128,512]{1,0:T(8,128)(2,1)} %get-tuple-element.53), channel_id=1, source_target_pairs={{0,8},{4,40},{8,16},{12,48},{16,24},{20,56},{24,0},{28,32},{32,12}... | collective-permute-start | bytes 393224 | tf_op jit(solution)/shard_map/ppermute | solution.py:420
  98.0 10.1 %collective-permute-start.23 = (bf16[128,512]{1,0:T(8,128)(2,1)}, bf16[128,512]{1,0:T(8,128)(2,1)S(1)}, u32[]{:S(2)}, u32[]{:S(2)}) collective-permute-start(bf16[128,512]{1,0:T(8,128)(2,1)} %get-tuple-element.54), channel_id=1, source_target_pairs={{0,16},{4,48},{8,24},{12,56},{16,0},{20,32},{24,8},{28,40},{32,20}... | collective-permute-start | bytes 393224 | tf_op jit(solution)/shard_map/ppermute | solution.py:420
  102.2 7.0 %collective-permute-start.24 = (bf16[128,512]{1,0:T(8,128)(2,1)}, bf16[128,512]{1,0:T(8,128)(2,1)S(1)}, u32[]{:S(2)}, u32[]{:S(2)}) collective-permute-start(bf16[128,512]{1,0:T(8,128)(2,1)} %get-tuple-element.55), channel_id=1, source_target_pairs={{0,24},{4,56},{8,0},{12,32},{16,8},{20,40},{24,16},{28,48},{32,28}... | collective-permute-start | bytes 393224 | tf_op jit(solution)/shard_map/ppermute | solution.py:420

commit v8 on v7

--- a/solution.py
+++ b/solution.py
@@ -281,9 +281,9 @@
 
 def slope_times(half, grads):
     t = jnp.tanh(half)
-    probs = half + half * t
-    slope = (1.0 + t + probs * (1.0 - t)).astype(BF)
-    return probs, grads * slope
+    up = 1.0 + t
+    probs = half * up
+    return probs, grads * (up + probs * (1.0 - t))
 
 
 def hist_dq(info, ga_ref, *refs):

time: 113 us -> 113 us (level)
  no operation moved by 1% of the time
where the time goes in v8:
time: 113 us; the launch traced here: 112 us
  starting transfers between devices  51.5 us (46%)
  Pallas kernels  45.4 us (40%)
  waiting for transfers between devices  8.24 us (7%)
  local copies, waits for them, and re-layouts  5.49 us (5%)
  between operations  1.85 us (2%)
    pallas_call x15, Pallas kernels, run(): got = made(*pinned, *after, *carry)  45.4 us
    ppermute x8, starting transfers between devices, crossed(): return lax.ppermute(value, ('c', 'y', 'xh'), pairs)  26.2 us
    ppermute x8, starting transfers between devices, along(): return lax.ppermute(value, ('c', 'z'), pairs)  9.73 us
    unnamed x23, local copies, waits for them, and re-layouts  5.41 us
    ppermute x6, starting transfers between devices, across(): return lax.ppermute(value, 'c', [(0, 1), (1, 0)])  4.27 us
    all_to_all x1, starting transfers between devices, per_device(): returned = lax.all_to_all(leaving, ('xl', 'xh', 'y'), 0, 0, tiled=True)  4.14 us
    ppermute x8, waiting for transfers between devices, crossed(): return lax.ppermute(value, ('c', 'y', 'xh'), pairs)  3.79 us
    all_to_all x1, starting transfers between devices, per_device(): arrived = lax.all_to_all(sent_cand, ('xl', 'xh', 'y'), 0, 0, tiled=True)  3.69 us
  transfers between devices with their start and end apart: 27, of which 4 were waited for; matrix products, arithmetic and copies ran while one was open for 0% of the time, Pallas kernels for 31%

profile of v8, /device:TPU:1, one launch (start us, length us, event | category | flops | bytes accessed | tf_op | source)
XLA Modules:
  0.0 112.5 jit_solution(3107055619767811539)
XLA Ops:
  1.4 0.1 stack.19.refs_0_
  1.4 4.6 %project_all.1 = (bf16[128,512]{1,0:T(8,128)(2,1)S(1)}, bf16[128,512]{1,0:T(8,128)(2,1)S(1)}, bf16[128,512]{1,0:T(8,128)(2,1)S(1)}, bf16[128,512]{1,0:T(8,128)(2...) custom-call(s32[5]{0:T(128)S(1)} %stack.19.refs_0_, ...), custom_call_target="tpu_custom_call" | custom-call | flops 700000000 | bytes 1048576 | tf_op jit(solution)/shard_map/project_all/pallas_call | solution.py:63
  6.0 6.0 %collective-permute-start = (bf16[128,512]{1,0:T(8,128)(2,1)S(1)}, bf16[128,512]{1,0:T(8,128)(2,1)S(1)}, u32[]{:S(2)}, u32[]{:S(2)}) collective-permute-start(bf16[128,512]{1,0:T(8,128)(2,1)S(1)} %get-tuple-element.33), channel_id=1, source_target_pairs={{0,0},{4,32},{8,8},{12,40},{16,16},{20,48},{24,24},{28,56},{32,4},... | collective-permute-start | bytes 393224 | tf_op jit(solution)/shard_map/ppermute | solution.py:420
  12.1 1.1 collective-permute-start.1
  13.2 5.6 %collective-permute-start.2 = (bf16[128,512]{1,0:T(8,128)(2,1)S(1)}, bf16[128,512]{1,0:T(8,128)(2,1)S(1)}, u32[]{:S(2)}, u32[]{:S(2)}) collective-permute-start(bf16[128,512]{1,0:T(8,128)(2,1)S(1)} %get-tuple-element.35), channel_id=1, source_target_pairs={{0,16},{4,48},{8,24},{12,56},{16,0},{20,32},{24,8},{28,40},{32,20}... | collective-permute-start | bytes 393224 | tf_op jit(solution)/shard_map/ppermute | solution.py:420
  18.7 0.8 collective-permute-start.3
  19.5 0.1 copy.15.refs_0_
  19.7 3.1 %project_cand.1 = (bf16[16,128,128]{2,1,0:T(8,128)(2,1)}, bf16[256,512]{1,0:T(8,128)(2,1)S(1)}) custom-call(s32[256,1]{1,0:T(8,128)S(1)} %copy.15.refs_0_, bf16[256,1024]{1,0:T(8,128)(2,1)S(1)} %copy-done, bf16[1024,2048]{1,0:T(8,128)(2,1)} %refs_5_.1, bf16[4,128,512]{2,1,0:T(8,128)(2,1)S(1)} %get-tuple-element.31.refs_3_), custom_call_target="tpu_custom_call" | custom-call | flops 700000000 | bytes 1048576 | tf_op jit(solution)/shard_map/project_cand/pallas_call | solution.py:63
  22.9 2.6 %collective-permute-done.3.refs_4_ = bf16[128,512]{1,0:T(8,128)(2,1)S(1)} collective-permute-done((bf16[128,512]{1,0:T(8,128)(2,1)S(1)}, bf16[128,512]{1,0:T(8,128)(2,1)S(1)}, u32[]{:S(2)}, u32[]{:S(2)}) %collective-permute-start.3) | collective-permute-done | bytes 131104 | tf_op jit(solution)/shard_map/ppermute | solution.py:420
  25.5 0.6 arrange.1
  26.1 3.8 %collective-permute-start.5 = (bf16[512,384]{1,0:T(8,128)(2,1)S(1)}, bf16[512,384]{1,0:T(8,128)(2,1)}, u32[]{:S(2)}, u32[]{:S(2)}) collective-permute-start(bf16[512,384]{1,0:T(8,128)(2,1)S(1)} %bitcast.7), channel_id=1, source_target_pairs={{0,1},{1,2},{2,3},{3,0},{32,35},{33,32},{34,33},{35,34},{4,5},{5,6... | collective-permute-start | bytes 1179656 | tf_op jit(solution)/shard_map/ppermute | solution.py:433
  30.0 3.7 %all-to-all-start = ((bf16[16,128,128]{2,1,0:T(8,128)(2,1)}), bf16[16,128,128]{2,1,0:T(8,128)(2,1)S(1)}, u32[]{:S(2)}, u32[]{:S(2)}) async-start(bf16[16,128,128]{2,1,0:T(8,128)(2,1)} %get-tuple-element.39), calls=%async_computation | async-start | bytes 1048576 | tf_op jit(solution)/shard_map/all_to_all | solution.py:475
  33.7 1.1 %collective-permute-start.4 = (bf16[512,384]{1,0:T(8,128)(2,1)S(1)}, bf16[512,384]{1,0:T(8,128)(2,1)S(1)}, u32[]{:S(2)}, u32[]{:S(2)}) collective-permute-start(bf16[512,384]{1,0:T(8,128)(2,1)S(1)} %bitcast.9), channel_id=1, source_target_pairs={{0,32},{32,0},{1,33},{33,1},{2,34},{34,2},{3,35},{35,3},{4,36},{36... | collective-permute-start | bytes 1179656 | tf_op jit(solution)/shard_map/ppermute | solution.py:424
  34.8 0.1 collective-permute-start.6
  34.9 3.0 %collective-permute-done.7.refs_5_.refs_6_ = bf16[512,384]{1,0:T(8,128)(2,1)} collective-permute-done((bf16[512,384]{1,0:T(8,128)(2,1)S(1)}, bf16[512,384]{1,0:T(8,128)(2,1)}, u32[]{:S(2)}, u32[]{:S(2)}) %collective-permute-start.7) | collective-permute-done | bytes 393248 | tf_op jit(solution)/shard_map/ppermute | solution.py:433
  37.9 0.4 collective-permute-start.10
  38.3 0.1 collective-permute-start.9
  38.4 1.4 %collective-permute-done.8.refs_6_.refs_7_ = bf16[512,384]{1,0:T(8,128)(2,1)S(1)} collective-permute-done((bf16[512,384]{1,0:T(8,128)(2,1)}, bf16[512,384]{1,0:T(8,128)(2,1)S(1)}, u32[]{:S(2)}, u32[]{:S(2)}) %collective-permute-start.8) | collective-permute-done | bytes 393248 | tf_op jit(solution)/shard_map/ppermute | solution.py:424
  39.8 3.1 %hist_begin.1.refs_7_.refs_8_ = f32[512,128]{1,0:T(8,128)S(1)} custom-call(s32[5]{0:T(128)S(1)} %stack.19.refs_0_, bf16[512,384]{1,0:T(8,128)(2,1)S(1)} %bitcast.10, bf16[512,384]{1,0:T(8,128)(2,1)S(1)} %collective-permute-done.4.refs_2_.refs_3_, bf16[512,384]{1,0:T(8,128)(2,1)} %collective-permute-done.5.refs_3_.refs_4_, ...), custom_call_target="tpu_custom_call" | custom-call | flops 1000 | bytes 1000 | tf_op jit(solution)/shard_map/hist_begin/pallas_call | solution.py:63
  42.9 0.7 copy-done.2
  43.6 0.8 copy-done.4
  44.4 0.7 copy-done.6
  45.2 1.0 copy-done.3
  46.2 1.0 copy-done.5
  47.2 1.0 copy-done.7
  48.2 9.0 %cand_attend.2.refs_9_.refs_3_ = f32[2048,128]{1,0:T(8,128)S(1)} custom-call(bf16[16,128,128]{2,1,0:T(8,128)(2,1)S(1)} %all-to-all-done.refs_0_, bf16[512,384]{1,0:T(8,128)(2,1)S(1)} %bitcast.11, bf16[512,384]{1,0:T(8,128)(2,1)S(1)} %copy-done.3, bf16[512,384]{1,0:T(8,128)(2,1)} %collective-permute-done.5.refs_3_.refs_4_, bf16[512,384]{1,0:T(8,128)(2,1)S(1)} %copy-done.5, ...), custom_call_target="tpu_custom_call" | custom-call | flops 3600000000 | bytes 1048576 | tf_op jit(solution)/shard_map/cand_attend/pallas_call | solution.py:63
  57.2 1.7 %hist_end.1 = (f32[512,128]{1,0:T(8,128)S(1)}, f32[8,512]{1,0:T(8,128)S(1)}) custom-call(s32[5]{0:T(128)S(1)} %stack.19.refs_0_, bf16[128,512]{1,0:T(8,128)(2,1)S(1)} %collective-permute-done.refs_1_, bf16[128,512]{1,0:T(8,128)(2,1)S(1)} %collective-permute-done.1.refs_2_, bf16[128,512]{1,0:T(8,128)(2,1)S(1)} %collective-permute-done.2.refs_3_, ...), custom_call_target="tpu_custom_call" | custom-call | flops 400000000 | bytes 1048576 | tf_op jit(solution)/shard_map/hist_end/pallas_call | solution.py:63
  58.9 0.0 collective-permute-start.11
  59.0 3.5 %collective-permute-start.12 = (f32[8,512]{1,0:T(8,128)S(1)}, f32[8,512]{1,0:T(8,128)S(1)}, u32[]{:S(2)}, u32[]{:S(2)}) collective-permute-start(f32[8,512]{1,0:T(8,128)S(1)} %get-tuple-element.41.refs_4_.refs_6_), channel_id=1, source_target_pairs={{0,16},{8,24},{16,0},{24,8},{1,17},{9,25},{17,1},{25,9},{2,18},{10... | collective-permute-start | bytes 49160 | tf_op jit(solution)/shard_map/ppermute | solution.py:411
  62.5 3.3 %cand_attend.3.refs_10_.refs_3_ = bf16[16,128,128]{2,1,0:T(8,128)(2,1)} custom-call(bf16[16,128,128]{2,1,0:T(8,128)(2,1)S(1)} %all-to-all-done.refs_0_, bf16[512,384]{1,0:T(8,128)(2,1)S(1)} %collective-permute-done.9.refs_6_.refs_1_.refs_8_.refs_4_, bf16[512,384]{1,0:T(8,128)(2,1)S(1)} %collective-permute-done.10.refs_7_.refs_2_.refs_9_.refs_5_, ...), custom_call_target="tpu_custom_call" | custom-call | flops 1200000000 | bytes 1048576 | tf_op jit(solution)/shard_map/cand_attend/pallas_call | solution.py:63
  65.7 1.0 normed_grads.1
  66.8 2.5 %collective-permute-start.15 = (bf16[512,128]{1,0:T(8,128)(2,1)S(1)}, bf16[512,128]{1,0:T(8,128)(2,1)S(1)}, u32[]{:S(2)}, u32[]{:S(2)}) collective-permute-start(bf16[512,128]{1,0:T(8,128)(2,1)S(1)} %get-tuple-element.42.refs_1_.refs_7_), channel_id=1, source_target_pairs={{0,1},{1,2},{2,3},{3,0},{32,35},{33,32},{34,33},{35,34},{4,5},{5,6... | collective-permute-start | bytes 393224 | tf_op jit(solution)/shard_map/ppermute | solution.py:433
  69.2 2.4 %collective-permute-start.14 = (bf16[512,128]{1,0:T(8,128)(2,1)S(1)}, bf16[512,128]{1,0:T(8,128)(2,1)S(1)}, u32[]{:S(2)}, u32[]{:S(2)}) collective-permute-start(bf16[512,128]{1,0:T(8,128)(2,1)S(1)} %get-tuple-element.42.refs_1_.refs_7_), channel_id=1, source_target_pairs={{0,32},{32,0},{1,33},{33,1},{2,34},{34,2},{3,35},{35,3},{4,36},{36... | collective-permute-start | bytes 393224 | tf_op jit(solution)/shard_map/ppermute | solution.py:424
  71.7 4.8 %hist_dq.1.refs_0_.refs_1_ = bf16[4,128,128]{2,1,0:T(8,128)(2,1)S(1)} custom-call(s32[5]{0:T(128)S(1)} %stack.19.refs_0_, bf16[512,128]{1,0:T(8,128)(2,1)S(1)} %get-tuple-element.42.refs_1_.refs_7_, bf16[512,384]{1,0:T(8,128)(2,1)S(1)} %bitcast.13, bf16[512,384]{1,0:T(8,128)(2,1)S(1)} %copy-done.3, bf16[512,384]{1,0:T(8,128)(2,1)} %collective-permute-done.5.refs_3_.refs_4_, ...), custom_call_target="tpu_custom_call" | custom-call | flops 2000000000 | bytes 1048576 | tf_op jit(solution)/shard_map/hist_dq/pallas_call | solution.py:63
  76.5 0.1 collective-permute-start.17
  76.6 0.5 collective-permute-start.18
  77.1 1.4 %collective-permute-start.19 = (bf16[512,128]{1,0:T(8,128)(2,1)S(1)}, bf16[512,128]{1,0:T(8,128)(2,1)S(1)}, u32[]{:S(2)}, u32[]{:S(2)}) collective-permute-start(bf16[512,128]{1,0:T(8,128)(2,1)S(1)} %get-tuple-element.43.refs_9_), channel_id=1, source_target_pairs={{0,1},{1,2},{2,3},{3,0},{32,35},{33,32},{34,33},{35,34},{4,5},{5,6... | collective-permute-start | bytes 393224 | tf_op jit(solution)/shard_map/ppermute | solution.py:433
  78.5 1.5 %collective-permute-start.20 = (bf16[512,128]{1,0:T(8,128)(2,1)S(1)}, bf16[512,128]{1,0:T(8,128)(2,1)S(1)}, u32[]{:S(2)}, u32[]{:S(2)}) collective-permute-start(bf16[512,128]{1,0:T(8,128)(2,1)S(1)} %get-tuple-element.43.refs_9_), channel_id=1, source_target_pairs={{0,33},{1,34},{2,35},{3,32},{32,3},{33,0},{34,1},{35,2},{4,37},{5,... | collective-permute-start | bytes 393224 | tf_op jit(solution)/shard_map/ppermute | solution.py:433
  80.0 4.6 %hist_dkv_begin.1.refs_0_.refs_8_ = f32[2,256,256]{2,1,0:T(8,128)S(1)} custom-call(s32[5]{0:T(128)S(1)} %stack.19.refs_0_, bf16[512,384]{1,0:T(8,128)(2,1)S(1)} %bitcast.14, bf16[512,384]{1,0:T(8,128)(2,1)S(1)} %copy-done.3, bf16[512,384]{1,0:T(8,128)(2,1)} %collective-permute-done.5.refs_3_.refs_4_, bf16[512,384]{1,0:T(8,128)(2,1)S(1)} %copy-done.5, ...), custom_call_target="tpu_custom_call" | custom-call | flops 2000000000 | bytes 1048576 | tf_op jit(solution)/shard_map/hist_dkv_begin/pallas_call | solution.py:63
  84.7 4.1 %all-to-all-start.1 = ((bf16[16,128,128]{2,1,0:T(8,128)(2,1)}), bf16[16,128,128]{2,1,0:T(8,128)(2,1)S(1)}, u32[]{:S(2)}, u32[]{:S(2)}) async-start(bf16[16,128,128]{2,1,0:T(8,128)(2,1)} %relay.3), calls=%async_computation.1 | async-start | bytes 1048576 | tf_op jit(solution)/shard_map/all_to_all | solution.py:522
  88.9 2.7 %hist_dkv_end.1 = (bf16[128,512]{1,0:T(8,128)(2,1)S(1)}, bf16[128,512]{1,0:T(8,128)(2,1)}, bf16[128,512]{1,0:T(8,128)(2,1)}, bf16[128,512]{1,0:T(8,128)(2,1)}) custom-call(s32[5]{0:T(128)S(1)} %stack.19.refs_0_, bf16[4,128,128]{2,1,0:T(8,128)(2,1)S(1)} %hist_dq.1.refs_0_.refs_1_, bf16[512,128]{1,0:T(8,128)(2,1)S(1)} %get-tuple-element.45.refs_2_, ...), custom_call_target="tpu_custom_call" | custom-call | flops 800000000 | bytes 1048576 | tf_op jit(solution)/shard_map/hist_dkv_end/pallas_call | solution.py:63
  91.5 4.3 %collective-permute-start.21 = (bf16[128,512]{1,0:T(8,128)(2,1)S(1)}, bf16[128,512]{1,0:T(8,128)(2,1)S(1)}, u32[]{:S(2)}, u32[]{:S(2)}) collective-permute-start(bf16[128,512]{1,0:T(8,128)(2,1)S(1)} %get-tuple-element.46.refs_8_), channel_id=1, source_target_pairs={{0,0},{4,32},{8,8},{12,40},{16,16},{20,48},{24,24},{28,56},{32,4},... | collective-permute-start | bytes 393224 | tf_op jit(solution)/shard_map/ppermute | solution.py:420
  95.8 2.1 %collective-permute-start.22 = (bf16[128,512]{1,0:T(8,128)(2,1)}, bf16[128,512]{1,0:T(8,128)(2,1)S(1)}, u32[]{:S(2)}, u32[]{:S(2)}) collective-permute-start(bf16[128,512]{1,0:T(8,128)(2,1)} %get-tuple-element.53), channel_id=1, source_target_pairs={{0,8},{4,40},{8,16},{12,48},{16,24},{20,56},{24,0},{28,32},{32,12}... | collective-permute-start | bytes 393224 | tf_op jit(solution)/shard_map/ppermute | solution.py:420
  98.0 4.2 %collective-permute-start.23 = (bf16[128,512]{1,0:T(8,128)(2,1)}, bf16[128,512]{1,0:T(8,128)(2,1)S(1)}, u32[]{:S(2)}, u32[]{:S(2)}) collective-permute-start(bf16[128,512]{1,0:T(8,128)(2,1)} %get-tuple-element.54), channel_id=1, source_target_pairs={{0,16},{4,48},{8,24},{12,56},{16,0},{20,32},{24,8},{28,40},{32,20}... | collective-permute-start | bytes 393224 | tf_op jit(solution)/shard_map/ppermute | solution.py:420
  102.1 2.1 %collective-permute-start.24 = (bf16[128,512]{1,0:T(8,128)(2,1)}, bf16[128,512]{1,0:T(8,128)(2,1)S(1)}, u32[]{:S(2)}, u32[]{:S(2)}) collective-permute-start(bf16[128,512]{1,0:T(8,128)(2,1)} %get-tuple-element.55), channel_id=1, source_target_pairs={{0,24},{4,56},{8,0},{12,32},{16,8},{20,40},{24,16},{28,48},{32,28}... | collective-permute-start | bytes 393224 | tf_op jit(solution)/shard_map/ppermute | solution.py:420
  104.2 3.8 %cand_close.1 = (bf16[256,1024]{1,0:T(8,128)(2,1)}, bf16[512,1024]{1,0:T(8,128)(2,1)S(1)}, bf16[4,1024,512]{2,1,0:T(8,128)(2,1)S(1)}, bf16[128,1024]{1,0:T(8,128)(2,1)S(1)}, bf16[128,1024]{1,0:T(8,128)(2,1)S(1)}) custom-call(s32[256,1]{1,0:T(8,128)S(1)} %copy.15.refs_0_, bf16[256,512]{1,0:T(8,128)(2,1)} %copy-done.1, ...), custom_call_target="tpu_custom_call" | custom-call | flops 400000000 | bytes 1048576 | tf_op jit(solution)/shard_map/cand_close/pallas_call | solution.py:63
  108.0 1.1 collective-permute-done.24.refs_11_
  109.2 3.1 %hist_close.1 = (bf16[1,128,1024]{2,1,0:T(8,128)(2,1)}, bf16[1,128,1024]{2,1,0:T(8,128)(2,1)}) custom-call(s32[5]{0:T(128)S(1)} %stack.19.refs_0_, bf16[128,1024]{1,0:T(8,128)(2,1)S(1)} %get-tuple-element.47.refs_1_, bf16[128,1024]{1,0:T(8,128)(2,1)S(1)} %get-tuple-element.48.refs_2_, bf16[4,128,512]{2,1,0:T(8,128)(2,1)S(1)} %get-tuple-element.31.refs_3_, ...), custom_call_target="tpu_custom_call" | custom-call | flops 700000000 | bytes 1048576 | tf_op jit(solution)/shard_map/hist_close/pallas_call | solution.py:63
  (45 shorter events, 0.1 us)
Async XLA Ops:
  0.6 18.9 %copy-start.10 = (s32[256,1]{0,1:T(1,128)S(1)}, s32[256,1]{0,1:T(1,128)}, u32[]{:S(2)}) copy-start(s32[256,1]{0,1:T(1,128)} %param.10) | copy-start | bytes 3076
  0.6 19.1 %copy-start = (bf16[256,1024]{1,0:T(8,128)(2,1)S(1)}, bf16[256,1024]{1,0:T(8,128)(2,1)}, u32[]{:S(2)}) copy-start(bf16[256,1024]{1,0:T(8,128)(2,1)} %refs_3_.3) | copy-start | bytes 1572868
  6.0 16.9 %collective-permute-start = (bf16[128,512]{1,0:T(8,128)(2,1)S(1)}, bf16[128,512]{1,0:T(8,128)(2,1)S(1)}, u32[]{:S(2)}, u32[]{:S(2)}) collective-permute-start(bf16[128,512]{1,0:T(8,128)(2,1)S(1)} %get-tuple-element.33), channel_id=1, source_target_pairs={{0,0},{4,32},{8,8},{12,40},{16,16},{20,48},{24,24},{28,56},{32,4},... | collective-permute-start | bytes 393224 | tf_op jit(solution)/shard_map/ppermute | solution.py:420
  12.1 10.8 %collective-permute-start.1 = (bf16[128,512]{1,0:T(8,128)(2,1)S(1)}, bf16[128,512]{1,0:T(8,128)(2,1)S(1)}, u32[]{:S(2)}, u32[]{:S(2)}) collective-permute-start(bf16[128,512]{1,0:T(8,128)(2,1)S(1)} %get-tuple-element.34), channel_id=1, source_target_pairs={{0,8},{4,40},{8,16},{12,48},{16,24},{20,56},{24,0},{28,32},{32,12}... | collective-permute-start | bytes 393224 | tf_op jit(solution)/shard_map/ppermute | solution.py:420
  13.2 9.7 %collective-permute-start.2 = (bf16[128,512]{1,0:T(8,128)(2,1)S(1)}, bf16[128,512]{1,0:T(8,128)(2,1)S(1)}, u32[]{:S(2)}, u32[]{:S(2)}) collective-permute-start(bf16[128,512]{1,0:T(8,128)(2,1)S(1)} %get-tuple-element.35), channel_id=1, source_target_pairs={{0,16},{4,48},{8,24},{12,56},{16,0},{20,32},{24,8},{28,40},{32,20}... | collective-permute-start | bytes 393224 | tf_op jit(solution)/shard_map/ppermute | solution.py:420
  18.7 6.8 %collective-permute-start.3 = (bf16[128,512]{1,0:T(8,128)(2,1)S(1)}, bf16[128,512]{1,0:T(8,128)(2,1)S(1)}, u32[]{:S(2)}, u32[]{:S(2)}) collective-permute-start(bf16[128,512]{1,0:T(8,128)(2,1)S(1)} %get-tuple-element.36), channel_id=1, source_target_pairs={{0,24},{4,56},{8,0},{12,32},{16,8},{20,40},{24,16},{28,48},{32,28}... | collective-permute-start | bytes 393224 | tf_op jit(solution)/shard_map/ppermute | solution.py:420
  22.9 34.3 %copy-start.1 = (bf16[256,512]{1,0:T(8,128)(2,1)}, bf16[256,512]{1,0:T(8,128)(2,1)S(1)}, u32[]{:S(2)}) copy-start(bf16[256,512]{1,0:T(8,128)(2,1)S(1)} %get-tuple-element.32.refs_5_.refs_1_) | copy-start | bytes 786436
  26.1 8.7 %collective-permute-start.5 = (bf16[512,384]{1,0:T(8,128)(2,1)S(1)}, bf16[512,384]{1,0:T(8,128)(2,1)}, u32[]{:S(2)}, u32[]{:S(2)}) collective-permute-start(bf16[512,384]{1,0:T(8,128)(2,1)S(1)} %bitcast.7), channel_id=1, source_target_pairs={{0,1},{1,2},{2,3},{3,0},{32,35},{33,32},{34,33},{35,34},{4,5},{5,6... | collective-permute-start | bytes 1179656 | tf_op jit(solution)/shard_map/ppermute | solution.py:433
  30.0 7.9 %collective-permute-start.7 = (bf16[512,384]{1,0:T(8,128)(2,1)S(1)}, bf16[512,384]{1,0:T(8,128)(2,1)}, u32[]{:S(2)}, u32[]{:S(2)}) collective-permute-start(bf16[512,384]{1,0:T(8,128)(2,1)S(1)} %bitcast.8), channel_id=1, source_target_pairs={{0,3},{1,0},{2,1},{3,2},{32,33},{33,34},{34,35},{35,32},{4,7},{5,4... | collective-permute-start | bytes 1179656 | tf_op jit(solution)/shard_map/ppermute | solution.py:433
  30.0 15.2 %all-to-all-start = ((bf16[16,128,128]{2,1,0:T(8,128)(2,1)}), bf16[16,128,128]{2,1,0:T(8,128)(2,1)S(1)}, u32[]{:S(2)}, u32[]{:S(2)}) async-start(bf16[16,128,128]{2,1,0:T(8,128)(2,1)} %get-tuple-element.39), calls=%async_computation | async-start | bytes 1048576 | tf_op jit(solution)/shard_map/all_to_all | solution.py:475
  33.7 4.8 %collective-permute-start.4 = (bf16[512,384]{1,0:T(8,128)(2,1)S(1)}, bf16[512,384]{1,0:T(8,128)(2,1)S(1)}, u32[]{:S(2)}, u32[]{:S(2)}) collective-permute-start(bf16[512,384]{1,0:T(8,128)(2,1)S(1)} %bitcast.9), channel_id=1, source_target_pairs={{0,32},{32,0},{1,33},{33,1},{2,34},{34,2},{3,35},{35,3},{4,36},{36... | collective-permute-start | bytes 1179656 | tf_op jit(solution)/shard_map/ppermute | solution.py:424
  34.8 3.6 %collective-permute-start.6 = (bf16[512,384]{1,0:T(8,128)(2,1)}, bf16[512,384]{1,0:T(8,128)(2,1)S(1)}, u32[]{:S(2)}, u32[]{:S(2)}) collective-permute-start(bf16[512,384]{1,0:T(8,128)(2,1)} %collective-permute-done.5.refs_3_.refs_4_), channel_id=1, source_target_pairs={{0,32},{32,0},{1,33},{33,1},{2,34},{34,2},{3,35},{35,3},{4,36},{36... | collective-permute-start | bytes 1179656 | tf_op jit(solution)/shard_map/ppermute | solution.py:424
  37.9 1.9 %collective-permute-start.8 = (bf16[512,384]{1,0:T(8,128)(2,1)}, bf16[512,384]{1,0:T(8,128)(2,1)S(1)}, u32[]{:S(2)}, u32[]{:S(2)}) collective-permute-start(bf16[512,384]{1,0:T(8,128)(2,1)} %collective-permute-done.7.refs_5_.refs_6_), channel_id=1, source_target_pairs={{0,32},{32,0},{1,33},{33,1},{2,34},{34,2},{3,35},{35,3},{4,36},{36... | collective-permute-start | bytes 1179656 | tf_op jit(solution)/shard_map/ppermute | solution.py:424
  37.9 19.3 %collective-permute-start.10 = (bf16[512,384]{1,0:T(8,128)(2,1)}, bf16[512,384]{1,0:T(8,128)(2,1)S(1)}, u32[]{:S(2)}, u32[]{:S(2)}) collective-permute-start(bf16[512,384]{1,0:T(8,128)(2,1)} %collective-permute-done.5.refs_3_.refs_4_), channel_id=1, source_target_pairs={{0,33},{1,34},{2,35},{3,32},{32,3},{33,0},{34,1},{35,2},{4,37},{5,... | collective-permute-start | bytes 1179656 | tf_op jit(solution)/shard_map/ppermute | solution.py:433
  38.3 18.9 %collective-permute-start.9 = (bf16[512,384]{1,0:T(8,128)(2,1)}, bf16[512,384]{1,0:T(8,128)(2,1)S(1)}, u32[]{:S(2)}, u32[]{:S(2)}) collective-permute-start(bf16[512,384]{1,0:T(8,128)(2,1)} %collective-permute-done.5.refs_3_.refs_4_), channel_id=1, source_target_pairs={{0,1},{1,2},{2,3},{3,0},{32,35},{33,32},{34,33},{35,34},{4,5},{5,6... | collective-permute-start | bytes 1179656 | tf_op jit(solution)/shard_map/ppermute | solution.py:433
  42.9 0.7 copy-start.2
  43.6 0.8 copy-start.4
  44.4 0.7 copy-start.6
  45.2 1.0 copy-start.3
  46.2 1.0 copy-start.5
  47.2 1.0 copy-start.7
  58.9 6.8 %collective-permute-start.11 = (f32[8,512]{1,0:T(8,128)S(1)}, f32[8,512]{1,0:T(8,128)S(1)}, u32[]{:S(2)}, u32[]{:S(2)}) collective-permute-start(f32[8,512]{1,0:T(8,128)S(1)} %get-tuple-element.41.refs_4_.refs_6_), channel_id=1, source_target_pairs={{0,8},{8,16},{16,24},{24,0},{1,9},{9,17},{17,25},{25,1},{2,10},{10... | collective-permute-start | bytes 49160 | tf_op jit(solution)/shard_map/ppermute | solution.py:411
  59.0 6.7 %collective-permute-start.12 = (f32[8,512]{1,0:T(8,128)S(1)}, f32[8,512]{1,0:T(8,128)S(1)}, u32[]{:S(2)}, u32[]{:S(2)}) collective-permute-start(f32[8,512]{1,0:T(8,128)S(1)} %get-tuple-element.41.refs_4_.refs_6_), channel_id=1, source_target_pairs={{0,16},{8,24},{16,0},{24,8},{1,17},{9,25},{17,1},{25,9},{2,18},{10... | collective-permute-start | bytes 49160 | tf_op jit(solution)/shard_map/ppermute | solution.py:411
  62.4 3.3 %collective-permute-start.13 = (f32[8,512]{1,0:T(8,128)S(1)}, f32[8,512]{1,0:T(8,128)S(1)}, u32[]{:S(2)}, u32[]{:S(2)}) collective-permute-start(f32[8,512]{1,0:T(8,128)S(1)} %get-tuple-element.41.refs_4_.refs_6_), channel_id=1, source_target_pairs={{0,24},{8,0},{16,8},{24,16},{1,25},{9,1},{17,9},{25,17},{2,26},{10... | collective-permute-start | bytes 49160 | tf_op jit(solution)/shard_map/ppermute | solution.py:411
  66.8 9.7 %collective-permute-start.15 = (bf16[512,128]{1,0:T(8,128)(2,1)S(1)}, bf16[512,128]{1,0:T(8,128)(2,1)S(1)}, u32[]{:S(2)}, u32[]{:S(2)}) collective-permute-start(bf16[512,128]{1,0:T(8,128)(2,1)S(1)} %get-tuple-element.42.refs_1_.refs_7_), channel_id=1, source_target_pairs={{0,1},{1,2},{2,3},{3,0},{32,35},{33,32},{34,33},{35,34},{4,5},{5,6... | collective-permute-start | bytes 393224 | tf_op jit(solution)/shard_map/ppermute | solution.py:433
  69.2 7.3 %collective-permute-start.16 = (bf16[512,128]{1,0:T(8,128)(2,1)S(1)}, bf16[512,128]{1,0:T(8,128)(2,1)S(1)}, u32[]{:S(2)}, u32[]{:S(2)}) collective-permute-start(bf16[512,128]{1,0:T(8,128)(2,1)S(1)} %get-tuple-element.42.refs_1_.refs_7_), channel_id=1, source_target_pairs={{0,3},{1,0},{2,1},{3,2},{32,33},{33,34},{34,35},{35,32},{4,7},{5,4... | collective-permute-start | bytes 393224 | tf_op jit(solution)/shard_map/ppermute | solution.py:433
  69.2 10.8 %collective-permute-start.14 = (bf16[512,128]{1,0:T(8,128)(2,1)S(1)}, bf16[512,128]{1,0:T(8,128)(2,1)S(1)}, u32[]{:S(2)}, u32[]{:S(2)}) collective-permute-start(bf16[512,128]{1,0:T(8,128)(2,1)S(1)} %get-tuple-element.42.refs_1_.refs_7_), channel_id=1, source_target_pairs={{0,32},{32,0},{1,33},{33,1},{2,34},{34,2},{3,35},{35,3},{4,36},{36... | collective-permute-start | bytes 393224 | tf_op jit(solution)/shard_map/ppermute | solution.py:424
  76.5 3.5 %collective-permute-start.17 = (bf16[512,128]{1,0:T(8,128)(2,1)S(1)}, bf16[512,128]{1,0:T(8,128)(2,1)S(1)}, u32[]{:S(2)}, u32[]{:S(2)}) collective-permute-start(bf16[512,128]{1,0:T(8,128)(2,1)S(1)} %get-tuple-element.43.refs_9_), channel_id=1, source_target_pairs={{0,32},{32,0},{1,33},{33,1},{2,34},{34,2},{3,35},{35,3},{4,36},{36... | collective-permute-start | bytes 393224 | tf_op jit(solution)/shard_map/ppermute | solution.py:424
  76.6 3.4 %collective-permute-start.18 = (bf16[512,128]{1,0:T(8,128)(2,1)S(1)}, bf16[512,128]{1,0:T(8,128)(2,1)S(1)}, u32[]{:S(2)}, u32[]{:S(2)}) collective-permute-start(bf16[512,128]{1,0:T(8,128)(2,1)S(1)} %get-tuple-element.44.refs_11_), channel_id=1, source_target_pairs={{0,32},{32,0},{1,33},{33,1},{2,34},{34,2},{3,35},{35,3},{4,36},{36... | collective-permute-start | bytes 393224 | tf_op jit(solution)/shard_map/ppermute | solution.py:424
  77.1 7.6 %collective-permute-start.19 = (bf16[512,128]{1,0:T(8,128)(2,1)S(1)}, bf16[512,128]{1,0:T(8,128)(2,1)S(1)}, u32[]{:S(2)}, u32[]{:S(2)}) collective-permute-start(bf16[512,128]{1,0:T(8,128)(2,1)S(1)} %get-tuple-element.43.refs_9_), channel_id=1, source_target_pairs={{0,1},{1,2},{2,3},{3,0},{32,35},{33,32},{34,33},{35,34},{4,5},{5,6... | collective-permute-start | bytes 393224 | tf_op jit(solution)/shard_map/ppermute | solution.py:433
  78.5 6.2 %collective-permute-start.20 = (bf16[512,128]{1,0:T(8,128)(2,1)S(1)}, bf16[512,128]{1,0:T(8,128)(2,1)S(1)}, u32[]{:S(2)}, u32[]{:S(2)}) collective-permute-start(bf16[512,128]{1,0:T(8,128)(2,1)S(1)} %get-tuple-element.43.refs_9_), channel_id=1, source_target_pairs={{0,33},{1,34},{2,35},{3,32},{32,3},{33,0},{34,1},{35,2},{4,37},{5,... | collective-permute-start | bytes 393224 | tf_op jit(solution)/shard_map/ppermute | solution.py:433
  84.7 19.5 %all-to-all-start.1 = ((bf16[16,128,128]{2,1,0:T(8,128)(2,1)}), bf16[16,128,128]{2,1,0:T(8,128)(2,1)S(1)}, u32[]{:S(2)}, u32[]{:S(2)}) async-start(bf16[16,128,128]{2,1,0:T(8,128)(2,1)} %relay.3), calls=%async_computation.1 | async-start | bytes 1048576 | tf_op jit(solution)/shard_map/all_to_all | solution.py:522
  91.5 17.6 %copy-start.8 = (bf16[128,512]{1,0:T(8,128)(2,1)S(1)}, bf16[128,512]{1,0:T(8,128)(2,1)}, u32[]{:S(2)}) copy-start(bf16[128,512]{1,0:T(8,128)(2,1)} %get-tuple-element.51.refs_6_) | copy-start | bytes 393220
  91.5 17.6 %copy-start.9 = (bf16[128,512]{1,0:T(8,128)(2,1)S(1)}, bf16[128,512]{1,0:T(8,128)(2,1)}, u32[]{:S(2)}) copy-start(bf16[128,512]{1,0:T(8,128)(2,1)} %get-tuple-element.52.refs_7_) | copy-start | bytes 393220
  91.5 16.5 %collective-permute-start.21 = (bf16[128,512]{1,0:T(8,128)(2,1)S(1)}, bf16[128,512]{1,0:T(8,128)(2,1)S(1)}, u32[]{:S(2)}, u32[]{:S(2)}) collective-permute-start(bf16[128,512]{1,0:T(8,128)(2,1)S(1)} %get-tuple-element.46.refs_8_), channel_id=1, source_target_pairs={{0,0},{4,32},{8,8},{12,40},{16,16},{20,48},{24,24},{28,56},{32,4},... | collective-permute-start | bytes 393224 | tf_op jit(solution)/shard_map/ppermute | solution.py:420
  95.8 12.2 %collective-permute-start.22 = (bf16[128,512]{1,0:T(8,128)(2,1)}, bf16[128,512]{1,0:T(8,128)(2,1)S(1)}, u32[]{:S(2)}, u32[]{:S(2)}) collective-permute-start(bf16[128,512]{1,0:T(8,128)(2,1)} %get-tuple-element.53), channel_id=1, source_target_pairs={{0,8},{4,40},{8,16},{12,48},{16,24},{20,56},{24,0},{28,32},{32,12}... | collective-permute-start | bytes 393224 | tf_op jit(solution)/shard_map/ppermute | solution.py:420
  98.0 10.1 %collective-permute-start.23 = (bf16[128,512]{1,0:T(8,128)(2,1)}, bf16[128,512]{1,0:T(8,128)(2,1)S(1)}, u32[]{:S(2)}, u32[]{:S(2)}) collective-permute-start(bf16[128,512]{1,0:T(8,128)(2,1)} %get-tuple-element.54), channel_id=1, source_target_pairs={{0,16},{4,48},{8,24},{12,56},{16,0},{20,32},{24,8},{28,40},{32,20}... | collective-permute-start | bytes 393224 | tf_op jit(solution)/shard_map/ppermute | solution.py:420
  102.1 7.0 %collective-permute-start.24 = (bf16[128,512]{1,0:T(8,128)(2,1)}, bf16[128,512]{1,0:T(8,128)(2,1)S(1)}, u32[]{:S(2)}, u32[]{:S(2)}) collective-permute-start(bf16[128,512]{1,0:T(8,128)(2,1)} %get-tuple-element.55), channel_id=1, source_target_pairs={{0,24},{4,56},{8,0},{12,32},{16,8},{20,40},{24,16},{28,48},{32,28}... | collective-permute-start | bytes 393224 | tf_op jit(solution)/shard_map/ppermute | solution.py:420
